TPU v7x, 32 devices: a whole 2x2x4 slice. The times are simulated.
32 devices in a mesh: gx: 16 (over z, y, x), ta: 2 (over core).
Axes of the slice: x: 2, y: 2, z: 4, core: 2. Of those that a mesh axis runs over, the one named last changes fastest.
Arguments:
- query_vecs: bfloat16 [256, 16, 5120], P('gx', None, 'ta'), may hold values from -32 to 32
- key_vecs: bfloat16 [256, 16, 5120], P('gx', None, 'ta'), may hold values from -6 to 6
- value_vecs: bfloat16 [256, 16, 5120], P('gx', None, 'ta'), may hold values from -6 to 6
- slot_map: int32 [16, 16], replicated, may hold values from 0 to 15, each once within a row
- edge_list: int32 [64, 2], replicated, may hold values from 0 to 15
- edge_types: int32 [64], replicated, may hold values from 0 to 2
- type_gain: float32 [2, 3, 5120], P(None, None, 'ta'), may hold values from 0.25 to 2
- norm_gain: float32 [2, 5120], P(None, 'ta'), may hold values from 0.5 to 2
- gate_proj: bfloat16 [2, 5120, 20480], P(None, 'ta', 'gx'), may hold values from -0.078125 to 0.078125
- up_proj: bfloat16 [2, 5120, 20480], P(None, 'ta', 'gx'), may hold values from -0.078125 to 0.078125
- down_proj: bfloat16 [2, 20480, 5120], P(None, 'gx', 'ta'), may hold values from -0.0390625 to 0.0390625
Outputs:
- node_states: bfloat16 [128, 5120], P('gx', 'ta')
All inputs are finite; a program needn't handle non-finite values.
Results may differ from a plain program's by a relative error of at most 0.04.
Values may be sent and summed in bfloat16 or wider, within the bound.
No kernel may reach another device: no remote copies, remote signals or barrier semaphores. Data moves between devices by JAX's collectives and lax.ppermute only.
A program may use at most 128 MiB of HBM per device.

v0:
```python
import jax
import jax.numpy as jnp
from jax import lax
from jax.sharding import PartitionSpec as P

D = 5120
HEAD_DIM = 128
VENUES = 16
STEPS = 16
NODE_STEPS = 8
ROUNDS = 2
ETYPES = 3


def settle_rows(nodes, hidden, down_local, row_begin, rows_dev):
    summed = lax.psum_scatter(
        jnp.dot(hidden, down_local, preferred_element_type=jnp.float32),
        "gx",
        scatter_dimension=0,
        tiled=True,
    )
    base_rows = lax.dynamic_slice_in_dim(nodes, row_begin, rows_dev, 0)
    return (base_rows.astype(jnp.float32) + summed).astype(jnp.bfloat16)


def per_device(
    query_vecs,
    key_vecs,
    value_vecs,
    slot_map,
    edge_list,
    edge_types,
    type_gain,
    norm_gain,
    gate_proj,
    up_proj,
    down_proj,
):
    pairs_dev = query_vecs.shape[0]
    inst_total = query_vecs.shape[1]
    feat_width = query_vecs.shape[2]
    head_count = feat_width // HEAD_DIM
    gx_count = lax.axis_size("gx")
    inst_local = inst_total // gx_count
    score_scale = 1.0 / HEAD_DIM**0.5
    venue_idx = lax.axis_index("gx") * pairs_dev // STEPS
    slot_order = lax.dynamic_index_in_dim(slot_map, venue_idx, 0, keepdims=False)
    split_shape = (pairs_dev, gx_count, inst_local, feat_width)
    sorted_queries = jnp.take(query_vecs, slot_order, axis=1).reshape(split_shape)
    sorted_keys = jnp.take(key_vecs, slot_order, axis=1).reshape(split_shape)
    sorted_values = jnp.take(value_vecs, slot_order, axis=1).reshape(split_shape)
    query_steps = jnp.arange(VENUES * NODE_STEPS) % NODE_STEPS + (STEPS - NODE_STEPS)
    key_steps = jnp.arange(VENUES * STEPS) % STEPS
    allowed = key_steps[None, :] <= query_steps[:, None]
    queries = lax.all_to_all(sorted_queries, "gx", split_axis=1, concat_axis=0, tiled=True)
    keyset = lax.all_to_all(sorted_keys, "gx", split_axis=1, concat_axis=0, tiled=True)
    valueset = lax.all_to_all(sorted_values, "gx", split_axis=1, concat_axis=0, tiled=True)
    pair_total = queries.shape[0]
    item_count = queries.shape[2]
    queries = queries.reshape(VENUES, STEPS, item_count, head_count, HEAD_DIM)[
        :, STEPS - NODE_STEPS :
    ]
    queries = queries.reshape(VENUES * NODE_STEPS, item_count, head_count, HEAD_DIM)
    keyset = keyset.reshape(pair_total, item_count, head_count, HEAD_DIM)
    valueset = valueset.reshape(pair_total, item_count, head_count, HEAD_DIM)
    scores = (
        jnp.einsum("qnhd,knhd->nhqk", queries, keyset, preferred_element_type=jnp.float32)
        * score_scale
    )
    scores = jnp.where(allowed[None, None], scores, jnp.float32(-1e30))
    row_max = jnp.max(scores, axis=-1, keepdims=True)
    expd = jnp.exp(scores - row_max)
    probs = (expd / jnp.sum(expd, axis=-1, keepdims=True)).astype(jnp.bfloat16)
    attended = jnp.einsum("nhqk,knhd->nqhd", probs, valueset, preferred_element_type=jnp.float32)
    attended = attended.reshape(item_count, VENUES, NODE_STEPS, feat_width)
    pooled = jnp.mean(attended, axis=1).astype(jnp.bfloat16)
    own_rows = pooled.reshape(inst_local * NODE_STEPS, feat_width)
    rows_dev = own_rows.shape[0]
    row_begin = lax.axis_index("gx") * rows_dev
    nodes = lax.all_gather(own_rows, "gx", axis=0, tiled=True)
    row_total = nodes.shape[0]
    node_ids = jnp.arange(inst_total)
    type_ids = jnp.arange(ETYPES)
    at_source = (edge_list[:, 0][:, None] == node_ids[None, :]).astype(jnp.float32)
    at_target = (edge_list[:, 1][:, None] == node_ids[None, :]).astype(jnp.float32)
    of_type = (edge_types[:, None] == type_ids[None, :]).astype(jnp.float32)
    adjacency = jnp.einsum("et,ei,ej->tij", of_type, at_target, at_source)
    degree = jnp.maximum(jnp.sum(at_target, axis=0), 1.0)
    adj_rows = adjacency.reshape(ETYPES * inst_total, inst_total).astype(jnp.bfloat16)
    for layer_idx in range(ROUNDS):
        flat_nodes = nodes.reshape(inst_total, NODE_STEPS * feat_width)
        gathered = jnp.dot(adj_rows, flat_nodes, preferred_element_type=jnp.float32)
        gathered = gathered.reshape(ETYPES, inst_total, NODE_STEPS, feat_width)
        message = (
            jnp.sum(gathered * type_gain[layer_idx][:, None, None, :], axis=0)
            / degree[:, None, None]
        )
        pre_norm = nodes.astype(jnp.float32) + message.reshape(row_total, feat_width)
        squares = lax.psum(jnp.sum(pre_norm * pre_norm, axis=-1), "ta")
        row_scale = lax.rsqrt(squares / D + 1e-05)[:, None]
        normed = (pre_norm * row_scale * norm_gain[layer_idx][None, :]).astype(jnp.bfloat16)
        gate_part = jnp.dot(normed, gate_proj[layer_idx], preferred_element_type=jnp.float32)
        up_part = jnp.dot(normed, up_proj[layer_idx], preferred_element_type=jnp.float32)
        gate_sum, up_sum = (
            lax.psum(gate_part.astype(jnp.bfloat16), "ta").astype(jnp.float32),
            lax.psum(up_part.astype(jnp.bfloat16), "ta").astype(jnp.float32),
        )
        hidden = (jax.nn.silu(gate_sum) * up_sum).astype(jnp.bfloat16)
        down_local = down_proj[layer_idx]
        if layer_idx == ROUNDS - 1:
            own_rows = settle_rows(nodes, hidden, down_local, row_begin, rows_dev)
        else:
            own_rows = settle_rows(nodes, hidden, down_local, row_begin, rows_dev)
            nodes = lax.all_gather(own_rows, "gx", axis=0, tiled=True)
    return own_rows


def solution(mesh):
    placed = (
        P("gx", None, "ta"),
        P("gx", None, "ta"),
        P("gx", None, "ta"),
        P(),
        P(),
        P(),
        P(None, None, "ta"),
        P(None, "ta"),
        P(None, "ta", "gx"),
        P(None, "ta", "gx"),
        P(None, "gx", "ta"),
    )
    return jax.shard_map(
        per_device, mesh=mesh, in_specs=placed, out_specs=P("gx", "ta"), check_vma=False
    )
```

profile of v0, /device:TPU:0, one launch (start us, length us, event | category | flops | bytes accessed | tf_op | source)
XLA Modules:
  0.0 472.4 jit_solution(14825802463736453189)
XLA Ops:
  7.9 5.4 %gather_fusion = bf16[16,16,2560]{2,0,1:T(8,128)(2,1)} fusion(bf16[16,16,2560]{2,1,0:T(8,128)(2,1)S(1)} %copy-done, s32[1024]{0:T(1024)S(1)} %pad_clamp_fusion), kind=kCustom, calls=%fused_computation.clone | custom fusion | bytes 2621504 | tf_op jit(solution)/shard_map/jit(_take)/gather | solution.py:51
  13.3 5.4 %gather_fusion.1 = bf16[16,16,2560]{2,0,1:T(8,128)(2,1)} fusion(bf16[16,16,2560]{2,1,0:T(8,128)(2,1)S(1)} %copy-done.2, s32[1024]{0:T(1024)S(1)} %pad_clamp_fusion), kind=kCustom, calls=%fused_computation.1.clone | custom fusion | bytes 2621504 | tf_op jit(solution)/shard_map/jit(_take)/gather | solution.py:49
  18.6 5.4 %gather_fusion.2 = bf16[16,16,2560]{2,0,1:T(8,128)(2,1)} fusion(bf16[16,16,2560]{2,1,0:T(8,128)(2,1)S(1)} %copy-done.3, s32[1024]{0:T(1024)S(1)} %pad_clamp_fusion), kind=kCustom, calls=%fused_computation.2.clone | custom fusion | bytes 2621504 | tf_op jit(solution)/shard_map/jit(_take)/gather | solution.py:50
  24.0 3.6 select_bitcast_fusion.1
  27.6 1.8 copy.24
  29.4 8.4 %all-to-all-start.1 = ((bf16[16,16,1,2560]{3,0,2,1:T(8,128)(2,1)}), bf16[16,16,1,2560]{3,0,2,1:T(8,128)(2,1)S(1)}, u32[]{:S(2)}, u32[]{:S(2)}) async-start(bf16[16,16,1,2560]{3,0,2,1:T(8,128)(2,1)} %copy.24), calls=%async_computation.1 | async-start | bytes 2621440 | tf_op jit(solution)/shard_map/all_to_all | solution.py:55
  37.9 1.8 copy.26
  39.7 27.7 %all-to-all-done.1 = bf16[16,16,1,2560]{3,0,2,1:T(8,128)(2,1)S(1)} async-done(((bf16[16,16,1,2560]{3,0,2,1:T(8,128)(2,1)}), bf16[16,16,1,2560]{3,0,2,1:T(8,128)(2,1)S(1)}, u32[]{:S(2)}, u32[]{:S(2)}) %all-to-all-start.1) | async-done | bytes 1310752 | tf_op jit(solution)/shard_map/all_to_all | solution.py:55
  67.3 6.6 %all-to-all-start.2 = ((bf16[16,16,1,2560]{3,0,2,1:T(8,128)(2,1)}), bf16[16,16,1,2560]{3,0,2,1:T(8,128)(2,1)S(1)}, u32[]{:S(2)}, u32[]{:S(2)}) async-start(bf16[16,16,1,2560]{3,0,2,1:T(8,128)(2,1)} %copy.26), calls=%async_computation.2 | async-start | bytes 2621440 | tf_op jit(solution)/shard_map/all_to_all | solution.py:56
  73.9 3.1 copy.23
  77.1 25.3 %all-to-all-done.2 = bf16[16,16,1,2560]{3,0,2,1:T(8,128)(2,1)S(1)} async-done(((bf16[16,16,1,2560]{3,0,2,1:T(8,128)(2,1)}), bf16[16,16,1,2560]{3,0,2,1:T(8,128)(2,1)S(1)}, u32[]{:S(2)}, u32[]{:S(2)}) %all-to-all-start.2) | async-done | bytes 1310752 | tf_op jit(solution)/shard_map/all_to_all | solution.py:56
  102.4 6.4 %all-to-all-start = ((bf16[16,16,1,2560]{3,0,2,1:T(8,128)(2,1)}), bf16[16,16,1,2560]{3,0,2,1:T(8,128)(2,1)}, u32[]{:S(2)}, u32[]{:S(2)}) async-start(bf16[16,16,1,2560]{3,0,2,1:T(8,128)(2,1)} %copy.23), calls=%async_computation | async-start | bytes 2621440 | tf_op jit(solution)/shard_map/all_to_all | solution.py:57
  111.3 2.1 slice.58
  114.2 2.4 fusion.94
  116.7 2.0 fusion.37
  118.7 18.7 %all-to-all-done = bf16[16,16,1,2560]{3,0,2,1:T(8,128)(2,1)} async-done(((bf16[16,16,1,2560]{3,0,2,1:T(8,128)(2,1)}), bf16[16,16,1,2560]{3,0,2,1:T(8,128)(2,1)}, u32[]{:S(2)}, u32[]{:S(2)}) %all-to-all-start) | async-done | bytes 1310752 | tf_op jit(solution)/shard_map/all_to_all | solution.py:57
  137.3 2.5 reshape.141
  139.9 6.8 %convolution_bitcast_fusion = f32[1,128,20,128]{1,3,2,0:T(8,128)S(1)} fusion(bf16[256,20,128]{2,1,0:T(8,128)(2,1)S(1)} %reshape.141, f32[20,128]{1,0:T(8,128)S(1)} %fusion.94, f32[20,128,256]{2,1,0:T(8,128)} %fusion.37, pred[128,256]{1,0:T(8,128)(4,1)S(1)} %broadcast_compare_fusion), kind=kOutput, calls=%fused_computation.34 | convolution fusion | flops 171051776 | bytes 5285888 | tf_op jit(solution)/shard_map/nhqk,knhd->nqhd/dot_general | solution.py:74
  147.5 44.4 %all_gather.6 = bf16[128,2560]{1,0:T(8,128)(2,1)S(1)} all-gather(bf16[8,2560]{1,0:T(8,128)(2,1)S(1)} %multiply_convert_fusion.2), channel_id=1, replica_groups=mesh['gx'=16,'ta'=2] {'gx'}, dimensions={0}, use_global_device_ids=true | all-gather | bytes 696320 | tf_op jit(solution)/shard_map/all_gather | solution.py:80
  193.7 2.7 psum.42
  196.4 5.3 %fusion.19 = bf16[128,1280]{1,0:T(8,128)(2,1)} fusion(bf16[2,2560,1280]{2,1,0:T(8,128)(2,1)} %param.21, f32[2560]{0:T(1024)S(1)} %get-tuple-element.6, f32[128]{0:T(128)S(1)} %add_rsqrt_fusion.1, f32[16,8,2560]{2,0,1:T(8,128)S(1)} %fusion.32, bf16[128,2560]{1,0:T(8,128)(2,1)S(1)} %all_gather.6, f32[128]{0:T(128)S(1)} %div.64), kind=kOutput, calls=%fused_computation.27 | convolution fusion | flops 840990720 | bytes 8858624 | tf_op jit(solution)/shard_map/dot_general | solution.py:102
  201.7 5.3 %fusion.22 = bf16[128,1280]{1,0:T(8,128)(2,1)} fusion(bf16[2,2560,1280]{2,1,0:T(8,128)(2,1)} %param.22, f32[2560]{0:T(1024)S(1)} %get-tuple-element.6, f32[128]{0:T(128)S(1)} %add_rsqrt_fusion.1, f32[16,8,2560]{2,0,1:T(8,128)S(1)} %fusion.32, bf16[128,2560]{1,0:T(8,128)(2,1)S(1)} %all_gather.6, f32[128]{0:T(128)S(1)} %div.64), kind=kOutput, calls=%fused_computation.28 | convolution fusion | flops 840990720 | bytes 8858624 | tf_op jit(solution)/shard_map/dot_general | solution.py:103
  207.0 15.1 %all-reduce.7.cloned.1.call-done = (bf16[128,1280]{1,0:T(8,128)(2,1)}, bf16[128,1280]{1,0:T(8,128)(2,1)}) async-done(((bf16[128,1280]{1,0:T(8,128)(2,1)}, bf16[128,1280]{1,0:T(8,128)(2,1)}), (bf16[128,1280]{1,0:T(8,128)(2,1)}, bf16[128,1280]{1,0:T(8,128)(2,1)})) %all-reduce.7.cloned.1.call-update) | async-done | bytes 655376 | tf_op jit(solution)/shard_map/psum | solution.py:106
  222.1 5.2 %fusion.7 = f32[128,2560]{1,0:T(8,128)} fusion(bf16[2,1280,2560]{2,1,0:T(8,128)(2,1)} %param.23, bf16[128,1280]{1,0:T(8,128)(2,1)} %get-tuple-element.10, bf16[128,1280]{1,0:T(8,128)(2,1)} %get-tuple-element.11), kind=kOutput, calls=%fused_computation.10 | convolution fusion | flops 840171520 | bytes 8519680 | tf_op jit(solution)/shard_map/dot_general | solution.py:17
  227.4 80.2 %reduce-scatter.3.cloned.1.call-done = f32[8,2560]{1,0:T(8,128)} async-done(((f32[128,2560]{1,0:T(8,128)}), f32[8,2560]{1,0:T(8,128)}) %reduce-scatter.3.cloned.1.call-update) | async-done | bytes 81936 | tf_op jit(solution)/shard_map/reduce_scatter | solution.py:16
  308.5 39.3 %all_gather.7 = bf16[128,2560]{1,0:T(8,128)(2,1)S(1)} all-gather(bf16[8,2560]{1,0:T(8,128)(2,1)S(1)} %add_convert_fusion.1), channel_id=1, replica_groups=mesh['gx'=16,'ta'=2] {'gx'}, dimensions={0}, use_global_device_ids=true | all-gather | bytes 696320 | tf_op jit(solution)/shard_map/all_gather | solution.py:114
  349.5 2.5 psum.45
  352.0 5.3 %fusion.25 = bf16[128,1280]{1,0:T(8,128)(2,1)} fusion(bf16[2,2560,1280]{2,1,0:T(8,128)(2,1)} %param.21, f32[2560]{0:T(1024)S(1)} %get-tuple-element.7, f32[128]{0:T(128)S(1)} %add_rsqrt_fusion, f32[16,8,2560]{2,0,1:T(8,128)S(1)} %fusion.33, bf16[128,2560]{1,0:T(8,128)(2,1)S(1)} %all_gather.7, f32[128]{0:T(128)S(1)} %div.64), kind=kOutput, calls=%fused_computation.29 | convolution fusion | flops 840990720 | bytes 8858624 | tf_op jit(solution)/shard_map/dot_general | solution.py:102
  357.3 5.3 %fusion.28 = bf16[128,1280]{1,0:T(8,128)(2,1)} fusion(bf16[2,2560,1280]{2,1,0:T(8,128)(2,1)} %param.22, f32[2560]{0:T(1024)S(1)} %get-tuple-element.7, f32[128]{0:T(128)S(1)} %add_rsqrt_fusion, f32[16,8,2560]{2,0,1:T(8,128)S(1)} %fusion.33, bf16[128,2560]{1,0:T(8,128)(2,1)S(1)} %all_gather.7, f32[128]{0:T(128)S(1)} %div.64), kind=kOutput, calls=%fused_computation.30 | convolution fusion | flops 840990720 | bytes 8858624 | tf_op jit(solution)/shard_map/dot_general | solution.py:103
  362.6 16.7 %all-reduce.5.cloned.1.call-done = (bf16[128,1280]{1,0:T(8,128)(2,1)}, bf16[128,1280]{1,0:T(8,128)(2,1)}) async-done(((bf16[128,1280]{1,0:T(8,128)(2,1)}, bf16[128,1280]{1,0:T(8,128)(2,1)}), (bf16[128,1280]{1,0:T(8,128)(2,1)}, bf16[128,1280]{1,0:T(8,128)(2,1)})) %all-reduce.5.cloned.1.call-update) | async-done | bytes 655376 | tf_op jit(solution)/shard_map/psum | solution.py:106
  379.3 5.3 %fusion.1 = f32[128,2560]{1,0:T(8,128)} fusion(bf16[2,1280,2560]{2,1,0:T(8,128)(2,1)} %param.23, bf16[128,1280]{1,0:T(8,128)(2,1)} %get-tuple-element.8, bf16[128,1280]{1,0:T(8,128)(2,1)} %get-tuple-element.9), kind=kOutput, calls=%fused_computation.4 | convolution fusion | flops 840171520 | bytes 8519680 | tf_op jit(solution)/shard_map/dot_general | solution.py:17
  384.6 79.8 %reduce-scatter.5.cloned.1.call-done = f32[8,2560]{1,0:T(8,128)} async-done(((f32[128,2560]{1,0:T(8,128)}), f32[8,2560]{1,0:T(8,128)}) %reduce-scatter.5.cloned.1.call-update) | async-done | bytes 81936 | tf_op jit(solution)/shard_map/reduce_scatter | solution.py:16
  (63 shorter events, 11.6 us)
Async XLA Ops:
  6.5 1.3 copy-start
  7.9 5.4 %copy-start.2 = (bf16[16,16,2560]{2,1,0:T(8,128)(2,1)S(1)}, bf16[16,16,2560]{2,1,0:T(8,128)(2,1)}, u32[]{:S(2)}) copy-start(bf16[16,16,2560]{2,1,0:T(8,128)(2,1)} %param.13) | copy-start | bytes 3932164
  13.3 5.4 %copy-start.3 = (bf16[16,16,2560]{2,1,0:T(8,128)(2,1)S(1)}, bf16[16,16,2560]{2,1,0:T(8,128)(2,1)}, u32[]{:S(2)}) copy-start(bf16[16,16,2560]{2,1,0:T(8,128)(2,1)} %param.14) | copy-start | bytes 3932164
  18.6 5.4 %copy-start.4 = (bf16[16,16,2560]{2,0,1:T(8,128)(2,1)S(1)}, bf16[16,16,2560]{2,0,1:T(8,128)(2,1)}, u32[]{:S(2)}) copy-start(bf16[16,16,2560]{2,0,1:T(8,128)(2,1)} %gather_fusion) | copy-start | bytes 3932164
  29.4 8.5 %copy-start.5 = (bf16[16,16,1,2560]{3,1,0,2:T(8,128)(2,1)S(1)}, bf16[16,16,1,2560]{3,1,0,2:T(8,128)(2,1)}, u32[]{:S(2)}) copy-start(bf16[16,16,1,2560]{3,1,0,2:T(8,128)(2,1)} %get-tuple-element.19) | copy-start | bytes 3932164
  29.4 37.9 %all-to-all-start.1 = ((bf16[16,16,1,2560]{3,0,2,1:T(8,128)(2,1)}), bf16[16,16,1,2560]{3,0,2,1:T(8,128)(2,1)S(1)}, u32[]{:S(2)}, u32[]{:S(2)}) async-start(bf16[16,16,1,2560]{3,0,2,1:T(8,128)(2,1)} %copy.24), calls=%async_computation.1 | async-start | bytes 2621440 | tf_op jit(solution)/shard_map/all_to_all | solution.py:55
  67.3 35.0 %all-to-all-start.2 = ((bf16[16,16,1,2560]{3,0,2,1:T(8,128)(2,1)}), bf16[16,16,1,2560]{3,0,2,1:T(8,128)(2,1)S(1)}, u32[]{:S(2)}, u32[]{:S(2)}) async-start(bf16[16,16,1,2560]{3,0,2,1:T(8,128)(2,1)} %copy.26), calls=%async_computation.2 | async-start | bytes 2621440 | tf_op jit(solution)/shard_map/all_to_all | solution.py:56
  77.0 31.8 %copy-start.7 = (f32[2,3,2560]{2,0,1:T(2,128)S(1)}, f32[2,3,2560]{2,0,1:T(2,128)}, u32[]{:S(2)}) copy-start(f32[2,3,2560]{2,0,1:T(2,128)} %param.19) | copy-start | bytes 184324
  77.0 31.9 %copy-start.9 = (s32[64,2]{0,1:T(2,128)S(1)}, s32[64,2]{0,1:T(2,128)}, u32[]{:S(2)}) copy-start(s32[64,2]{0,1:T(2,128)} %param.17) | copy-start | bytes 1540
  77.0 32.2 %copy-start.10 = (s32[64]{0:T(128)S(1)}, s32[64]{0:T(128)}, u32[]{:S(2)}) copy-start(s32[64]{0:T(128)} %param.18) | copy-start | bytes 772
  77.1 32.4 %copy-start.8 = (f32[2,2560]{1,0:T(2,128)S(1)}, f32[2,2560]{1,0:T(2,128)}, u32[]{:S(2)}) copy-start(f32[2,2560]{1,0:T(2,128)} %param.20) | copy-start | bytes 61444
  102.4 35.0 %all-to-all-start = ((bf16[16,16,1,2560]{3,0,2,1:T(8,128)(2,1)}), bf16[16,16,1,2560]{3,0,2,1:T(8,128)(2,1)}, u32[]{:S(2)}, u32[]{:S(2)}) async-start(bf16[16,16,1,2560]{3,0,2,1:T(8,128)(2,1)} %copy.23), calls=%async_computation | async-start | bytes 2621440 | tf_op jit(solution)/shard_map/all_to_all | solution.py:57
  108.8 113.3 %all-reduce.7.cloned.1.call-start = ((), (), s32[]{:S(2)}) async-start(), calls=%async_computation.8 | async-start | bytes 1310720 | tf_op jit(solution)/shard_map/psum | solution.py:106
  114.2 2.4 copy-start.6
  207.0 100.6 %reduce-scatter.3.cloned.1.call-start = ((), (), s32[]{:S(2)}) async-start(), calls=%async_computation.5 | async-start | bytes 1392640 | tf_op jit(solution)/shard_map/reduce_scatter | solution.py:16
  227.3 152.0 %all-reduce.5.cloned.1.call-start = ((), (), s32[]{:S(2)}) async-start(), calls=%async_computation.7 | async-start | bytes 1310720 | tf_op jit(solution)/shard_map/psum | solution.py:106
  362.5 101.9 %reduce-scatter.5.cloned.1.call-start = ((), (), s32[]{:S(2)}) async-start(), calls=%async_computation.6 | async-start | bytes 1392640 | tf_op jit(solution)/shard_map/reduce_scatter | solution.py:16
  379.3 86.6 %copy-start.1 = (bf16[16,16,2560]{2,1,0:T(8,128)(2,1)S(1)}, bf16[16,16,2560]{2,1,0:T(8,128)(2,1)}, u32[]{:S(2)}) copy-start(bf16[16,16,2560]{2,1,0:T(8,128)(2,1)} %param.15) | copy-start | bytes 3932164
Sparse Core Ops, SparseCore 0:
  207.1 14.9 all-reduce.6
  227.4 80.0 reduce-scatter.2
  362.7 16.5 all-reduce.4
  384.7 79.6 reduce-scatter.4
where the time goes:
time: 473 us; the launch traced here: 472 us
  waiting for transfers between devices  263 us (56%)
  blocking collectives  88.8 us (19%)
  matrix products  44.2 us (9%)
  local copies, waits for them, and re-layouts  32.3 us (7%)
  starting transfers between devices  21.6 us (5%)
  between operations  13.4 us (3%)
  other arithmetic  8.78 us (2%)
    reduce_scatter x2, waiting for transfers between devices, settle_rows(): lax.psum_scatter(jnp.dot(hidden, down_local, preferred_element_type=jnp.f...  160 us
    all_gather x2, blocking collectives, per_device(): nodes = lax.all_gather(own_rows, 'gx', axis=0, tiled=True)  83.7 us
    psum x2, waiting for transfers between devices, per_device(): lax.psum(up_part.astype(jnp.bfloat16), 'ta').astype(jnp.float32)  31.7 us
    all_to_all x1, waiting for transfers between devices, per_device(): lax.all_to_all(sorted_queries, 'gx', split_axis=1, concat_axis=0, tiled=T...  27.7 us
    all_to_all x1, waiting for transfers between devices, per_device(): lax.all_to_all(sorted_keys, 'gx', split_axis=1, concat_axis=0, tiled=True)  25.3 us
    all_to_all x1, waiting for transfers between devices, per_device(): lax.all_to_all(sorted_values, 'gx', split_axis=1, concat_axis=0, tiled=True)  18.7 us
    dot_general x2, matrix products, per_device(): jnp.dot(normed, gate_proj[layer_idx], preferred_element_type=jnp.float32)  10.6 us
    dot_general x2, matrix products, per_device(): jnp.dot(normed, up_proj[layer_idx], preferred_element_type=jnp.float32)  10.5 us
  transfers between devices with their start and end apart: 7, of which 7 were waited for; matrix products, arithmetic and copies ran while one was open for 3% of the time, Pallas kernels for 0%

commit v1 on v0

v1 whole, which is shorter than its diff:
```python
import jax
import jax.numpy as jnp
from jax import lax
from jax.sharding import PartitionSpec as P

D = 5120
HEAD_DIM = 128
VENUES = 16
STEPS = 16
NODE_STEPS = 8
ROUNDS = 2
ETYPES = 3


def flip_pairs(count, bit):
    return [(i, i ^ (1 << bit)) for i in range(count)]


def stage_bits(count):
    return list(range(count.bit_length() - 1))


def scatter_rows(partial, gx_count):
    me = lax.axis_index("gx")
    held = partial.astype(jnp.float32)
    for bit in stage_bits(gx_count):
        half = held.shape[0] // 2
        side = (me >> bit) & 1
        keep = lax.dynamic_slice_in_dim(held, side * half, half, 0)
        give = lax.dynamic_slice_in_dim(held, (1 - side) * half, half, 0).astype(jnp.bfloat16)
        held = keep + lax.ppermute(give, "gx", flip_pairs(gx_count, bit)).astype(jnp.float32)
    return held


def gather_rows(own, gx_count):
    me = lax.axis_index("gx")
    held = own
    for bit in reversed(stage_bits(gx_count)):
        side = (me >> bit) & 1
        other = lax.ppermute(held, "gx", flip_pairs(gx_count, bit))
        held = jnp.where(
            side == 0,
            jnp.concatenate([held, other], axis=0),
            jnp.concatenate([other, held], axis=0),
        )
    return held


def sum_over_ta(part, ta_count):
    if ta_count == 2:
        return part.astype(jnp.float32) + lax.ppermute(part, "ta", [(0, 1), (1, 0)]).astype(
            jnp.float32
        )
    return lax.psum(part, "ta").astype(jnp.float32)


def per_device(
    query_vecs,
    key_vecs,
    value_vecs,
    slot_map,
    edge_list,
    edge_types,
    type_gain,
    norm_gain,
    gate_proj,
    up_proj,
    down_proj,
):
    pairs_dev, inst_total, feat_width = query_vecs.shape
    head_count = feat_width // HEAD_DIM
    gx_count = lax.axis_size("gx")
    ta_count = lax.axis_size("ta")
    inst_local = inst_total // gx_count
    score_scale = 1.0 / HEAD_DIM**0.5
    venue_idx = lax.axis_index("gx") * pairs_dev // STEPS
    slot_order = lax.dynamic_index_in_dim(slot_map, venue_idx, 0, keepdims=False)

    def by_instrument(vecs):
        pairs = vecs.shape[0]
        rows = pairs * inst_total
        row = jnp.arange(rows)
        source = (row % pairs) * inst_total + slot_order[row // pairs]
        pick = (source[:, None] == row[None, :]).astype(jnp.bfloat16)
        return jnp.dot(
            pick, vecs.reshape(rows, feat_width), preferred_element_type=jnp.float32
        ).astype(jnp.bfloat16)

    def to_instrument(vecs):
        rows = by_instrument(vecs)
        return lax.all_to_all(rows, "gx", split_axis=0, concat_axis=0, tiled=True)

    whole_venue = pairs_dev == STEPS
    if whole_venue:
        query_vecs = query_vecs[STEPS - NODE_STEPS :]
    queries = to_instrument(query_vecs)
    keyset = to_instrument(key_vecs)
    valueset = to_instrument(value_vecs)
    pair_total = VENUES * STEPS
    if whole_venue:
        queries = queries.reshape(VENUES * NODE_STEPS, head_count, HEAD_DIM)
    else:
        queries = queries.reshape(VENUES, STEPS, head_count, HEAD_DIM)[:, STEPS - NODE_STEPS :]
        queries = queries.reshape(VENUES * NODE_STEPS, head_count, HEAD_DIM)
    keyset = keyset.reshape(pair_total, head_count, HEAD_DIM)
    valueset = valueset.reshape(pair_total, head_count, HEAD_DIM)
    query_steps = jnp.arange(VENUES * NODE_STEPS) % NODE_STEPS + (STEPS - NODE_STEPS)
    key_steps = jnp.arange(pair_total) % STEPS
    allowed = key_steps[None, :] <= query_steps[:, None]
    scores = (
        jnp.einsum("qhd,khd->hqk", queries, keyset, preferred_element_type=jnp.float32)
        * score_scale
    )
    scores = jnp.where(allowed[None], scores, jnp.float32(-1e30))
    row_max = jnp.max(scores, axis=-1, keepdims=True)
    expd = jnp.exp(scores - row_max)
    probs = (expd / jnp.sum(expd, axis=-1, keepdims=True)).astype(jnp.bfloat16)
    attended = jnp.einsum("hqk,khd->qhd", probs, valueset, preferred_element_type=jnp.float32)
    attended = attended.reshape(VENUES, NODE_STEPS, feat_width)
    own_rows = jnp.mean(attended, axis=0).astype(jnp.bfloat16)

    bits = stage_bits(gx_count)
    place = jnp.arange(inst_total)
    inst_at = sum((((place >> b) & 1) << (len(bits) - 1 - b)) for b in bits)
    at_source = (edge_list[:, 0][:, None] == inst_at[None, :]).astype(jnp.float32)
    at_target = (edge_list[:, 1][:, None] == inst_at[None, :]).astype(jnp.float32)
    of_type = (edge_types[:, None] == jnp.arange(ETYPES)[None, :]).astype(jnp.float32)
    adjacency = jnp.einsum("et,ei,ej->tij", of_type, at_target, at_source)
    degree = jnp.maximum(jnp.sum(at_target, axis=0), 1.0)
    adj_rows = adjacency.reshape(ETYPES * inst_total, inst_total).astype(jnp.bfloat16)
    row_total = inst_total * NODE_STEPS
    ff_dev = gate_proj.shape[2]
    for layer_idx in range(ROUNDS):
        nodes = gather_rows(own_rows, gx_count)
        flat_nodes = nodes.reshape(inst_total, NODE_STEPS * feat_width)
        gathered = jnp.dot(adj_rows, flat_nodes, preferred_element_type=jnp.float32)
        gathered = gathered.reshape(ETYPES, inst_total, NODE_STEPS, feat_width)
        message = (
            jnp.sum(gathered * type_gain[layer_idx][:, None, None, :], axis=0)
            / degree[:, None, None]
        )
        pre_norm = nodes.astype(jnp.float32) + message.reshape(row_total, feat_width)
        squares = lax.psum(jnp.sum(pre_norm * pre_norm, axis=-1), "ta")
        row_scale = lax.rsqrt(squares / D + 1e-05)[:, None]
        normed = (pre_norm * row_scale * norm_gain[layer_idx][None, :]).astype(jnp.bfloat16)
        gate_part = jnp.dot(normed, gate_proj[layer_idx], preferred_element_type=jnp.float32)
        up_part = jnp.dot(normed, up_proj[layer_idx], preferred_element_type=jnp.float32)
        both = jnp.concatenate(
            [gate_part.astype(jnp.bfloat16), up_part.astype(jnp.bfloat16)], axis=1
        )
        both = sum_over_ta(both, ta_count)
        hidden = (jax.nn.silu(both[:, :ff_dev]) * both[:, ff_dev:]).astype(jnp.bfloat16)
        update = jnp.dot(hidden, down_proj[layer_idx], preferred_element_type=jnp.float32)
        own_rows = (own_rows.astype(jnp.float32) + scatter_rows(update, gx_count)).astype(
            jnp.bfloat16
        )
    return own_rows


def solution(mesh):
    placed = (
        P("gx", None, "ta"),
        P("gx", None, "ta"),
        P("gx", None, "ta"),
        P(),
        P(),
        P(),
        P(None, None, "ta"),
        P(None, "ta"),
        P(None, "ta", "gx"),
        P(None, "ta", "gx"),
        P(None, "gx", "ta"),
    )
    return jax.shard_map(
        per_device, mesh=mesh, in_specs=placed, out_specs=P("gx", "ta"), check_vma=False
    )
```

time: 473 us -> 261 us (0.55)
  waiting for transfers between devices: 263 us -> 126 us
  blocking collectives: 88.8 us -> 5.33 us
  starting transfers between devices: 21.6 us -> 48.2 us
  local copies, waits for them, and re-layouts: 32.3 us -> 10.1 us
  other arithmetic: 8.78 us -> 25.7 us
  between operations: 13.4 us -> 0.52 us
    reduce_scatter x2 -> x0, waiting for transfers between devices: 160 us -> none  [settle_rows(): lax.psum_scatter(jnp.dot(hidden, down_local, preferred_element_type=jnp.f...]
    all_gather x2 -> x0, blocking collectives: 83.7 us -> none  [per_device(): nodes = lax.all_gather(own_rows, 'gx', axis=0, tiled=True)]
    ppermute x0 -> x18, waiting for transfers between devices: none -> 71.7 us  [the longest x8 37.3 us: scatter_rows(): lax.ppermute(give, 'gx', flip_pairs(gx_count, bit)).astype(jnp.float32)]
    psum x2 -> x0, waiting for transfers between devices: 31.7 us -> none  [per_device(): lax.psum(up_part.astype(jnp.bfloat16), 'ta').astype(jnp.float32)]
    ppermute x0 -> x18, starting transfers between devices: none -> 28.8 us  [the longest x8 14.5 us: gather_rows(): other = lax.ppermute(held, 'gx', flip_pairs(gx_count, bit))]
    all_to_all x3, waiting for transfers between devices: 71.6 us -> 54.4 us  [to_instrument(): return lax.all_to_all(rows, 'gx', split_axis=0, concat_axis=0, tiled=True)]
    add x0 -> x11, other arithmetic: none -> 16.2 us  [the longest x2 15.6 us: by_instrument(): source = row % pairs * inst_total + slot_order[row // pairs]]
    gather x3 -> x1, local copies, waits for them, and re-layouts: 16.1 us -> 0.71 us  [by_instrument(): source = row % pairs * inst_total + slot_order[row // pairs]]
  transfers between devices with their start and end apart: 7 -> 21, of which waited for: 7 -> 21; matrix products, arithmetic and copies ran while one was open for 3% -> 8% of each run, Pallas kernels for 0% -> 0%
where the time goes in v1:
time: 261 us; the launch traced here: 260 us
  waiting for transfers between devices  126 us (48%)
  starting transfers between devices  48.2 us (18%)
  matrix products  44 us (17%)
  other arithmetic  25.7 us (10%)
  local copies, waits for them, and re-layouts  10.1 us (4%)
  blocking collectives  5.33 us (2%)
    all_to_all x3, waiting for transfers between devices, to_instrument(): return lax.all_to_all(rows, 'gx', split_axis=0, concat_axis=0, tiled=True)  54.4 us
    ppermute x8, waiting for transfers between devices, scatter_rows(): lax.ppermute(give, 'gx', flip_pairs(gx_count, bit)).astype(jnp.float32)  37.3 us
    ppermute x8, waiting for transfers between devices, gather_rows(): other = lax.ppermute(held, 'gx', flip_pairs(gx_count, bit))  30.6 us
    all_to_all x3, starting transfers between devices, to_instrument(): return lax.all_to_all(rows, 'gx', split_axis=0, concat_axis=0, tiled=True)  19.4 us
    add x2, other arithmetic, by_instrument(): source = row % pairs * inst_total + slot_order[row // pairs]  15.6 us
    ppermute x8, starting transfers between devices, gather_rows(): other = lax.ppermute(held, 'gx', flip_pairs(gx_count, bit))  14.5 us
    ppermute x8, starting transfers between devices, scatter_rows(): lax.ppermute(give, 'gx', flip_pairs(gx_count, bit)).astype(jnp.float32)  13.8 us
    dot_general x2, matrix products, per_device(): jnp.dot(normed, gate_proj[layer_idx], preferred_element_type=jnp.float32)  8.29 us
  transfers between devices with their start and end apart: 21, of which 21 were waited for; matrix products, arithmetic and copies ran while one was open for 8% of the time, Pallas kernels for 0%

profile of v1, /device:TPU:0, one launch (start us, length us, event | category | flops | bytes accessed | tf_op | source)
XLA Modules:
  0.0 260.0 jit_solution(17877212190103484807)
XLA Ops:
  1.6 10.0 %fusion.101 = s32[128]{0:T(128)S(1)} fusion(s32[]{:T(128)} %bitcast.9, s32[]{:T(128)} %bitcast.10, s32[]{:T(128)} %bitcast.11, s32[]{:T(128)} %bitcast.12, s32[]{:T(128)} %bitcast.13, s32[]{:T(128)} %bitcast.15, s32[]{:T(128)} %bitcast.14, s32[]{:T(128)} %bitcast, s32[]{:T(128)} %bitcast.1, s32[]{:T(128)} %bitcast.2, s32[]{:T(128)} %bitcast.3, s32[]{:T(128)} %bitcast.4, ...), kind=kLoop, calls=%fused_computation.191 | loop fusion | flops 6272 | bytes 576 | tf_op jit(solution)/shard_map/add | solution.py:83
  12.8 8.3 %all-to-all-start.1 = ((bf16[16,8,2560]{2,1,0:T(8,128)(2,1)}), bf16[16,8,2560]{2,1,0:T(8,128)(2,1)S(1)}, u32[]{:S(2)}, u32[]{:S(2)}) async-start(bf16[16,8,2560]{2,1,0:T(8,128)(2,1)} %fusion.19), calls=%async_computation.1 | async-start | bytes 1310720 | tf_op jit(solution)/shard_map/all_to_all | solution.py:91
  21.2 4.3 %compare_select_fusion.1 = s32[256,1]{0,1:T(1,128)S(1)} fusion(s32[]{:T(128)} %bitcast.9, s32[]{:T(128)} %bitcast.10, s32[]{:T(128)} %bitcast.11, s32[]{:T(128)} %bitcast.12, s32[]{:T(128)} %bitcast.13, s32[]{:T(128)} %bitcast.15, s32[]{:T(128)} %bitcast.14), kind=kLoop, calls=%fused_computation.139 | loop fusion | flops 5888 | bytes 1052 | tf_op jit(solution)/shard_map/gather | solution.py:83
  25.6 5.7 %select_add_fusion = s32[256]{0:T(256)S(1)} fusion(pred[256]{0:T(512)(128)(4,1)S(1)} %get-tuple-element.31, pred[256]{0:T(512)(128)(4,1)S(1)} %get-tuple-element.32, pred[256]{0:T(512)(128)(4,1)S(1)} %get-tuple-element.33, pred[256]{0:T(512)(128)(4,1)S(1)} %get-tuple-element.34, pred[256]{0:T(512)(128)(4,1)S(1)} %get-tuple-element.35, ...), kind=kLoop, calls=%fused_computation.175 | loop fusion | flops 4352 | bytes 4388 | tf_op jit(solution)/shard_map/add | solution.py:83
  32.8 5.7 %all-to-all-done.1 = bf16[16,8,2560]{2,1,0:T(8,128)(2,1)S(1)} async-done(((bf16[16,8,2560]{2,1,0:T(8,128)(2,1)}), bf16[16,8,2560]{2,1,0:T(8,128)(2,1)S(1)}, u32[]{:S(2)}, u32[]{:S(2)}) %all-to-all-start.1) | async-done | bytes 655392 | tf_op jit(solution)/shard_map/all_to_all | solution.py:91
  38.5 4.6 %all-to-all-start.2 = ((bf16[16,16,2560]{2,1,0:T(8,128)(2,1)}), bf16[16,16,2560]{2,1,0:T(8,128)(2,1)S(1)}, u32[]{:S(2)}, u32[]{:S(2)}) async-start(bf16[16,16,2560]{2,1,0:T(8,128)(2,1)} %bitcast.32), calls=%async_computation.2 | async-start | bytes 2621440 | tf_op jit(solution)/shard_map/all_to_all | solution.py:91
  44.7 26.9 %all-to-all-done.2 = bf16[16,16,2560]{2,1,0:T(8,128)(2,1)S(1)} async-done(((bf16[16,16,2560]{2,1,0:T(8,128)(2,1)}), bf16[16,16,2560]{2,1,0:T(8,128)(2,1)S(1)}, u32[]{:S(2)}, u32[]{:S(2)}) %all-to-all-start.2) | async-done | bytes 1310752 | tf_op jit(solution)/shard_map/all_to_all | solution.py:91
  71.7 6.5 %all-to-all-start = ((bf16[16,16,2560]{2,1,0:T(8,128)(2,1)}), bf16[16,16,2560]{2,1,0:T(8,128)(2,1)}, u32[]{:S(2)}, u32[]{:S(2)}) async-start(bf16[16,16,2560]{2,1,0:T(8,128)(2,1)} %bitcast.18), calls=%async_computation | async-start | bytes 2621440 | tf_op jit(solution)/shard_map/all_to_all | solution.py:91
  85.0 21.8 %all-to-all-done = bf16[16,16,2560]{2,1,0:T(8,128)(2,1)} async-done(((bf16[16,16,2560]{2,1,0:T(8,128)(2,1)}), bf16[16,16,2560]{2,1,0:T(8,128)(2,1)}, u32[]{:S(2)}, u32[]{:S(2)}) %all-to-all-start) | async-done | bytes 1310752 | tf_op jit(solution)/shard_map/all_to_all | solution.py:91
  109.3 6.8 %convolution_bitcast_fusion = f32[128,20,128]{0,2,1:T(8,128)S(1)} fusion(bf16[256,20,128]{2,1,0:T(8,128)(2,1)S(1)} %reshape.596, f32[20,128]{1,0:T(8,128)S(1)} %fusion.113, f32[20,128,256]{2,1,0:T(8,128)} %fusion.46, pred[128,256]{1,0:T(8,128)(4,1)S(1)} %broadcast_compare_fusion), kind=kOutput, calls=%fused_computation.39 | convolution fusion | flops 171051776 | bytes 5285888 | tf_op jit(solution)/shard_map/hqk,khd->qhd/dot_general | solution.py:118
  117.0 4.8 %collective-permute-start = (bf16[8,2560]{1,0:T(8,128)(2,1)S(1)}, bf16[8,2560]{1,0:T(8,128)(2,1)S(1)}, u32[]{:S(2)}, u32[]{:S(2)}) collective-permute-start(bf16[8,2560]{1,0:T(8,128)(2,1)S(1)} %multiply_convert_fusion), channel_id=1, source_target_pairs={{0,16},{2,18},{4,20},{6,22},{8,24},{10,26},{12,28},{14,30},{16,0},... | collective-permute-start | bytes 122888 | tf_op jit(solution)/shard_map/ppermute | solution.py:40
  130.4 3.3 %collective-permute-done.2 = bf16[32,2560]{1,0:T(8,128)(2,1)S(1)} collective-permute-done((bf16[32,2560]{1,0:T(8,128)(2,1)S(1)}, bf16[32,2560]{1,0:T(8,128)(2,1)S(1)}, u32[]{:S(2)}, u32[]{:S(2)}) %collective-permute-start.2) | collective-permute-done | bytes 163872 | tf_op jit(solution)/shard_map/ppermute | solution.py:40
  134.6 6.4 %collective-permute-done.3 = bf16[64,2560]{1,0:T(8,128)(2,1)S(1)} collective-permute-done((bf16[64,2560]{1,0:T(8,128)(2,1)S(1)}, bf16[64,2560]{1,0:T(8,128)(2,1)S(1)}, u32[]{:S(2)}, u32[]{:S(2)}) %collective-permute-start.3) | collective-permute-done | bytes 327712 | tf_op jit(solution)/shard_map/ppermute | solution.py:40
  144.9 2.6 %psum.14 = f32[128]{0:T(128)S(1)} all-reduce(f32[128]{0:T(128)S(1)} %fusion.36), channel_id=1, replica_groups=mesh['gx'=16,'ta'=2] {'ta'}, use_global_device_ids=true, to_apply=%region_6.7 | all-reduce | flops 128 | bytes 1024 | tf_op jit(solution)/shard_map/psum | solution.py:143
  148.6 4.1 %fusion.20 = bf16[128,1280]{1,0:T(8,128)(2,1)S(1)} fusion(bf16[2,2560,1280]{2,1,0:T(8,128)(2,1)} %param.19, bf16[16,8,2560]{2,0,1:T(8,128)(2,1)S(1)} %fusion.44), kind=kOutput, calls=%fused_computation.28 | convolution fusion | flops 839024640 | bytes 7536640 | tf_op jit(solution)/shard_map/dot_general | solution.py:146
  152.7 4.1 %fusion.23 = bf16[128,1280]{1,0:T(8,128)(2,1)S(1)} fusion(bf16[2,2560,1280]{2,1,0:T(8,128)(2,1)} %param.20, bf16[16,8,2560]{2,0,1:T(8,128)(2,1)S(1)} %fusion.44), kind=kOutput, calls=%fused_computation.29 | convolution fusion | flops 839024640 | bytes 7536640 | tf_op jit(solution)/shard_map/dot_general | solution.py:147
  159.3 3.9 %fusion.7 = f32[128,2560]{1,0:T(8,128)S(1)} fusion(bf16[2,1280,2560]{2,1,0:T(8,128)(2,1)} %param.21, f32[128,2560]{1,0:T(8,128)S(1)} %convert_add_fusion.3), kind=kOutput, calls=%fused_computation.7 | convolution fusion | flops 839843840 | bytes 9175040 | tf_op jit(solution)/shard_map/dot_general | solution.py:153
  163.6 9.5 %collective-permute-done.5 = bf16[64,2560]{1,0:T(8,128)(2,1)S(1)} collective-permute-done((bf16[64,2560]{1,0:T(8,128)(2,1)S(1)}, bf16[64,2560]{1,0:T(8,128)(2,1)S(1)}, u32[]{:S(2)}, u32[]{:S(2)}) %collective-permute-start.5) | collective-permute-done | bytes 327712 | tf_op jit(solution)/shard_map/ppermute | solution.py:31
  175.1 3.7 %collective-permute-done.6 = bf16[32,2560]{1,0:T(8,128)(2,1)S(1)} collective-permute-done((bf16[32,2560]{1,0:T(8,128)(2,1)S(1)}, bf16[32,2560]{1,0:T(8,128)(2,1)S(1)}, u32[]{:S(2)}, u32[]{:S(2)}) %collective-permute-start.6) | collective-permute-done | bytes 163872 | tf_op jit(solution)/shard_map/ppermute | solution.py:31
  183.4 3.7 %collective-permute-start.8 = (bf16[8,2560]{1,0:T(8,128)(2,1)S(1)}, bf16[8,2560]{1,0:T(8,128)(2,1)S(1)}, u32[]{:S(2)}, u32[]{:S(2)}) collective-permute-start(bf16[8,2560]{1,0:T(8,128)(2,1)S(1)} %dynamic-slice_convert_fusion.7), channel_id=1, source_target_pairs={{0,16},{2,18},{4,20},{6,22},{8,24},{10,26},{12,28},{14,30},{16,0},... | collective-permute-start | bytes 122888 | tf_op jit(solution)/shard_map/ppermute | solution.py:31
  189.5 2.8 %collective-permute-start.9 = (bf16[8,2560]{1,0:T(8,128)(2,1)S(1)}, bf16[8,2560]{1,0:T(8,128)(2,1)S(1)}, u32[]{:S(2)}, u32[]{:S(2)}) collective-permute-start(bf16[8,2560]{1,0:T(8,128)(2,1)S(1)} %add_convert_fusion.1), channel_id=1, source_target_pairs={{0,16},{2,18},{4,20},{6,22},{8,24},{10,26},{12,28},{14,30},{16,0},... | collective-permute-start | bytes 122888 | tf_op jit(solution)/shard_map/ppermute | solution.py:40
  196.0 3.0 %collective-permute-done.10 = bf16[16,2560]{1,0:T(8,128)(2,1)S(1)} collective-permute-done((bf16[16,2560]{1,0:T(8,128)(2,1)S(1)}, bf16[16,2560]{1,0:T(8,128)(2,1)S(1)}, u32[]{:S(2)}, u32[]{:S(2)}) %collective-permute-start.10) | collective-permute-done | bytes 81952 | tf_op jit(solution)/shard_map/ppermute | solution.py:40
  200.0 4.4 %collective-permute-done.11 = bf16[32,2560]{1,0:T(8,128)(2,1)S(1)} collective-permute-done((bf16[32,2560]{1,0:T(8,128)(2,1)S(1)}, bf16[32,2560]{1,0:T(8,128)(2,1)S(1)}, u32[]{:S(2)}, u32[]{:S(2)}) %collective-permute-start.11) | collective-permute-done | bytes 163872 | tf_op jit(solution)/shard_map/ppermute | solution.py:40
  204.6 7.0 %collective-permute-done.12 = bf16[64,2560]{1,0:T(8,128)(2,1)S(1)} collective-permute-done((bf16[64,2560]{1,0:T(8,128)(2,1)S(1)}, bf16[64,2560]{1,0:T(8,128)(2,1)S(1)}, u32[]{:S(2)}, u32[]{:S(2)}) %collective-permute-start.12) | collective-permute-done | bytes 327712 | tf_op jit(solution)/shard_map/ppermute | solution.py:40
  215.6 2.7 %psum.15 = f32[128]{0:T(128)S(1)} all-reduce(f32[128]{0:T(128)S(1)} %fusion.38), channel_id=1, replica_groups=mesh['gx'=16,'ta'=2] {'ta'}, use_global_device_ids=true, to_apply=%region_9.10 | all-reduce | flops 128 | bytes 1024 | tf_op jit(solution)/shard_map/psum | solution.py:143
  219.3 4.2 %fusion.26 = bf16[128,1280]{1,0:T(8,128)(2,1)S(1)} fusion(bf16[2,2560,1280]{2,1,0:T(8,128)(2,1)} %param.19, bf16[16,8,2560]{2,0,1:T(8,128)(2,1)S(1)} %fusion.41), kind=kOutput, calls=%fused_computation.30 | convolution fusion | flops 839024640 | bytes 7536640 | tf_op jit(solution)/shard_map/dot_general | solution.py:146
  223.5 4.2 %fusion.29 = bf16[128,1280]{1,0:T(8,128)(2,1)S(1)} fusion(bf16[2,2560,1280]{2,1,0:T(8,128)(2,1)} %param.20, bf16[16,8,2560]{2,0,1:T(8,128)(2,1)S(1)} %fusion.41), kind=kOutput, calls=%fused_computation.31 | convolution fusion | flops 839024640 | bytes 7536640 | tf_op jit(solution)/shard_map/dot_general | solution.py:147
  230.0 4.0 %fusion.1 = f32[128,2560]{1,0:T(8,128)S(1)} fusion(bf16[2,1280,2560]{2,1,0:T(8,128)(2,1)} %param.21, f32[128,2560]{1,0:T(8,128)S(1)} %convert_add_fusion.2), kind=kOutput, calls=%fused_computation.1 | convolution fusion | flops 839843840 | bytes 9175040 | tf_op jit(solution)/shard_map/dot_general | solution.py:153
  234.1 9.8 %collective-permute-done.14 = bf16[64,2560]{1,0:T(8,128)(2,1)S(1)} collective-permute-done((bf16[64,2560]{1,0:T(8,128)(2,1)S(1)}, bf16[64,2560]{1,0:T(8,128)(2,1)S(1)}, u32[]{:S(2)}, u32[]{:S(2)}) %collective-permute-start.14) | collective-permute-done | bytes 327712 | tf_op jit(solution)/shard_map/ppermute | solution.py:31
  245.0 4.5 %collective-permute-done.15 = bf16[32,2560]{1,0:T(8,128)(2,1)S(1)} collective-permute-done((bf16[32,2560]{1,0:T(8,128)(2,1)S(1)}, bf16[32,2560]{1,0:T(8,128)(2,1)S(1)}, u32[]{:S(2)}, u32[]{:S(2)}) %collective-permute-start.15) | collective-permute-done | bytes 163872 | tf_op jit(solution)/shard_map/ppermute | solution.py:31
  251.1 3.0 %collective-permute-done.16 = bf16[16,2560]{1,0:T(8,128)(2,1)S(1)} collective-permute-done((bf16[16,2560]{1,0:T(8,128)(2,1)S(1)}, bf16[16,2560]{1,0:T(8,128)(2,1)S(1)}, u32[]{:S(2)}, u32[]{:S(2)}) %collective-permute-start.16) | collective-permute-done | bytes 81952 | tf_op jit(solution)/shard_map/ppermute | solution.py:31
  254.1 3.2 %collective-permute-start.17 = (bf16[8,2560]{1,0:T(8,128)(2,1)S(1)}, bf16[8,2560]{1,0:T(8,128)(2,1)S(1)}, u32[]{:S(2)}, u32[]{:S(2)}) collective-permute-start(bf16[8,2560]{1,0:T(8,128)(2,1)S(1)} %dynamic-slice_convert_fusion.6), channel_id=1, source_target_pairs={{0,16},{2,18},{4,20},{6,22},{8,24},{10,26},{12,28},{14,30},{16,0},... | collective-permute-start | bytes 122888 | tf_op jit(solution)/shard_map/ppermute | solution.py:31
  (117 shorter events, 60.0 us)
Async XLA Ops:
  0.0 31.2 %copy-start = (bf16[16,16,2560]{2,1,0:T(8,128)(2,1)S(1)}, bf16[16,16,2560]{2,1,0:T(8,128)(2,1)}, u32[]{:S(2)}) copy-start(bf16[16,16,2560]{2,1,0:T(8,128)(2,1)} %param.12) | copy-start | bytes 3932164
  0.0 11.5 %slice-start = ((bf16[16,16,2560]{2,1,0:T(8,128)(2,1)}), bf16[8,16,2560]{2,1,0:T(8,128)(2,1)S(1)}, s32[]{:S(2)}) async-start(bf16[16,16,2560]{2,1,0:T(8,128)(2,1)} %param.11), calls=%async_computation.3 | async-start | bytes 1310720 | tf_op jit(solution)/shard_map/slice | solution.py:95
  12.8 25.7 %all-to-all-start.1 = ((bf16[16,8,2560]{2,1,0:T(8,128)(2,1)}), bf16[16,8,2560]{2,1,0:T(8,128)(2,1)S(1)}, u32[]{:S(2)}, u32[]{:S(2)}) async-start(bf16[16,8,2560]{2,1,0:T(8,128)(2,1)} %fusion.19), calls=%async_computation.1 | async-start | bytes 1310720 | tf_op jit(solution)/shard_map/all_to_all | solution.py:91
  38.5 4.6 %copy-start.3 = (bf16[16,16,2560]{2,1,0:T(8,128)(2,1)S(1)}, bf16[16,16,2560]{2,1,0:T(8,128)(2,1)}, u32[]{:S(2)}) copy-start(bf16[16,16,2560]{2,1,0:T(8,128)(2,1)} %param.13) | copy-start | bytes 3932164
  38.5 33.1 %all-to-all-start.2 = ((bf16[16,16,2560]{2,1,0:T(8,128)(2,1)}), bf16[16,16,2560]{2,1,0:T(8,128)(2,1)S(1)}, u32[]{:S(2)}, u32[]{:S(2)}) async-start(bf16[16,16,2560]{2,1,0:T(8,128)(2,1)} %bitcast.32), calls=%async_computation.2 | async-start | bytes 2621440 | tf_op jit(solution)/shard_map/all_to_all | solution.py:91
  71.6 6.6 %copy-start.6 = (s32[64,2]{0,1:T(2,128)S(1)}, s32[64,2]{0,1:T(2,128)}, u32[]{:S(2)}) copy-start(s32[64,2]{0,1:T(2,128)} %param.15) | copy-start | bytes 1540
  71.6 6.7 %copy-start.4 = (f32[2,3,2560]{2,0,1:T(2,128)S(1)}, f32[2,3,2560]{2,0,1:T(2,128)}, u32[]{:S(2)}) copy-start(f32[2,3,2560]{2,0,1:T(2,128)} %param.17) | copy-start | bytes 184324
  71.7 35.1 %all-to-all-start = ((bf16[16,16,2560]{2,1,0:T(8,128)(2,1)}), bf16[16,16,2560]{2,1,0:T(8,128)(2,1)}, u32[]{:S(2)}, u32[]{:S(2)}) async-start(bf16[16,16,2560]{2,1,0:T(8,128)(2,1)} %bitcast.18), calls=%async_computation | async-start | bytes 2621440 | tf_op jit(solution)/shard_map/all_to_all | solution.py:91
  80.5 2.4 copy-start.2
  116.9 13.4 %copy-start.7 = (s32[64]{0:T(128)S(1)}, s32[64]{0:T(128)}, u32[]{:S(2)}) copy-start(s32[64]{0:T(128)} %param.16) | copy-start | bytes 772
  116.9 17.6 %copy-start.5 = (f32[2,2560]{1,0:T(2,128)S(1)}, f32[2,2560]{1,0:T(2,128)}, u32[]{:S(2)}) copy-start(f32[2,2560]{1,0:T(2,128)} %param.18) | copy-start | bytes 61444
  117.0 6.8 %collective-permute-start = (bf16[8,2560]{1,0:T(8,128)(2,1)S(1)}, bf16[8,2560]{1,0:T(8,128)(2,1)S(1)}, u32[]{:S(2)}, u32[]{:S(2)}) collective-permute-start(bf16[8,2560]{1,0:T(8,128)(2,1)S(1)} %multiply_convert_fusion), channel_id=1, source_target_pairs={{0,16},{2,18},{4,20},{6,22},{8,24},{10,26},{12,28},{14,30},{16,0},... | collective-permute-start | bytes 122888 | tf_op jit(solution)/shard_map/ppermute | solution.py:40
  123.8 4.5 %collective-permute-start.1 = (bf16[16,2560]{1,0:T(8,128)(2,1)S(1)}, bf16[16,2560]{1,0:T(8,128)(2,1)S(1)}, u32[]{:S(2)}, u32[]{:S(2)}) collective-permute-start(bf16[16,2560]{1,0:T(8,128)(2,1)S(1)} %maximum_select_fusion.6), channel_id=1, source_target_pairs={{0,8},{2,10},{4,12},{6,14},{8,0},{10,2},{12,4},{14,6},{16,24},{18,... | collective-permute-start | bytes 245768 | tf_op jit(solution)/shard_map/ppermute | solution.py:40
  128.4 5.4 %collective-permute-start.2 = (bf16[32,2560]{1,0:T(8,128)(2,1)S(1)}, bf16[32,2560]{1,0:T(8,128)(2,1)S(1)}, u32[]{:S(2)}, u32[]{:S(2)}) collective-permute-start(bf16[32,2560]{1,0:T(8,128)(2,1)S(1)} %maximum_select_fusion.4), channel_id=1, source_target_pairs={{0,4},{2,6},{4,0},{6,2},{8,12},{10,14},{12,8},{14,10},{16,20},{18,... | collective-permute-start | bytes 491528 | tf_op jit(solution)/shard_map/ppermute | solution.py:40
  133.8 7.1 %collective-permute-start.3 = (bf16[64,2560]{1,0:T(8,128)(2,1)S(1)}, bf16[64,2560]{1,0:T(8,128)(2,1)S(1)}, u32[]{:S(2)}, u32[]{:S(2)}) collective-permute-start(bf16[64,2560]{1,0:T(8,128)(2,1)S(1)} %maximum_select_fusion.2), channel_id=1, source_target_pairs={{0,2},{2,0},{4,6},{6,4},{8,10},{10,8},{12,14},{14,12},{16,18},{18,... | collective-permute-start | bytes 983048 | tf_op jit(solution)/shard_map/ppermute | solution.py:40
  156.9 2.2 collective-permute-start.4
  163.3 9.9 %collective-permute-start.5 = (bf16[64,2560]{1,0:T(8,128)(2,1)S(1)}, bf16[64,2560]{1,0:T(8,128)(2,1)S(1)}, u32[]{:S(2)}, u32[]{:S(2)}) collective-permute-start(bf16[64,2560]{1,0:T(8,128)(2,1)S(1)} %dynamic-slice_convert_fusion.1), channel_id=1, source_target_pairs={{0,2},{2,0},{4,6},{6,4},{8,10},{10,8},{12,14},{14,12},{16,18},{18,... | collective-permute-start | bytes 983048 | tf_op jit(solution)/shard_map/ppermute | solution.py:31
  173.2 5.6 %collective-permute-start.6 = (bf16[32,2560]{1,0:T(8,128)(2,1)S(1)}, bf16[32,2560]{1,0:T(8,128)(2,1)S(1)}, u32[]{:S(2)}, u32[]{:S(2)}) collective-permute-start(bf16[32,2560]{1,0:T(8,128)(2,1)S(1)} %dynamic-slice_convert_fusion.3), channel_id=1, source_target_pairs={{0,4},{2,6},{4,0},{6,2},{8,12},{10,14},{12,8},{14,10},{16,20},{18,... | collective-permute-start | bytes 491528 | tf_op jit(solution)/shard_map/ppermute | solution.py:31
  178.9 4.5 %collective-permute-start.7 = (bf16[16,2560]{1,0:T(8,128)(2,1)S(1)}, bf16[16,2560]{1,0:T(8,128)(2,1)S(1)}, u32[]{:S(2)}, u32[]{:S(2)}) collective-permute-start(bf16[16,2560]{1,0:T(8,128)(2,1)S(1)} %dynamic-slice_convert_fusion.5), channel_id=1, source_target_pairs={{0,8},{2,10},{4,12},{6,14},{8,0},{10,2},{12,4},{14,6},{16,24},{18,... | collective-permute-start | bytes 245768 | tf_op jit(solution)/shard_map/ppermute | solution.py:31
  183.4 6.1 %collective-permute-start.8 = (bf16[8,2560]{1,0:T(8,128)(2,1)S(1)}, bf16[8,2560]{1,0:T(8,128)(2,1)S(1)}, u32[]{:S(2)}, u32[]{:S(2)}) collective-permute-start(bf16[8,2560]{1,0:T(8,128)(2,1)S(1)} %dynamic-slice_convert_fusion.7), channel_id=1, source_target_pairs={{0,16},{2,18},{4,20},{6,22},{8,24},{10,26},{12,28},{14,30},{16,0},... | collective-permute-start | bytes 122888 | tf_op jit(solution)/shard_map/ppermute | solution.py:31
  189.5 5.0 %collective-permute-start.9 = (bf16[8,2560]{1,0:T(8,128)(2,1)S(1)}, bf16[8,2560]{1,0:T(8,128)(2,1)S(1)}, u32[]{:S(2)}, u32[]{:S(2)}) collective-permute-start(bf16[8,2560]{1,0:T(8,128)(2,1)S(1)} %add_convert_fusion.1), channel_id=1, source_target_pairs={{0,16},{2,18},{4,20},{6,22},{8,24},{10,26},{12,28},{14,30},{16,0},... | collective-permute-start | bytes 122888 | tf_op jit(solution)/shard_map/ppermute | solution.py:40
  194.5 4.5 %collective-permute-start.10 = (bf16[16,2560]{1,0:T(8,128)(2,1)S(1)}, bf16[16,2560]{1,0:T(8,128)(2,1)S(1)}, u32[]{:S(2)}, u32[]{:S(2)}) collective-permute-start(bf16[16,2560]{1,0:T(8,128)(2,1)S(1)} %maximum_select_fusion.7), channel_id=1, source_target_pairs={{0,8},{2,10},{4,12},{6,14},{8,0},{10,2},{12,4},{14,6},{16,24},{18,... | collective-permute-start | bytes 245768 | tf_op jit(solution)/shard_map/ppermute | solution.py:40
  199.0 5.4 %collective-permute-start.11 = (bf16[32,2560]{1,0:T(8,128)(2,1)S(1)}, bf16[32,2560]{1,0:T(8,128)(2,1)S(1)}, u32[]{:S(2)}, u32[]{:S(2)}) collective-permute-start(bf16[32,2560]{1,0:T(8,128)(2,1)S(1)} %maximum_select_fusion.5), channel_id=1, source_target_pairs={{0,4},{2,6},{4,0},{6,2},{8,12},{10,14},{12,8},{14,10},{16,20},{18,... | collective-permute-start | bytes 491528 | tf_op jit(solution)/shard_map/ppermute | solution.py:40
  204.5 7.1 %collective-permute-start.12 = (bf16[64,2560]{1,0:T(8,128)(2,1)S(1)}, bf16[64,2560]{1,0:T(8,128)(2,1)S(1)}, u32[]{:S(2)}, u32[]{:S(2)}) collective-permute-start(bf16[64,2560]{1,0:T(8,128)(2,1)S(1)} %maximum_select_fusion.3), channel_id=1, source_target_pairs={{0,2},{2,0},{4,6},{6,4},{8,10},{10,8},{12,14},{14,12},{16,18},{18,... | collective-permute-start | bytes 983048 | tf_op jit(solution)/shard_map/ppermute | solution.py:40
  227.7 2.2 collective-permute-start.13
  234.0 9.9 %collective-permute-start.14 = (bf16[64,2560]{1,0:T(8,128)(2,1)S(1)}, bf16[64,2560]{1,0:T(8,128)(2,1)S(1)}, u32[]{:S(2)}, u32[]{:S(2)}) collective-permute-start(bf16[64,2560]{1,0:T(8,128)(2,1)S(1)} %dynamic-slice_convert_fusion), channel_id=1, source_target_pairs={{0,2},{2,0},{4,6},{6,4},{8,10},{10,8},{12,14},{14,12},{16,18},{18,... | collective-permute-start | bytes 983048 | tf_op jit(solution)/shard_map/ppermute | solution.py:31
  243.9 16.1 %copy-start.1 = (bf16[16,16,2560]{2,1,0:T(8,128)(2,1)S(1)}, bf16[16,16,2560]{2,1,0:T(8,128)(2,1)}, u32[]{:S(2)}) copy-start(bf16[16,16,2560]{2,1,0:T(8,128)(2,1)} %param.12) | copy-start | bytes 3932164
  244.0 5.5 %collective-permute-start.15 = (bf16[32,2560]{1,0:T(8,128)(2,1)S(1)}, bf16[32,2560]{1,0:T(8,128)(2,1)S(1)}, u32[]{:S(2)}, u32[]{:S(2)}) collective-permute-start(bf16[32,2560]{1,0:T(8,128)(2,1)S(1)} %dynamic-slice_convert_fusion.2), channel_id=1, source_target_pairs={{0,4},{2,6},{4,0},{6,2},{8,12},{10,14},{12,8},{14,10},{16,20},{18,... | collective-permute-start | bytes 491528 | tf_op jit(solution)/shard_map/ppermute | solution.py:31
  249.6 4.5 %collective-permute-start.16 = (bf16[16,2560]{1,0:T(8,128)(2,1)S(1)}, bf16[16,2560]{1,0:T(8,128)(2,1)S(1)}, u32[]{:S(2)}, u32[]{:S(2)}) collective-permute-start(bf16[16,2560]{1,0:T(8,128)(2,1)S(1)} %dynamic-slice_convert_fusion.4), channel_id=1, source_target_pairs={{0,8},{2,10},{4,12},{6,14},{8,0},{10,2},{12,4},{14,6},{16,24},{18,... | collective-permute-start | bytes 245768 | tf_op jit(solution)/shard_map/ppermute | solution.py:31
  254.1 5.2 %collective-permute-start.17 = (bf16[8,2560]{1,0:T(8,128)(2,1)S(1)}, bf16[8,2560]{1,0:T(8,128)(2,1)S(1)}, u32[]{:S(2)}, u32[]{:S(2)}) collective-permute-start(bf16[8,2560]{1,0:T(8,128)(2,1)S(1)} %dynamic-slice_convert_fusion.6), channel_id=1, source_target_pairs={{0,16},{2,18},{4,20},{6,22},{8,24},{10,26},{12,28},{14,30},{16,0},... | collective-permute-start | bytes 122888 | tf_op jit(solution)/shard_map/ppermute | solution.py:31

commit v2 on v1

--- a/solution.py
+++ b/solution.py
@@ -1,6 +1,8 @@
 import jax
 import jax.numpy as jnp
 from jax import lax
+from jax.experimental import pallas as pl
+from jax.experimental.pallas import tpu as pltpu
 from jax.sharding import PartitionSpec as P
 
 D = 5120
@@ -10,6 +12,11 @@
 NODE_STEPS = 8
 ROUNDS = 2
 ETYPES = 3
+HALF_VENUES = VENUES // 2
+HEADS_STEP = 5
+COLS_STEP = HEADS_STEP * HEAD_DIM
+ROWS_HALF = HALF_VENUES * NODE_STEPS
+KEYS_HALF = HALF_VENUES * STEPS
 
 
 def flip_pairs(count, bit):
@@ -32,10 +39,10 @@
     return held
 
 
-def gather_rows(own, gx_count):
+def gather_rows(own, gx_count, bits):
     me = lax.axis_index("gx")
     held = own
-    for bit in reversed(stage_bits(gx_count)):
+    for bit in reversed(bits):
         side = (me >> bit) & 1
         other = lax.ppermute(held, "gx", flip_pairs(gx_count, bit))
         held = jnp.where(
@@ -52,6 +59,141 @@
             jnp.float32
         )
     return lax.psum(part, "ta").astype(jnp.float32)
+
+
+def arrange_body(pick_ref, key_ref, value_ref, out_ref):
+    chunks, rows, cols = out_ref.shape
+    pick = pick_ref[...]
+    for side, ref in enumerate((key_ref, value_ref)):
+        moved = jnp.dot(pick, ref[...], preferred_element_type=jnp.float32)
+        moved = moved.reshape(chunks, rows // 2, cols).astype(jnp.bfloat16)
+        out_ref[:, side * (rows // 2) : (side + 1) * (rows // 2), :] = moved
+
+
+def arrange(pick, keys, values, chunks):
+    rows, width = keys.shape
+    per_chunk = 2 * rows // chunks
+    return pl.pallas_call(
+        arrange_body,
+        grid=(width // COLS_STEP,),
+        in_specs=[
+            pl.BlockSpec((rows, rows), lambda j: (0, 0)),
+            pl.BlockSpec((rows, COLS_STEP), lambda j: (0, j)),
+            pl.BlockSpec((rows, COLS_STEP), lambda j: (0, j)),
+        ],
+        out_specs=pl.BlockSpec((chunks, per_chunk, COLS_STEP), lambda j: (0, 0, j)),
+        out_shape=jax.ShapeDtypeStruct((chunks, per_chunk, width), jnp.bfloat16),
+        compiler_params=pltpu.CompilerParams(vmem_limit_bytes=24 << 20),
+        name="arrange",
+    )(pick, keys, values)
+
+
+def score_body(own_ref, far_ref, kv_ref, probs_ref, lse_ref):
+    step = pl.program_id(0)
+
+    @pl.when(step == 0)
+    def _():
+        lse_ref[...] = jnp.zeros_like(lse_ref)
+
+    shape = (HALF_VENUES, 2, NODE_STEPS, COLS_STEP)
+    own = own_ref[...].astype(jnp.float32).reshape(shape)
+    far = far_ref[...].astype(jnp.float32).reshape(shape)
+    full = (2 * ROWS_HALF, KEYS_HALF)
+    query_step = lax.broadcasted_iota(jnp.int32, full, 0) % NODE_STEPS + (STEPS - NODE_STEPS)
+    key_step = lax.broadcasted_iota(jnp.int32, full, 1) % STEPS
+    allowed = key_step <= query_step
+    lane = lax.broadcasted_iota(jnp.int32, lse_ref.shape, 1)
+    lse = lse_ref[...]
+    for item in range(2):
+        queries = jnp.concatenate(
+            [
+                own[:, item].reshape(ROWS_HALF, COLS_STEP),
+                far[:, item].reshape(ROWS_HALF, COLS_STEP),
+            ],
+            axis=0,
+        ).astype(jnp.bfloat16)
+        keys = kv_ref[:, item].reshape(KEYS_HALF, COLS_STEP)
+        for head in range(HEADS_STEP):
+            span = slice(head * HEAD_DIM, (head + 1) * HEAD_DIM)
+            scores = lax.dot_general(
+                queries[:, span],
+                keys[:, span],
+                (((1,), (1,)), ((), ())),
+                preferred_element_type=jnp.float32,
+            ) * (1.0 / HEAD_DIM**0.5)
+            scores = jnp.where(allowed, scores, -1e30)
+            top = jnp.max(scores, axis=1, keepdims=True)
+            expd = jnp.exp(scores - top)
+            total = jnp.sum(expd, axis=1, keepdims=True)
+            probs_ref[head, item] = (expd * (1.0 / total)).astype(jnp.bfloat16)
+            column = (step * HEADS_STEP + head) * 2 + item
+            lse = jnp.where(lane == column, top + jnp.log(total), lse)
+    lse_ref[...] = lse
+
+
+def half_scores(own, far, kv):
+    width = own.shape[1]
+    rows = own.shape[0]
+    heads = width // HEAD_DIM
+    return pl.pallas_call(
+        score_body,
+        grid=(width // COLS_STEP,),
+        in_specs=[
+            pl.BlockSpec((rows, COLS_STEP), lambda j: (0, j)),
+            pl.BlockSpec((rows, COLS_STEP), lambda j: (0, j)),
+            pl.BlockSpec((HALF_VENUES, 2, STEPS, COLS_STEP), lambda j: (0, 0, 0, j)),
+        ],
+        out_specs=[
+            pl.BlockSpec((HEADS_STEP, 2, 2 * ROWS_HALF, KEYS_HALF), lambda j: (j, 0, 0, 0)),
+            pl.BlockSpec((2 * ROWS_HALF, 128), lambda j: (0, 0)),
+        ],
+        out_shape=[
+            jax.ShapeDtypeStruct((heads, 2, 2 * ROWS_HALF, KEYS_HALF), jnp.bfloat16),
+            jax.ShapeDtypeStruct((2 * ROWS_HALF, 128), jnp.float32),
+        ],
+        compiler_params=pltpu.CompilerParams(vmem_limit_bytes=24 << 20),
+        name="half_scores",
+    )(own, far, kv)
+
+
+def pool_body(probs_ref, lse_ref, far_ref, kv_ref, out_ref):
+    step = pl.program_id(0)
+    far = jnp.concatenate([far_ref[ROWS_HALF:, :], far_ref[:ROWS_HALF, :]], axis=0)
+    share = 1.0 / (1.0 + jnp.exp(far - lse_ref[...])) * (1.0 / VENUES)
+    lane = lax.broadcasted_iota(jnp.int32, lse_ref.shape, 1)
+    for head in range(HEADS_STEP):
+        span = slice(head * HEAD_DIM, (head + 1) * HEAD_DIM)
+        pooled = []
+        for item in range(2):
+            column = (step * HEADS_STEP + head) * 2 + item
+            factor = jnp.sum(jnp.where(lane == column, share, 0.0), axis=1, keepdims=True)
+            weights = probs_ref[head, item].astype(jnp.float32) * factor
+            weights = jnp.sum(weights.reshape(VENUES, NODE_STEPS, KEYS_HALF), axis=0)
+            values = kv_ref[:, item, :, span].reshape(KEYS_HALF, HEAD_DIM)
+            pooled.append(
+                jnp.dot(
+                    weights.astype(jnp.bfloat16), values, preferred_element_type=jnp.float32
+                )
+            )
+        out_ref[:, span] = jnp.concatenate(pooled, axis=0).astype(jnp.bfloat16)
+
+
+def half_pool(probs, lse, far_lse, kv):
+    width = kv.shape[3]
+    return pl.pallas_call(
+        pool_body,
+        grid=(width // COLS_STEP,),
+        in_specs=[
+            pl.BlockSpec((HEADS_STEP, 2, 2 * ROWS_HALF, KEYS_HALF), lambda j: (j, 0, 0, 0)),
+            pl.BlockSpec((2 * ROWS_HALF, 128), lambda j: (0, 0)),
+            pl.BlockSpec((2 * ROWS_HALF, 128), lambda j: (0, 0)),
+            pl.BlockSpec((HALF_VENUES, 2, STEPS, COLS_STEP), lambda j: (0, 1, 0, j)),
+        ],
+        out_specs=pl.BlockSpec((2 * NODE_STEPS, COLS_STEP), lambda j: (0, j)),
+        out_shape=jax.ShapeDtypeStruct((2 * NODE_STEPS, width), jnp.bfloat16),
+        compiler_params=pltpu.CompilerParams(vmem_limit_bytes=24 << 20),
+        name="half_pool",
+    )(probs, lse, far_lse, kv)
 
 
 def per_device(
@@ -68,58 +210,60 @@
     down_proj,
 ):
     pairs_dev, inst_total, feat_width = query_vecs.shape
-    head_count = feat_width // HEAD_DIM
     gx_count = lax.axis_size("gx")
     ta_count = lax.axis_size("ta")
-    inst_local = inst_total // gx_count
-    score_scale = 1.0 / HEAD_DIM**0.5
-    venue_idx = lax.axis_index("gx") * pairs_dev // STEPS
+    me = lax.axis_index("gx")
+    bits = stage_bits(gx_count)
+    chunks = gx_count // 2
+    groups = [list(range(chunks)), list(range(chunks, gx_count))]
+    far_half = flip_pairs(gx_count, bits[-1])
+    venue_idx = me * pairs_dev // STEPS
     slot_order = lax.dynamic_index_in_dim(slot_map, venue_idx, 0, keepdims=False)
 
-    def by_instrument(vecs):
-        pairs = vecs.shape[0]
+    def picker(pairs):
         rows = pairs * inst_total
-        row = jnp.arange(rows)
-        source = (row % pairs) * inst_total + slot_order[row // pairs]
-        pick = (source[:, None] == row[None, :]).astype(jnp.bfloat16)
-        return jnp.dot(
-            pick, vecs.reshape(rows, feat_width), preferred_element_type=jnp.float32
-        ).astype(jnp.bfloat16)
-
-    def to_instrument(vecs):
-        rows = by_instrument(vecs)
-        return lax.all_to_all(rows, "gx", split_axis=0, concat_axis=0, tiled=True)
+        row = lax.broadcasted_iota(jnp.int32, (rows, inst_total), 0)
+        inst = (row // pairs % 2) * chunks + row // (2 * pairs)
+        hit = inst == lax.broadcasted_iota(jnp.int32, (rows, inst_total), 1)
+        slot = jnp.sum(jnp.where(hit, slot_order[None, :], 0), axis=1, keepdims=True)
+        line = lax.broadcasted_iota(jnp.int32, (rows, rows), 0)
+        source = line % pairs * inst_total + slot
+        return (source == lax.broadcasted_iota(jnp.int32, (rows, rows), 1)).astype(jnp.bfloat16)
 
     whole_venue = pairs_dev == STEPS
     if whole_venue:
         query_vecs = query_vecs[STEPS - NODE_STEPS :]
-    queries = to_instrument(query_vecs)
-    keyset = to_instrument(key_vecs)
-    valueset = to_instrument(value_vecs)
-    pair_total = VENUES * STEPS
-    if whole_venue:
-        queries = queries.reshape(VENUES * NODE_STEPS, head_count, HEAD_DIM)
-    else:
-        queries = queries.reshape(VENUES, STEPS, head_count, HEAD_DIM)[:, STEPS - NODE_STEPS :]
-        queries = queries.reshape(VENUES * NODE_STEPS, head_count, HEAD_DIM)
-    keyset = keyset.reshape(pair_total, head_count, HEAD_DIM)
-    valueset = valueset.reshape(pair_total, head_count, HEAD_DIM)
-    query_steps = jnp.arange(VENUES * NODE_STEPS) % NODE_STEPS + (STEPS - NODE_STEPS)
-    key_steps = jnp.arange(pair_total) % STEPS
-    allowed = key_steps[None, :] <= query_steps[:, None]
-    scores = (
-        jnp.einsum("qhd,khd->hqk", queries, keyset, preferred_element_type=jnp.float32)
-        * score_scale
+    query_pairs = query_vecs.shape[0]
+    query_rows = query_pairs * inst_total
+    queries = jnp.dot(
+        picker(query_pairs),
+        query_vecs.reshape(query_rows, feat_width),
+        preferred_element_type=jnp.float32,
+    ).astype(jnp.bfloat16)
+    queries = lax.all_to_all(queries, "gx", 0, 0, axis_index_groups=groups, tiled=True)
+    kv_rows = pairs_dev * inst_total
+    kv = arrange(
+        picker(pairs_dev),
+        key_vecs.reshape(kv_rows, feat_width),
+        value_vecs.reshape(kv_rows, feat_width),
+        chunks,
     )
-    scores = jnp.where(allowed[None], scores, jnp.float32(-1e30))
-    row_max = jnp.max(scores, axis=-1, keepdims=True)
-    expd = jnp.exp(scores - row_max)
-    probs = (expd / jnp.sum(expd, axis=-1, keepdims=True)).astype(jnp.bfloat16)
-    attended = jnp.einsum("hqk,khd->qhd", probs, valueset, preferred_element_type=jnp.float32)
-    attended = attended.reshape(VENUES, NODE_STEPS, feat_width)
-    own_rows = jnp.mean(attended, axis=0).astype(jnp.bfloat16)
-
-    bits = stage_bits(gx_count)
+    kv, queries = lax.optimization_barrier((kv, queries))
+    if not whole_venue:
+        queries = queries.reshape(HALF_VENUES, STEPS // pairs_dev, 2, pairs_dev, feat_width)
+        queries = queries[:, (STEPS - NODE_STEPS) // pairs_dev :].transpose(0, 2, 1, 3, 4)
+        queries = queries.reshape(2 * ROWS_HALF, feat_width)
+    far_queries = lax.ppermute(queries, "gx", far_half)
+    kv = lax.all_to_all(kv, "gx", 0, 0, axis_index_groups=groups, tiled=True)
+    kv = kv.reshape(HALF_VENUES, STEPS // pairs_dev, 4, pairs_dev, feat_width)
+    kv = kv.transpose(0, 2, 1, 3, 4).reshape(HALF_VENUES, 4, STEPS, feat_width)
+    probs, lse = half_scores(queries, far_queries, kv)
+    far_lse = lax.ppermute(lse, "gx", far_half)
+    pooled = half_pool(probs, lse, far_lse, kv)
+    far_pooled = lax.ppermute(pooled, "gx", far_half)
+    pooled = (pooled.astype(jnp.float32) + far_pooled.astype(jnp.float32)).astype(jnp.bfloat16)
+    own_rows = lax.dynamic_slice_in_dim(pooled, me // chunks * NODE_STEPS, NODE_STEPS, 0)
+
     place = jnp.arange(inst_total)
     inst_at = sum((((place >> b) & 1) << (len(bits) - 1 - b)) for b in bits)
     at_source = (edge_list[:, 0][:, None] == inst_at[None, :]).astype(jnp.float32)
@@ -131,7 +275,10 @@
     row_total = inst_total * NODE_STEPS
     ff_dev = gate_proj.shape[2]
     for layer_idx in range(ROUNDS):
-        nodes = gather_rows(own_rows, gx_count)
+        if layer_idx == 0:
+            nodes = gather_rows(pooled, gx_count, bits[:-1])
+        else:
+            nodes = gather_rows(own_rows, gx_count, bits)
         flat_nodes = nodes.reshape(inst_total, NODE_STEPS * feat_width)
         gathered = jnp.dot(adj_rows, flat_nodes, preferred_element_type=jnp.float32)
         gathered = gathered.reshape(ETYPES, inst_total, NODE_STEPS, feat_width)

time: 261 us -> 223 us (0.85)
  other arithmetic: 25.7 us -> 5.94 us
  matrix products: 44 us -> 29.6 us
  Pallas kernels: 0 us -> 6.5 us
  waiting for transfers between devices: 126 us -> 121 us
  starting transfers between devices: 48.2 us -> 45.5 us
    ppermute x0 -> x3, waiting for transfers between devices: none -> 47 us  [the longest x1 38.9 us: per_device(): far_queries = lax.ppermute(queries, 'gx', far_half)]
    all_to_all x3 -> x2, waiting for transfers between devices: 54.4 us -> 7.99 us  [the longest x1 6.48 us: per_device(): lax.all_to_all(queries, 'gx', 0, 0, axis_index_groups=groups, tiled=True)]
    add x3 -> x0, other arithmetic: 15.6 us -> none  [the longest x2 15.6 us: by_instrument(): source = row % pairs * inst_total + slot_order[row // pairs]]
    dot_general x5 -> x1, matrix products: 13.3 us -> 1.25 us  [per_device(): jnp.dot(picker(query_pairs), query_vecs.reshape(query_rows, feat_width),...]
    all_to_all x3 -> x2, starting transfers between devices: 19.4 us -> 9.94 us  [the longest x1 6.18 us: per_device(): lax.all_to_all(queries, 'gx', 0, 0, axis_index_groups=groups, tiled=True)]
    pallas_call x0 -> x3, Pallas kernels: none -> 6.5 us  [the longest x1 2.87 us: half_scores(): pl.pallas_call(score_body, grid=(width // COLS_STEP,), in_specs=[pl.Block...]
    ppermute x0 -> x3, starting transfers between devices: none -> 5.88 us  [the longest x1 2.65 us: per_device(): far_queries = lax.ppermute(queries, 'gx', far_half)]
    reshape x4 -> x0, local copies, waits for them, and re-layouts: 4.84 us -> none  [the longest x1 2.54 us: per_device(): valueset = valueset.reshape(pair_total, head_count, HEAD_DIM)]
  transfers between devices with their start and end apart: 21 -> 22, of which waited for: 21 -> 22; matrix products, arithmetic and copies ran while one was open for 8% -> 0% of each run, Pallas kernels for 0% -> 1%
where the time goes in v2:
time: 223 us; the launch traced here: 222 us
  waiting for transfers between devices  121 us (54%)
  starting transfers between devices  45.5 us (20%)
  matrix products  29.6 us (13%)
  local copies, waits for them, and re-layouts  7.5 us (3%)
  Pallas kernels  6.5 us (3%)
  other arithmetic  5.94 us (3%)
  blocking collectives  5.33 us (2%)
    ppermute x1, waiting for transfers between devices, per_device(): far_queries = lax.ppermute(queries, 'gx', far_half)  38.9 us
    ppermute x8, waiting for transfers between devices, scatter_rows(): lax.ppermute(give, 'gx', flip_pairs(gx_count, bit)).astype(jnp.float32)  36.1 us
    ppermute x7, waiting for transfers between devices, gather_rows(): other = lax.ppermute(held, 'gx', flip_pairs(gx_count, bit))  26.1 us
    ppermute x7, starting transfers between devices, gather_rows(): other = lax.ppermute(held, 'gx', flip_pairs(gx_count, bit))  15.1 us
    ppermute x8, starting transfers between devices, scatter_rows(): lax.ppermute(give, 'gx', flip_pairs(gx_count, bit)).astype(jnp.float32)  14.2 us
    dot_general x2, matrix products, per_device(): jnp.dot(normed, gate_proj[layer_idx], preferred_element_type=jnp.float32)  8.29 us
    dot_general x2, matrix products, per_device(): jnp.dot(normed, up_proj[layer_idx], preferred_element_type=jnp.float32)  8.29 us
    dot_general x2, matrix products, per_device(): jnp.dot(hidden, down_proj[layer_idx], preferred_element_type=jnp.float32)  7.93 us
  transfers between devices with their start and end apart: 22, of which 22 were waited for; matrix products, arithmetic and copies ran while one was open for 0% of the time, Pallas kernels for 1%

profile of v2, /device:TPU:0, one launch (start us, length us, event | category | flops | bytes accessed | tf_op | source)
XLA Modules:
  0.0 221.9 jit_solution(12634745006578917460)
XLA Ops:
  2.4 6.2 %all-to-all-start = ((bf16[8,16,2560]{2,1,0:T(8,128)(2,1)}), bf16[8,16,2560]{2,1,0:T(8,128)(2,1)S(1)}, u32[]{:S(2)}, u32[]{:S(2)}) async-start(bf16[8,16,2560]{2,1,0:T(8,128)(2,1)} %bitcast.100), calls=%async_computation | async-start | bytes 1310720 | tf_op jit(solution)/shard_map/all_to_all | solution.py:243
  12.4 6.5 %all-to-all-done = bf16[8,16,2560]{2,1,0:T(8,128)(2,1)S(1)} async-done(((bf16[8,16,2560]{2,1,0:T(8,128)(2,1)}), bf16[8,16,2560]{2,1,0:T(8,128)(2,1)S(1)}, u32[]{:S(2)}, u32[]{:S(2)}) %all-to-all-start) | async-done | bytes 655392 | tf_op jit(solution)/shard_map/all_to_all | solution.py:243
  18.9 3.8 %all-to-all-start.1 = ((bf16[8,64,2560]{2,1,0:T(8,128)(2,1)}), bf16[8,64,2560]{2,1,0:T(8,128)(2,1)S(1)}, u32[]{:S(2)}, u32[]{:S(2)}) async-start(bf16[8,64,2560]{2,1,0:T(8,128)(2,1)} %copy-done.2), calls=%async_computation.1 | async-start | bytes 5242880 | tf_op jit(solution)/shard_map/all_to_all | solution.py:257
  22.7 2.7 %collective-permute-start = (bf16[128,2560]{1,0:T(8,128)(2,1)S(1)}, bf16[128,2560]{1,0:T(8,128)(2,1)S(1)}, u32[]{:S(2)}, u32[]{:S(2)}) collective-permute-start(bf16[128,2560]{1,0:T(8,128)(2,1)S(1)} %bitcast.96), channel_id=1, source_target_pairs={{0,16},{2,18},{4,20},{6,22},{8,24},{10,26},{12,28},{14,30},{16,0},... | collective-permute-start | bytes 1966088 | tf_op jit(solution)/shard_map/ppermute | solution.py:256
  25.4 38.9 %collective-permute-done.far_ref = bf16[128,2560]{1,0:T(8,128)(2,1)S(1)} collective-permute-done((bf16[128,2560]{1,0:T(8,128)(2,1)S(1)}, bf16[128,2560]{1,0:T(8,128)(2,1)S(1)}, u32[]{:S(2)}, u32[]{:S(2)}) %collective-permute-start) | collective-permute-done | bytes 655392 | tf_op jit(solution)/shard_map/ppermute | solution.py:256
  67.7 2.9 %half_scores.1 = (bf16[20,2,128,128]{3,2,1,0:T(8,128)(2,1)S(1)}, f32[128,128]{1,0:T(8,128)S(1)}) custom-call(bf16[128,2560]{1,0:T(8,128)(2,1)S(1)} %bitcast.97, bf16[128,2560]{1,0:T(8,128)(2,1)S(1)} %copy-done.6, bf16[8,4,16,2560]{3,2,1,0:T(8,128)(2,1)S(1)} %bitcast.94), custom_call_target="tpu_custom_call" | custom-call | tf_op jit(solution)/shard_map/half_scores/pallas_call | solution.py:138
  72.6 4.0 %collective-permute-done.1.far_ref = f32[128,128]{1,0:T(8,128)S(1)} collective-permute-done((f32[128,128]{1,0:T(8,128)S(1)}, f32[128,128]{1,0:T(8,128)S(1)}, u32[]{:S(2)}, u32[]{:S(2)}) %collective-permute-start.1) | collective-permute-done | bytes 65568 | tf_op jit(solution)/shard_map/ppermute | solution.py:261
  79.5 4.1 %collective-permute-done.2 = bf16[16,2560]{1,0:T(8,128)(2,1)S(1)} collective-permute-done((bf16[16,2560]{1,0:T(8,128)(2,1)S(1)}, bf16[16,2560]{1,0:T(8,128)(2,1)S(1)}, u32[]{:S(2)}, u32[]{:S(2)}) %collective-permute-start.2) | collective-permute-done | bytes 81952 | tf_op jit(solution)/shard_map/ppermute | solution.py:263
  83.6 2.9 %collective-permute-start.3 = (bf16[16,2560]{1,0:T(8,128)(2,1)S(1)}, bf16[16,2560]{1,0:T(8,128)(2,1)S(1)}, u32[]{:S(2)}, u32[]{:S(2)}) collective-permute-start(bf16[16,2560]{1,0:T(8,128)(2,1)S(1)} %add_convert_fusion), channel_id=1, source_target_pairs={{0,8},{2,10},{4,12},{6,14},{8,0},{10,2},{12,4},{14,6},{16,24},{18,... | collective-permute-start | bytes 245768 | tf_op jit(solution)/shard_map/ppermute | solution.py:47
  90.4 4.0 %collective-permute-done.4 = bf16[32,2560]{1,0:T(8,128)(2,1)S(1)} collective-permute-done((bf16[32,2560]{1,0:T(8,128)(2,1)S(1)}, bf16[32,2560]{1,0:T(8,128)(2,1)S(1)}, u32[]{:S(2)}, u32[]{:S(2)}) %collective-permute-start.4) | collective-permute-done | bytes 163872 | tf_op jit(solution)/shard_map/ppermute | solution.py:47
  94.4 3.9 %collective-permute-start.5 = (bf16[64,2560]{1,0:T(8,128)(2,1)S(1)}, bf16[64,2560]{1,0:T(8,128)(2,1)S(1)}, u32[]{:S(2)}, u32[]{:S(2)}) collective-permute-start(bf16[64,2560]{1,0:T(8,128)(2,1)S(1)} %maximum_select_fusion.2), channel_id=1, source_target_pairs={{0,2},{2,0},{4,6},{6,4},{8,10},{10,8},{12,14},{14,12},{16,18},{18,... | collective-permute-start | bytes 983048 | tf_op jit(solution)/shard_map/ppermute | solution.py:47
  98.7 4.6 %collective-permute-done.5 = bf16[64,2560]{1,0:T(8,128)(2,1)S(1)} collective-permute-done((bf16[64,2560]{1,0:T(8,128)(2,1)S(1)}, bf16[64,2560]{1,0:T(8,128)(2,1)S(1)}, u32[]{:S(2)}, u32[]{:S(2)}) %collective-permute-start.5) | collective-permute-done | bytes 327712 | tf_op jit(solution)/shard_map/ppermute | solution.py:47
  107.3 2.6 %psum.14 = f32[128]{0:T(128)S(1)} all-reduce(f32[128]{0:T(128)S(1)} %fusion.33), channel_id=1, replica_groups=mesh['gx'=16,'ta'=2] {'ta'}, use_global_device_ids=true, to_apply=%region_5.6 | all-reduce | flops 128 | bytes 1024 | tf_op jit(solution)/shard_map/psum | solution.py:290
  111.0 4.1 %fusion.21 = bf16[128,1280]{1,0:T(8,128)(2,1)S(1)} fusion(bf16[2,2560,1280]{2,1,0:T(8,128)(2,1)} %param.20, bf16[16,8,2560]{2,0,1:T(8,128)(2,1)S(1)} %fusion.41), kind=kOutput, calls=%fused_computation.22 | convolution fusion | flops 839024640 | bytes 7536640 | tf_op jit(solution)/shard_map/dot_general | solution.py:294
  115.2 4.1 %fusion.18 = bf16[128,1280]{1,0:T(8,128)(2,1)S(1)} fusion(bf16[2,2560,1280]{2,1,0:T(8,128)(2,1)} %param.19, bf16[16,8,2560]{2,0,1:T(8,128)(2,1)S(1)} %fusion.41), kind=kOutput, calls=%fused_computation.21 | convolution fusion | flops 839024640 | bytes 7536640 | tf_op jit(solution)/shard_map/dot_general | solution.py:293
  121.7 3.9 %fusion.6 = f32[128,2560]{1,0:T(8,128)S(1)} fusion(bf16[2,1280,2560]{2,1,0:T(8,128)(2,1)} %param.21, f32[128,2560]{1,0:T(8,128)S(1)} %convert_add_fusion.3), kind=kOutput, calls=%fused_computation.6 | convolution fusion | flops 839843840 | bytes 9175040 | tf_op jit(solution)/shard_map/dot_general | solution.py:300
  127.8 8.0 %collective-permute-done.7 = bf16[64,2560]{1,0:T(8,128)(2,1)S(1)} collective-permute-done((bf16[64,2560]{1,0:T(8,128)(2,1)S(1)}, bf16[64,2560]{1,0:T(8,128)(2,1)S(1)}, u32[]{:S(2)}, u32[]{:S(2)}) %collective-permute-start.7) | collective-permute-done | bytes 327712 | tf_op jit(solution)/shard_map/ppermute | solution.py:38
  137.5 4.3 %collective-permute-done.8 = bf16[32,2560]{1,0:T(8,128)(2,1)S(1)} collective-permute-done((bf16[32,2560]{1,0:T(8,128)(2,1)S(1)}, bf16[32,2560]{1,0:T(8,128)(2,1)S(1)}, u32[]{:S(2)}, u32[]{:S(2)}) %collective-permute-start.8) | collective-permute-done | bytes 163872 | tf_op jit(solution)/shard_map/ppermute | solution.py:38
  143.9 2.4 %collective-permute-done.9 = bf16[16,2560]{1,0:T(8,128)(2,1)S(1)} collective-permute-done((bf16[16,2560]{1,0:T(8,128)(2,1)S(1)}, bf16[16,2560]{1,0:T(8,128)(2,1)S(1)}, u32[]{:S(2)}, u32[]{:S(2)}) %collective-permute-start.9) | collective-permute-done | bytes 81952 | tf_op jit(solution)/shard_map/ppermute | solution.py:38
  147.8 3.6 %collective-permute-done.10 = bf16[8,2560]{1,0:T(8,128)(2,1)S(1)} collective-permute-done((bf16[8,2560]{1,0:T(8,128)(2,1)S(1)}, bf16[8,2560]{1,0:T(8,128)(2,1)S(1)}, u32[]{:S(2)}, u32[]{:S(2)}) %collective-permute-start.10) | collective-permute-done | bytes 40992 | tf_op jit(solution)/shard_map/ppermute | solution.py:38
  152.8 3.6 %collective-permute-done.11 = bf16[8,2560]{1,0:T(8,128)(2,1)S(1)} collective-permute-done((bf16[8,2560]{1,0:T(8,128)(2,1)S(1)}, bf16[8,2560]{1,0:T(8,128)(2,1)S(1)}, u32[]{:S(2)}, u32[]{:S(2)}) %collective-permute-start.11) | collective-permute-done | bytes 40992 | tf_op jit(solution)/shard_map/ppermute | solution.py:47
  158.7 2.4 %collective-permute-done.12 = bf16[16,2560]{1,0:T(8,128)(2,1)S(1)} collective-permute-done((bf16[16,2560]{1,0:T(8,128)(2,1)S(1)}, bf16[16,2560]{1,0:T(8,128)(2,1)S(1)}, u32[]{:S(2)}, u32[]{:S(2)}) %collective-permute-start.12) | collective-permute-done | bytes 81952 | tf_op jit(solution)/shard_map/ppermute | solution.py:47
  162.7 3.8 %collective-permute-done.13 = bf16[32,2560]{1,0:T(8,128)(2,1)S(1)} collective-permute-done((bf16[32,2560]{1,0:T(8,128)(2,1)S(1)}, bf16[32,2560]{1,0:T(8,128)(2,1)S(1)}, u32[]{:S(2)}, u32[]{:S(2)}) %collective-permute-start.13) | collective-permute-done | bytes 163872 | tf_op jit(solution)/shard_map/ppermute | solution.py:47
  168.4 5.3 %collective-permute-done.14 = bf16[64,2560]{1,0:T(8,128)(2,1)S(1)} collective-permute-done((bf16[64,2560]{1,0:T(8,128)(2,1)S(1)}, bf16[64,2560]{1,0:T(8,128)(2,1)S(1)}, u32[]{:S(2)}, u32[]{:S(2)}) %collective-permute-start.14) | collective-permute-done | bytes 327712 | tf_op jit(solution)/shard_map/ppermute | solution.py:47
  177.7 2.7 %psum.15 = f32[128]{0:T(128)S(1)} all-reduce(f32[128]{0:T(128)S(1)} %fusion.35), channel_id=1, replica_groups=mesh['gx'=16,'ta'=2] {'ta'}, use_global_device_ids=true, to_apply=%region_8.9 | all-reduce | flops 128 | bytes 1024 | tf_op jit(solution)/shard_map/psum | solution.py:290
  181.4 4.1 %fusion.27 = bf16[128,1280]{1,0:T(8,128)(2,1)S(1)} fusion(bf16[2,2560,1280]{2,1,0:T(8,128)(2,1)} %param.20, bf16[16,8,2560]{2,0,1:T(8,128)(2,1)S(1)} %fusion.38), kind=kOutput, calls=%fused_computation.24 | convolution fusion | flops 839024640 | bytes 7536640 | tf_op jit(solution)/shard_map/dot_general | solution.py:294
  185.6 4.1 %fusion.24 = bf16[128,1280]{1,0:T(8,128)(2,1)S(1)} fusion(bf16[2,2560,1280]{2,1,0:T(8,128)(2,1)} %param.19, bf16[16,8,2560]{2,0,1:T(8,128)(2,1)S(1)} %fusion.38), kind=kOutput, calls=%fused_computation.23 | convolution fusion | flops 839024640 | bytes 7536640 | tf_op jit(solution)/shard_map/dot_general | solution.py:293
  192.1 4.0 %fusion = f32[128,2560]{1,0:T(8,128)S(1)} fusion(bf16[2,1280,2560]{2,1,0:T(8,128)(2,1)} %param.21, f32[128,2560]{1,0:T(8,128)S(1)} %convert_add_fusion.2), kind=kOutput, calls=%fused_computation | convolution fusion | flops 839843840 | bytes 9175040 | tf_op jit(solution)/shard_map/dot_general | solution.py:300
  198.0 8.0 %collective-permute-done.16 = bf16[64,2560]{1,0:T(8,128)(2,1)S(1)} collective-permute-done((bf16[64,2560]{1,0:T(8,128)(2,1)S(1)}, bf16[64,2560]{1,0:T(8,128)(2,1)S(1)}, u32[]{:S(2)}, u32[]{:S(2)}) %collective-permute-start.16) | collective-permute-done | bytes 327712 | tf_op jit(solution)/shard_map/ppermute | solution.py:38
  207.6 4.0 %collective-permute-done.17 = bf16[32,2560]{1,0:T(8,128)(2,1)S(1)} collective-permute-done((bf16[32,2560]{1,0:T(8,128)(2,1)S(1)}, bf16[32,2560]{1,0:T(8,128)(2,1)S(1)}, u32[]{:S(2)}, u32[]{:S(2)}) %collective-permute-start.17) | collective-permute-done | bytes 163872 | tf_op jit(solution)/shard_map/ppermute | solution.py:38
  213.8 2.4 %collective-permute-done.18 = bf16[16,2560]{1,0:T(8,128)(2,1)S(1)} collective-permute-done((bf16[16,2560]{1,0:T(8,128)(2,1)S(1)}, bf16[16,2560]{1,0:T(8,128)(2,1)S(1)}, u32[]{:S(2)}, u32[]{:S(2)}) %collective-permute-start.18) | collective-permute-done | bytes 81952 | tf_op jit(solution)/shard_map/ppermute | solution.py:38
  217.9 3.3 %collective-permute-done.19 = bf16[8,2560]{1,0:T(8,128)(2,1)S(1)} collective-permute-done((bf16[8,2560]{1,0:T(8,128)(2,1)S(1)}, bf16[8,2560]{1,0:T(8,128)(2,1)S(1)}, u32[]{:S(2)}, u32[]{:S(2)}) %collective-permute-start.19) | collective-permute-done | bytes 40992 | tf_op jit(solution)/shard_map/ppermute | solution.py:38
  (117 shorter events, 56.0 us)
Async XLA Ops:
  0.0 1.1 slice-start
  1.1 7.8 %copy-start.3 = (bf16[16,16,2560]{2,1,0:T(8,128)(2,1)S(1)}, bf16[16,16,2560]{2,1,0:T(8,128)(2,1)}, u32[]{:S(2)}) copy-start(bf16[16,16,2560]{2,1,0:T(8,128)(2,1)} %param.12) | copy-start | bytes 3932164
  1.1 7.8 %copy-start.4 = (bf16[16,16,2560]{2,1,0:T(8,128)(2,1)S(1)}, bf16[16,16,2560]{2,1,0:T(8,128)(2,1)}, u32[]{:S(2)}) copy-start(bf16[16,16,2560]{2,1,0:T(8,128)(2,1)} %param.13) | copy-start | bytes 3932164
  2.4 16.5 %all-to-all-start = ((bf16[8,16,2560]{2,1,0:T(8,128)(2,1)}), bf16[8,16,2560]{2,1,0:T(8,128)(2,1)S(1)}, u32[]{:S(2)}, u32[]{:S(2)}) async-start(bf16[8,16,2560]{2,1,0:T(8,128)(2,1)} %bitcast.100), calls=%async_computation | async-start | bytes 1310720 | tf_op jit(solution)/shard_map/all_to_all | solution.py:243
  10.9 1.5 copy-start.2
  18.9 6.4 %copy-start.7 = (f32[2,3,2560]{2,0,1:T(2,128)S(1)}, f32[2,3,2560]{2,0,1:T(2,128)}, u32[]{:S(2)}) copy-start(f32[2,3,2560]{2,0,1:T(2,128)} %param.17) | copy-start | bytes 184324
  18.9 47.8 %all-to-all-start.1 = ((bf16[8,64,2560]{2,1,0:T(8,128)(2,1)}), bf16[8,64,2560]{2,1,0:T(8,128)(2,1)S(1)}, u32[]{:S(2)}, u32[]{:S(2)}) async-start(bf16[8,64,2560]{2,1,0:T(8,128)(2,1)} %copy-done.2), calls=%async_computation.1 | async-start | bytes 5242880 | tf_op jit(solution)/shard_map/all_to_all | solution.py:257
  22.7 41.6 %collective-permute-start = (bf16[128,2560]{1,0:T(8,128)(2,1)S(1)}, bf16[128,2560]{1,0:T(8,128)(2,1)S(1)}, u32[]{:S(2)}, u32[]{:S(2)}) collective-permute-start(bf16[128,2560]{1,0:T(8,128)(2,1)S(1)} %bitcast.96), channel_id=1, source_target_pairs={{0,16},{2,18},{4,20},{6,22},{8,24},{10,26},{12,28},{14,30},{16,0},... | collective-permute-start | bytes 1966088 | tf_op jit(solution)/shard_map/ppermute | solution.py:256
  66.6 1.1 copy-start.6
  67.7 4.8 %copy-start.9 = (s32[64,2]{0,1:T(2,128)S(1)}, s32[64,2]{0,1:T(2,128)}, u32[]{:S(2)}) copy-start(s32[64,2]{0,1:T(2,128)} %param.15) | copy-start | bytes 1540
  70.6 5.9 %collective-permute-start.1 = (f32[128,128]{1,0:T(8,128)S(1)}, f32[128,128]{1,0:T(8,128)S(1)}, u32[]{:S(2)}, u32[]{:S(2)}) collective-permute-start(f32[128,128]{1,0:T(8,128)S(1)} %get-tuple-element.12.lse_ref), channel_id=1, source_target_pairs={{0,16},{2,18},{4,20},{6,22},{8,24},{10,26},{12,28},{14,30},{16,0},... | collective-permute-start | bytes 196616 | tf_op jit(solution)/shard_map/ppermute | solution.py:261
  76.5 13.6 %copy-start.10 = (s32[64]{0:T(128)S(1)}, s32[64]{0:T(128)}, u32[]{:S(2)}) copy-start(s32[64]{0:T(128)} %param.16) | copy-start | bytes 772
  78.2 20.5 %copy-start.8 = (f32[2,2560]{1,0:T(2,128)S(1)}, f32[2,2560]{1,0:T(2,128)}, u32[]{:S(2)}) copy-start(f32[2,2560]{1,0:T(2,128)} %param.18) | copy-start | bytes 61444
  78.2 5.4 %collective-permute-start.2 = (bf16[16,2560]{1,0:T(8,128)(2,1)S(1)}, bf16[16,2560]{1,0:T(8,128)(2,1)S(1)}, u32[]{:S(2)}, u32[]{:S(2)}) collective-permute-start(bf16[16,2560]{1,0:T(8,128)(2,1)S(1)} %half_pool.1), channel_id=1, source_target_pairs={{0,16},{2,18},{4,20},{6,22},{8,24},{10,26},{12,28},{14,30},{16,0},... | collective-permute-start | bytes 245768 | tf_op jit(solution)/shard_map/ppermute | solution.py:263
  83.6 5.3 %collective-permute-start.3 = (bf16[16,2560]{1,0:T(8,128)(2,1)S(1)}, bf16[16,2560]{1,0:T(8,128)(2,1)S(1)}, u32[]{:S(2)}, u32[]{:S(2)}) collective-permute-start(bf16[16,2560]{1,0:T(8,128)(2,1)S(1)} %add_convert_fusion), channel_id=1, source_target_pairs={{0,8},{2,10},{4,12},{6,14},{8,0},{10,2},{12,4},{14,6},{16,24},{18,... | collective-permute-start | bytes 245768 | tf_op jit(solution)/shard_map/ppermute | solution.py:47
  88.9 5.4 %collective-permute-start.4 = (bf16[32,2560]{1,0:T(8,128)(2,1)S(1)}, bf16[32,2560]{1,0:T(8,128)(2,1)S(1)}, u32[]{:S(2)}, u32[]{:S(2)}) collective-permute-start(bf16[32,2560]{1,0:T(8,128)(2,1)S(1)} %maximum_select_fusion.4), channel_id=1, source_target_pairs={{0,4},{2,6},{4,0},{6,2},{8,12},{10,14},{12,8},{14,10},{16,20},{18,... | collective-permute-start | bytes 491528 | tf_op jit(solution)/shard_map/ppermute | solution.py:47
  94.4 9.0 %collective-permute-start.5 = (bf16[64,2560]{1,0:T(8,128)(2,1)S(1)}, bf16[64,2560]{1,0:T(8,128)(2,1)S(1)}, u32[]{:S(2)}, u32[]{:S(2)}) collective-permute-start(bf16[64,2560]{1,0:T(8,128)(2,1)S(1)} %maximum_select_fusion.2), channel_id=1, source_target_pairs={{0,2},{2,0},{4,6},{6,4},{8,10},{10,8},{12,14},{14,12},{16,18},{18,... | collective-permute-start | bytes 983048 | tf_op jit(solution)/shard_map/ppermute | solution.py:47
  119.4 2.2 collective-permute-start.6
  125.7 10.1 %collective-permute-start.7 = (bf16[64,2560]{1,0:T(8,128)(2,1)S(1)}, bf16[64,2560]{1,0:T(8,128)(2,1)S(1)}, u32[]{:S(2)}, u32[]{:S(2)}) collective-permute-start(bf16[64,2560]{1,0:T(8,128)(2,1)S(1)} %dynamic-slice_convert_fusion.1), channel_id=1, source_target_pairs={{0,2},{2,0},{4,6},{6,4},{8,10},{10,8},{12,14},{14,12},{16,18},{18,... | collective-permute-start | bytes 983048 | tf_op jit(solution)/shard_map/ppermute | solution.py:38
  135.9 5.8 %collective-permute-start.8 = (bf16[32,2560]{1,0:T(8,128)(2,1)S(1)}, bf16[32,2560]{1,0:T(8,128)(2,1)S(1)}, u32[]{:S(2)}, u32[]{:S(2)}) collective-permute-start(bf16[32,2560]{1,0:T(8,128)(2,1)S(1)} %dynamic-slice_convert_fusion.3), channel_id=1, source_target_pairs={{0,4},{2,6},{4,0},{6,2},{8,12},{10,14},{12,8},{14,10},{16,20},{18,... | collective-permute-start | bytes 491528 | tf_op jit(solution)/shard_map/ppermute | solution.py:38
  141.8 4.5 %collective-permute-start.9 = (bf16[16,2560]{1,0:T(8,128)(2,1)S(1)}, bf16[16,2560]{1,0:T(8,128)(2,1)S(1)}, u32[]{:S(2)}, u32[]{:S(2)}) collective-permute-start(bf16[16,2560]{1,0:T(8,128)(2,1)S(1)} %dynamic-slice_convert_fusion.5), channel_id=1, source_target_pairs={{0,8},{2,10},{4,12},{6,14},{8,0},{10,2},{12,4},{14,6},{16,24},{18,... | collective-permute-start | bytes 245768 | tf_op jit(solution)/shard_map/ppermute | solution.py:38
  146.4 5.0 %collective-permute-start.10 = (bf16[8,2560]{1,0:T(8,128)(2,1)S(1)}, bf16[8,2560]{1,0:T(8,128)(2,1)S(1)}, u32[]{:S(2)}, u32[]{:S(2)}) collective-permute-start(bf16[8,2560]{1,0:T(8,128)(2,1)S(1)} %dynamic-slice_convert_fusion.7), channel_id=1, source_target_pairs={{0,16},{2,18},{4,20},{6,22},{8,24},{10,26},{12,28},{14,30},{16,0},... | collective-permute-start | bytes 122888 | tf_op jit(solution)/shard_map/ppermute | solution.py:38
  151.4 5.0 %collective-permute-start.11 = (bf16[8,2560]{1,0:T(8,128)(2,1)S(1)}, bf16[8,2560]{1,0:T(8,128)(2,1)S(1)}, u32[]{:S(2)}, u32[]{:S(2)}) collective-permute-start(bf16[8,2560]{1,0:T(8,128)(2,1)S(1)} %add_convert_fusion.2), channel_id=1, source_target_pairs={{0,16},{2,18},{4,20},{6,22},{8,24},{10,26},{12,28},{14,30},{16,0},... | collective-permute-start | bytes 122888 | tf_op jit(solution)/shard_map/ppermute | solution.py:47
  156.4 4.7 %collective-permute-start.12 = (bf16[16,2560]{1,0:T(8,128)(2,1)S(1)}, bf16[16,2560]{1,0:T(8,128)(2,1)S(1)}, u32[]{:S(2)}, u32[]{:S(2)}) collective-permute-start(bf16[16,2560]{1,0:T(8,128)(2,1)S(1)} %maximum_select_fusion.6), channel_id=1, source_target_pairs={{0,8},{2,10},{4,12},{6,14},{8,0},{10,2},{12,4},{14,6},{16,24},{18,... | collective-permute-start | bytes 245768 | tf_op jit(solution)/shard_map/ppermute | solution.py:47
  161.1 5.4 %collective-permute-start.13 = (bf16[32,2560]{1,0:T(8,128)(2,1)S(1)}, bf16[32,2560]{1,0:T(8,128)(2,1)S(1)}, u32[]{:S(2)}, u32[]{:S(2)}) collective-permute-start(bf16[32,2560]{1,0:T(8,128)(2,1)S(1)} %maximum_select_fusion.5), channel_id=1, source_target_pairs={{0,4},{2,6},{4,0},{6,2},{8,12},{10,14},{12,8},{14,10},{16,20},{18,... | collective-permute-start | bytes 491528 | tf_op jit(solution)/shard_map/ppermute | solution.py:47
  166.6 7.1 %collective-permute-start.14 = (bf16[64,2560]{1,0:T(8,128)(2,1)S(1)}, bf16[64,2560]{1,0:T(8,128)(2,1)S(1)}, u32[]{:S(2)}, u32[]{:S(2)}) collective-permute-start(bf16[64,2560]{1,0:T(8,128)(2,1)S(1)} %maximum_select_fusion.3), channel_id=1, source_target_pairs={{0,2},{2,0},{4,6},{6,4},{8,10},{10,8},{12,14},{14,12},{16,18},{18,... | collective-permute-start | bytes 983048 | tf_op jit(solution)/shard_map/ppermute | solution.py:47
  189.8 2.2 collective-permute-start.15
  196.2 9.8 %collective-permute-start.16 = (bf16[64,2560]{1,0:T(8,128)(2,1)S(1)}, bf16[64,2560]{1,0:T(8,128)(2,1)S(1)}, u32[]{:S(2)}, u32[]{:S(2)}) collective-permute-start(bf16[64,2560]{1,0:T(8,128)(2,1)S(1)} %dynamic-slice_convert_fusion), channel_id=1, source_target_pairs={{0,2},{2,0},{4,6},{6,4},{8,10},{10,8},{12,14},{14,12},{16,18},{18,... | collective-permute-start | bytes 983048 | tf_op jit(solution)/shard_map/ppermute | solution.py:38
  206.0 15.8 %copy-start.1 = (s32[16,16]{1,0:T(8,128)S(1)}, s32[16,16]{1,0:T(8,128)}, u32[]{:S(2)}) copy-start(s32[16,16]{1,0:T(8,128)} %param.14) | copy-start | bytes 3076
  206.1 5.5 %collective-permute-start.17 = (bf16[32,2560]{1,0:T(8,128)(2,1)S(1)}, bf16[32,2560]{1,0:T(8,128)(2,1)S(1)}, u32[]{:S(2)}, u32[]{:S(2)}) collective-permute-start(bf16[32,2560]{1,0:T(8,128)(2,1)S(1)} %dynamic-slice_convert_fusion.2), channel_id=1, source_target_pairs={{0,4},{2,6},{4,0},{6,2},{8,12},{10,14},{12,8},{14,10},{16,20},{18,... | collective-permute-start | bytes 491528 | tf_op jit(solution)/shard_map/ppermute | solution.py:38
  211.7 4.5 %collective-permute-start.18 = (bf16[16,2560]{1,0:T(8,128)(2,1)S(1)}, bf16[16,2560]{1,0:T(8,128)(2,1)S(1)}, u32[]{:S(2)}, u32[]{:S(2)}) collective-permute-start(bf16[16,2560]{1,0:T(8,128)(2,1)S(1)} %dynamic-slice_convert_fusion.4), channel_id=1, source_target_pairs={{0,8},{2,10},{4,12},{6,14},{8,0},{10,2},{12,4},{14,6},{16,24},{18,... | collective-permute-start | bytes 245768 | tf_op jit(solution)/shard_map/ppermute | solution.py:38
  216.2 5.0 %collective-permute-start.19 = (bf16[8,2560]{1,0:T(8,128)(2,1)S(1)}, bf16[8,2560]{1,0:T(8,128)(2,1)S(1)}, u32[]{:S(2)}, u32[]{:S(2)}) collective-permute-start(bf16[8,2560]{1,0:T(8,128)(2,1)S(1)} %dynamic-slice_convert_fusion.6), channel_id=1, source_target_pairs={{0,16},{2,18},{4,20},{6,22},{8,24},{10,26},{12,28},{14,30},{16,0},... | collective-permute-start | bytes 122888 | tf_op jit(solution)/shard_map/ppermute | solution.py:38
  (2 other events, 1.5 us)

commit v3 on v2

--- a/solution.py
+++ b/solution.py
@@ -1,3 +1,5 @@
+import functools
+
 import jax
 import jax.numpy as jnp
 from jax import lax
@@ -17,48 +19,43 @@
 COLS_STEP = HEADS_STEP * HEAD_DIM
 ROWS_HALF = HALF_VENUES * NODE_STEPS
 KEYS_HALF = HALF_VENUES * STEPS
-
-
-def flip_pairs(count, bit):
-    return [(i, i ^ (1 << bit)) for i in range(count)]
+LSE_ITEM = 64
 
 
 def stage_bits(count):
     return list(range(count.bit_length() - 1))
 
 
-def scatter_rows(partial, gx_count):
-    me = lax.axis_index("gx")
-    held = partial.astype(jnp.float32)
-    for bit in stage_bits(gx_count):
+def bit_orders(gx_count, ta_count):
+    plain = stage_bits(gx_count)
+    if ta_count != 2:
+        return [plain] * ta_count
+    return [plain, [plain[1], plain[0]] + plain[2:]]
+
+
+def swap_stage(block, orders, stage):
+    gx_count, ta_count = lax.axis_size("gx"), lax.axis_size("ta")
+    pairs = [
+        (g * ta_count + t, (g ^ (1 << orders[t][stage])) * ta_count + t)
+        for g in range(gx_count)
+        for t in range(ta_count)
+    ]
+    return lax.ppermute(block, ("gx", "ta"), pairs)
+
+
+def scatter_rows(keep, give, orders):
+    held = keep + swap_stage(give, orders, 0).astype(jnp.float32)
+    for stage in range(1, len(orders[0])):
         half = held.shape[0] // 2
-        side = (me >> bit) & 1
-        keep = lax.dynamic_slice_in_dim(held, side * half, half, 0)
-        give = lax.dynamic_slice_in_dim(held, (1 - side) * half, half, 0).astype(jnp.bfloat16)
-        held = keep + lax.ppermute(give, "gx", flip_pairs(gx_count, bit)).astype(jnp.float32)
+        give = held[half:].astype(jnp.bfloat16)
+        held = held[:half] + swap_stage(give, orders, stage).astype(jnp.float32)
     return held
 
 
-def gather_rows(own, gx_count, bits):
-    me = lax.axis_index("gx")
-    held = own
-    for bit in reversed(bits):
-        side = (me >> bit) & 1
-        other = lax.ppermute(held, "gx", flip_pairs(gx_count, bit))
-        held = jnp.where(
-            side == 0,
-            jnp.concatenate([held, other], axis=0),
-            jnp.concatenate([other, held], axis=0),
-        )
-    return held
-
-
-def sum_over_ta(part, ta_count):
-    if ta_count == 2:
-        return part.astype(jnp.float32) + lax.ppermute(part, "ta", [(0, 1), (1, 0)]).astype(
-            jnp.float32
-        )
-    return lax.psum(part, "ta").astype(jnp.float32)
+def gather_rows(held, orders, stages):
+    for stage in reversed(range(1, stages)):
+        held = jnp.concatenate([held, swap_stage(held, orders, stage)], axis=0)
+    return held, swap_stage(held, orders, 0)
 
 
 def arrange_body(pick_ref, key_ref, value_ref, out_ref):
@@ -108,7 +105,7 @@
         queries = jnp.concatenate(
             [
                 own[:, item].reshape(ROWS_HALF, COLS_STEP),
-                far[:, item].reshape(ROWS_HALF, COLS_STEP),
+                far[:, 1 - item].reshape(ROWS_HALF, COLS_STEP),
             ],
             axis=0,
         ).astype(jnp.bfloat16)
@@ -126,7 +123,7 @@
             expd = jnp.exp(scores - top)
             total = jnp.sum(expd, axis=1, keepdims=True)
             probs_ref[head, item] = (expd * (1.0 / total)).astype(jnp.bfloat16)
-            column = (step * HEADS_STEP + head) * 2 + item
+            column = step * HEADS_STEP + head + item * LSE_ITEM
             lse = jnp.where(lane == column, top + jnp.log(total), lse)
     lse_ref[...] = lse
 
@@ -159,13 +156,14 @@
 def pool_body(probs_ref, lse_ref, far_ref, kv_ref, out_ref):
     step = pl.program_id(0)
     far = jnp.concatenate([far_ref[ROWS_HALF:, :], far_ref[:ROWS_HALF, :]], axis=0)
+    far = jnp.concatenate([far[:, LSE_ITEM:], far[:, :LSE_ITEM]], axis=1)
     share = 1.0 / (1.0 + jnp.exp(far - lse_ref[...])) * (1.0 / VENUES)
     lane = lax.broadcasted_iota(jnp.int32, lse_ref.shape, 1)
     for head in range(HEADS_STEP):
         span = slice(head * HEAD_DIM, (head + 1) * HEAD_DIM)
         pooled = []
         for item in range(2):
-            column = (step * HEADS_STEP + head) * 2 + item
+            column = step * HEADS_STEP + head + item * LSE_ITEM
             factor = jnp.sum(jnp.where(lane == column, share, 0.0), axis=1, keepdims=True)
             weights = probs_ref[head, item].astype(jnp.float32) * factor
             weights = jnp.sum(weights.reshape(VENUES, NODE_STEPS, KEYS_HALF), axis=0)
@@ -194,6 +192,136 @@
         compiler_params=pltpu.CompilerParams(vmem_limit_bytes=24 << 20),
         name="half_pool",
     )(probs, lse, far_lse, kv)
+
+
+def pad_lanes(width):
+    return -(-width // 128) * 128
+
+
+def expand_body(near_ref, far_ref, mix_ref, inv_ref, gain_ref, norm_ref, gate_ref, up_ref, out_ref, total_ref, square_ref):
+    step = pl.program_id(0)
+    steps = pl.num_programs(0)
+    width = gate_ref.shape[1]
+    padded = pad_lanes(width)
+
+    @pl.when(step == 0)
+    def _():
+        total_ref[...] = jnp.zeros_like(total_ref)
+        square_ref[...] = jnp.zeros_like(square_ref)
+
+    nodes = jnp.concatenate([near_ref[...], far_ref[...]], axis=0)
+    message = 0.0
+    for kind in range(ETYPES):
+        message += gain_ref[kind : kind + 1, :] * jnp.dot(
+            mix_ref[kind], nodes, preferred_element_type=jnp.float32
+        )
+    pre = nodes.astype(jnp.float32) + message * inv_ref[...]
+    square_ref[...] += jnp.sum(pre * pre, axis=1, keepdims=True)
+    scaled = (pre * norm_ref[...]).astype(jnp.bfloat16)
+    total_ref[:, :width] += jnp.dot(scaled, gate_ref[...], preferred_element_type=jnp.float32)
+    total_ref[:, padded : padded + width] += jnp.dot(
+        scaled, up_ref[...], preferred_element_type=jnp.float32
+    )
+
+    @pl.when(step == steps - 1)
+    def _():
+        out_ref[:, : 2 * padded] = total_ref[...].astype(jnp.bfloat16)
+        squares = square_ref[...]
+        high = squares.astype(jnp.bfloat16).astype(jnp.float32)
+        lane = lax.broadcasted_iota(jnp.int32, (squares.shape[0], 128), 1)
+        parts = jnp.where(lane == 0, high, jnp.where(lane == 1, squares - high, 0.0))
+        out_ref[:, 2 * padded :] = parts.astype(jnp.bfloat16)
+
+def expand(near, far, mix, inv, gain, norm, gate, up, layer, tile):
+    half, feat = near.shape
+    rows = 2 * half
+    width = gate.shape[2]
+    padded = pad_lanes(width)
+    return pl.pallas_call(
+        expand_body,
+        grid=(feat // tile,),
+        in_specs=[
+            pl.BlockSpec((half, tile), lambda k: (0, k)),
+            pl.BlockSpec((half, tile), lambda k: (0, k)),
+            pl.BlockSpec((ETYPES, rows, rows), lambda k: (0, 0, 0)),
+            pl.BlockSpec((rows, 1), lambda k: (0, 0)),
+            pl.BlockSpec((None, ETYPES, tile), lambda k: (layer, 0, k)),
+            pl.BlockSpec((None, 1, tile), lambda k: (layer, 0, k)),
+            pl.BlockSpec((None, tile, width), lambda k: (layer, k, 0)),
+            pl.BlockSpec((None, tile, width), lambda k: (layer, k, 0)),
+        ],
+        out_specs=pl.BlockSpec((rows, 2 * padded + 128), lambda k: (0, 0)),
+        out_shape=jax.ShapeDtypeStruct((rows, 2 * padded + 128), jnp.bfloat16),
+        scratch_shapes=[
+            pltpu.VMEM((rows, 2 * padded), jnp.float32),
+            pltpu.VMEM((rows, 1), jnp.float32),
+        ],
+        compiler_params=pltpu.CompilerParams(vmem_limit_bytes=24 << 20),
+        name="expand",
+    )(near, far, mix, inv, gain, norm, gate, up)
+
+def contract_body(near_ref, far_ref, down_ref, keep_ref, give_ref, hidden_ref, total_ref, *, swap):
+    step = pl.program_id(0)
+    steps = pl.num_programs(0)
+    rows, width = hidden_ref.shape
+    padded = pad_lanes(width)
+    tile = down_ref.shape[0]
+
+    @pl.when(step == 0)
+    def _():
+        far = far_ref[...].astype(jnp.float32)
+        if swap:
+            part = rows // 4
+            far = jnp.concatenate(
+                [far[:part], far[2 * part : 3 * part], far[part : 2 * part], far[3 * part :]], axis=0
+            )
+        both = near_ref[...].astype(jnp.float32) + far
+        squares = jnp.sum(both[:, 2 * padded :], axis=1, keepdims=True)
+        scale = lax.rsqrt(squares * (1.0 / D) + 1e-05)
+        gate = both[:, :width] * scale
+        up = both[:, padded : padded + width] * scale
+        hidden_ref[...] = (gate * (1.0 / (1.0 + jnp.exp(-gate))) * up).astype(jnp.bfloat16)
+        total_ref[...] = jnp.zeros_like(total_ref)
+
+    if tile == width:
+        hidden = hidden_ref[...]
+    else:
+        hidden = hidden_ref[:, pl.ds(pl.multiple_of(step * tile, 128), tile)]
+    total_ref[...] += jnp.dot(hidden, down_ref[...], preferred_element_type=jnp.float32)
+
+    @pl.when(step == steps - 1)
+    def _():
+        keep_ref[...] = total_ref[: rows // 2, :]
+        give_ref[...] = total_ref[rows // 2 :, :].astype(jnp.bfloat16)
+
+
+def contract(near, far, down, layer, swap, tile):
+    rows = near.shape[0]
+    width, feat = down.shape[1:]
+    half = rows // 2
+    return pl.pallas_call(
+        functools.partial(contract_body, swap=swap),
+        grid=(width // tile,),
+        in_specs=[
+            pl.BlockSpec(near.shape, lambda k: (0, 0)),
+            pl.BlockSpec(far.shape, lambda k: (0, 0)),
+            pl.BlockSpec((None, tile, feat), lambda k: (layer, k, 0)),
+        ],
+        out_specs=[
+            pl.BlockSpec((half, feat), lambda k: (0, 0)),
+            pl.BlockSpec((half, feat), lambda k: (0, 0)),
+        ],
+        out_shape=[
+            jax.ShapeDtypeStruct((half, feat), jnp.float32),
+            jax.ShapeDtypeStruct((half, feat), jnp.bfloat16),
+        ],
+        scratch_shapes=[
+            pltpu.VMEM((rows, width), jnp.bfloat16),
+            pltpu.VMEM((rows, feat), jnp.float32),
+        ],
+        compiler_params=pltpu.CompilerParams(vmem_limit_bytes=24 << 20),
+        name="contract",
+    )(near, far, down)
 
 
 def per_device(
@@ -213,17 +341,17 @@
     gx_count = lax.axis_size("gx")
     ta_count = lax.axis_size("ta")
     me = lax.axis_index("gx")
-    bits = stage_bits(gx_count)
+    orders = bit_orders(gx_count, ta_count)
+    last = len(orders[0]) - 1
     chunks = gx_count // 2
     groups = [list(range(chunks)), list(range(chunks, gx_count))]
-    far_half = flip_pairs(gx_count, bits[-1])
     venue_idx = me * pairs_dev // STEPS
     slot_order = lax.dynamic_index_in_dim(slot_map, venue_idx, 0, keepdims=False)
 
     def picker(pairs):
         rows = pairs * inst_total
         row = lax.broadcasted_iota(jnp.int32, (rows, inst_total), 0)
-        inst = (row // pairs % 2) * chunks + row // (2 * pairs)
+        inst = (row // pairs % 2 ^ me // chunks) * chunks + row // (2 * pairs)
         hit = inst == lax.broadcasted_iota(jnp.int32, (rows, inst_total), 1)
         slot = jnp.sum(jnp.where(hit, slot_order[None, :], 0), axis=1, keepdims=True)
         line = lax.broadcasted_iota(jnp.int32, (rows, rows), 0)
@@ -253,52 +381,53 @@
         queries = queries.reshape(HALF_VENUES, STEPS // pairs_dev, 2, pairs_dev, feat_width)
         queries = queries[:, (STEPS - NODE_STEPS) // pairs_dev :].transpose(0, 2, 1, 3, 4)
         queries = queries.reshape(2 * ROWS_HALF, feat_width)
-    far_queries = lax.ppermute(queries, "gx", far_half)
+    far_queries = swap_stage(queries, orders, last)
     kv = lax.all_to_all(kv, "gx", 0, 0, axis_index_groups=groups, tiled=True)
     kv = kv.reshape(HALF_VENUES, STEPS // pairs_dev, 4, pairs_dev, feat_width)
     kv = kv.transpose(0, 2, 1, 3, 4).reshape(HALF_VENUES, 4, STEPS, feat_width)
     probs, lse = half_scores(queries, far_queries, kv)
-    far_lse = lax.ppermute(lse, "gx", far_half)
+    far_lse = swap_stage(lse, orders, last)
     pooled = half_pool(probs, lse, far_lse, kv)
-    far_pooled = lax.ppermute(pooled, "gx", far_half)
+    far_pooled = swap_stage(pooled, orders, last)
+    far_pooled = jnp.concatenate([far_pooled[NODE_STEPS:], far_pooled[:NODE_STEPS]], axis=0)
     pooled = (pooled.astype(jnp.float32) + far_pooled.astype(jnp.float32)).astype(jnp.bfloat16)
-    own_rows = lax.dynamic_slice_in_dim(pooled, me // chunks * NODE_STEPS, NODE_STEPS, 0)
-
-    place = jnp.arange(inst_total)
-    inst_at = sum((((place >> b) & 1) << (len(bits) - 1 - b)) for b in bits)
-    at_source = (edge_list[:, 0][:, None] == inst_at[None, :]).astype(jnp.float32)
-    at_target = (edge_list[:, 1][:, None] == inst_at[None, :]).astype(jnp.float32)
-    of_type = (edge_types[:, None] == jnp.arange(ETYPES)[None, :]).astype(jnp.float32)
-    adjacency = jnp.einsum("et,ei,ej->tij", of_type, at_target, at_source)
-    degree = jnp.maximum(jnp.sum(at_target, axis=0), 1.0)
-    adj_rows = adjacency.reshape(ETYPES * inst_total, inst_total).astype(jnp.bfloat16)
+    own_rows = pooled[:NODE_STEPS]
+
     row_total = inst_total * NODE_STEPS
-    ff_dev = gate_proj.shape[2]
+    row = jnp.arange(row_total)
+    place = row // NODE_STEPS
+    inst_at = [
+        me ^ sum((place >> (last - stage) & 1) << bit for stage, bit in enumerate(order))
+        for order in orders[:2]
+    ]
+    inst_at = jnp.where(lax.axis_index("ta") % 2 == 0, inst_at[0], inst_at[1])
+    at_source = (edge_list[:, 0][:, None] == inst_at[None, :]).astype(jnp.bfloat16)
+    at_target = edge_list[:, 1][:, None] == inst_at[None, :]
+    same_step = row[:, None] % NODE_STEPS == row[None, :] % NODE_STEPS
+    typed = at_target[None] & (edge_types[None, :] == jnp.arange(ETYPES)[:, None])[:, :, None]
+    mix = jnp.einsum(
+        "ter,ec->trc", typed.astype(jnp.bfloat16), at_source, preferred_element_type=jnp.float32
+    )
+    mix = jnp.where(same_step[None], mix, 0.0).astype(jnp.bfloat16)
+    degree = jnp.maximum(jnp.sum(at_target.astype(jnp.float32), axis=0), 1.0)
+    inverse = (1.0 / degree)[:, None]
+    norm_rows = norm_gain[:, None, :]
+    down_tile = 640 if down_proj.shape[1] % 640 == 0 else down_proj.shape[1]
+    expand_tile = 512 if feat_width % 512 == 0 else 128
     for layer_idx in range(ROUNDS):
         if layer_idx == 0:
-            nodes = gather_rows(pooled, gx_count, bits[:-1])
+            near, far = gather_rows(pooled, orders, last)
         else:
-            nodes = gather_rows(own_rows, gx_count, bits)
-        flat_nodes = nodes.reshape(inst_total, NODE_STEPS * feat_width)
-        gathered = jnp.dot(adj_rows, flat_nodes, preferred_element_type=jnp.float32)
-        gathered = gathered.reshape(ETYPES, inst_total, NODE_STEPS, feat_width)
-        message = (
-            jnp.sum(gathered * type_gain[layer_idx][:, None, None, :], axis=0)
-            / degree[:, None, None]
+            near, far = gather_rows(own_rows, orders, last + 1)
+        near_sums = expand(
+            near, far, mix, inverse, type_gain, norm_rows, gate_proj, up_proj, layer_idx, expand_tile
         )
-        pre_norm = nodes.astype(jnp.float32) + message.reshape(row_total, feat_width)
-        squares = lax.psum(jnp.sum(pre_norm * pre_norm, axis=-1), "ta")
-        row_scale = lax.rsqrt(squares / D + 1e-05)[:, None]
-        normed = (pre_norm * row_scale * norm_gain[layer_idx][None, :]).astype(jnp.bfloat16)
-        gate_part = jnp.dot(normed, gate_proj[layer_idx], preferred_element_type=jnp.float32)
-        up_part = jnp.dot(normed, up_proj[layer_idx], preferred_element_type=jnp.float32)
-        both = jnp.concatenate(
-            [gate_part.astype(jnp.bfloat16), up_part.astype(jnp.bfloat16)], axis=1
-        )
-        both = sum_over_ta(both, ta_count)
-        hidden = (jax.nn.silu(both[:, :ff_dev]) * both[:, ff_dev:]).astype(jnp.bfloat16)
-        update = jnp.dot(hidden, down_proj[layer_idx], preferred_element_type=jnp.float32)
-        own_rows = (own_rows.astype(jnp.float32) + scatter_rows(update, gx_count)).astype(
+        if ta_count == 2:
+            far_sums = lax.ppermute(near_sums, "ta", [(0, 1), (1, 0)])
+        else:
+            far_sums = lax.psum(near_sums.astype(jnp.float32), "ta") - near_sums.astype(jnp.float32)
+        keep, give = contract(near_sums, far_sums, down_proj, layer_idx, ta_count == 2, down_tile)
+        own_rows = (own_rows.astype(jnp.float32) + scatter_rows(keep, give, orders)).astype(
             jnp.bfloat16
         )
     return own_rows

time: 223 us -> 223 us (level)
  local copies, waits for them, and re-layouts: 7.5 us -> 35.7 us
  matrix products: 29.6 us -> 1.56 us
  Pallas kernels: 6.5 us -> 19.3 us
  blocking collectives: 5.33 us -> 0 us
  other arithmetic: 5.94 us -> 1.7 us
  waiting for transfers between devices: 121 us -> 118 us
    unnamed x24 -> x37, local copies, waits for them, and re-layouts: 4.11 us -> 34.2 us
    dot_general x9 -> x1, matrix products: 28.4 us -> 0.32 us  [per_device(): jnp.einsum('ter,ec->trc', typed.astype(jnp.bfloat16), at_source, preferre...]
    pallas_call x0 -> x4, Pallas kernels: none -> 12.5 us  [the longest x2 8.33 us: expand(): pl.pallas_call(expand_body, grid=(feat // tile,), in_specs=[pl.BlockSpec(...]
    psum x2 -> x0, blocking collectives: 5.33 us -> none  [per_device(): squares = lax.psum(jnp.sum(pre_norm * pre_norm, axis=-1), 'ta')]
    ppermute x20, waiting for transfers between devices: 113 us -> 110 us  [the longest x18 106 us: swap_stage(): return lax.ppermute(block, ('gx', 'ta'), pairs)]
    select_n x2 -> x0, local copies, waits for them, and re-layouts: 2.28 us -> none  [gather_rows(): jnp.where(side == 0, jnp.concatenate([held, other], axis=0), jnp.concaten...]
where the time goes in v3:
time: 223 us; the launch traced here: 222 us
  waiting for transfers between devices  118 us (53%)
  starting transfers between devices  45.3 us (20%)
  local copies, waits for them, and re-layouts  35.7 us (16%)
  Pallas kernels  19.3 us (9%)
    ppermute x18, waiting for transfers between devices, swap_stage(): return lax.ppermute(block, ('gx', 'ta'), pairs)  106 us
    ppermute x18, starting transfers between devices, swap_stage(): return lax.ppermute(block, ('gx', 'ta'), pairs)  35.3 us
    unnamed x37, local copies, waits for them, and re-layouts  34.2 us
    pallas_call x2, Pallas kernels, expand(): pl.pallas_call(expand_body, grid=(feat // tile,), in_specs=[pl.BlockSpec(...  8.33 us
    all_to_all x1, waiting for transfers between devices, per_device(): lax.all_to_all(queries, 'gx', 0, 0, axis_index_groups=groups, tiled=True)  6.51 us
    all_to_all x1, starting transfers between devices, per_device(): lax.all_to_all(queries, 'gx', 0, 0, axis_index_groups=groups, tiled=True)  6.21 us
  transfers between devices with their start and end apart: 22, of which 22 were waited for; matrix products, arithmetic and copies ran while one was open for 0% of the time, Pallas kernels for 1%

profile of v3, /device:TPU:0, one launch (start us, length us, event | category | flops | bytes accessed | tf_op | source)
XLA Modules:
  0.0 222.4 jit_solution(10915740925081967416)
XLA Ops:
  2.7 6.2 %all-to-all-start = ((bf16[8,16,2560]{2,1,0:T(8,128)(2,1)}), bf16[8,16,2560]{2,1,0:T(8,128)(2,1)S(1)}, u32[]{:S(2)}, u32[]{:S(2)}) async-start(bf16[8,16,2560]{2,1,0:T(8,128)(2,1)} %bitcast.24), calls=%async_computation | async-start | bytes 1310720 | tf_op jit(solution)/shard_map/all_to_all | solution.py:371
  12.8 6.5 %all-to-all-done = bf16[8,16,2560]{2,1,0:T(8,128)(2,1)S(1)} async-done(((bf16[8,16,2560]{2,1,0:T(8,128)(2,1)}), bf16[8,16,2560]{2,1,0:T(8,128)(2,1)S(1)}, u32[]{:S(2)}, u32[]{:S(2)}) %all-to-all-start) | async-done | bytes 655392 | tf_op jit(solution)/shard_map/all_to_all | solution.py:371
  19.3 3.6 %all-to-all-start.1 = ((bf16[8,64,2560]{2,1,0:T(8,128)(2,1)}), bf16[8,64,2560]{2,1,0:T(8,128)(2,1)S(1)}, u32[]{:S(2)}, u32[]{:S(2)}) async-start(bf16[8,64,2560]{2,1,0:T(8,128)(2,1)} %copy-done.7), calls=%async_computation.1 | async-start | bytes 5242880 | tf_op jit(solution)/shard_map/all_to_all | solution.py:385
  22.9 2.7 %collective-permute-start = (bf16[128,2560]{1,0:T(8,128)(2,1)S(1)}, bf16[128,2560]{1,0:T(8,128)(2,1)S(1)}, u32[]{:S(2)}, u32[]{:S(2)}) collective-permute-start(bf16[128,2560]{1,0:T(8,128)(2,1)S(1)} %bitcast.20), channel_id=1, source_target_pairs={{0,16},{1,17},{2,18},{3,19},{4,20},{5,21},{6,22},{7,23},{8,24},{9,... | collective-permute-start | bytes 1966088 | tf_op jit(solution)/shard_map/ppermute | solution.py:43
  25.7 38.9 %collective-permute-done.far_ref = bf16[128,2560]{1,0:T(8,128)(2,1)S(1)} collective-permute-done((bf16[128,2560]{1,0:T(8,128)(2,1)S(1)}, bf16[128,2560]{1,0:T(8,128)(2,1)S(1)}, u32[]{:S(2)}, u32[]{:S(2)}) %collective-permute-start) | collective-permute-done | bytes 655392 | tf_op jit(solution)/shard_map/ppermute | solution.py:43
  68.0 2.9 %half_scores.1 = (bf16[20,2,128,128]{3,2,1,0:T(8,128)(2,1)S(1)}, f32[128,128]{1,0:T(8,128)S(1)}) custom-call(bf16[128,2560]{1,0:T(8,128)(2,1)S(1)} %bitcast.21, bf16[128,2560]{1,0:T(8,128)(2,1)S(1)} %copy-done.13, bf16[8,4,16,2560]{3,2,1,0:T(8,128)(2,1)S(1)} %bitcast.18), custom_call_target="tpu_custom_call" | custom-call | tf_op jit(solution)/shard_map/half_scores/pallas_call | solution.py:135
  73.9 4.0 %collective-permute-done.1.far_ref = f32[128,128]{1,0:T(8,128)S(1)} collective-permute-done((f32[128,128]{1,0:T(8,128)S(1)}, f32[128,128]{1,0:T(8,128)S(1)}, u32[]{:S(2)}, u32[]{:S(2)}) %collective-permute-start.1) | collective-permute-done | bytes 65568 | tf_op jit(solution)/shard_map/ppermute | solution.py:43
  82.5 4.1 %collective-permute-done.2 = bf16[16,2560]{1,0:T(8,128)(2,1)S(1)} collective-permute-done((bf16[16,2560]{1,0:T(8,128)(2,1)S(1)}, bf16[16,2560]{1,0:T(8,128)(2,1)S(1)}, u32[]{:S(2)}, u32[]{:S(2)}) %collective-permute-start.2) | collective-permute-done | bytes 81952 | tf_op jit(solution)/shard_map/ppermute | solution.py:43
  86.6 2.9 %collective-permute-start.3 = (bf16[16,2560]{1,0:T(8,128)(2,1)S(1)}, bf16[16,2560]{1,0:T(8,128)(2,1)S(1)}, u32[]{:S(2)}, u32[]{:S(2)}) collective-permute-start(bf16[16,2560]{1,0:T(8,128)(2,1)S(1)} %add_convert_fusion), channel_id=1, source_target_pairs={{0,8},{1,9},{2,10},{3,11},{4,12},{5,13},{6,14},{7,15},{8,0},{9,1},... | collective-permute-start | bytes 245768 | tf_op jit(solution)/shard_map/ppermute | solution.py:43
  93.3 5.6 %collective-permute-done.4 = bf16[32,2560]{1,0:T(8,128)(2,1)S(1)} collective-permute-done((bf16[32,2560]{1,0:T(8,128)(2,1)S(1)}, bf16[32,2560]{1,0:T(8,128)(2,1)S(1)}, u32[]{:S(2)}, u32[]{:S(2)}) %collective-permute-start.4) | collective-permute-done | bytes 163872 | tf_op jit(solution)/shard_map/ppermute | solution.py:43
  98.9 4.0 %collective-permute-start.5 = (bf16[64,2560]{1,0:T(8,128)(2,1)S(1)}, bf16[64,2560]{1,0:T(8,128)(2,1)S(1)}, u32[]{:S(2)}, u32[]{:S(2)}) collective-permute-start(bf16[64,2560]{1,0:T(8,128)(2,1)S(1)} %pad_maximum_fusion.near_ref), channel_id=1, source_target_pairs={{0,2},{1,5},{2,0},{3,7},{4,6},{5,1},{6,4},{7,3},{8,10},{9,13},{10,... | collective-permute-start | bytes 983048 | tf_op jit(solution)/shard_map/ppermute | solution.py:43
  103.5 4.6 %collective-permute-done.5.far_ref = bf16[64,2560]{1,0:T(8,128)(2,1)S(1)} collective-permute-done((bf16[64,2560]{1,0:T(8,128)(2,1)S(1)}, bf16[64,2560]{1,0:T(8,128)(2,1)S(1)}, u32[]{:S(2)}, u32[]{:S(2)}) %collective-permute-start.5) | collective-permute-done | bytes 327712 | tf_op jit(solution)/shard_map/ppermute | solution.py:43
  108.0 4.7 %copy-done.1 = bf16[2,2560,1280]{2,1,0:T(8,128)(2,1)S(1)} copy-done((bf16[2,2560,1280]{2,1,0:T(8,128)(2,1)S(1)}, bf16[2,2560,1280]{2,1,0:T(8,128)(2,1)}, u32[]{:S(2)}) %copy-start.1) | copy-done | bytes 13107224
  112.8 4.7 %copy-done.3 = bf16[2,2560,1280]{2,1,0:T(8,128)(2,1)S(1)} copy-done((bf16[2,2560,1280]{2,1,0:T(8,128)(2,1)S(1)}, bf16[2,2560,1280]{2,1,0:T(8,128)(2,1)}, u32[]{:S(2)}) %copy-start.3) | copy-done | bytes 13107224
  117.5 4.3 %expand.2.near_ref = bf16[128,2688]{1,0:T(8,128)(2,1)S(1)} custom-call(bf16[64,2560]{1,0:T(8,128)(2,1)S(1)} %pad_maximum_fusion.near_ref, bf16[64,2560]{1,0:T(8,128)(2,1)S(1)} %collective-permute-done.5.far_ref, bf16[3,128,128]{2,1,0:T(8,128)(2,1)S(1)} %fusion.mix_ref, f32[128,1]{1,0:T(8,128)S(1)} %copy.16.inv_ref, f32[2,3,2560]{2,1,0:T(4,128)S(1)} %copy.17.gain_ref, ...), custom_call_target="tpu_custom_call" | custom-call | tf_op jit(solution)/shard_map/expand/pallas_call | solution.py:240
  124.0 4.7 %copy-done.5 = bf16[2,1280,2560]{2,1,0:T(8,128)(2,1)S(1)} copy-done((bf16[2,1280,2560]{2,1,0:T(8,128)(2,1)S(1)}, bf16[2,1280,2560]{2,1,0:T(8,128)(2,1)}, u32[]{:S(2)}) %copy-start.5) | copy-done | bytes 13107224
  132.9 5.1 %collective-permute-done.7 = bf16[64,2560]{1,0:T(8,128)(2,1)S(1)} collective-permute-done((bf16[64,2560]{1,0:T(8,128)(2,1)S(1)}, bf16[64,2560]{1,0:T(8,128)(2,1)S(1)}, u32[]{:S(2)}, u32[]{:S(2)}) %collective-permute-start.7) | collective-permute-done | bytes 327712 | tf_op jit(solution)/shard_map/ppermute | solution.py:43
  139.5 3.9 %collective-permute-done.8 = bf16[32,2560]{1,0:T(8,128)(2,1)S(1)} collective-permute-done((bf16[32,2560]{1,0:T(8,128)(2,1)S(1)}, bf16[32,2560]{1,0:T(8,128)(2,1)S(1)}, u32[]{:S(2)}, u32[]{:S(2)}) %collective-permute-start.8) | collective-permute-done | bytes 163872 | tf_op jit(solution)/shard_map/ppermute | solution.py:43
  145.5 2.4 %collective-permute-done.9 = bf16[16,2560]{1,0:T(8,128)(2,1)S(1)} collective-permute-done((bf16[16,2560]{1,0:T(8,128)(2,1)S(1)}, bf16[16,2560]{1,0:T(8,128)(2,1)S(1)}, u32[]{:S(2)}, u32[]{:S(2)}) %collective-permute-start.9) | collective-permute-done | bytes 81952 | tf_op jit(solution)/shard_map/ppermute | solution.py:43
  149.5 3.5 %collective-permute-done.10 = bf16[8,2560]{1,0:T(8,128)(2,1)S(1)} collective-permute-done((bf16[8,2560]{1,0:T(8,128)(2,1)S(1)}, bf16[8,2560]{1,0:T(8,128)(2,1)S(1)}, u32[]{:S(2)}, u32[]{:S(2)}) %collective-permute-start.10) | collective-permute-done | bytes 40992 | tf_op jit(solution)/shard_map/ppermute | solution.py:43
  154.5 3.5 %collective-permute-done.11 = bf16[8,2560]{1,0:T(8,128)(2,1)S(1)} collective-permute-done((bf16[8,2560]{1,0:T(8,128)(2,1)S(1)}, bf16[8,2560]{1,0:T(8,128)(2,1)S(1)}, u32[]{:S(2)}, u32[]{:S(2)}) %collective-permute-start.11) | collective-permute-done | bytes 40992 | tf_op jit(solution)/shard_map/ppermute | solution.py:43
  164.2 5.2 %collective-permute-done.13 = bf16[32,2560]{1,0:T(8,128)(2,1)S(1)} collective-permute-done((bf16[32,2560]{1,0:T(8,128)(2,1)S(1)}, bf16[32,2560]{1,0:T(8,128)(2,1)S(1)}, u32[]{:S(2)}, u32[]{:S(2)}) %collective-permute-start.13) | collective-permute-done | bytes 163872 | tf_op jit(solution)/shard_map/ppermute | solution.py:43
  171.3 5.3 %collective-permute-done.14.far_ref = bf16[64,2560]{1,0:T(8,128)(2,1)S(1)} collective-permute-done((bf16[64,2560]{1,0:T(8,128)(2,1)S(1)}, bf16[64,2560]{1,0:T(8,128)(2,1)S(1)}, u32[]{:S(2)}, u32[]{:S(2)}) %collective-permute-start.14) | collective-permute-done | bytes 327712 | tf_op jit(solution)/shard_map/ppermute | solution.py:43
  176.6 4.7 %copy-done.2 = bf16[2,2560,1280]{2,1,0:T(8,128)(2,1)S(1)} copy-done((bf16[2,2560,1280]{2,1,0:T(8,128)(2,1)S(1)}, bf16[2,2560,1280]{2,1,0:T(8,128)(2,1)}, u32[]{:S(2)}) %copy-start.2) | copy-done | bytes 13107224
  181.3 4.7 %copy-done.4 = bf16[2,2560,1280]{2,1,0:T(8,128)(2,1)S(1)} copy-done((bf16[2,2560,1280]{2,1,0:T(8,128)(2,1)S(1)}, bf16[2,2560,1280]{2,1,0:T(8,128)(2,1)}, u32[]{:S(2)}) %copy-start.4) | copy-done | bytes 13107224
  186.0 4.1 %expand.3.near_ref = bf16[128,2688]{1,0:T(8,128)(2,1)S(1)} custom-call(bf16[64,2560]{1,0:T(8,128)(2,1)S(1)} %pad_maximum_fusion.1.near_ref, bf16[64,2560]{1,0:T(8,128)(2,1)S(1)} %collective-permute-done.14.far_ref, bf16[3,128,128]{2,1,0:T(8,128)(2,1)S(1)} %fusion.mix_ref, f32[128,1]{1,0:T(8,128)S(1)} %copy.16.inv_ref, f32[2,3,2560]{2,1,0:T(4,128)S(1)} %copy.17.gain_ref, ...), custom_call_target="tpu_custom_call" | custom-call | tf_op jit(solution)/shard_map/expand/pallas_call | solution.py:240
  192.3 4.7 %copy-done.6 = bf16[2,1280,2560]{2,1,0:T(8,128)(2,1)S(1)} copy-done((bf16[2,1280,2560]{2,1,0:T(8,128)(2,1)S(1)}, bf16[2,1280,2560]{2,1,0:T(8,128)(2,1)}, u32[]{:S(2)}) %copy-start.6) | copy-done | bytes 13107224
  200.9 5.3 %collective-permute-done.16 = bf16[64,2560]{1,0:T(8,128)(2,1)S(1)} collective-permute-done((bf16[64,2560]{1,0:T(8,128)(2,1)S(1)}, bf16[64,2560]{1,0:T(8,128)(2,1)S(1)}, u32[]{:S(2)}, u32[]{:S(2)}) %collective-permute-start.16) | collective-permute-done | bytes 327712 | tf_op jit(solution)/shard_map/ppermute | solution.py:43
  207.8 3.9 %collective-permute-done.17 = bf16[32,2560]{1,0:T(8,128)(2,1)S(1)} collective-permute-done((bf16[32,2560]{1,0:T(8,128)(2,1)S(1)}, bf16[32,2560]{1,0:T(8,128)(2,1)S(1)}, u32[]{:S(2)}, u32[]{:S(2)}) %collective-permute-start.17) | collective-permute-done | bytes 163872 | tf_op jit(solution)/shard_map/ppermute | solution.py:43
  211.8 2.6 %collective-permute-start.18 = (bf16[16,2560]{1,0:T(8,128)(2,1)S(1)}, bf16[16,2560]{1,0:T(8,128)(2,1)S(1)}, u32[]{:S(2)}, u32[]{:S(2)}) collective-permute-start(bf16[16,2560]{1,0:T(8,128)(2,1)S(1)} %slice.118), channel_id=1, source_target_pairs={{0,8},{1,9},{2,10},{3,11},{4,12},{5,13},{6,14},{7,15},{8,0},{9,1},... | collective-permute-start | bytes 245768 | tf_op jit(solution)/shard_map/ppermute | solution.py:43
  214.3 2.4 %collective-permute-done.18 = bf16[16,2560]{1,0:T(8,128)(2,1)S(1)} collective-permute-done((bf16[16,2560]{1,0:T(8,128)(2,1)S(1)}, bf16[16,2560]{1,0:T(8,128)(2,1)S(1)}, u32[]{:S(2)}, u32[]{:S(2)}) %collective-permute-start.18) | collective-permute-done | bytes 81952 | tf_op jit(solution)/shard_map/ppermute | solution.py:43
  218.1 3.7 %collective-permute-done.19 = bf16[8,2560]{1,0:T(8,128)(2,1)S(1)} collective-permute-done((bf16[8,2560]{1,0:T(8,128)(2,1)S(1)}, bf16[8,2560]{1,0:T(8,128)(2,1)S(1)}, u32[]{:S(2)}, u32[]{:S(2)}) %collective-permute-start.19) | collective-permute-done | bytes 40992 | tf_op jit(solution)/shard_map/ppermute | solution.py:43
  (104 shorter events, 52.6 us)
Async XLA Ops:
  0.0 9.3 %copy-start.11 = (bf16[16,16,2560]{2,1,0:T(8,128)(2,1)S(1)}, bf16[16,16,2560]{2,1,0:T(8,128)(2,1)}, u32[]{:S(2)}) copy-start(bf16[16,16,2560]{2,1,0:T(8,128)(2,1)} %param.13) | copy-start | bytes 3932164
  0.0 9.3 %copy-start.10 = (bf16[16,16,2560]{2,1,0:T(8,128)(2,1)S(1)}, bf16[16,16,2560]{2,1,0:T(8,128)(2,1)}, u32[]{:S(2)}) copy-start(bf16[16,16,2560]{2,1,0:T(8,128)(2,1)} %param.12) | copy-start | bytes 3932164
  2.7 16.6 %all-to-all-start = ((bf16[8,16,2560]{2,1,0:T(8,128)(2,1)}), bf16[8,16,2560]{2,1,0:T(8,128)(2,1)S(1)}, u32[]{:S(2)}, u32[]{:S(2)}) async-start(bf16[8,16,2560]{2,1,0:T(8,128)(2,1)} %bitcast.24), calls=%async_computation | async-start | bytes 1310720 | tf_op jit(solution)/shard_map/all_to_all | solution.py:371
  19.3 47.6 %all-to-all-start.1 = ((bf16[8,64,2560]{2,1,0:T(8,128)(2,1)}), bf16[8,64,2560]{2,1,0:T(8,128)(2,1)S(1)}, u32[]{:S(2)}, u32[]{:S(2)}) async-start(bf16[8,64,2560]{2,1,0:T(8,128)(2,1)} %copy-done.7), calls=%async_computation.1 | async-start | bytes 5242880 | tf_op jit(solution)/shard_map/all_to_all | solution.py:385
  22.9 51.0 %copy-start.16 = (s32[64,2]{0,1:T(2,128)S(1)}, s32[64,2]{0,1:T(2,128)}, u32[]{:S(2)}) copy-start(s32[64,2]{0,1:T(2,128)} %param.15) | copy-start | bytes 1540
  22.9 41.6 %collective-permute-start = (bf16[128,2560]{1,0:T(8,128)(2,1)S(1)}, bf16[128,2560]{1,0:T(8,128)(2,1)S(1)}, u32[]{:S(2)}, u32[]{:S(2)}) collective-permute-start(bf16[128,2560]{1,0:T(8,128)(2,1)S(1)} %bitcast.20), channel_id=1, source_target_pairs={{0,16},{1,17},{2,18},{3,19},{4,20},{5,21},{6,22},{7,23},{8,24},{9,... | collective-permute-start | bytes 1966088 | tf_op jit(solution)/shard_map/ppermute | solution.py:43
  72.0 21.2 %copy-start.17 = (s32[64]{0:T(128)S(1)}, s32[64]{0:T(128)}, u32[]{:S(2)}) copy-start(s32[64]{0:T(128)} %param.16) | copy-start | bytes 772
  72.0 5.9 %collective-permute-start.1 = (f32[128,128]{1,0:T(8,128)S(1)}, f32[128,128]{1,0:T(8,128)S(1)}, u32[]{:S(2)}, u32[]{:S(2)}) collective-permute-start(f32[128,128]{1,0:T(8,128)S(1)} %get-tuple-element.16.lse_ref), channel_id=1, source_target_pairs={{0,16},{1,17},{2,18},{3,19},{4,20},{5,21},{6,22},{7,23},{8,24},{9,... | collective-permute-start | bytes 196616 | tf_op jit(solution)/shard_map/ppermute | solution.py:43
  79.2 23.8 %copy-start.15 = (f32[2,2560]{1,0:T(2,128)S(1)}, f32[2,2560]{1,0:T(2,128)}, u32[]{:S(2)}) copy-start(f32[2,2560]{1,0:T(2,128)} %param.18) | copy-start | bytes 61444
  79.2 23.9 %copy-start.14 = (f32[2,3,2560]{2,0,1:T(2,128)S(1)}, f32[2,3,2560]{2,0,1:T(2,128)}, u32[]{:S(2)}) copy-start(f32[2,3,2560]{2,0,1:T(2,128)} %param.17) | copy-start | bytes 184324
  81.2 5.4 %collective-permute-start.2 = (bf16[16,2560]{1,0:T(8,128)(2,1)S(1)}, bf16[16,2560]{1,0:T(8,128)(2,1)S(1)}, u32[]{:S(2)}, u32[]{:S(2)}) collective-permute-start(bf16[16,2560]{1,0:T(8,128)(2,1)S(1)} %half_pool.1), channel_id=1, source_target_pairs={{0,16},{1,17},{2,18},{3,19},{4,20},{5,21},{6,22},{7,23},{8,24},{9,... | collective-permute-start | bytes 245768 | tf_op jit(solution)/shard_map/ppermute | solution.py:43
  86.6 5.3 %collective-permute-start.3 = (bf16[16,2560]{1,0:T(8,128)(2,1)S(1)}, bf16[16,2560]{1,0:T(8,128)(2,1)S(1)}, u32[]{:S(2)}, u32[]{:S(2)}) collective-permute-start(bf16[16,2560]{1,0:T(8,128)(2,1)S(1)} %add_convert_fusion), channel_id=1, source_target_pairs={{0,8},{1,9},{2,10},{3,11},{4,12},{5,13},{6,14},{7,15},{8,0},{9,1},... | collective-permute-start | bytes 245768 | tf_op jit(solution)/shard_map/ppermute | solution.py:43
  92.0 6.9 %collective-permute-start.4 = (bf16[32,2560]{1,0:T(8,128)(2,1)S(1)}, bf16[32,2560]{1,0:T(8,128)(2,1)S(1)}, u32[]{:S(2)}, u32[]{:S(2)}) collective-permute-start(bf16[32,2560]{1,0:T(8,128)(2,1)S(1)} %pad_maximum_fusion.2), channel_id=1, source_target_pairs={{0,4},{1,3},{2,6},{3,1},{4,0},{5,7},{6,2},{7,5},{8,12},{9,11},{10,... | collective-permute-start | bytes 491528 | tf_op jit(solution)/shard_map/ppermute | solution.py:43
  98.9 9.1 %collective-permute-start.5 = (bf16[64,2560]{1,0:T(8,128)(2,1)S(1)}, bf16[64,2560]{1,0:T(8,128)(2,1)S(1)}, u32[]{:S(2)}, u32[]{:S(2)}) collective-permute-start(bf16[64,2560]{1,0:T(8,128)(2,1)S(1)} %pad_maximum_fusion.near_ref), channel_id=1, source_target_pairs={{0,2},{1,5},{2,0},{3,7},{4,6},{5,1},{6,4},{7,3},{8,10},{9,13},{10,... | collective-permute-start | bytes 983048 | tf_op jit(solution)/shard_map/ppermute | solution.py:43
  108.0 4.7 %copy-start.1 = (bf16[2,2560,1280]{2,1,0:T(8,128)(2,1)S(1)}, bf16[2,2560,1280]{2,1,0:T(8,128)(2,1)}, u32[]{:S(2)}) copy-start(bf16[2,2560,1280]{2,1,0:T(8,128)(2,1)} %gate_ref.3) | copy-start | bytes 39321604
  121.8 2.2 collective-permute-start.6
  124.0 4.7 %copy-start.5 = (bf16[2,1280,2560]{2,1,0:T(8,128)(2,1)S(1)}, bf16[2,1280,2560]{2,1,0:T(8,128)(2,1)}, u32[]{:S(2)}) copy-start(bf16[2,1280,2560]{2,1,0:T(8,128)(2,1)} %down_ref.3) | copy-start | bytes 39321604
  130.8 7.1 %collective-permute-start.7 = (bf16[64,2560]{1,0:T(8,128)(2,1)S(1)}, bf16[64,2560]{1,0:T(8,128)(2,1)S(1)}, u32[]{:S(2)}, u32[]{:S(2)}) collective-permute-start(bf16[64,2560]{1,0:T(8,128)(2,1)S(1)} %get-tuple-element.18), channel_id=1, source_target_pairs={{0,2},{1,5},{2,0},{3,7},{4,6},{5,1},{6,4},{7,3},{8,10},{9,13},{10,... | collective-permute-start | bytes 983048 | tf_op jit(solution)/shard_map/ppermute | solution.py:43
  138.0 5.4 %collective-permute-start.8 = (bf16[32,2560]{1,0:T(8,128)(2,1)S(1)}, bf16[32,2560]{1,0:T(8,128)(2,1)S(1)}, u32[]{:S(2)}, u32[]{:S(2)}) collective-permute-start(bf16[32,2560]{1,0:T(8,128)(2,1)S(1)} %slice.117), channel_id=1, source_target_pairs={{0,4},{1,3},{2,6},{3,1},{4,0},{5,7},{6,2},{7,5},{8,12},{9,11},{10,... | collective-permute-start | bytes 491528 | tf_op jit(solution)/shard_map/ppermute | solution.py:43
  143.5 4.5 %collective-permute-start.9 = (bf16[16,2560]{1,0:T(8,128)(2,1)S(1)}, bf16[16,2560]{1,0:T(8,128)(2,1)S(1)}, u32[]{:S(2)}, u32[]{:S(2)}) collective-permute-start(bf16[16,2560]{1,0:T(8,128)(2,1)S(1)} %slice.119), channel_id=1, source_target_pairs={{0,8},{1,9},{2,10},{3,11},{4,12},{5,13},{6,14},{7,15},{8,0},{9,1},... | collective-permute-start | bytes 245768 | tf_op jit(solution)/shard_map/ppermute | solution.py:43
  148.0 5.0 %collective-permute-start.10 = (bf16[8,2560]{1,0:T(8,128)(2,1)S(1)}, bf16[8,2560]{1,0:T(8,128)(2,1)S(1)}, u32[]{:S(2)}, u32[]{:S(2)}) collective-permute-start(bf16[8,2560]{1,0:T(8,128)(2,1)S(1)} %slice.121), channel_id=1, source_target_pairs={{0,16},{1,17},{2,18},{3,19},{4,20},{5,21},{6,22},{7,23},{8,24},{9,... | collective-permute-start | bytes 122888 | tf_op jit(solution)/shard_map/ppermute | solution.py:43
  153.0 5.0 %collective-permute-start.11 = (bf16[8,2560]{1,0:T(8,128)(2,1)S(1)}, bf16[8,2560]{1,0:T(8,128)(2,1)S(1)}, u32[]{:S(2)}, u32[]{:S(2)}) collective-permute-start(bf16[8,2560]{1,0:T(8,128)(2,1)S(1)} %fusion.6), channel_id=1, source_target_pairs={{0,16},{1,17},{2,18},{3,19},{4,20},{5,21},{6,22},{7,23},{8,24},{9,... | collective-permute-start | bytes 122888 | tf_op jit(solution)/shard_map/ppermute | solution.py:43
  158.0 4.7 %collective-permute-start.12 = (bf16[16,2560]{1,0:T(8,128)(2,1)S(1)}, bf16[16,2560]{1,0:T(8,128)(2,1)S(1)}, u32[]{:S(2)}, u32[]{:S(2)}) collective-permute-start(bf16[16,2560]{1,0:T(8,128)(2,1)S(1)} %pad_maximum_fusion.4), channel_id=1, source_target_pairs={{0,8},{1,9},{2,10},{3,11},{4,12},{5,13},{6,14},{7,15},{8,0},{9,1},... | collective-permute-start | bytes 245768 | tf_op jit(solution)/shard_map/ppermute | solution.py:43
  162.7 6.7 %collective-permute-start.13 = (bf16[32,2560]{1,0:T(8,128)(2,1)S(1)}, bf16[32,2560]{1,0:T(8,128)(2,1)S(1)}, u32[]{:S(2)}, u32[]{:S(2)}) collective-permute-start(bf16[32,2560]{1,0:T(8,128)(2,1)S(1)} %pad_maximum_fusion.3), channel_id=1, source_target_pairs={{0,4},{1,3},{2,6},{3,1},{4,0},{5,7},{6,2},{7,5},{8,12},{9,11},{10,... | collective-permute-start | bytes 491528 | tf_op jit(solution)/shard_map/ppermute | solution.py:43
  169.5 7.1 %collective-permute-start.14 = (bf16[64,2560]{1,0:T(8,128)(2,1)S(1)}, bf16[64,2560]{1,0:T(8,128)(2,1)S(1)}, u32[]{:S(2)}, u32[]{:S(2)}) collective-permute-start(bf16[64,2560]{1,0:T(8,128)(2,1)S(1)} %pad_maximum_fusion.1.near_ref), channel_id=1, source_target_pairs={{0,2},{1,5},{2,0},{3,7},{4,6},{5,1},{6,4},{7,3},{8,10},{9,13},{10,... | collective-permute-start | bytes 983048 | tf_op jit(solution)/shard_map/ppermute | solution.py:43
  176.6 4.7 %copy-start.2 = (bf16[2,2560,1280]{2,1,0:T(8,128)(2,1)S(1)}, bf16[2,2560,1280]{2,1,0:T(8,128)(2,1)}, u32[]{:S(2)}) copy-start(bf16[2,2560,1280]{2,1,0:T(8,128)(2,1)} %gate_ref.3) | copy-start | bytes 39321604
  190.1 2.2 collective-permute-start.15
  192.3 4.7 %copy-start.6 = (bf16[2,1280,2560]{2,1,0:T(8,128)(2,1)S(1)}, bf16[2,1280,2560]{2,1,0:T(8,128)(2,1)}, u32[]{:S(2)}) copy-start(bf16[2,1280,2560]{2,1,0:T(8,128)(2,1)} %down_ref.3) | copy-start | bytes 39321604
  199.1 7.1 %collective-permute-start.16 = (bf16[64,2560]{1,0:T(8,128)(2,1)S(1)}, bf16[64,2560]{1,0:T(8,128)(2,1)S(1)}, u32[]{:S(2)}, u32[]{:S(2)}) collective-permute-start(bf16[64,2560]{1,0:T(8,128)(2,1)S(1)} %get-tuple-element.20), channel_id=1, source_target_pairs={{0,2},{1,5},{2,0},{3,7},{4,6},{5,1},{6,4},{7,3},{8,10},{9,13},{10,... | collective-permute-start | bytes 983048 | tf_op jit(solution)/shard_map/ppermute | solution.py:43
  206.3 5.4 %collective-permute-start.17 = (bf16[32,2560]{1,0:T(8,128)(2,1)S(1)}, bf16[32,2560]{1,0:T(8,128)(2,1)S(1)}, u32[]{:S(2)}, u32[]{:S(2)}) collective-permute-start(bf16[32,2560]{1,0:T(8,128)(2,1)S(1)} %slice.116), channel_id=1, source_target_pairs={{0,4},{1,3},{2,6},{3,1},{4,0},{5,7},{6,2},{7,5},{8,12},{9,11},{10,... | collective-permute-start | bytes 491528 | tf_op jit(solution)/shard_map/ppermute | solution.py:43
  211.8 5.0 %collective-permute-start.18 = (bf16[16,2560]{1,0:T(8,128)(2,1)S(1)}, bf16[16,2560]{1,0:T(8,128)(2,1)S(1)}, u32[]{:S(2)}, u32[]{:S(2)}) collective-permute-start(bf16[16,2560]{1,0:T(8,128)(2,1)S(1)} %slice.118), channel_id=1, source_target_pairs={{0,8},{1,9},{2,10},{3,11},{4,12},{5,13},{6,14},{7,15},{8,0},{9,1},... | collective-permute-start | bytes 245768 | tf_op jit(solution)/shard_map/ppermute | solution.py:43
  216.8 5.0 %collective-permute-start.19 = (bf16[8,2560]{1,0:T(8,128)(2,1)S(1)}, bf16[8,2560]{1,0:T(8,128)(2,1)S(1)}, u32[]{:S(2)}, u32[]{:S(2)}) collective-permute-start(bf16[8,2560]{1,0:T(8,128)(2,1)S(1)} %slice.120), channel_id=1, source_target_pairs={{0,16},{1,17},{2,18},{3,19},{4,20},{5,21},{6,22},{7,23},{8,24},{9,... | collective-permute-start | bytes 122888 | tf_op jit(solution)/shard_map/ppermute | solution.py:43
  (8 other events, 16.7 us)

commit v4 on v3

--- a/solution.py
+++ b/solution.py
@@ -20,6 +20,7 @@
 ROWS_HALF = HALF_VENUES * NODE_STEPS
 KEYS_HALF = HALF_VENUES * STEPS
 LSE_ITEM = 64
+VMEM_LIMIT = 56 << 20
 
 
 def stage_bits(count):
@@ -58,31 +59,32 @@
     return held, swap_stage(held, orders, 0)
 
 
-def arrange_body(pick_ref, key_ref, value_ref, out_ref):
+def arrange_body(pick_ref, *refs):
+    sources, out_ref = refs[:-1], refs[-1]
     chunks, rows, cols = out_ref.shape
+    part = rows // len(sources)
     pick = pick_ref[...]
-    for side, ref in enumerate((key_ref, value_ref)):
+    for side, ref in enumerate(sources):
         moved = jnp.dot(pick, ref[...], preferred_element_type=jnp.float32)
-        moved = moved.reshape(chunks, rows // 2, cols).astype(jnp.bfloat16)
-        out_ref[:, side * (rows // 2) : (side + 1) * (rows // 2), :] = moved
-
-
-def arrange(pick, keys, values, chunks):
-    rows, width = keys.shape
-    per_chunk = 2 * rows // chunks
+        moved = moved.reshape(chunks, part, cols).astype(jnp.bfloat16)
+        out_ref[:, side * part : (side + 1) * part, :] = moved
+
+
+def arrange(pick, sources, chunks):
+    rows = pick.shape[0]
+    total, width = sources[0].shape
+    per_chunk = len(sources) * rows // chunks
+    last = total // rows - 1
     return pl.pallas_call(
         arrange_body,
         grid=(width // COLS_STEP,),
-        in_specs=[
-            pl.BlockSpec((rows, rows), lambda j: (0, 0)),
-            pl.BlockSpec((rows, COLS_STEP), lambda j: (0, j)),
-            pl.BlockSpec((rows, COLS_STEP), lambda j: (0, j)),
-        ],
+        in_specs=[pl.BlockSpec((rows, rows), lambda j: (0, 0))]
+        + [pl.BlockSpec((rows, COLS_STEP), lambda j: (last, j)) for _ in sources],
         out_specs=pl.BlockSpec((chunks, per_chunk, COLS_STEP), lambda j: (0, 0, j)),
         out_shape=jax.ShapeDtypeStruct((chunks, per_chunk, width), jnp.bfloat16),
-        compiler_params=pltpu.CompilerParams(vmem_limit_bytes=24 << 20),
+        compiler_params=pltpu.CompilerParams(vmem_limit_bytes=VMEM_LIMIT),
         name="arrange",
-    )(pick, keys, values)
+    )(pick, *sources)
 
 
 def score_body(own_ref, far_ref, kv_ref, probs_ref, lse_ref):
@@ -148,7 +150,7 @@
             jax.ShapeDtypeStruct((heads, 2, 2 * ROWS_HALF, KEYS_HALF), jnp.bfloat16),
             jax.ShapeDtypeStruct((2 * ROWS_HALF, 128), jnp.float32),
         ],
-        compiler_params=pltpu.CompilerParams(vmem_limit_bytes=24 << 20),
+        compiler_params=pltpu.CompilerParams(vmem_limit_bytes=VMEM_LIMIT),
         name="half_scores",
     )(own, far, kv)
 
@@ -189,7 +191,7 @@
         ],
         out_specs=pl.BlockSpec((2 * NODE_STEPS, COLS_STEP), lambda j: (0, j)),
         out_shape=jax.ShapeDtypeStruct((2 * NODE_STEPS, width), jnp.bfloat16),
-        compiler_params=pltpu.CompilerParams(vmem_limit_bytes=24 << 20),
+        compiler_params=pltpu.CompilerParams(vmem_limit_bytes=VMEM_LIMIT),
         name="half_pool",
     )(probs, lse, far_lse, kv)
 
@@ -256,7 +258,7 @@
             pltpu.VMEM((rows, 2 * padded), jnp.float32),
             pltpu.VMEM((rows, 1), jnp.float32),
         ],
-        compiler_params=pltpu.CompilerParams(vmem_limit_bytes=24 << 20),
+        compiler_params=pltpu.CompilerParams(vmem_limit_bytes=VMEM_LIMIT),
         name="expand",
     )(near, far, mix, inv, gain, norm, gate, up)
 
@@ -319,7 +321,7 @@
             pltpu.VMEM((rows, width), jnp.bfloat16),
             pltpu.VMEM((rows, feat), jnp.float32),
         ],
-        compiler_params=pltpu.CompilerParams(vmem_limit_bytes=24 << 20),
+        compiler_params=pltpu.CompilerParams(vmem_limit_bytes=VMEM_LIMIT),
         name="contract",
     )(near, far, down)
 
@@ -359,21 +361,14 @@
         return (source == lax.broadcasted_iota(jnp.int32, (rows, rows), 1)).astype(jnp.bfloat16)
 
     whole_venue = pairs_dev == STEPS
-    if whole_venue:
-        query_vecs = query_vecs[STEPS - NODE_STEPS :]
-    query_pairs = query_vecs.shape[0]
-    query_rows = query_pairs * inst_total
-    queries = jnp.dot(
-        picker(query_pairs),
-        query_vecs.reshape(query_rows, feat_width),
-        preferred_element_type=jnp.float32,
-    ).astype(jnp.bfloat16)
+    query_pairs = NODE_STEPS if whole_venue else pairs_dev
+    rows = pairs_dev * inst_total
+    queries = arrange(picker(query_pairs), [query_vecs.reshape(rows, feat_width)], chunks)
     queries = lax.all_to_all(queries, "gx", 0, 0, axis_index_groups=groups, tiled=True)
-    kv_rows = pairs_dev * inst_total
+    queries = queries.reshape(query_pairs * inst_total, feat_width)
     kv = arrange(
         picker(pairs_dev),
-        key_vecs.reshape(kv_rows, feat_width),
-        value_vecs.reshape(kv_rows, feat_width),
+        [key_vecs.reshape(rows, feat_width), value_vecs.reshape(rows, feat_width)],
         chunks,
     )
     kv, queries = lax.optimization_barrier((kv, queries))

time: 223 us -> 223 us (level)
  local copies, waits for them, and re-layouts: 35.7 us -> 8.09 us
  Pallas kernels: 19.3 us -> 46 us
  other arithmetic: 1.7 us -> 6.21 us
  starting transfers between devices: 45.3 us -> 42.6 us
    unnamed x37 -> x29, local copies, waits for them, and re-layouts: 34.2 us -> 6.65 us
    pallas_call x2, Pallas kernels: 8.33 us -> 17.6 us  [expand(): pl.pallas_call(expand_body, grid=(feat // tile,), in_specs=[pl.BlockSpec(...]
    pallas_call x2, Pallas kernels: 4.13 us -> 10.6 us  [contract(): pl.pallas_call(functools.partial(contract_body, swap=swap), grid=(width /...]
    pallas_call x1 -> x2, Pallas kernels: 1.97 us -> 8.33 us  [arrange(): pl.pallas_call(arrange_body, grid=(width // COLS_STEP,), in_specs=[pl.Blo...]
    ppermute x18, starting transfers between devices: 35.3 us -> 32.7 us  [swap_stage(): return lax.ppermute(block, ('gx', 'ta'), pairs)]
    pallas_call x1, Pallas kernels: 1.98 us -> 4.38 us  [half_pool(): pl.pallas_call(pool_body, grid=(width // COLS_STEP,), in_specs=[pl.BlockS...]
  transfers between devices with their start and end apart: 22 -> 22, of which waited for: 22 -> 22; matrix products, arithmetic and copies ran while one was open for 0% -> 2% of each run, Pallas kernels for 1% -> 2%
where the time goes in v4:
time: 223 us; the launch traced here: 222 us
  waiting for transfers between devices  118 us (53%)
  Pallas kernels  46 us (21%)
  starting transfers between devices  42.6 us (19%)
  local copies, waits for them, and re-layouts  8.09 us (4%)
  other arithmetic  6.21 us (3%)
    ppermute x18, waiting for transfers between devices, swap_stage(): return lax.ppermute(block, ('gx', 'ta'), pairs)  106 us
    ppermute x18, starting transfers between devices, swap_stage(): return lax.ppermute(block, ('gx', 'ta'), pairs)  32.7 us
    pallas_call x2, Pallas kernels, expand(): pl.pallas_call(expand_body, grid=(feat // tile,), in_specs=[pl.BlockSpec(...  17.6 us
    pallas_call x2, Pallas kernels, contract(): pl.pallas_call(functools.partial(contract_body, swap=swap), grid=(width /...  10.6 us
    pallas_call x2, Pallas kernels, arrange(): pl.pallas_call(arrange_body, grid=(width // COLS_STEP,), in_specs=[pl.Blo...  8.33 us
    unnamed x29, local copies, waits for them, and re-layouts  6.65 us
    all_to_all x1, starting transfers between devices, per_device(): lax.all_to_all(queries, 'gx', 0, 0, axis_index_groups=groups, tiled=True)  6.18 us
    pallas_call x1, Pallas kernels, half_scores(): pl.pallas_call(score_body, grid=(width // COLS_STEP,), in_specs=[pl.Block...  5.08 us
  transfers between devices with their start and end apart: 22, of which 22 were waited for; matrix products, arithmetic and copies ran while one was open for 2% of the time, Pallas kernels for 2%

profile of v4, /device:TPU:0, one launch (start us, length us, event | category | flops | bytes accessed | tf_op | source)
XLA Modules:
  0.0 221.7 jit_solution(5297102202013105874)
XLA Ops:
  1.5 3.6 %arrange.3 = bf16[8,16,2560]{2,1,0:T(8,128)(2,1)} custom-call(bf16[128,128]{1,0:T(8,128)(2,1)} %fusion.7.pick_ref, bf16[256,2560]{1,0:T(8,128)(2,1)} %bitcast.20), custom_call_target="tpu_custom_call" | custom-call | tf_op jit(solution)/shard_map/arrange/pallas_call | solution.py:78
  5.1 6.2 %all-to-all-start = ((bf16[8,16,2560]{2,1,0:T(8,128)(2,1)}), bf16[8,16,2560]{2,1,0:T(8,128)(2,1)S(1)}, u32[]{:S(2)}, u32[]{:S(2)}) async-start(bf16[8,16,2560]{2,1,0:T(8,128)(2,1)} %arrange.3), calls=%async_computation | async-start | bytes 1310720 | tf_op jit(solution)/shard_map/all_to_all | solution.py:367
  12.3 4.8 %arrange.2 = bf16[8,64,2560]{2,1,0:T(8,128)(2,1)} custom-call(bf16[256,256]{1,0:T(8,128)(2,1)} %fusion.1.pick_ref, bf16[256,2560]{1,0:T(8,128)(2,1)} %bitcast.21, bf16[256,2560]{1,0:T(8,128)(2,1)} %bitcast.22), custom_call_target="tpu_custom_call" | custom-call | tf_op jit(solution)/shard_map/arrange/pallas_call | solution.py:78
  17.1 4.6 %all-to-all-done = bf16[8,16,2560]{2,1,0:T(8,128)(2,1)S(1)} async-done(((bf16[8,16,2560]{2,1,0:T(8,128)(2,1)}), bf16[8,16,2560]{2,1,0:T(8,128)(2,1)S(1)}, u32[]{:S(2)}, u32[]{:S(2)}) %all-to-all-start) | async-done | bytes 655392 | tf_op jit(solution)/shard_map/all_to_all | solution.py:367
  21.7 3.6 %all-to-all-start.1 = ((bf16[8,64,2560]{2,1,0:T(8,128)(2,1)}), bf16[8,64,2560]{2,1,0:T(8,128)(2,1)S(1)}, u32[]{:S(2)}, u32[]{:S(2)}) async-start(bf16[8,64,2560]{2,1,0:T(8,128)(2,1)} %arrange.2), calls=%async_computation.1 | async-start | bytes 5242880 | tf_op jit(solution)/shard_map/all_to_all | solution.py:380
  25.3 2.7 %collective-permute-start = (bf16[128,2560]{1,0:T(8,128)(2,1)S(1)}, bf16[128,2560]{1,0:T(8,128)(2,1)}, u32[]{:S(2)}, u32[]{:S(2)}) collective-permute-start(bf16[128,2560]{1,0:T(8,128)(2,1)S(1)} %bitcast.18), channel_id=1, source_target_pairs={{0,16},{1,17},{2,18},{3,19},{4,20},{5,21},{6,22},{7,23},{8,24},{9,... | collective-permute-start | bytes 1966088 | tf_op jit(solution)/shard_map/ppermute | solution.py:44
  28.1 38.9 %collective-permute-done.far_ref = bf16[128,2560]{1,0:T(8,128)(2,1)} collective-permute-done((bf16[128,2560]{1,0:T(8,128)(2,1)S(1)}, bf16[128,2560]{1,0:T(8,128)(2,1)}, u32[]{:S(2)}, u32[]{:S(2)}) %collective-permute-start) | collective-permute-done | bytes 655392 | tf_op jit(solution)/shard_map/ppermute | solution.py:44
  66.9 2.4 %all-to-all-done.1 = bf16[8,64,2560]{2,1,0:T(8,128)(2,1)S(1)} async-done(((bf16[8,64,2560]{2,1,0:T(8,128)(2,1)}), bf16[8,64,2560]{2,1,0:T(8,128)(2,1)S(1)}, u32[]{:S(2)}, u32[]{:S(2)}) %all-to-all-start.1) | async-done | bytes 2621472 | tf_op jit(solution)/shard_map/all_to_all | solution.py:380
  70.8 5.1 %half_scores.1 = (bf16[20,2,128,128]{3,2,1,0:T(8,128)(2,1)}, f32[128,128]{1,0:T(8,128)}) custom-call(bf16[128,2560]{1,0:T(8,128)(2,1)} %bitcast.19, bf16[128,2560]{1,0:T(8,128)(2,1)} %collective-permute-done.far_ref, bf16[8,4,16,2560]{3,2,1,0:T(8,128)(2,1)} %bitcast.16), custom_call_target="tpu_custom_call" | custom-call | tf_op jit(solution)/shard_map/half_scores/pallas_call | solution.py:137
  77.0 4.5 %collective-permute-done.1.far_ref = f32[128,128]{1,0:T(8,128)S(1)} collective-permute-done((f32[128,128]{1,0:T(8,128)}, f32[128,128]{1,0:T(8,128)S(1)}, u32[]{:S(2)}, u32[]{:S(2)}) %collective-permute-start.1) | collective-permute-done | bytes 65568 | tf_op jit(solution)/shard_map/ppermute | solution.py:44
  82.1 4.4 %half_pool.1 = bf16[16,2560]{1,0:T(8,128)(2,1)} custom-call(bf16[20,2,128,128]{3,2,1,0:T(8,128)(2,1)} %get-tuple-element.15.probs_ref, f32[128,128]{1,0:T(8,128)} %get-tuple-element.16.lse_ref, f32[128,128]{1,0:T(8,128)} %copy-done.9, bf16[8,4,16,2560]{3,2,1,0:T(8,128)(2,1)} %bitcast.17), custom_call_target="tpu_custom_call" | custom-call | tf_op jit(solution)/shard_map/half_pool/pallas_call | solution.py:183
  87.4 4.6 %collective-permute-done.2 = bf16[16,2560]{1,0:T(8,128)(2,1)S(1)} collective-permute-done((bf16[16,2560]{1,0:T(8,128)(2,1)}, bf16[16,2560]{1,0:T(8,128)(2,1)S(1)}, u32[]{:S(2)}, u32[]{:S(2)}) %collective-permute-start.2) | collective-permute-done | bytes 81952 | tf_op jit(solution)/shard_map/ppermute | solution.py:44
  93.0 3.2 %collective-permute-start.3 = (bf16[16,2560]{1,0:T(8,128)(2,1)S(1)}, bf16[16,2560]{1,0:T(8,128)(2,1)S(1)}, u32[]{:S(2)}, u32[]{:S(2)}) collective-permute-start(bf16[16,2560]{1,0:T(8,128)(2,1)S(1)} %add_convert_fusion), channel_id=1, source_target_pairs={{0,8},{1,9},{2,10},{3,11},{4,12},{5,13},{6,14},{7,15},{8,0},{9,1},... | collective-permute-start | bytes 245768 | tf_op jit(solution)/shard_map/ppermute | solution.py:44
  99.9 5.8 %collective-permute-done.4 = bf16[32,2560]{1,0:T(8,128)(2,1)S(1)} collective-permute-done((bf16[32,2560]{1,0:T(8,128)(2,1)S(1)}, bf16[32,2560]{1,0:T(8,128)(2,1)S(1)}, u32[]{:S(2)}, u32[]{:S(2)}) %collective-permute-start.4) | collective-permute-done | bytes 163872 | tf_op jit(solution)/shard_map/ppermute | solution.py:44
  105.7 3.2 %collective-permute-start.5 = (bf16[64,2560]{1,0:T(8,128)(2,1)S(1)}, bf16[64,2560]{1,0:T(8,128)(2,1)S(1)}, u32[]{:S(2)}, u32[]{:S(2)}) collective-permute-start(bf16[64,2560]{1,0:T(8,128)(2,1)S(1)} %pad_maximum_fusion.near_ref), channel_id=1, source_target_pairs={{0,2},{1,5},{2,0},{3,7},{4,6},{5,1},{6,4},{7,3},{8,10},{9,13},{10,... | collective-permute-start | bytes 983048 | tf_op jit(solution)/shard_map/ppermute | solution.py:44
  114.7 8.8 %expand.2.near_ref = bf16[128,2688]{1,0:T(8,128)(2,1)} custom-call(bf16[64,2560]{1,0:T(8,128)(2,1)} %copy-done.3, bf16[64,2560]{1,0:T(8,128)(2,1)} %copy-done.7, bf16[3,128,128]{2,1,0:T(8,128)(2,1)} %fusion.mix_ref, f32[128,1]{1,0:T(8,128)} %copy.16.inv_ref, f32[2,3,2560]{2,1,0:T(4,128)} %copy.17.gain_ref, f32[2,1,2560]{2,1,0:T(1,128)} %broadcast_in_dim.56.norm_ref, ...), custom_call_target="tpu_custom_call" | custom-call | tf_op jit(solution)/shard_map/expand/pallas_call | solution.py:242
  123.5 2.3 %collective-permute-done.6.far_ref = bf16[128,2688]{1,0:T(8,128)(2,1)S(1)} collective-permute-done((bf16[128,2688]{1,0:T(8,128)(2,1)}, bf16[128,2688]{1,0:T(8,128)(2,1)S(1)}, u32[]{:S(2)}, u32[]{:S(2)}) %collective-permute-start.6) | collective-permute-done | bytes 688160 | tf_op jit(solution)/shard_map/ppermute | solution.py:421
  126.8 5.3 %contract.2 = (f32[64,2560]{1,0:T(8,128)}, bf16[64,2560]{1,0:T(8,128)(2,1)}) custom-call(bf16[128,2688]{1,0:T(8,128)(2,1)} %expand.2.near_ref, bf16[128,2688]{1,0:T(8,128)(2,1)} %copy-done.5, bf16[2,1280,2560]{2,1,0:T(8,128)(2,1)} %down_ref.3), custom_call_target="tpu_custom_call" | custom-call | tf_op jit(solution)/shard_map/contract/pallas_call | solution.py:304
  134.1 5.3 %collective-permute-done.7 = bf16[64,2560]{1,0:T(8,128)(2,1)S(1)} collective-permute-done((bf16[64,2560]{1,0:T(8,128)(2,1)}, bf16[64,2560]{1,0:T(8,128)(2,1)S(1)}, u32[]{:S(2)}, u32[]{:S(2)}) %collective-permute-start.7) | collective-permute-done | bytes 327712 | tf_op jit(solution)/shard_map/ppermute | solution.py:44
  142.0 3.9 %collective-permute-done.8 = bf16[32,2560]{1,0:T(8,128)(2,1)S(1)} collective-permute-done((bf16[32,2560]{1,0:T(8,128)(2,1)S(1)}, bf16[32,2560]{1,0:T(8,128)(2,1)S(1)}, u32[]{:S(2)}, u32[]{:S(2)}) %collective-permute-start.8) | collective-permute-done | bytes 163872 | tf_op jit(solution)/shard_map/ppermute | solution.py:44
  148.1 2.4 %collective-permute-done.9 = bf16[16,2560]{1,0:T(8,128)(2,1)S(1)} collective-permute-done((bf16[16,2560]{1,0:T(8,128)(2,1)S(1)}, bf16[16,2560]{1,0:T(8,128)(2,1)S(1)}, u32[]{:S(2)}, u32[]{:S(2)}) %collective-permute-start.9) | collective-permute-done | bytes 81952 | tf_op jit(solution)/shard_map/ppermute | solution.py:44
  152.1 3.4 %collective-permute-done.10 = bf16[8,2560]{1,0:T(8,128)(2,1)S(1)} collective-permute-done((bf16[8,2560]{1,0:T(8,128)(2,1)S(1)}, bf16[8,2560]{1,0:T(8,128)(2,1)S(1)}, u32[]{:S(2)}, u32[]{:S(2)}) %collective-permute-start.10) | collective-permute-done | bytes 40992 | tf_op jit(solution)/shard_map/ppermute | solution.py:44
  157.1 3.4 %collective-permute-done.11 = bf16[8,2560]{1,0:T(8,128)(2,1)S(1)} collective-permute-done((bf16[8,2560]{1,0:T(8,128)(2,1)S(1)}, bf16[8,2560]{1,0:T(8,128)(2,1)S(1)}, u32[]{:S(2)}, u32[]{:S(2)}) %collective-permute-start.11) | collective-permute-done | bytes 40992 | tf_op jit(solution)/shard_map/ppermute | solution.py:44
  162.7 2.4 %collective-permute-done.12 = bf16[16,2560]{1,0:T(8,128)(2,1)S(1)} collective-permute-done((bf16[16,2560]{1,0:T(8,128)(2,1)S(1)}, bf16[16,2560]{1,0:T(8,128)(2,1)S(1)}, u32[]{:S(2)}, u32[]{:S(2)}) %collective-permute-start.12) | collective-permute-done | bytes 81952 | tf_op jit(solution)/shard_map/ppermute | solution.py:44
  166.6 5.7 %collective-permute-done.13 = bf16[32,2560]{1,0:T(8,128)(2,1)S(1)} collective-permute-done((bf16[32,2560]{1,0:T(8,128)(2,1)S(1)}, bf16[32,2560]{1,0:T(8,128)(2,1)S(1)}, u32[]{:S(2)}, u32[]{:S(2)}) %collective-permute-start.13) | collective-permute-done | bytes 163872 | tf_op jit(solution)/shard_map/ppermute | solution.py:44
  174.0 5.6 %collective-permute-done.14.far_ref = bf16[64,2560]{1,0:T(8,128)(2,1)S(1)} collective-permute-done((bf16[64,2560]{1,0:T(8,128)(2,1)S(1)}, bf16[64,2560]{1,0:T(8,128)(2,1)S(1)}, u32[]{:S(2)}, u32[]{:S(2)}) %collective-permute-start.14) | collective-permute-done | bytes 327712 | tf_op jit(solution)/shard_map/ppermute | solution.py:44
  180.3 8.8 %expand.3.near_ref = bf16[128,2688]{1,0:T(8,128)(2,1)} custom-call(bf16[64,2560]{1,0:T(8,128)(2,1)} %copy-done.4, bf16[64,2560]{1,0:T(8,128)(2,1)} %copy-done.8, bf16[3,128,128]{2,1,0:T(8,128)(2,1)} %fusion.mix_ref, f32[128,1]{1,0:T(8,128)} %copy.16.inv_ref, f32[2,3,2560]{2,1,0:T(4,128)} %copy.17.gain_ref, f32[2,1,2560]{2,1,0:T(1,128)} %broadcast_in_dim.56.norm_ref, ...), custom_call_target="tpu_custom_call" | custom-call | tf_op jit(solution)/shard_map/expand/pallas_call | solution.py:242
  192.3 5.3 %contract.3 = (f32[64,2560]{1,0:T(8,128)}, bf16[64,2560]{1,0:T(8,128)(2,1)}) custom-call(bf16[128,2688]{1,0:T(8,128)(2,1)} %expand.3.near_ref, bf16[128,2688]{1,0:T(8,128)(2,1)} %copy-done.6, bf16[2,1280,2560]{2,1,0:T(8,128)(2,1)} %down_ref.3), custom_call_target="tpu_custom_call" | custom-call | tf_op jit(solution)/shard_map/contract/pallas_call | solution.py:304
  199.1 5.8 %collective-permute-done.16 = bf16[64,2560]{1,0:T(8,128)(2,1)S(1)} collective-permute-done((bf16[64,2560]{1,0:T(8,128)(2,1)}, bf16[64,2560]{1,0:T(8,128)(2,1)S(1)}, u32[]{:S(2)}, u32[]{:S(2)}) %collective-permute-start.16) | collective-permute-done | bytes 327712 | tf_op jit(solution)/shard_map/ppermute | solution.py:44
  207.6 3.9 %collective-permute-done.17 = bf16[32,2560]{1,0:T(8,128)(2,1)S(1)} collective-permute-done((bf16[32,2560]{1,0:T(8,128)(2,1)S(1)}, bf16[32,2560]{1,0:T(8,128)(2,1)S(1)}, u32[]{:S(2)}, u32[]{:S(2)}) %collective-permute-start.17) | collective-permute-done | bytes 163872 | tf_op jit(solution)/shard_map/ppermute | solution.py:44
  213.6 2.4 %collective-permute-done.18 = bf16[16,2560]{1,0:T(8,128)(2,1)S(1)} collective-permute-done((bf16[16,2560]{1,0:T(8,128)(2,1)S(1)}, bf16[16,2560]{1,0:T(8,128)(2,1)S(1)}, u32[]{:S(2)}, u32[]{:S(2)}) %collective-permute-start.18) | collective-permute-done | bytes 81952 | tf_op jit(solution)/shard_map/ppermute | solution.py:44
  217.6 3.4 %collective-permute-done.19 = bf16[8,2560]{1,0:T(8,128)(2,1)S(1)} collective-permute-done((bf16[8,2560]{1,0:T(8,128)(2,1)S(1)}, bf16[8,2560]{1,0:T(8,128)(2,1)S(1)}, u32[]{:S(2)}, u32[]{:S(2)}) %collective-permute-start.19) | collective-permute-done | bytes 40992 | tf_op jit(solution)/shard_map/ppermute | solution.py:44
  (96 shorter events, 45.7 us)
Async XLA Ops:
  5.1 16.5 %all-to-all-start = ((bf16[8,16,2560]{2,1,0:T(8,128)(2,1)}), bf16[8,16,2560]{2,1,0:T(8,128)(2,1)S(1)}, u32[]{:S(2)}, u32[]{:S(2)}) async-start(bf16[8,16,2560]{2,1,0:T(8,128)(2,1)} %arrange.3), calls=%async_computation | async-start | bytes 1310720 | tf_op jit(solution)/shard_map/all_to_all | solution.py:367
  21.6 3.6 %copy-start.2 = (bf16[8,16,2560]{2,1,0:T(8,128)(2,1)}, bf16[8,16,2560]{2,1,0:T(8,128)(2,1)S(1)}, u32[]{:S(2)}) copy-start(bf16[8,16,2560]{2,1,0:T(8,128)(2,1)S(1)} %all-to-all-done) | copy-start | bytes 1966084
  21.7 47.6 %all-to-all-start.1 = ((bf16[8,64,2560]{2,1,0:T(8,128)(2,1)}), bf16[8,64,2560]{2,1,0:T(8,128)(2,1)S(1)}, u32[]{:S(2)}, u32[]{:S(2)}) async-start(bf16[8,64,2560]{2,1,0:T(8,128)(2,1)} %arrange.2), calls=%async_computation.1 | async-start | bytes 5242880 | tf_op jit(solution)/shard_map/all_to_all | solution.py:380
  25.3 51.7 %copy-start.12 = (s32[64,2]{0,1:T(2,128)S(1)}, s32[64,2]{0,1:T(2,128)}, u32[]{:S(2)}) copy-start(s32[64,2]{0,1:T(2,128)} %param.15) | copy-start | bytes 1540
  25.3 41.6 %collective-permute-start = (bf16[128,2560]{1,0:T(8,128)(2,1)S(1)}, bf16[128,2560]{1,0:T(8,128)(2,1)}, u32[]{:S(2)}, u32[]{:S(2)}) collective-permute-start(bf16[128,2560]{1,0:T(8,128)(2,1)S(1)} %bitcast.18), channel_id=1, source_target_pairs={{0,16},{1,17},{2,18},{3,19},{4,20},{5,21},{6,22},{7,23},{8,24},{9,... | collective-permute-start | bytes 1966088 | tf_op jit(solution)/shard_map/ppermute | solution.py:44
  69.3 1.5 copy-start.1
  75.8 23.9 %copy-start.13 = (s32[64]{0:T(128)S(1)}, s32[64]{0:T(128)}, u32[]{:S(2)}) copy-start(s32[64]{0:T(128)} %param.16) | copy-start | bytes 772
  75.8 5.7 %collective-permute-start.1 = (f32[128,128]{1,0:T(8,128)}, f32[128,128]{1,0:T(8,128)S(1)}, u32[]{:S(2)}, u32[]{:S(2)}) collective-permute-start(f32[128,128]{1,0:T(8,128)} %get-tuple-element.16.lse_ref), channel_id=1, source_target_pairs={{0,16},{1,17},{2,18},{3,19},{4,20},{5,21},{6,22},{7,23},{8,24},{9,... | collective-permute-start | bytes 196616 | tf_op jit(solution)/shard_map/ppermute | solution.py:44
  82.1 26.8 %copy-start.11 = (f32[2,2560]{1,0:T(2,128)S(1)}, f32[2,2560]{1,0:T(2,128)}, u32[]{:S(2)}) copy-start(f32[2,2560]{1,0:T(2,128)} %param.18) | copy-start | bytes 61444
  82.1 28.2 %copy-start.10 = (f32[2,3,2560]{2,0,1:T(2,128)S(1)}, f32[2,3,2560]{2,0,1:T(2,128)}, u32[]{:S(2)}) copy-start(f32[2,3,2560]{2,0,1:T(2,128)} %param.17) | copy-start | bytes 184324
  86.5 5.6 %collective-permute-start.2 = (bf16[16,2560]{1,0:T(8,128)(2,1)}, bf16[16,2560]{1,0:T(8,128)(2,1)S(1)}, u32[]{:S(2)}, u32[]{:S(2)}) collective-permute-start(bf16[16,2560]{1,0:T(8,128)(2,1)} %half_pool.1), channel_id=1, source_target_pairs={{0,16},{1,17},{2,18},{3,19},{4,20},{5,21},{6,22},{7,23},{8,24},{9,... | collective-permute-start | bytes 245768 | tf_op jit(solution)/shard_map/ppermute | solution.py:44
  93.0 5.6 %collective-permute-start.3 = (bf16[16,2560]{1,0:T(8,128)(2,1)S(1)}, bf16[16,2560]{1,0:T(8,128)(2,1)S(1)}, u32[]{:S(2)}, u32[]{:S(2)}) collective-permute-start(bf16[16,2560]{1,0:T(8,128)(2,1)S(1)} %add_convert_fusion), channel_id=1, source_target_pairs={{0,8},{1,9},{2,10},{3,11},{4,12},{5,13},{6,14},{7,15},{8,0},{9,1},... | collective-permute-start | bytes 245768 | tf_op jit(solution)/shard_map/ppermute | solution.py:44
  98.6 7.1 %collective-permute-start.4 = (bf16[32,2560]{1,0:T(8,128)(2,1)S(1)}, bf16[32,2560]{1,0:T(8,128)(2,1)S(1)}, u32[]{:S(2)}, u32[]{:S(2)}) collective-permute-start(bf16[32,2560]{1,0:T(8,128)(2,1)S(1)} %pad_maximum_fusion.2), channel_id=1, source_target_pairs={{0,4},{1,3},{2,6},{3,1},{4,0},{5,7},{6,2},{7,5},{8,12},{9,11},{10,... | collective-permute-start | bytes 491528 | tf_op jit(solution)/shard_map/ppermute | solution.py:44
  105.7 8.3 %copy-start.3 = (bf16[64,2560]{1,0:T(8,128)(2,1)}, bf16[64,2560]{1,0:T(8,128)(2,1)S(1)}, u32[]{:S(2)}) copy-start(bf16[64,2560]{1,0:T(8,128)(2,1)S(1)} %pad_maximum_fusion.near_ref) | copy-start | bytes 983044
  105.7 8.3 %collective-permute-start.5 = (bf16[64,2560]{1,0:T(8,128)(2,1)S(1)}, bf16[64,2560]{1,0:T(8,128)(2,1)S(1)}, u32[]{:S(2)}, u32[]{:S(2)}) collective-permute-start(bf16[64,2560]{1,0:T(8,128)(2,1)S(1)} %pad_maximum_fusion.near_ref), channel_id=1, source_target_pairs={{0,2},{1,5},{2,0},{3,7},{4,6},{5,1},{6,4},{7,3},{8,10},{9,13},{10,... | collective-permute-start | bytes 983048 | tf_op jit(solution)/shard_map/ppermute | solution.py:44
  123.5 2.4 %collective-permute-start.6 = (bf16[128,2688]{1,0:T(8,128)(2,1)}, bf16[128,2688]{1,0:T(8,128)(2,1)S(1)}, u32[]{:S(2)}, u32[]{:S(2)}) collective-permute-start(bf16[128,2688]{1,0:T(8,128)(2,1)} %expand.2.near_ref), channel_id=1, source_target_pairs={{0,1},{1,0},{2,3},{3,2},{4,5},{5,4},{6,7},{7,6},{8,9},{9,8},{10,11... | collective-permute-start | bytes 2064392 | tf_op jit(solution)/shard_map/ppermute | solution.py:421
  125.9 0.9 copy-start.5
  132.1 7.3 %collective-permute-start.7 = (bf16[64,2560]{1,0:T(8,128)(2,1)}, bf16[64,2560]{1,0:T(8,128)(2,1)S(1)}, u32[]{:S(2)}, u32[]{:S(2)}) collective-permute-start(bf16[64,2560]{1,0:T(8,128)(2,1)} %get-tuple-element.18), channel_id=1, source_target_pairs={{0,2},{1,5},{2,0},{3,7},{4,6},{5,1},{6,4},{7,3},{8,10},{9,13},{10,... | collective-permute-start | bytes 983048 | tf_op jit(solution)/shard_map/ppermute | solution.py:44
  140.6 5.4 %collective-permute-start.8 = (bf16[32,2560]{1,0:T(8,128)(2,1)S(1)}, bf16[32,2560]{1,0:T(8,128)(2,1)S(1)}, u32[]{:S(2)}, u32[]{:S(2)}) collective-permute-start(bf16[32,2560]{1,0:T(8,128)(2,1)S(1)} %slice.113), channel_id=1, source_target_pairs={{0,4},{1,3},{2,6},{3,1},{4,0},{5,7},{6,2},{7,5},{8,12},{9,11},{10,... | collective-permute-start | bytes 491528 | tf_op jit(solution)/shard_map/ppermute | solution.py:44
  146.0 4.5 %collective-permute-start.9 = (bf16[16,2560]{1,0:T(8,128)(2,1)S(1)}, bf16[16,2560]{1,0:T(8,128)(2,1)S(1)}, u32[]{:S(2)}, u32[]{:S(2)}) collective-permute-start(bf16[16,2560]{1,0:T(8,128)(2,1)S(1)} %slice.115), channel_id=1, source_target_pairs={{0,8},{1,9},{2,10},{3,11},{4,12},{5,13},{6,14},{7,15},{8,0},{9,1},... | collective-permute-start | bytes 245768 | tf_op jit(solution)/shard_map/ppermute | solution.py:44
  150.6 5.0 %collective-permute-start.10 = (bf16[8,2560]{1,0:T(8,128)(2,1)S(1)}, bf16[8,2560]{1,0:T(8,128)(2,1)S(1)}, u32[]{:S(2)}, u32[]{:S(2)}) collective-permute-start(bf16[8,2560]{1,0:T(8,128)(2,1)S(1)} %slice.117), channel_id=1, source_target_pairs={{0,16},{1,17},{2,18},{3,19},{4,20},{5,21},{6,22},{7,23},{8,24},{9,... | collective-permute-start | bytes 122888 | tf_op jit(solution)/shard_map/ppermute | solution.py:44
  155.6 5.0 %collective-permute-start.11 = (bf16[8,2560]{1,0:T(8,128)(2,1)S(1)}, bf16[8,2560]{1,0:T(8,128)(2,1)S(1)}, u32[]{:S(2)}, u32[]{:S(2)}) collective-permute-start(bf16[8,2560]{1,0:T(8,128)(2,1)S(1)} %fusion.6), channel_id=1, source_target_pairs={{0,16},{1,17},{2,18},{3,19},{4,20},{5,21},{6,22},{7,23},{8,24},{9,... | collective-permute-start | bytes 122888 | tf_op jit(solution)/shard_map/ppermute | solution.py:44
  160.5 4.6 %collective-permute-start.12 = (bf16[16,2560]{1,0:T(8,128)(2,1)S(1)}, bf16[16,2560]{1,0:T(8,128)(2,1)S(1)}, u32[]{:S(2)}, u32[]{:S(2)}) collective-permute-start(bf16[16,2560]{1,0:T(8,128)(2,1)S(1)} %pad_maximum_fusion.4), channel_id=1, source_target_pairs={{0,8},{1,9},{2,10},{3,11},{4,12},{5,13},{6,14},{7,15},{8,0},{9,1},... | collective-permute-start | bytes 245768 | tf_op jit(solution)/shard_map/ppermute | solution.py:44
  165.1 7.2 %collective-permute-start.13 = (bf16[32,2560]{1,0:T(8,128)(2,1)S(1)}, bf16[32,2560]{1,0:T(8,128)(2,1)S(1)}, u32[]{:S(2)}, u32[]{:S(2)}) collective-permute-start(bf16[32,2560]{1,0:T(8,128)(2,1)S(1)} %pad_maximum_fusion.3), channel_id=1, source_target_pairs={{0,4},{1,3},{2,6},{3,1},{4,0},{5,7},{6,2},{7,5},{8,12},{9,11},{10,... | collective-permute-start | bytes 491528 | tf_op jit(solution)/shard_map/ppermute | solution.py:44
  172.4 7.2 %copy-start.4 = (bf16[64,2560]{1,0:T(8,128)(2,1)}, bf16[64,2560]{1,0:T(8,128)(2,1)S(1)}, u32[]{:S(2)}) copy-start(bf16[64,2560]{1,0:T(8,128)(2,1)S(1)} %pad_maximum_fusion.1.near_ref) | copy-start | bytes 983044
  172.4 7.1 %collective-permute-start.14 = (bf16[64,2560]{1,0:T(8,128)(2,1)S(1)}, bf16[64,2560]{1,0:T(8,128)(2,1)S(1)}, u32[]{:S(2)}, u32[]{:S(2)}) collective-permute-start(bf16[64,2560]{1,0:T(8,128)(2,1)S(1)} %pad_maximum_fusion.1.near_ref), channel_id=1, source_target_pairs={{0,2},{1,5},{2,0},{3,7},{4,6},{5,1},{6,4},{7,3},{8,10},{9,13},{10,... | collective-permute-start | bytes 983048 | tf_op jit(solution)/shard_map/ppermute | solution.py:44
  189.0 2.4 %collective-permute-start.15 = (bf16[128,2688]{1,0:T(8,128)(2,1)}, bf16[128,2688]{1,0:T(8,128)(2,1)S(1)}, u32[]{:S(2)}, u32[]{:S(2)}) collective-permute-start(bf16[128,2688]{1,0:T(8,128)(2,1)} %expand.3.near_ref), channel_id=1, source_target_pairs={{0,1},{1,0},{2,3},{3,2},{4,5},{5,4},{6,7},{7,6},{8,9},{9,8},{10,11... | collective-permute-start | bytes 2064392 | tf_op jit(solution)/shard_map/ppermute | solution.py:421
  191.4 0.9 copy-start.6
  197.6 7.3 %collective-permute-start.16 = (bf16[64,2560]{1,0:T(8,128)(2,1)}, bf16[64,2560]{1,0:T(8,128)(2,1)S(1)}, u32[]{:S(2)}, u32[]{:S(2)}) collective-permute-start(bf16[64,2560]{1,0:T(8,128)(2,1)} %get-tuple-element.20), channel_id=1, source_target_pairs={{0,2},{1,5},{2,0},{3,7},{4,6},{5,1},{6,4},{7,3},{8,10},{9,13},{10,... | collective-permute-start | bytes 983048 | tf_op jit(solution)/shard_map/ppermute | solution.py:44
  206.1 5.4 %collective-permute-start.17 = (bf16[32,2560]{1,0:T(8,128)(2,1)S(1)}, bf16[32,2560]{1,0:T(8,128)(2,1)S(1)}, u32[]{:S(2)}, u32[]{:S(2)}) collective-permute-start(bf16[32,2560]{1,0:T(8,128)(2,1)S(1)} %slice.112), channel_id=1, source_target_pairs={{0,4},{1,3},{2,6},{3,1},{4,0},{5,7},{6,2},{7,5},{8,12},{9,11},{10,... | collective-permute-start | bytes 491528 | tf_op jit(solution)/shard_map/ppermute | solution.py:44
  211.5 4.5 %collective-permute-start.18 = (bf16[16,2560]{1,0:T(8,128)(2,1)S(1)}, bf16[16,2560]{1,0:T(8,128)(2,1)S(1)}, u32[]{:S(2)}, u32[]{:S(2)}) collective-permute-start(bf16[16,2560]{1,0:T(8,128)(2,1)S(1)} %slice.114), channel_id=1, source_target_pairs={{0,8},{1,9},{2,10},{3,11},{4,12},{5,13},{6,14},{7,15},{8,0},{9,1},... | collective-permute-start | bytes 245768 | tf_op jit(solution)/shard_map/ppermute | solution.py:44
  216.1 5.0 %collective-permute-start.19 = (bf16[8,2560]{1,0:T(8,128)(2,1)S(1)}, bf16[8,2560]{1,0:T(8,128)(2,1)S(1)}, u32[]{:S(2)}, u32[]{:S(2)}) collective-permute-start(bf16[8,2560]{1,0:T(8,128)(2,1)S(1)} %slice.116), channel_id=1, source_target_pairs={{0,16},{1,17},{2,18},{3,19},{4,20},{5,21},{6,22},{7,23},{8,24},{9,... | collective-permute-start | bytes 122888 | tf_op jit(solution)/shard_map/ppermute | solution.py:44
  (4 other events, 2.8 us)

commit v5 on v4

--- a/solution.py
+++ b/solution.py
@@ -20,7 +20,7 @@
 ROWS_HALF = HALF_VENUES * NODE_STEPS
 KEYS_HALF = HALF_VENUES * STEPS
 LSE_ITEM = 64
-VMEM_LIMIT = 56 << 20
+VMEM_LIMIT = 8 << 20
 
 
 def stage_bits(count):
@@ -42,15 +42,6 @@
         for t in range(ta_count)
     ]
     return lax.ppermute(block, ("gx", "ta"), pairs)
-
-
-def scatter_rows(keep, give, orders):
-    held = keep + swap_stage(give, orders, 0).astype(jnp.float32)
-    for stage in range(1, len(orders[0])):
-        half = held.shape[0] // 2
-        give = held[half:].astype(jnp.bfloat16)
-        held = held[:half] + swap_stage(give, orders, stage).astype(jnp.float32)
-    return held
 
 
 def gather_rows(held, orders, stages):
@@ -75,12 +66,13 @@
     total, width = sources[0].shape
     per_chunk = len(sources) * rows // chunks
     last = total // rows - 1
+    cols = 1280 if width % 1280 == 0 else COLS_STEP
     return pl.pallas_call(
         arrange_body,
-        grid=(width // COLS_STEP,),
+        grid=(width // cols,),
         in_specs=[pl.BlockSpec((rows, rows), lambda j: (0, 0))]
-        + [pl.BlockSpec((rows, COLS_STEP), lambda j: (last, j)) for _ in sources],
-        out_specs=pl.BlockSpec((chunks, per_chunk, COLS_STEP), lambda j: (0, 0, j)),
+        + [pl.BlockSpec((rows, cols), lambda j: (last, j)) for _ in sources],
+        out_specs=pl.BlockSpec((chunks, per_chunk, cols), lambda j: (0, 0, j)),
         out_shape=jax.ShapeDtypeStruct((chunks, per_chunk, width), jnp.bfloat16),
         compiler_params=pltpu.CompilerParams(vmem_limit_bytes=VMEM_LIMIT),
         name="arrange",
@@ -155,7 +147,8 @@
     )(own, far, kv)
 
 
-def pool_body(probs_ref, lse_ref, far_ref, kv_ref, out_ref):
+def pool_body(probs_ref, lse_ref, far_ref, kv_ref, token_ref, out_ref):
+    del token_ref
     step = pl.program_id(0)
     far = jnp.concatenate([far_ref[ROWS_HALF:, :], far_ref[:ROWS_HALF, :]], axis=0)
     far = jnp.concatenate([far[:, LSE_ITEM:], far[:, :LSE_ITEM]], axis=1)
@@ -178,7 +171,7 @@
         out_ref[:, span] = jnp.concatenate(pooled, axis=0).astype(jnp.bfloat16)
 
 
-def half_pool(probs, lse, far_lse, kv):
+def half_pool(probs, lse, far_lse, kv, token):
     width = kv.shape[3]
     return pl.pallas_call(
         pool_body,
@@ -188,142 +181,145 @@
             pl.BlockSpec((2 * ROWS_HALF, 128), lambda j: (0, 0)),
             pl.BlockSpec((2 * ROWS_HALF, 128), lambda j: (0, 0)),
             pl.BlockSpec((HALF_VENUES, 2, STEPS, COLS_STEP), lambda j: (0, 1, 0, j)),
+            pl.BlockSpec(memory_space=pl.ANY),
         ],
         out_specs=pl.BlockSpec((2 * NODE_STEPS, COLS_STEP), lambda j: (0, j)),
         out_shape=jax.ShapeDtypeStruct((2 * NODE_STEPS, width), jnp.bfloat16),
         compiler_params=pltpu.CompilerParams(vmem_limit_bytes=VMEM_LIMIT),
         name="half_pool",
-    )(probs, lse, far_lse, kv)
+    )(probs, lse, far_lse, kv, token)
 
 
 def pad_lanes(width):
     return -(-width // 128) * 128
 
 
-def expand_body(near_ref, far_ref, mix_ref, inv_ref, gain_ref, norm_ref, gate_ref, up_ref, out_ref, total_ref, square_ref):
-    step = pl.program_id(0)
-    steps = pl.num_programs(0)
-    width = gate_ref.shape[1]
+def stage_body(*refs, layer):
+    count = (len(refs) - 3) // 2
+    token_ref, sems = refs[-2:]
+    copies = []
+    for place in range(count):
+        copy = pltpu.make_async_copy(refs[place].at[layer], refs[count + 1 + place], sems.at[place])
+        copy.start()
+        copies.append(copy)
+    token_ref[...] = jnp.zeros_like(token_ref)
+    for copy in copies:
+        copy.wait()
+
+
+def stage_weights(weights, layer, after):
+    held = [pltpu.with_memory_space_constraint(a, pltpu.HBM) for a in weights]
+    shapes = [pltpu.VMEM(a.shape[1:], a.dtype) for a in weights]
+    size = sum(a.size for a in weights) // ROUNDS
+    out = pl.pallas_call(
+        functools.partial(stage_body, layer=layer),
+        in_specs=[pl.BlockSpec(memory_space=pl.ANY)] * (len(held) + 1),
+        out_specs=[pl.BlockSpec(memory_space=pltpu.VMEM)] * (len(shapes) + 1),
+        out_shape=shapes + [jax.ShapeDtypeStruct((8, 128), jnp.float32)],
+        scratch_shapes=[pltpu.SemaphoreType.DMA((len(held),))],
+        compiler_params=pltpu.CompilerParams(vmem_limit_bytes=2 << 20),
+        cost_estimate=pl.CostEstimate(flops=0, transcendentals=0, bytes_accessed=4 * size),
+        name="stage_weights",
+    )(*held, after)
+    return out[:-1], out[-1]
+
+
+def column_tiles(width, tile):
+    tile = tile if width % tile == 0 else width
+    return [slice(start, start + tile) for start in range(0, width, tile)]
+
+
+def expand_body(
+    near_ref, far_ref, mix_ref, gain_ref, norm_ref, gate_ref, up_ref, token_ref, out_ref,
+    scaled_ref, *, layer
+):
+    del token_ref
+    feat, width = gate_ref.shape
     padded = pad_lanes(width)
-
-    @pl.when(step == 0)
-    def _():
-        total_ref[...] = jnp.zeros_like(total_ref)
-        square_ref[...] = jnp.zeros_like(square_ref)
-
-    nodes = jnp.concatenate([near_ref[...], far_ref[...]], axis=0)
-    message = 0.0
-    for kind in range(ETYPES):
-        message += gain_ref[kind : kind + 1, :] * jnp.dot(
-            mix_ref[kind], nodes, preferred_element_type=jnp.float32
-        )
-    pre = nodes.astype(jnp.float32) + message * inv_ref[...]
-    square_ref[...] += jnp.sum(pre * pre, axis=1, keepdims=True)
-    scaled = (pre * norm_ref[...]).astype(jnp.bfloat16)
-    total_ref[:, :width] += jnp.dot(scaled, gate_ref[...], preferred_element_type=jnp.float32)
-    total_ref[:, padded : padded + width] += jnp.dot(
-        scaled, up_ref[...], preferred_element_type=jnp.float32
-    )
-
-    @pl.when(step == steps - 1)
-    def _():
-        out_ref[:, : 2 * padded] = total_ref[...].astype(jnp.bfloat16)
-        squares = square_ref[...]
-        high = squares.astype(jnp.bfloat16).astype(jnp.float32)
-        lane = lax.broadcasted_iota(jnp.int32, (squares.shape[0], 128), 1)
-        parts = jnp.where(lane == 0, high, jnp.where(lane == 1, squares - high, 0.0))
-        out_ref[:, 2 * padded :] = parts.astype(jnp.bfloat16)
-
-def expand(near, far, mix, inv, gain, norm, gate, up, layer, tile):
+    edges = sum(mix_ref[kind].astype(jnp.float32) for kind in range(ETYPES))
+    inverse = 1.0 / jnp.maximum(jnp.sum(edges, axis=1, keepdims=True), 1.0)
+    squares = 0.0
+    for span in column_tiles(feat, 512):
+        nodes = jnp.concatenate([near_ref[:, span], far_ref[:, span]], axis=0)
+        message = 0.0
+        for kind in range(ETYPES):
+            message += gain_ref[layer, kind : kind + 1, span] * jnp.dot(
+                mix_ref[kind], nodes, preferred_element_type=jnp.float32
+            )
+        pre = nodes.astype(jnp.float32) + message * inverse
+        squares += jnp.sum(pre * pre, axis=1, keepdims=True)
+        scaled_ref[:, span] = (pre * norm_ref[layer : layer + 1, span]).astype(jnp.bfloat16)
+    if padded != width:
+        out_ref[...] = jnp.zeros_like(out_ref)
+    for place, ref in enumerate((gate_ref, up_ref)):
+        for span in column_tiles(width, 256):
+            sums = jnp.dot(scaled_ref[...], ref[:, span], preferred_element_type=jnp.float32)
+            start = place * padded + span.start
+            out_ref[:, start : start + sums.shape[1]] = sums.astype(jnp.bfloat16)
+    high = squares.astype(jnp.bfloat16).astype(jnp.float32)
+    lane = lax.broadcasted_iota(jnp.int32, (squares.shape[0], 128), 1)
+    parts = jnp.where(lane == 0, high, jnp.where(lane == 1, squares - high, 0.0))
+    out_ref[:, 2 * padded :] = parts.astype(jnp.bfloat16)
+
+
+def expand(near, far, mix, gain, norm, gate, up, token, layer):
     half, feat = near.shape
     rows = 2 * half
-    width = gate.shape[2]
-    padded = pad_lanes(width)
+    columns = 2 * pad_lanes(gate.shape[1]) + 128
+    held = [pltpu.with_memory_space_constraint(a, pltpu.VMEM) for a in (gate, up)]
     return pl.pallas_call(
-        expand_body,
-        grid=(feat // tile,),
-        in_specs=[
-            pl.BlockSpec((half, tile), lambda k: (0, k)),
-            pl.BlockSpec((half, tile), lambda k: (0, k)),
-            pl.BlockSpec((ETYPES, rows, rows), lambda k: (0, 0, 0)),
-            pl.BlockSpec((rows, 1), lambda k: (0, 0)),
-            pl.BlockSpec((None, ETYPES, tile), lambda k: (layer, 0, k)),
-            pl.BlockSpec((None, 1, tile), lambda k: (layer, 0, k)),
-            pl.BlockSpec((None, tile, width), lambda k: (layer, k, 0)),
-            pl.BlockSpec((None, tile, width), lambda k: (layer, k, 0)),
-        ],
-        out_specs=pl.BlockSpec((rows, 2 * padded + 128), lambda k: (0, 0)),
-        out_shape=jax.ShapeDtypeStruct((rows, 2 * padded + 128), jnp.bfloat16),
-        scratch_shapes=[
-            pltpu.VMEM((rows, 2 * padded), jnp.float32),
-            pltpu.VMEM((rows, 1), jnp.float32),
-        ],
+        functools.partial(expand_body, layer=layer),
+        in_specs=[pl.BlockSpec(memory_space=pltpu.VMEM)] * 8,
+        out_specs=pl.BlockSpec(memory_space=pltpu.VMEM),
+        out_shape=jax.ShapeDtypeStruct((rows, columns), jnp.bfloat16),
+        scratch_shapes=[pltpu.VMEM((rows, feat), jnp.bfloat16)],
         compiler_params=pltpu.CompilerParams(vmem_limit_bytes=VMEM_LIMIT),
         name="expand",
-    )(near, far, mix, inv, gain, norm, gate, up)
-
-def contract_body(near_ref, far_ref, down_ref, keep_ref, give_ref, hidden_ref, total_ref, *, swap):
-    step = pl.program_id(0)
-    steps = pl.num_programs(0)
-    rows, width = hidden_ref.shape
+    )(near, far, mix, gain, norm, *held, token)
+
+
+def contract_body(near_ref, far_ref, down_ref, keep_ref, give_ref, *, swap):
+    rows = near_ref.shape[0]
+    width, feat = down_ref.shape
     padded = pad_lanes(width)
-    tile = down_ref.shape[0]
-
-    @pl.when(step == 0)
-    def _():
-        far = far_ref[...].astype(jnp.float32)
+
+    def both(span):
+        far = far_ref[:, span].astype(jnp.float32)
         if swap:
             part = rows // 4
             far = jnp.concatenate(
                 [far[:part], far[2 * part : 3 * part], far[part : 2 * part], far[3 * part :]], axis=0
             )
-        both = near_ref[...].astype(jnp.float32) + far
-        squares = jnp.sum(both[:, 2 * padded :], axis=1, keepdims=True)
-        scale = lax.rsqrt(squares * (1.0 / D) + 1e-05)
-        gate = both[:, :width] * scale
-        up = both[:, padded : padded + width] * scale
-        hidden_ref[...] = (gate * (1.0 / (1.0 + jnp.exp(-gate))) * up).astype(jnp.bfloat16)
-        total_ref[...] = jnp.zeros_like(total_ref)
-
-    if tile == width:
-        hidden = hidden_ref[...]
-    else:
-        hidden = hidden_ref[:, pl.ds(pl.multiple_of(step * tile, 128), tile)]
-    total_ref[...] += jnp.dot(hidden, down_ref[...], preferred_element_type=jnp.float32)
-
-    @pl.when(step == steps - 1)
-    def _():
-        keep_ref[...] = total_ref[: rows // 2, :]
-        give_ref[...] = total_ref[rows // 2 :, :].astype(jnp.bfloat16)
-
-
-def contract(near, far, down, layer, swap, tile):
-    rows = near.shape[0]
-    width, feat = down.shape[1:]
-    half = rows // 2
+        return near_ref[:, span].astype(jnp.float32) + far
+
+    squares = jnp.sum(both(slice(2 * padded, 2 * padded + 128)), axis=1, keepdims=True)
+    scale = lax.rsqrt(squares * (1.0 / D) + 1e-05)
+    hidden = []
+    for span in column_tiles(width, 256):
+        gate = both(span) * scale
+        up = both(slice(padded + span.start, padded + span.stop)) * scale
+        hidden.append((gate * (1.0 / (1.0 + jnp.exp(-gate))) * up).astype(jnp.bfloat16))
+    hidden = hidden[0] if len(hidden) == 1 else jnp.concatenate(hidden, axis=1)
+    for span in column_tiles(feat, 512):
+        total = jnp.dot(hidden, down_ref[:, span], preferred_element_type=jnp.float32)
+        keep_ref[:, span] = total[: rows // 2]
+        give_ref[:, span] = total[rows // 2 :].astype(jnp.bfloat16)
+
+
+def contract(near, far, down, swap):
+    half, feat = near.shape[0] // 2, down.shape[1]
+    held = pltpu.with_memory_space_constraint(down, pltpu.VMEM)
     return pl.pallas_call(
         functools.partial(contract_body, swap=swap),
-        grid=(width // tile,),
-        in_specs=[
-            pl.BlockSpec(near.shape, lambda k: (0, 0)),
-            pl.BlockSpec(far.shape, lambda k: (0, 0)),
-            pl.BlockSpec((None, tile, feat), lambda k: (layer, k, 0)),
-        ],
-        out_specs=[
-            pl.BlockSpec((half, feat), lambda k: (0, 0)),
-            pl.BlockSpec((half, feat), lambda k: (0, 0)),
-        ],
+        in_specs=[pl.BlockSpec(memory_space=pltpu.VMEM)] * 3,
+        out_specs=[pl.BlockSpec(memory_space=pltpu.VMEM)] * 2,
         out_shape=[
             jax.ShapeDtypeStruct((half, feat), jnp.float32),
             jax.ShapeDtypeStruct((half, feat), jnp.bfloat16),
         ],
-        scratch_shapes=[
-            pltpu.VMEM((rows, width), jnp.bfloat16),
-            pltpu.VMEM((rows, feat), jnp.float32),
-        ],
         compiler_params=pltpu.CompilerParams(vmem_limit_bytes=VMEM_LIMIT),
         name="contract",
-    )(near, far, down)
+    )(near, far, held)
 
 
 def per_device(
@@ -380,14 +376,6 @@
     kv = lax.all_to_all(kv, "gx", 0, 0, axis_index_groups=groups, tiled=True)
     kv = kv.reshape(HALF_VENUES, STEPS // pairs_dev, 4, pairs_dev, feat_width)
     kv = kv.transpose(0, 2, 1, 3, 4).reshape(HALF_VENUES, 4, STEPS, feat_width)
-    probs, lse = half_scores(queries, far_queries, kv)
-    far_lse = swap_stage(lse, orders, last)
-    pooled = half_pool(probs, lse, far_lse, kv)
-    far_pooled = swap_stage(pooled, orders, last)
-    far_pooled = jnp.concatenate([far_pooled[NODE_STEPS:], far_pooled[:NODE_STEPS]], axis=0)
-    pooled = (pooled.astype(jnp.float32) + far_pooled.astype(jnp.float32)).astype(jnp.bfloat16)
-    own_rows = pooled[:NODE_STEPS]
-
     row_total = inst_total * NODE_STEPS
     row = jnp.arange(row_total)
     place = row // NODE_STEPS
@@ -404,27 +392,40 @@
         "ter,ec->trc", typed.astype(jnp.bfloat16), at_source, preferred_element_type=jnp.float32
     )
     mix = jnp.where(same_step[None], mix, 0.0).astype(jnp.bfloat16)
-    degree = jnp.maximum(jnp.sum(at_target.astype(jnp.float32), axis=0), 1.0)
-    inverse = (1.0 / degree)[:, None]
-    norm_rows = norm_gain[:, None, :]
-    down_tile = 640 if down_proj.shape[1] % 640 == 0 else down_proj.shape[1]
-    expand_tile = 512 if feat_width % 512 == 0 else 128
+    kv, mix, type_gain = lax.optimization_barrier((kv, mix, type_gain))
+    probs, lse = half_scores(queries, far_queries, kv)
+    far_lse = swap_stage(lse, orders, last)
+    (gate, up), token = stage_weights([gate_proj, up_proj], 0, lse)
+    pooled = half_pool(probs, lse, far_lse, kv, token)
+    far_pooled = swap_stage(pooled, orders, last)
+    (down,), token = stage_weights([down_proj], 0, pooled)
+    far_pooled, token = lax.optimization_barrier((far_pooled, token))
+    far_pooled = jnp.concatenate([far_pooled[NODE_STEPS:], far_pooled[:NODE_STEPS]], axis=0)
+    pooled = (pooled.astype(jnp.float32) + far_pooled.astype(jnp.float32)).astype(jnp.bfloat16)
+    own_rows = pooled[:NODE_STEPS]
+    near, far = gather_rows(pooled, orders, last)
     for layer_idx in range(ROUNDS):
-        if layer_idx == 0:
-            near, far = gather_rows(pooled, orders, last)
-        else:
-            near, far = gather_rows(own_rows, orders, last + 1)
-        near_sums = expand(
-            near, far, mix, inverse, type_gain, norm_rows, gate_proj, up_proj, layer_idx, expand_tile
-        )
+        near_sums = expand(near, far, mix, type_gain, norm_gain, gate, up, token, layer_idx)
         if ta_count == 2:
             far_sums = lax.ppermute(near_sums, "ta", [(0, 1), (1, 0)])
         else:
             far_sums = lax.psum(near_sums.astype(jnp.float32), "ta") - near_sums.astype(jnp.float32)
-        keep, give = contract(near_sums, far_sums, down_proj, layer_idx, ta_count == 2, down_tile)
-        own_rows = (own_rows.astype(jnp.float32) + scatter_rows(keep, give, orders)).astype(
-            jnp.bfloat16
-        )
+        held, give = contract(near_sums, far_sums, down, ta_count == 2)
+        for stage in range(last + 1):
+            if stage:
+                half = held.shape[0] // 2
+                held, give = held[:half], held[half:].astype(jnp.bfloat16)
+            taken = swap_stage(give, orders, stage)
+            if layer_idx + 1 < ROUNDS and stage < 2:
+                if stage == 0:
+                    (gate, up), token = stage_weights([gate_proj, up_proj], layer_idx + 1, give)
+                else:
+                    (down,), token = stage_weights([down_proj], layer_idx + 1, give)
+                taken, token = lax.optimization_barrier((taken, token))
+            held = held + taken.astype(jnp.float32)
+        own_rows = (own_rows.astype(jnp.float32) + held).astype(jnp.bfloat16)
+        if layer_idx + 1 < ROUNDS:
+            near, far = gather_rows(own_rows, orders, last + 1)
     return own_rows
 
 

time: 223 us -> 189 us (0.85)
  waiting for transfers between devices: 118 us -> 98.1 us
  Pallas kernels: 46 us -> 32.1 us
  starting transfers between devices: 42.6 us -> 49.5 us
  other arithmetic: 6.21 us -> 1.72 us
    ppermute x18, waiting for transfers between devices: 106 us -> 48.6 us  [swap_stage(): return lax.ppermute(block, ('gx', 'ta'), pairs)]
    all_to_all x1, waiting for transfers between devices: 2.36 us -> 40.8 us  [per_device(): kv = lax.all_to_all(kv, 'gx', 0, 0, axis_index_groups=groups, tiled=True)]
    pallas_call x6 -> x10, Pallas kernels: 36.6 us -> 26.2 us  [the longest x4 15.9 us: stage_weights(): pl.pallas_call(functools.partial(stage_body, layer=layer), in_specs=[pl.B...]
    ppermute x18, starting transfers between devices: 32.7 us -> 39.4 us  [swap_stage(): return lax.ppermute(block, ('gx', 'ta'), pairs)]
    pallas_call x1, Pallas kernels: 4.38 us -> 2 us  [half_pool(): pl.pallas_call(pool_body, grid=(width // COLS_STEP,), in_specs=[pl.BlockS...]
    unnamed x29 -> x20, local copies, waits for them, and re-layouts: 6.65 us -> 6.08 us
  transfers between devices with their start and end apart: 22 -> 22, of which waited for: 22 -> 19; matrix products, arithmetic and copies ran while one was open for 2% -> 0% of each run, Pallas kernels for 2% -> 9%
where the time goes in v5:
time: 189 us; the launch traced here: 188 us
  waiting for transfers between devices  98.1 us (52%)
  starting transfers between devices  49.5 us (26%)
  Pallas kernels  32.1 us (17%)
  local copies, waits for them, and re-layouts  6.19 us (3%)
    ppermute x18, waiting for transfers between devices, swap_stage(): return lax.ppermute(block, ('gx', 'ta'), pairs)  48.6 us
    all_to_all x1, waiting for transfers between devices, per_device(): kv = lax.all_to_all(kv, 'gx', 0, 0, axis_index_groups=groups, tiled=True)  40.8 us
    ppermute x18, starting transfers between devices, swap_stage(): return lax.ppermute(block, ('gx', 'ta'), pairs)  39.4 us
    pallas_call x4, Pallas kernels, stage_weights(): pl.pallas_call(functools.partial(stage_body, layer=layer), in_specs=[pl.B...  15.9 us
    all_to_all x1, starting transfers between devices, per_device(): lax.all_to_all(queries, 'gx', 0, 0, axis_index_groups=groups, tiled=True)  6.31 us
    unnamed x20, local copies, waits for them, and re-layouts  6.08 us
    pallas_call x2, Pallas kernels, expand(): pl.pallas_call(functools.partial(expand_body, layer=layer), in_specs=[pl....  5.14 us
    all_to_all x1, waiting for transfers between devices, per_device(): lax.all_to_all(queries, 'gx', 0, 0, axis_index_groups=groups, tiled=True)  4.48 us
  transfers between devices with their start and end apart: 22, of which 19 were waited for; matrix products, arithmetic and copies ran while one was open for 0% of the time, Pallas kernels for 9%

profile of v5, /device:TPU:0, one launch (start us, length us, event | category | flops | bytes accessed | tf_op | source)
XLA Modules:
  0.0 188.3 jit_solution(15041598138576881820)
XLA Ops:
  3.6 6.3 %all-to-all-start = ((bf16[8,16,2560]{2,1,0:T(8,128)(2,1)}), bf16[8,16,2560]{2,1,0:T(8,128)(2,1)S(1)}, u32[]{:S(2)}, u32[]{:S(2)}) async-start(bf16[8,16,2560]{2,1,0:T(8,128)(2,1)} %arrange.3), calls=%async_computation | async-start | bytes 1310720 | tf_op jit(solution)/shard_map/all_to_all | solution.py:363
  15.8 4.5 %all-to-all-done = bf16[8,16,2560]{2,1,0:T(8,128)(2,1)S(1)} async-done(((bf16[8,16,2560]{2,1,0:T(8,128)(2,1)}), bf16[8,16,2560]{2,1,0:T(8,128)(2,1)S(1)}, u32[]{:S(2)}, u32[]{:S(2)}) %all-to-all-start) | async-done | bytes 655392 | tf_op jit(solution)/shard_map/all_to_all | solution.py:363
  20.2 3.6 %all-to-all-start.1 = ((bf16[8,64,2560]{2,1,0:T(8,128)(2,1)}), bf16[8,64,2560]{2,1,0:T(8,128)(2,1)S(1)}, u32[]{:S(2)}, u32[]{:S(2)}) async-start(bf16[8,64,2560]{2,1,0:T(8,128)(2,1)} %copy-done.2), calls=%async_computation.1 | async-start | bytes 5242880 | tf_op jit(solution)/shard_map/all_to_all | solution.py:376
  24.0 2.7 %collective-permute-start = (bf16[128,2560]{1,0:T(8,128)(2,1)S(1)}, bf16[128,2560]{1,0:T(8,128)(2,1)}, u32[]{:S(2)}, u32[]{:S(2)}) collective-permute-start(bf16[128,2560]{1,0:T(8,128)(2,1)S(1)} %bitcast.16), channel_id=1, source_target_pairs={{0,16},{1,17},{2,18},{3,19},{4,20},{5,21},{6,22},{7,23},{8,24},{9,... | collective-permute-start | bytes 1966088 | tf_op jit(solution)/shard_map/ppermute | solution.py:44
  27.1 40.8 %all-to-all-done.1 = bf16[8,64,2560]{2,1,0:T(8,128)(2,1)S(1)} async-done(((bf16[8,64,2560]{2,1,0:T(8,128)(2,1)}), bf16[8,64,2560]{2,1,0:T(8,128)(2,1)S(1)}, u32[]{:S(2)}, u32[]{:S(2)}) %all-to-all-start.1) | async-done | bytes 2621472 | tf_op jit(solution)/shard_map/all_to_all | solution.py:376
  67.9 3.9 %half_scores.1 = (bf16[20,2,128,128]{3,2,1,0:T(8,128)(2,1)S(1)}, f32[128,128]{1,0:T(8,128)S(1)}) custom-call(bf16[128,2560]{1,0:T(8,128)(2,1)S(1)} %bitcast.17, bf16[128,2560]{1,0:T(8,128)(2,1)} %collective-permute-done.far_ref, bf16[8,4,16,2560]{3,2,1,0:T(8,128)(2,1)S(1)} %bitcast.14), custom_call_target="tpu_custom_call" | custom-call | tf_op jit(solution)/shard_map/half_scores/pallas_call | solution.py:129
  72.9 4.8 %stage_weights.4 = (bf16[2560,1280]{1,0:T(8,128)(2,1)S(1)}, bf16[2560,1280]{1,0:T(8,128)(2,1)S(1)}, f32[8,128]{1,0:T(8,128)S(1)}) custom-call(bf16[2,2560,1280]{2,1,0:T(8,128)(2,1)} %refs_0_.7, bf16[2,2560,1280]{2,1,0:T(8,128)(2,1)} %refs_1_.3, f32[128,128]{1,0:T(8,128)S(1)} %get-tuple-element.33.refs_2_.lse_ref), custom_call_target="tpu_custom_call" | custom-call | bytes 26214400 | tf_op jit(solution)/shard_map/stage_weights/pallas_call | solution.py:214
  81.6 2.9 %stage_weights.5 = (bf16[1280,2560]{1,0:T(8,128)(2,1)S(1)}, f32[8,128]{1,0:T(8,128)S(1)}) custom-call(bf16[2,1280,2560]{2,1,0:T(8,128)(2,1)} %refs_0_.6, bf16[16,2560]{1,0:T(8,128)(2,1)S(1)} %half_pool.1.refs_1_), custom_call_target="tpu_custom_call" | custom-call | bytes 13107200 | tf_op jit(solution)/shard_map/stage_weights/pallas_call | solution.py:214
  85.2 2.2 %collective-permute-start.3 = (bf16[16,2560]{1,0:T(8,128)(2,1)S(1)}, bf16[16,2560]{1,0:T(8,128)(2,1)S(1)}, u32[]{:S(2)}, u32[]{:S(2)}) collective-permute-start(bf16[16,2560]{1,0:T(8,128)(2,1)S(1)} %add_convert_fusion), channel_id=1, source_target_pairs={{0,8},{1,9},{2,10},{3,11},{4,12},{5,13},{6,14},{7,15},{8,0},{9,1},... | collective-permute-start | bytes 245768 | tf_op jit(solution)/shard_map/ppermute | solution.py:44
  87.4 2.4 %collective-permute-done.3 = bf16[16,2560]{1,0:T(8,128)(2,1)S(1)} collective-permute-done((bf16[16,2560]{1,0:T(8,128)(2,1)S(1)}, bf16[16,2560]{1,0:T(8,128)(2,1)S(1)}, u32[]{:S(2)}, u32[]{:S(2)}) %collective-permute-start.3) | collective-permute-done | bytes 81952 | tf_op jit(solution)/shard_map/ppermute | solution.py:44
  91.5 3.8 %collective-permute-done.4 = bf16[32,2560]{1,0:T(8,128)(2,1)S(1)} collective-permute-done((bf16[32,2560]{1,0:T(8,128)(2,1)S(1)}, bf16[32,2560]{1,0:T(8,128)(2,1)S(1)}, u32[]{:S(2)}, u32[]{:S(2)}) %collective-permute-start.4) | collective-permute-done | bytes 163872 | tf_op jit(solution)/shard_map/ppermute | solution.py:44
  95.2 5.9 %collective-permute-start.5 = (bf16[64,2560]{1,0:T(8,128)(2,1)S(1)}, bf16[64,2560]{1,0:T(8,128)(2,1)S(1)}, u32[]{:S(2)}, u32[]{:S(2)}) collective-permute-start(bf16[64,2560]{1,0:T(8,128)(2,1)S(1)} %pad_maximum_fusion.near_ref), channel_id=1, source_target_pairs={{0,2},{1,5},{2,0},{3,7},{4,6},{5,1},{6,4},{7,3},{8,10},{9,13},{10,... | collective-permute-start | bytes 983048 | tf_op jit(solution)/shard_map/ppermute | solution.py:44
  101.2 5.0 %collective-permute-done.5.far_ref = bf16[64,2560]{1,0:T(8,128)(2,1)S(1)} collective-permute-done((bf16[64,2560]{1,0:T(8,128)(2,1)S(1)}, bf16[64,2560]{1,0:T(8,128)(2,1)S(1)}, u32[]{:S(2)}, u32[]{:S(2)}) %collective-permute-start.5) | collective-permute-done | bytes 327712 | tf_op jit(solution)/shard_map/ppermute | solution.py:44
  106.2 2.6 %expand.2.near_ref = bf16[128,2688]{1,0:T(8,128)(2,1)S(1)} custom-call(bf16[64,2560]{1,0:T(8,128)(2,1)S(1)} %pad_maximum_fusion.near_ref, bf16[64,2560]{1,0:T(8,128)(2,1)S(1)} %collective-permute-done.5.far_ref, bf16[3,128,128]{2,1,0:T(8,128)(2,1)S(1)} %fusion.mix_ref, f32[2,3,2560]{2,1,0:T(4,128)S(1)} %copy.14.gain_ref, f32[2,2560]{1,0:T(2,128)S(1)} %copy-done.6, ...), custom_call_target="tpu_custom_call" | custom-call | tf_op jit(solution)/shard_map/expand/pallas_call | solution.py:270
  108.9 2.1 %collective-permute-done.6.far_ref = bf16[128,2688]{1,0:T(8,128)(2,1)S(1)} collective-permute-done((bf16[128,2688]{1,0:T(8,128)(2,1)S(1)}, bf16[128,2688]{1,0:T(8,128)(2,1)S(1)}, u32[]{:S(2)}, u32[]{:S(2)}) %collective-permute-start.6) | collective-permute-done | bytes 688160 | tf_op jit(solution)/shard_map/ppermute | solution.py:410
  114.4 5.1 %collective-permute-done.7 = bf16[64,2560]{1,0:T(8,128)(2,1)S(1)} collective-permute-done((bf16[64,2560]{1,0:T(8,128)(2,1)S(1)}, bf16[64,2560]{1,0:T(8,128)(2,1)S(1)}, u32[]{:S(2)}, u32[]{:S(2)}) %collective-permute-start.7) | collective-permute-done | bytes 327712 | tf_op jit(solution)/shard_map/ppermute | solution.py:44
  121.1 2.9 %stage_weights.6 = (bf16[1280,2560]{1,0:T(8,128)(2,1)S(1)}, f32[8,128]{1,0:T(8,128)S(1)}) custom-call(bf16[2,1280,2560]{2,1,0:T(8,128)(2,1)} %refs_0_.6, bf16[32,2560]{1,0:T(8,128)(2,1)S(1)} %slice.111.refs_1_), custom_call_target="tpu_custom_call" | custom-call | bytes 13107200 | tf_op jit(solution)/shard_map/stage_weights/pallas_call | solution.py:214
  126.6 2.8 %collective-permute-done.9 = bf16[16,2560]{1,0:T(8,128)(2,1)S(1)} collective-permute-done((bf16[16,2560]{1,0:T(8,128)(2,1)S(1)}, bf16[16,2560]{1,0:T(8,128)(2,1)S(1)}, u32[]{:S(2)}, u32[]{:S(2)}) %collective-permute-start.9) | collective-permute-done | bytes 81952 | tf_op jit(solution)/shard_map/ppermute | solution.py:44
  129.5 2.2 %collective-permute-start.10 = (bf16[8,2560]{1,0:T(8,128)(2,1)S(1)}, bf16[8,2560]{1,0:T(8,128)(2,1)S(1)}, u32[]{:S(2)}, u32[]{:S(2)}) collective-permute-start(bf16[8,2560]{1,0:T(8,128)(2,1)S(1)} %slice.115), channel_id=1, source_target_pairs={{0,16},{1,17},{2,18},{3,19},{4,20},{5,21},{6,22},{7,23},{8,24},{9,... | collective-permute-start | bytes 122888 | tf_op jit(solution)/shard_map/ppermute | solution.py:44
  131.7 2.9 %collective-permute-done.10 = bf16[8,2560]{1,0:T(8,128)(2,1)S(1)} collective-permute-done((bf16[8,2560]{1,0:T(8,128)(2,1)S(1)}, bf16[8,2560]{1,0:T(8,128)(2,1)S(1)}, u32[]{:S(2)}, u32[]{:S(2)}) %collective-permute-start.10) | collective-permute-done | bytes 40992 | tf_op jit(solution)/shard_map/ppermute | solution.py:44
  134.6 2.1 %collective-permute-start.11 = (bf16[8,2560]{1,0:T(8,128)(2,1)S(1)}, bf16[8,2560]{1,0:T(8,128)(2,1)S(1)}, u32[]{:S(2)}, u32[]{:S(2)}) collective-permute-start(bf16[8,2560]{1,0:T(8,128)(2,1)S(1)} %fusion.6), channel_id=1, source_target_pairs={{0,16},{1,17},{2,18},{3,19},{4,20},{5,21},{6,22},{7,23},{8,24},{9,... | collective-permute-start | bytes 122888 | tf_op jit(solution)/shard_map/ppermute | solution.py:44
  136.7 2.9 %collective-permute-done.11 = bf16[8,2560]{1,0:T(8,128)(2,1)S(1)} collective-permute-done((bf16[8,2560]{1,0:T(8,128)(2,1)S(1)}, bf16[8,2560]{1,0:T(8,128)(2,1)S(1)}, u32[]{:S(2)}, u32[]{:S(2)}) %collective-permute-start.11) | collective-permute-done | bytes 40992 | tf_op jit(solution)/shard_map/ppermute | solution.py:44
  141.5 2.5 %collective-permute-done.12 = bf16[16,2560]{1,0:T(8,128)(2,1)S(1)} collective-permute-done((bf16[16,2560]{1,0:T(8,128)(2,1)S(1)}, bf16[16,2560]{1,0:T(8,128)(2,1)S(1)}, u32[]{:S(2)}, u32[]{:S(2)}) %collective-permute-start.12) | collective-permute-done | bytes 81952 | tf_op jit(solution)/shard_map/ppermute | solution.py:44
  145.6 5.1 %collective-permute-done.13 = bf16[32,2560]{1,0:T(8,128)(2,1)S(1)} collective-permute-done((bf16[32,2560]{1,0:T(8,128)(2,1)S(1)}, bf16[32,2560]{1,0:T(8,128)(2,1)S(1)}, u32[]{:S(2)}, u32[]{:S(2)}) %collective-permute-start.13) | collective-permute-done | bytes 163872 | tf_op jit(solution)/shard_map/ppermute | solution.py:44
  152.5 5.3 %stage_weights.7 = (bf16[2560,1280]{1,0:T(8,128)(2,1)S(1)}, bf16[2560,1280]{1,0:T(8,128)(2,1)S(1)}, f32[8,128]{1,0:T(8,128)}) custom-call(bf16[2,2560,1280]{2,1,0:T(8,128)(2,1)} %refs_0_.7, bf16[2,2560,1280]{2,1,0:T(8,128)(2,1)} %refs_1_.3, bf16[64,2560]{1,0:T(8,128)(2,1)S(1)} %get-tuple-element.44.refs_2_), custom_call_target="tpu_custom_call" | custom-call | bytes 26214400 | tf_op jit(solution)/shard_map/stage_weights/pallas_call | solution.py:214
  157.9 2.6 %expand.3.near_ref = bf16[128,2688]{1,0:T(8,128)(2,1)S(1)} custom-call(bf16[64,2560]{1,0:T(8,128)(2,1)S(1)} %pad_maximum_fusion.1.near_ref, bf16[64,2560]{1,0:T(8,128)(2,1)S(1)} %collective-permute-done.14.far_ref, bf16[3,128,128]{2,1,0:T(8,128)(2,1)S(1)} %fusion.mix_ref, f32[2,3,2560]{2,1,0:T(4,128)S(1)} %copy.14.gain_ref, f32[2,2560]{1,0:T(2,128)S(1)} %copy-done.6, ...), custom_call_target="tpu_custom_call" | custom-call | tf_op jit(solution)/shard_map/expand/pallas_call | solution.py:270
  160.5 2.1 %collective-permute-done.15.far_ref = bf16[128,2688]{1,0:T(8,128)(2,1)S(1)} collective-permute-done((bf16[128,2688]{1,0:T(8,128)(2,1)S(1)}, bf16[128,2688]{1,0:T(8,128)(2,1)S(1)}, u32[]{:S(2)}, u32[]{:S(2)}) %collective-permute-start.15) | collective-permute-done | bytes 688160 | tf_op jit(solution)/shard_map/ppermute | solution.py:410
  165.6 5.4 %collective-permute-done.16 = bf16[64,2560]{1,0:T(8,128)(2,1)S(1)} collective-permute-done((bf16[64,2560]{1,0:T(8,128)(2,1)S(1)}, bf16[64,2560]{1,0:T(8,128)(2,1)S(1)}, u32[]{:S(2)}, u32[]{:S(2)}) %collective-permute-start.16) | collective-permute-done | bytes 327712 | tf_op jit(solution)/shard_map/ppermute | solution.py:44
  172.6 3.9 %collective-permute-done.17 = bf16[32,2560]{1,0:T(8,128)(2,1)S(1)} collective-permute-done((bf16[32,2560]{1,0:T(8,128)(2,1)S(1)}, bf16[32,2560]{1,0:T(8,128)(2,1)S(1)}, u32[]{:S(2)}, u32[]{:S(2)}) %collective-permute-start.17) | collective-permute-done | bytes 163872 | tf_op jit(solution)/shard_map/ppermute | solution.py:44
  178.1 2.9 %collective-permute-done.18 = bf16[16,2560]{1,0:T(8,128)(2,1)S(1)} collective-permute-done((bf16[16,2560]{1,0:T(8,128)(2,1)S(1)}, bf16[16,2560]{1,0:T(8,128)(2,1)S(1)}, u32[]{:S(2)}, u32[]{:S(2)}) %collective-permute-start.18) | collective-permute-done | bytes 81952 | tf_op jit(solution)/shard_map/ppermute | solution.py:44
  181.1 4.2 %collective-permute-start.19 = (bf16[8,2560]{1,0:T(8,128)(2,1)S(1)}, bf16[8,2560]{1,0:T(8,128)(2,1)S(1)}, u32[]{:S(2)}, u32[]{:S(2)}) collective-permute-start(bf16[8,2560]{1,0:T(8,128)(2,1)S(1)} %slice.114), channel_id=1, source_target_pairs={{0,16},{1,17},{2,18},{3,19},{4,20},{5,21},{6,22},{7,23},{8,24},{9,... | collective-permute-start | bytes 122888 | tf_op jit(solution)/shard_map/ppermute | solution.py:44
  185.2 2.4 %collective-permute-done.19 = bf16[8,2560]{1,0:T(8,128)(2,1)S(1)} collective-permute-done((bf16[8,2560]{1,0:T(8,128)(2,1)S(1)}, bf16[8,2560]{1,0:T(8,128)(2,1)S(1)}, u32[]{:S(2)}, u32[]{:S(2)}) %collective-permute-start.19) | collective-permute-done | bytes 40992 | tf_op jit(solution)/shard_map/ppermute | solution.py:44
  (88 shorter events, 37.3 us)
Async XLA Ops:
  0.0 0.7 copy-start
  0.9 1.3 copy-start.3
  3.6 20.3 %copy-start.8 = (s32[64,2]{0,1:T(2,128)S(1)}, s32[64,2]{0,1:T(2,128)}, u32[]{:S(2)}) copy-start(s32[64,2]{0,1:T(2,128)} %param.15) | copy-start | bytes 1540
  3.6 23.1 %copy-start.9 = (s32[64]{0:T(128)S(1)}, s32[64]{0:T(128)}, u32[]{:S(2)}) copy-start(s32[64]{0:T(128)} %param.16) | copy-start | bytes 772
  3.6 16.7 %all-to-all-start = ((bf16[8,16,2560]{2,1,0:T(8,128)(2,1)}), bf16[8,16,2560]{2,1,0:T(8,128)(2,1)S(1)}, u32[]{:S(2)}, u32[]{:S(2)}) async-start(bf16[8,16,2560]{2,1,0:T(8,128)(2,1)} %arrange.3), calls=%async_computation | async-start | bytes 1310720 | tf_op jit(solution)/shard_map/all_to_all | solution.py:363
  10.2 1.3 copy-start.4
  11.6 1.3 copy-start.5
  14.3 1.5 copy-start.2
  20.2 47.6 %all-to-all-start.1 = ((bf16[8,64,2560]{2,1,0:T(8,128)(2,1)}), bf16[8,64,2560]{2,1,0:T(8,128)(2,1)S(1)}, u32[]{:S(2)}, u32[]{:S(2)}) async-start(bf16[8,64,2560]{2,1,0:T(8,128)(2,1)} %copy-done.2), calls=%async_computation.1 | async-start | bytes 5242880 | tf_op jit(solution)/shard_map/all_to_all | solution.py:376
  24.0 43.9 %collective-permute-start = (bf16[128,2560]{1,0:T(8,128)(2,1)S(1)}, bf16[128,2560]{1,0:T(8,128)(2,1)}, u32[]{:S(2)}, u32[]{:S(2)}) collective-permute-start(bf16[128,2560]{1,0:T(8,128)(2,1)S(1)} %bitcast.16), channel_id=1, source_target_pairs={{0,16},{1,17},{2,18},{3,19},{4,20},{5,21},{6,22},{7,23},{8,24},{9,... | collective-permute-start | bytes 1966088 | tf_op jit(solution)/shard_map/ppermute | solution.py:44
  71.7 6.0 %collective-permute-start.1 = (f32[128,128]{1,0:T(8,128)S(1)}, f32[128,128]{1,0:T(8,128)S(1)}, u32[]{:S(2)}, u32[]{:S(2)}) collective-permute-start(f32[128,128]{1,0:T(8,128)S(1)} %get-tuple-element.33.refs_2_.lse_ref), channel_id=1, source_target_pairs={{0,16},{1,17},{2,18},{3,19},{4,20},{5,21},{6,22},{7,23},{8,24},{9,... | collective-permute-start | bytes 196616 | tf_op jit(solution)/shard_map/ppermute | solution.py:44
  79.7 21.4 %copy-start.7 = (f32[2,3,2560]{2,0,1:T(2,128)S(1)}, f32[2,3,2560]{2,0,1:T(2,128)}, u32[]{:S(2)}) copy-start(f32[2,3,2560]{2,0,1:T(2,128)} %param.17) | copy-start | bytes 184324
  79.7 26.5 %copy-start.6 = (f32[2,2560]{1,0:T(2,128)S(1)}, f32[2,2560]{1,0:T(2,128)}, u32[]{:S(2)}) copy-start(f32[2,2560]{1,0:T(2,128)} %norm_ref.3) | copy-start | bytes 61444
  79.7 5.4 %collective-permute-start.2 = (bf16[16,2560]{1,0:T(8,128)(2,1)S(1)}, bf16[16,2560]{1,0:T(8,128)(2,1)S(1)}, u32[]{:S(2)}, u32[]{:S(2)}) collective-permute-start(bf16[16,2560]{1,0:T(8,128)(2,1)S(1)} %half_pool.1.refs_1_), channel_id=1, source_target_pairs={{0,16},{1,17},{2,18},{3,19},{4,20},{5,21},{6,22},{7,23},{8,24},{9,... | collective-permute-start | bytes 245768 | tf_op jit(solution)/shard_map/ppermute | solution.py:44
  85.2 4.6 %collective-permute-start.3 = (bf16[16,2560]{1,0:T(8,128)(2,1)S(1)}, bf16[16,2560]{1,0:T(8,128)(2,1)S(1)}, u32[]{:S(2)}, u32[]{:S(2)}) collective-permute-start(bf16[16,2560]{1,0:T(8,128)(2,1)S(1)} %add_convert_fusion), channel_id=1, source_target_pairs={{0,8},{1,9},{2,10},{3,11},{4,12},{5,13},{6,14},{7,15},{8,0},{9,1},... | collective-permute-start | bytes 245768 | tf_op jit(solution)/shard_map/ppermute | solution.py:44
  89.8 5.4 %collective-permute-start.4 = (bf16[32,2560]{1,0:T(8,128)(2,1)S(1)}, bf16[32,2560]{1,0:T(8,128)(2,1)S(1)}, u32[]{:S(2)}, u32[]{:S(2)}) collective-permute-start(bf16[32,2560]{1,0:T(8,128)(2,1)S(1)} %pad_maximum_fusion.2), channel_id=1, source_target_pairs={{0,4},{1,3},{2,6},{3,1},{4,0},{5,7},{6,2},{7,5},{8,12},{9,11},{10,... | collective-permute-start | bytes 491528 | tf_op jit(solution)/shard_map/ppermute | solution.py:44
  95.2 11.0 %collective-permute-start.5 = (bf16[64,2560]{1,0:T(8,128)(2,1)S(1)}, bf16[64,2560]{1,0:T(8,128)(2,1)S(1)}, u32[]{:S(2)}, u32[]{:S(2)}) collective-permute-start(bf16[64,2560]{1,0:T(8,128)(2,1)S(1)} %pad_maximum_fusion.near_ref), channel_id=1, source_target_pairs={{0,2},{1,5},{2,0},{3,7},{4,6},{5,1},{6,4},{7,3},{8,10},{9,13},{10,... | collective-permute-start | bytes 983048 | tf_op jit(solution)/shard_map/ppermute | solution.py:44
  108.8 2.2 %collective-permute-start.6 = (bf16[128,2688]{1,0:T(8,128)(2,1)S(1)}, bf16[128,2688]{1,0:T(8,128)(2,1)S(1)}, u32[]{:S(2)}, u32[]{:S(2)}) collective-permute-start(bf16[128,2688]{1,0:T(8,128)(2,1)S(1)} %expand.2.near_ref), channel_id=1, source_target_pairs={{0,1},{1,0},{2,3},{3,2},{4,5},{5,4},{6,7},{7,6},{8,9},{9,8},{10,11... | collective-permute-start | bytes 2064392 | tf_op jit(solution)/shard_map/ppermute | solution.py:410
  112.3 7.1 %collective-permute-start.7 = (bf16[64,2560]{1,0:T(8,128)(2,1)S(1)}, bf16[64,2560]{1,0:T(8,128)(2,1)S(1)}, u32[]{:S(2)}, u32[]{:S(2)}) collective-permute-start(bf16[64,2560]{1,0:T(8,128)(2,1)S(1)} %get-tuple-element.44.refs_2_), channel_id=1, source_target_pairs={{0,2},{1,5},{2,0},{3,7},{4,6},{5,1},{6,4},{7,3},{8,10},{9,13},{10,... | collective-permute-start | bytes 983048 | tf_op jit(solution)/shard_map/ppermute | solution.py:44
  119.5 5.4 %collective-permute-start.8 = (bf16[32,2560]{1,0:T(8,128)(2,1)S(1)}, bf16[32,2560]{1,0:T(8,128)(2,1)S(1)}, u32[]{:S(2)}, u32[]{:S(2)}) collective-permute-start(bf16[32,2560]{1,0:T(8,128)(2,1)S(1)} %slice.111.refs_1_), channel_id=1, source_target_pairs={{0,4},{1,3},{2,6},{3,1},{4,0},{5,7},{6,2},{7,5},{8,12},{9,11},{10,... | collective-permute-start | bytes 491528 | tf_op jit(solution)/shard_map/ppermute | solution.py:44
  125.0 4.5 %collective-permute-start.9 = (bf16[16,2560]{1,0:T(8,128)(2,1)S(1)}, bf16[16,2560]{1,0:T(8,128)(2,1)S(1)}, u32[]{:S(2)}, u32[]{:S(2)}) collective-permute-start(bf16[16,2560]{1,0:T(8,128)(2,1)S(1)} %slice.113), channel_id=1, source_target_pairs={{0,8},{1,9},{2,10},{3,11},{4,12},{5,13},{6,14},{7,15},{8,0},{9,1},... | collective-permute-start | bytes 245768 | tf_op jit(solution)/shard_map/ppermute | solution.py:44
  129.5 5.1 %collective-permute-start.10 = (bf16[8,2560]{1,0:T(8,128)(2,1)S(1)}, bf16[8,2560]{1,0:T(8,128)(2,1)S(1)}, u32[]{:S(2)}, u32[]{:S(2)}) collective-permute-start(bf16[8,2560]{1,0:T(8,128)(2,1)S(1)} %slice.115), channel_id=1, source_target_pairs={{0,16},{1,17},{2,18},{3,19},{4,20},{5,21},{6,22},{7,23},{8,24},{9,... | collective-permute-start | bytes 122888 | tf_op jit(solution)/shard_map/ppermute | solution.py:44
  134.6 5.0 %collective-permute-start.11 = (bf16[8,2560]{1,0:T(8,128)(2,1)S(1)}, bf16[8,2560]{1,0:T(8,128)(2,1)S(1)}, u32[]{:S(2)}, u32[]{:S(2)}) collective-permute-start(bf16[8,2560]{1,0:T(8,128)(2,1)S(1)} %fusion.6), channel_id=1, source_target_pairs={{0,16},{1,17},{2,18},{3,19},{4,20},{5,21},{6,22},{7,23},{8,24},{9,... | collective-permute-start | bytes 122888 | tf_op jit(solution)/shard_map/ppermute | solution.py:44
  139.6 4.4 %collective-permute-start.12 = (bf16[16,2560]{1,0:T(8,128)(2,1)S(1)}, bf16[16,2560]{1,0:T(8,128)(2,1)S(1)}, u32[]{:S(2)}, u32[]{:S(2)}) collective-permute-start(bf16[16,2560]{1,0:T(8,128)(2,1)S(1)} %pad_maximum_fusion.4), channel_id=1, source_target_pairs={{0,8},{1,9},{2,10},{3,11},{4,12},{5,13},{6,14},{7,15},{8,0},{9,1},... | collective-permute-start | bytes 245768 | tf_op jit(solution)/shard_map/ppermute | solution.py:44
  144.0 6.6 %collective-permute-start.13 = (bf16[32,2560]{1,0:T(8,128)(2,1)S(1)}, bf16[32,2560]{1,0:T(8,128)(2,1)S(1)}, u32[]{:S(2)}, u32[]{:S(2)}) collective-permute-start(bf16[32,2560]{1,0:T(8,128)(2,1)S(1)} %pad_maximum_fusion.3), channel_id=1, source_target_pairs={{0,4},{1,3},{2,6},{3,1},{4,0},{5,7},{6,2},{7,5},{8,12},{9,11},{10,... | collective-permute-start | bytes 491528 | tf_op jit(solution)/shard_map/ppermute | solution.py:44
  150.7 7.2 %collective-permute-start.14 = (bf16[64,2560]{1,0:T(8,128)(2,1)S(1)}, bf16[64,2560]{1,0:T(8,128)(2,1)S(1)}, u32[]{:S(2)}, u32[]{:S(2)}) collective-permute-start(bf16[64,2560]{1,0:T(8,128)(2,1)S(1)} %pad_maximum_fusion.1.near_ref), channel_id=1, source_target_pairs={{0,2},{1,5},{2,0},{3,7},{4,6},{5,1},{6,4},{7,3},{8,10},{9,13},{10,... | collective-permute-start | bytes 983048 | tf_op jit(solution)/shard_map/ppermute | solution.py:44
  157.9 30.4 %copy-start.1 = (s32[16,16]{1,0:T(8,128)S(1)}, s32[16,16]{1,0:T(8,128)}, u32[]{:S(2)}) copy-start(s32[16,16]{1,0:T(8,128)} %param.14) | copy-start | bytes 3076
  160.4 2.2 %collective-permute-start.15 = (bf16[128,2688]{1,0:T(8,128)(2,1)S(1)}, bf16[128,2688]{1,0:T(8,128)(2,1)S(1)}, u32[]{:S(2)}, u32[]{:S(2)}) collective-permute-start(bf16[128,2688]{1,0:T(8,128)(2,1)S(1)} %expand.3.near_ref), channel_id=1, source_target_pairs={{0,1},{1,0},{2,3},{3,2},{4,5},{5,4},{6,7},{7,6},{8,9},{9,8},{10,11... | collective-permute-start | bytes 2064392 | tf_op jit(solution)/shard_map/ppermute | solution.py:410
  163.9 7.1 %collective-permute-start.16 = (bf16[64,2560]{1,0:T(8,128)(2,1)S(1)}, bf16[64,2560]{1,0:T(8,128)(2,1)S(1)}, u32[]{:S(2)}, u32[]{:S(2)}) collective-permute-start(bf16[64,2560]{1,0:T(8,128)(2,1)S(1)} %get-tuple-element.52), channel_id=1, source_target_pairs={{0,2},{1,5},{2,0},{3,7},{4,6},{5,1},{6,4},{7,3},{8,10},{9,13},{10,... | collective-permute-start | bytes 983048 | tf_op jit(solution)/shard_map/ppermute | solution.py:44
  171.1 5.4 %collective-permute-start.17 = (bf16[32,2560]{1,0:T(8,128)(2,1)S(1)}, bf16[32,2560]{1,0:T(8,128)(2,1)S(1)}, u32[]{:S(2)}, u32[]{:S(2)}) collective-permute-start(bf16[32,2560]{1,0:T(8,128)(2,1)S(1)} %slice.110), channel_id=1, source_target_pairs={{0,4},{1,3},{2,6},{3,1},{4,0},{5,7},{6,2},{7,5},{8,12},{9,11},{10,... | collective-permute-start | bytes 491528 | tf_op jit(solution)/shard_map/ppermute | solution.py:44
  176.5 4.5 %collective-permute-start.18 = (bf16[16,2560]{1,0:T(8,128)(2,1)S(1)}, bf16[16,2560]{1,0:T(8,128)(2,1)S(1)}, u32[]{:S(2)}, u32[]{:S(2)}) collective-permute-start(bf16[16,2560]{1,0:T(8,128)(2,1)S(1)} %slice.112), channel_id=1, source_target_pairs={{0,8},{1,9},{2,10},{3,11},{4,12},{5,13},{6,14},{7,15},{8,0},{9,1},... | collective-permute-start | bytes 245768 | tf_op jit(solution)/shard_map/ppermute | solution.py:44
  181.1 6.5 %collective-permute-start.19 = (bf16[8,2560]{1,0:T(8,128)(2,1)S(1)}, bf16[8,2560]{1,0:T(8,128)(2,1)S(1)}, u32[]{:S(2)}, u32[]{:S(2)}) collective-permute-start(bf16[8,2560]{1,0:T(8,128)(2,1)S(1)} %slice.114), channel_id=1, source_target_pairs={{0,16},{1,17},{2,18},{3,19},{4,20},{5,21},{6,22},{7,23},{8,24},{9,... | collective-permute-start | bytes 122888 | tf_op jit(solution)/shard_map/ppermute | solution.py:44

commit v6 on v5

--- a/solution.py
+++ b/solution.py
@@ -34,20 +34,33 @@
     return [plain, [plain[1], plain[0]] + plain[2:]]
 
 
-def swap_stage(block, orders, stage):
+def swap_stage(block, orders, *stages):
     gx_count, ta_count = lax.axis_size("gx"), lax.axis_size("ta")
+    flips = [sum(1 << order[stage] for stage in stages) for order in orders]
     pairs = [
-        (g * ta_count + t, (g ^ (1 << orders[t][stage])) * ta_count + t)
+        (g * ta_count + t, (g ^ flips[t]) * ta_count + t)
         for g in range(gx_count)
         for t in range(ta_count)
     ]
     return lax.ppermute(block, ("gx", "ta"), pairs)
 
 
-def gather_rows(held, orders, stages):
-    for stage in reversed(range(1, stages)):
+def gather_rows(held, orders, last):
+    for stage in reversed(range(2, last)):
         held = jnp.concatenate([held, swap_stage(held, orders, stage)], axis=0)
-    return held, swap_stage(held, orders, 0)
+    return [
+        held,
+        swap_stage(held, orders, 1),
+        swap_stage(held, orders, 0),
+        swap_stage(held, orders, 0, 1),
+    ]
+
+
+def join_pair(mine, orders, last):
+    taken = swap_stage(mine, orders, last)
+    half = mine.shape[0] // 2
+    taken = jnp.concatenate([taken[half:], taken[:half]], axis=0)
+    return mine.astype(jnp.float32) + taken.astype(jnp.float32)
 
 
 def arrange_body(pick_ref, *refs):
@@ -79,7 +92,7 @@
     )(pick, *sources)
 
 
-def score_body(own_ref, far_ref, kv_ref, probs_ref, lse_ref):
+def score_body(own_ref, far_ref, key_ref, probs_ref, lse_ref):
     step = pl.program_id(0)
 
     @pl.when(step == 0)
@@ -103,7 +116,7 @@
             ],
             axis=0,
         ).astype(jnp.bfloat16)
-        keys = kv_ref[:, item].reshape(KEYS_HALF, COLS_STEP)
+        keys = key_ref[:, item].reshape(KEYS_HALF, COLS_STEP)
         for head in range(HEADS_STEP):
             span = slice(head * HEAD_DIM, (head + 1) * HEAD_DIM)
             scores = lax.dot_general(
@@ -147,8 +160,7 @@
     )(own, far, kv)
 
 
-def pool_body(probs_ref, lse_ref, far_ref, kv_ref, token_ref, out_ref):
-    del token_ref
+def pool_body(probs_ref, lse_ref, far_ref, value_ref, out_ref):
     step = pl.program_id(0)
     far = jnp.concatenate([far_ref[ROWS_HALF:, :], far_ref[:ROWS_HALF, :]], axis=0)
     far = jnp.concatenate([far[:, LSE_ITEM:], far[:, :LSE_ITEM]], axis=1)
@@ -162,7 +174,7 @@
             factor = jnp.sum(jnp.where(lane == column, share, 0.0), axis=1, keepdims=True)
             weights = probs_ref[head, item].astype(jnp.float32) * factor
             weights = jnp.sum(weights.reshape(VENUES, NODE_STEPS, KEYS_HALF), axis=0)
-            values = kv_ref[:, item, :, span].reshape(KEYS_HALF, HEAD_DIM)
+            values = value_ref[:, item, :, span].reshape(KEYS_HALF, HEAD_DIM)
             pooled.append(
                 jnp.dot(
                     weights.astype(jnp.bfloat16), values, preferred_element_type=jnp.float32
@@ -171,7 +183,7 @@
         out_ref[:, span] = jnp.concatenate(pooled, axis=0).astype(jnp.bfloat16)
 
 
-def half_pool(probs, lse, far_lse, kv, token):
+def half_pool(probs, lse, far_lse, kv):
     width = kv.shape[3]
     return pl.pallas_call(
         pool_body,
@@ -181,25 +193,24 @@
             pl.BlockSpec((2 * ROWS_HALF, 128), lambda j: (0, 0)),
             pl.BlockSpec((2 * ROWS_HALF, 128), lambda j: (0, 0)),
             pl.BlockSpec((HALF_VENUES, 2, STEPS, COLS_STEP), lambda j: (0, 1, 0, j)),
-            pl.BlockSpec(memory_space=pl.ANY),
         ],
         out_specs=pl.BlockSpec((2 * NODE_STEPS, COLS_STEP), lambda j: (0, j)),
         out_shape=jax.ShapeDtypeStruct((2 * NODE_STEPS, width), jnp.bfloat16),
         compiler_params=pltpu.CompilerParams(vmem_limit_bytes=VMEM_LIMIT),
         name="half_pool",
-    )(probs, lse, far_lse, kv, token)
+    )(probs, lse, far_lse, kv)
 
 
 def pad_lanes(width):
     return -(-width // 128) * 128
 
 
-def stage_body(*refs, layer):
-    count = (len(refs) - 3) // 2
+def stage_body(*refs, layer, count):
+    first = len(refs) - count - 2
     token_ref, sems = refs[-2:]
     copies = []
     for place in range(count):
-        copy = pltpu.make_async_copy(refs[place].at[layer], refs[count + 1 + place], sems.at[place])
+        copy = pltpu.make_async_copy(refs[place].at[layer], refs[first + place], sems.at[place])
         copy.start()
         copies.append(copy)
     token_ref[...] = jnp.zeros_like(token_ref)
@@ -212,15 +223,15 @@
     shapes = [pltpu.VMEM(a.shape[1:], a.dtype) for a in weights]
     size = sum(a.size for a in weights) // ROUNDS
     out = pl.pallas_call(
-        functools.partial(stage_body, layer=layer),
-        in_specs=[pl.BlockSpec(memory_space=pl.ANY)] * (len(held) + 1),
+        functools.partial(stage_body, layer=layer, count=len(held)),
+        in_specs=[pl.BlockSpec(memory_space=pl.ANY)] * (len(held) + len(after)),
         out_specs=[pl.BlockSpec(memory_space=pltpu.VMEM)] * (len(shapes) + 1),
         out_shape=shapes + [jax.ShapeDtypeStruct((8, 128), jnp.float32)],
         scratch_shapes=[pltpu.SemaphoreType.DMA((len(held),))],
         compiler_params=pltpu.CompilerParams(vmem_limit_bytes=2 << 20),
         cost_estimate=pl.CostEstimate(flops=0, transcendentals=0, bytes_accessed=4 * size),
         name="stage_weights",
-    )(*held, after)
+    )(*held, *after)
     return out[:-1], out[-1]
 
 
@@ -229,18 +240,16 @@
     return [slice(start, start + tile) for start in range(0, width, tile)]
 
 
-def expand_body(
-    near_ref, far_ref, mix_ref, gain_ref, norm_ref, gate_ref, up_ref, token_ref, out_ref,
-    scaled_ref, *, layer
-):
-    del token_ref
+def expand_body(*refs, layer):
+    node_refs, refs = refs[:4], refs[4:]
+    mix_ref, gain_ref, norm_ref, gate_ref, up_ref, _, out_ref, scaled_ref = refs
     feat, width = gate_ref.shape
     padded = pad_lanes(width)
     edges = sum(mix_ref[kind].astype(jnp.float32) for kind in range(ETYPES))
     inverse = 1.0 / jnp.maximum(jnp.sum(edges, axis=1, keepdims=True), 1.0)
     squares = 0.0
     for span in column_tiles(feat, 512):
-        nodes = jnp.concatenate([near_ref[:, span], far_ref[:, span]], axis=0)
+        nodes = jnp.concatenate([ref[:, span] for ref in node_refs], axis=0)
         message = 0.0
         for kind in range(ETYPES):
             message += gain_ref[layer, kind : kind + 1, span] * jnp.dot(
@@ -262,20 +271,21 @@
     out_ref[:, 2 * padded :] = parts.astype(jnp.bfloat16)
 
 
-def expand(near, far, mix, gain, norm, gate, up, token, layer):
-    half, feat = near.shape
-    rows = 2 * half
+def expand(nodes, mix, gain, norm, gate, up, token, layer):
+    part, feat = nodes[0].shape
+    rows = len(nodes) * part
     columns = 2 * pad_lanes(gate.shape[1]) + 128
     held = [pltpu.with_memory_space_constraint(a, pltpu.VMEM) for a in (gate, up)]
+    operands = [*nodes, mix, gain, norm, *held, token]
     return pl.pallas_call(
         functools.partial(expand_body, layer=layer),
-        in_specs=[pl.BlockSpec(memory_space=pltpu.VMEM)] * 8,
+        in_specs=[pl.BlockSpec(memory_space=pltpu.VMEM)] * len(operands),
         out_specs=pl.BlockSpec(memory_space=pltpu.VMEM),
         out_shape=jax.ShapeDtypeStruct((rows, columns), jnp.bfloat16),
         scratch_shapes=[pltpu.VMEM((rows, feat), jnp.bfloat16)],
         compiler_params=pltpu.CompilerParams(vmem_limit_bytes=VMEM_LIMIT),
         name="expand",
-    )(near, far, mix, gain, norm, *held, token)
+    )(*operands)
 
 
 def contract_body(near_ref, far_ref, down_ref, keep_ref, give_ref, *, swap):
@@ -372,7 +382,7 @@
         queries = queries.reshape(HALF_VENUES, STEPS // pairs_dev, 2, pairs_dev, feat_width)
         queries = queries[:, (STEPS - NODE_STEPS) // pairs_dev :].transpose(0, 2, 1, 3, 4)
         queries = queries.reshape(2 * ROWS_HALF, feat_width)
-    far_queries = swap_stage(queries, orders, last)
+    far = swap_stage(queries, orders, last)
     kv = lax.all_to_all(kv, "gx", 0, 0, axis_index_groups=groups, tiled=True)
     kv = kv.reshape(HALF_VENUES, STEPS // pairs_dev, 4, pairs_dev, feat_width)
     kv = kv.transpose(0, 2, 1, 3, 4).reshape(HALF_VENUES, 4, STEPS, feat_width)
@@ -393,40 +403,40 @@
     )
     mix = jnp.where(same_step[None], mix, 0.0).astype(jnp.bfloat16)
     kv, mix, type_gain = lax.optimization_barrier((kv, mix, type_gain))
-    probs, lse = half_scores(queries, far_queries, kv)
+    probs, lse = half_scores(queries, far, kv)
     far_lse = swap_stage(lse, orders, last)
-    (gate, up), token = stage_weights([gate_proj, up_proj], 0, lse)
-    pooled = half_pool(probs, lse, far_lse, kv, token)
-    far_pooled = swap_stage(pooled, orders, last)
-    (down,), token = stage_weights([down_proj], 0, pooled)
-    far_pooled, token = lax.optimization_barrier((far_pooled, token))
-    far_pooled = jnp.concatenate([far_pooled[NODE_STEPS:], far_pooled[:NODE_STEPS]], axis=0)
-    pooled = (pooled.astype(jnp.float32) + far_pooled.astype(jnp.float32)).astype(jnp.bfloat16)
-    own_rows = pooled[:NODE_STEPS]
-    near, far = gather_rows(pooled, orders, last)
+    (gate,), token = stage_weights([gate_proj], 0, [lse])
+    far_lse, token = lax.optimization_barrier((far_lse, token))
+    pooled = half_pool(probs, lse, far_lse, kv)
+    (up,), token = stage_weights([up_proj], 0, [pooled, token])
+    pooled = join_pair(pooled, orders, last).astype(jnp.bfloat16)
+    pooled, token = lax.optimization_barrier((pooled, token))
+    (down,), token = stage_weights([down_proj], 0, [token])
     for layer_idx in range(ROUNDS):
-        near_sums = expand(near, far, mix, type_gain, norm_gain, gate, up, token, layer_idx)
+        nodes = gather_rows(pooled, orders, last)
+        near_sums = expand(nodes, mix, type_gain, norm_gain, gate, up, token, layer_idx)
         if ta_count == 2:
             far_sums = lax.ppermute(near_sums, "ta", [(0, 1), (1, 0)])
         else:
             far_sums = lax.psum(near_sums.astype(jnp.float32), "ta") - near_sums.astype(jnp.float32)
         held, give = contract(near_sums, far_sums, down, ta_count == 2)
-        for stage in range(last + 1):
+        final = layer_idx + 1 == ROUNDS
+        for stage in range(last + 1 if final else last):
             if stage:
                 half = held.shape[0] // 2
                 held, give = held[:half], held[half:].astype(jnp.bfloat16)
             taken = swap_stage(give, orders, stage)
-            if layer_idx + 1 < ROUNDS and stage < 2:
-                if stage == 0:
-                    (gate, up), token = stage_weights([gate_proj, up_proj], layer_idx + 1, give)
-                else:
-                    (down,), token = stage_weights([down_proj], layer_idx + 1, give)
+            if not final and stage == 0:
+                (gate, up), token = stage_weights([gate_proj, up_proj], layer_idx + 1, [give])
+                taken, token = lax.optimization_barrier((taken, token))
+            elif not final and stage == 1:
+                (down,), token = stage_weights([down_proj], layer_idx + 1, [give])
                 taken, token = lax.optimization_barrier((taken, token))
             held = held + taken.astype(jnp.float32)
-        own_rows = (own_rows.astype(jnp.float32) + held).astype(jnp.bfloat16)
-        if layer_idx + 1 < ROUNDS:
-            near, far = gather_rows(own_rows, orders, last + 1)
-    return own_rows
+        if final:
+            return (pooled[:NODE_STEPS].astype(jnp.float32) + held).astype(jnp.bfloat16)
+        held = join_pair(held.astype(jnp.bfloat16), orders, last)
+        pooled = (pooled.astype(jnp.float32) + held).astype(jnp.bfloat16)
 
 
 def solution(mesh):

time: 189 us -> 172 us (0.910)
  waiting for transfers between devices: 98.1 us -> 87.5 us
  starting transfers between devices: 49.5 us -> 42.6 us
    ppermute x18 -> x19, waiting for transfers between devices: 48.6 us -> 38 us  [swap_stage(): return lax.ppermute(block, ('gx', 'ta'), pairs)]
    ppermute x18 -> x19, starting transfers between devices: 39.4 us -> 32.5 us  [swap_stage(): return lax.ppermute(block, ('gx', 'ta'), pairs)]
    pallas_call x4 -> x5, Pallas kernels: 15.9 us -> 16.9 us  [stage_weights(): pl.pallas_call(functools.partial(stage_body, layer=layer, count=len(held)...]
    unnamed x20 -> x21, local copies, waits for them, and re-layouts: 6.08 us -> 6.1 us
  transfers between devices with their start and end apart: 22 -> 23, of which waited for: 19 -> 17; matrix products, arithmetic and copies ran while one was open for 0% -> 0% of each run, Pallas kernels for 9% -> 11%
where the time goes in v6:
time: 172 us
  waiting for transfers between devices  87.5 us (51%)
  starting transfers between devices  42.6 us (25%)
  Pallas kernels  33 us (19%)
  local copies, waits for them, and re-layouts  6.22 us (4%)
    all_to_all x1, waiting for transfers between devices, per_device(): kv = lax.all_to_all(kv, 'gx', 0, 0, axis_index_groups=groups, tiled=True)  40.8 us
    ppermute x19, waiting for transfers between devices, swap_stage(): return lax.ppermute(block, ('gx', 'ta'), pairs)  38 us
    ppermute x19, starting transfers between devices, swap_stage(): return lax.ppermute(block, ('gx', 'ta'), pairs)  32.5 us
    pallas_call x5, Pallas kernels, stage_weights(): pl.pallas_call(functools.partial(stage_body, layer=layer, count=len(held)...  16.9 us
    all_to_all x1, starting transfers between devices, per_device(): lax.all_to_all(queries, 'gx', 0, 0, axis_index_groups=groups, tiled=True)  6.31 us
    unnamed x21, local copies, waits for them, and re-layouts  6.1 us
    pallas_call x2, Pallas kernels, expand(): pl.pallas_call(functools.partial(expand_body, layer=layer), in_specs=[pl....  5.16 us
    all_to_all x1, waiting for transfers between devices, per_device(): lax.all_to_all(queries, 'gx', 0, 0, axis_index_groups=groups, tiled=True)  4.46 us
  transfers between devices with their start and end apart: 23, of which 17 were waited for; matrix products, arithmetic and copies ran while one was open for 0% of the time, Pallas kernels for 11%

profile of v6, /device:TPU:0, one launch (start us, length us, event | category | flops | bytes accessed | tf_op | source)
XLA Modules:
  0.0 171.7 jit_solution(1754801977888714441)
XLA Ops:
  3.5 6.3 %all-to-all-start = ((bf16[8,16,2560]{2,1,0:T(8,128)(2,1)}), bf16[8,16,2560]{2,1,0:T(8,128)(2,1)S(1)}, u32[]{:S(2)}, u32[]{:S(2)}) async-start(bf16[8,16,2560]{2,1,0:T(8,128)(2,1)} %arrange.3), calls=%async_computation | async-start | bytes 1310720 | tf_op jit(solution)/shard_map/all_to_all | solution.py:373
  15.7 4.5 %all-to-all-done = bf16[8,16,2560]{2,1,0:T(8,128)(2,1)S(1)} async-done(((bf16[8,16,2560]{2,1,0:T(8,128)(2,1)}), bf16[8,16,2560]{2,1,0:T(8,128)(2,1)S(1)}, u32[]{:S(2)}, u32[]{:S(2)}) %all-to-all-start) | async-done | bytes 655392 | tf_op jit(solution)/shard_map/all_to_all | solution.py:373
  20.2 3.6 %all-to-all-start.1 = ((bf16[8,64,2560]{2,1,0:T(8,128)(2,1)}), bf16[8,64,2560]{2,1,0:T(8,128)(2,1)S(1)}, u32[]{:S(2)}, u32[]{:S(2)}) async-start(bf16[8,64,2560]{2,1,0:T(8,128)(2,1)} %copy-done.2), calls=%async_computation.1 | async-start | bytes 5242880 | tf_op jit(solution)/shard_map/all_to_all | solution.py:386
  24.0 2.7 %collective-permute-start = (bf16[128,2560]{1,0:T(8,128)(2,1)S(1)}, bf16[128,2560]{1,0:T(8,128)(2,1)}, u32[]{:S(2)}, u32[]{:S(2)}) collective-permute-start(bf16[128,2560]{1,0:T(8,128)(2,1)S(1)} %bitcast.16), channel_id=1, source_target_pairs={{0,16},{1,17},{2,18},{3,19},{4,20},{5,21},{6,22},{7,23},{8,24},{9,... | collective-permute-start | bytes 1966088 | tf_op jit(solution)/shard_map/ppermute | solution.py:45
  27.0 40.8 %all-to-all-done.1 = bf16[8,64,2560]{2,1,0:T(8,128)(2,1)S(1)} async-done(((bf16[8,64,2560]{2,1,0:T(8,128)(2,1)}), bf16[8,64,2560]{2,1,0:T(8,128)(2,1)S(1)}, u32[]{:S(2)}, u32[]{:S(2)}) %all-to-all-start.1) | async-done | bytes 2621472 | tf_op jit(solution)/shard_map/all_to_all | solution.py:386
  67.8 3.9 %half_scores.1 = (bf16[20,2,128,128]{3,2,1,0:T(8,128)(2,1)S(1)}, f32[128,128]{1,0:T(8,128)S(1)}) custom-call(bf16[128,2560]{1,0:T(8,128)(2,1)S(1)} %bitcast.17, bf16[128,2560]{1,0:T(8,128)(2,1)} %collective-permute-done.far_ref, bf16[8,4,16,2560]{3,2,1,0:T(8,128)(2,1)S(1)} %bitcast.14), custom_call_target="tpu_custom_call" | custom-call | tf_op jit(solution)/shard_map/half_scores/pallas_call | solution.py:142
  72.9 2.9 %stage_weights.5 = (bf16[2560,1280]{1,0:T(8,128)(2,1)S(1)}, f32[8,128]{1,0:T(8,128)S(1)}) custom-call(bf16[2,2560,1280]{2,1,0:T(8,128)(2,1)} %refs_0_.9, f32[128,128]{1,0:T(8,128)S(1)} %get-tuple-element.36.refs_1_.lse_ref), custom_call_target="tpu_custom_call" | custom-call | bytes 13107200 | tf_op jit(solution)/shard_map/stage_weights/pallas_call | solution.py:225
  80.2 2.9 %stage_weights.6 = (bf16[2560,1280]{1,0:T(8,128)(2,1)S(1)}, f32[8,128]{1,0:T(8,128)S(1)}) custom-call(bf16[2,2560,1280]{2,1,0:T(8,128)(2,1)} %refs_1_.1, bf16[16,2560]{1,0:T(8,128)(2,1)S(1)} %half_pool.1.refs_1_, f32[8,128]{1,0:T(8,128)S(1)} %get-tuple-element.39.refs_2_), custom_call_target="tpu_custom_call" | custom-call | bytes 13107200 | tf_op jit(solution)/shard_map/stage_weights/pallas_call | solution.py:225
  84.7 3.4 %collective-permute-start.3 = (bf16[16,2560]{1,0:T(8,128)(2,1)S(1)}, bf16[16,2560]{1,0:T(8,128)(2,1)S(1)}, u32[]{:S(2)}, u32[]{:S(2)}) collective-permute-start(bf16[16,2560]{1,0:T(8,128)(2,1)S(1)} %add_convert_fusion.1), channel_id=1, source_target_pairs={{0,8},{1,9},{2,10},{3,11},{4,12},{5,13},{6,14},{7,15},{8,0},{9,1},... | collective-permute-start | bytes 245768 | tf_op jit(solution)/shard_map/ppermute | solution.py:45
  88.1 2.4 %collective-permute-done.3 = bf16[16,2560]{1,0:T(8,128)(2,1)S(1)} collective-permute-done((bf16[16,2560]{1,0:T(8,128)(2,1)S(1)}, bf16[16,2560]{1,0:T(8,128)(2,1)S(1)}, u32[]{:S(2)}, u32[]{:S(2)}) %collective-permute-start.3) | collective-permute-done | bytes 81952 | tf_op jit(solution)/shard_map/ppermute | solution.py:45
  90.5 3.8 %collective-permute-start.6 = (bf16[32,2560]{1,0:T(8,128)(2,1)S(1)}, bf16[32,2560]{1,0:T(8,128)(2,1)S(1)}, u32[]{:S(2)}, u32[]{:S(2)}) collective-permute-start(bf16[32,2560]{1,0:T(8,128)(2,1)S(1)} %constant_dynamic-update-slice_fusion.refs_0_), channel_id=1, source_target_pairs={{0,6},{1,7},{2,4},{3,5},{4,2},{5,3},{6,0},{7,1},{8,14},{9,15},{10,... | collective-permute-start | bytes 491528 | tf_op jit(solution)/shard_map/ppermute | solution.py:45
  95.0 2.9 %stage_weights.7 = (bf16[1280,2560]{1,0:T(8,128)(2,1)S(1)}, f32[8,128]{1,0:T(8,128)S(1)}) custom-call(bf16[2,1280,2560]{2,1,0:T(8,128)(2,1)} %refs_0_.8, f32[8,128]{1,0:T(8,128)S(1)} %get-tuple-element.46.refs_1_), custom_call_target="tpu_custom_call" | custom-call | bytes 13107200 | tf_op jit(solution)/shard_map/stage_weights/pallas_call | solution.py:225
  99.6 2.6 %expand.2.near_ref = bf16[128,2688]{1,0:T(8,128)(2,1)S(1)} custom-call(bf16[32,2560]{1,0:T(8,128)(2,1)S(1)} %constant_dynamic-update-slice_fusion.refs_0_, bf16[32,2560]{1,0:T(8,128)(2,1)S(1)} %collective-permute-done.4.refs_1_, bf16[32,2560]{1,0:T(8,128)(2,1)S(1)} %collective-permute-done.5.refs_2_, bf16[32,2560]{1,0:T(8,128)(2,1)S(1)} %collective-permute-done.6.refs_3_, ...), custom_call_target="tpu_custom_call" | custom-call | tf_op jit(solution)/shard_map/expand/pallas_call | solution.py:280
  102.3 2.1 %collective-permute-done.7.far_ref = bf16[128,2688]{1,0:T(8,128)(2,1)S(1)} collective-permute-done((bf16[128,2688]{1,0:T(8,128)(2,1)S(1)}, bf16[128,2688]{1,0:T(8,128)(2,1)S(1)}, u32[]{:S(2)}, u32[]{:S(2)}) %collective-permute-start.7) | collective-permute-done | bytes 688160 | tf_op jit(solution)/shard_map/ppermute | solution.py:419
  105.7 2.1 %collective-permute-start.8 = (bf16[64,2560]{1,0:T(8,128)(2,1)S(1)}, bf16[64,2560]{1,0:T(8,128)(2,1)S(1)}, u32[]{:S(2)}, u32[]{:S(2)}) collective-permute-start(bf16[64,2560]{1,0:T(8,128)(2,1)S(1)} %get-tuple-element.50.refs_2_), channel_id=1, source_target_pairs={{0,2},{1,5},{2,0},{3,7},{4,6},{5,1},{6,4},{7,3},{8,10},{9,13},{10,... | collective-permute-start | bytes 983048 | tf_op jit(solution)/shard_map/ppermute | solution.py:45
  107.8 5.1 %collective-permute-done.8 = bf16[64,2560]{1,0:T(8,128)(2,1)S(1)} collective-permute-done((bf16[64,2560]{1,0:T(8,128)(2,1)S(1)}, bf16[64,2560]{1,0:T(8,128)(2,1)S(1)}, u32[]{:S(2)}, u32[]{:S(2)}) %collective-permute-start.8) | collective-permute-done | bytes 327712 | tf_op jit(solution)/shard_map/ppermute | solution.py:45
  114.2 2.9 %stage_weights.8 = (bf16[1280,2560]{1,0:T(8,128)(2,1)S(1)}, f32[8,128]{1,0:T(8,128)S(1)}) custom-call(bf16[2,1280,2560]{2,1,0:T(8,128)(2,1)} %refs_0_.8, bf16[32,2560]{1,0:T(8,128)(2,1)S(1)} %slice.108.refs_1_), custom_call_target="tpu_custom_call" | custom-call | bytes 13107200 | tf_op jit(solution)/shard_map/stage_weights/pallas_call | solution.py:225
  118.4 2.1 %collective-permute-start.10 = (bf16[16,2560]{1,0:T(8,128)(2,1)S(1)}, bf16[16,2560]{1,0:T(8,128)(2,1)S(1)}, u32[]{:S(2)}, u32[]{:S(2)}) collective-permute-start(bf16[16,2560]{1,0:T(8,128)(2,1)S(1)} %slice.110), channel_id=1, source_target_pairs={{0,8},{1,9},{2,10},{3,11},{4,12},{5,13},{6,14},{7,15},{8,0},{9,1},... | collective-permute-start | bytes 245768 | tf_op jit(solution)/shard_map/ppermute | solution.py:45
  120.5 2.4 %collective-permute-done.10 = bf16[16,2560]{1,0:T(8,128)(2,1)S(1)} collective-permute-done((bf16[16,2560]{1,0:T(8,128)(2,1)S(1)}, bf16[16,2560]{1,0:T(8,128)(2,1)S(1)}, u32[]{:S(2)}, u32[]{:S(2)}) %collective-permute-start.10) | collective-permute-done | bytes 81952 | tf_op jit(solution)/shard_map/ppermute | solution.py:45
  124.4 4.0 %collective-permute-done.11 = bf16[16,2560]{1,0:T(8,128)(2,1)S(1)} collective-permute-done((bf16[16,2560]{1,0:T(8,128)(2,1)S(1)}, bf16[16,2560]{1,0:T(8,128)(2,1)S(1)}, u32[]{:S(2)}, u32[]{:S(2)}) %collective-permute-start.11) | collective-permute-done | bytes 81952 | tf_op jit(solution)/shard_map/ppermute | solution.py:45
  128.4 2.7 %collective-permute-start.12 = (bf16[16,2560]{1,0:T(8,128)(2,1)S(1)}, bf16[16,2560]{1,0:T(8,128)(2,1)S(1)}, u32[]{:S(2)}, u32[]{:S(2)}) collective-permute-start(bf16[16,2560]{1,0:T(8,128)(2,1)S(1)} %add_convert_fusion), channel_id=1, source_target_pairs={{0,8},{1,9},{2,10},{3,11},{4,12},{5,13},{6,14},{7,15},{8,0},{9,1},... | collective-permute-start | bytes 245768 | tf_op jit(solution)/shard_map/ppermute | solution.py:45
  131.1 2.4 %collective-permute-done.12 = bf16[16,2560]{1,0:T(8,128)(2,1)S(1)} collective-permute-done((bf16[16,2560]{1,0:T(8,128)(2,1)S(1)}, bf16[16,2560]{1,0:T(8,128)(2,1)S(1)}, u32[]{:S(2)}, u32[]{:S(2)}) %collective-permute-start.12) | collective-permute-done | bytes 81952 | tf_op jit(solution)/shard_map/ppermute | solution.py:45
  133.5 3.1 %collective-permute-start.15 = (bf16[32,2560]{1,0:T(8,128)(2,1)S(1)}, bf16[32,2560]{1,0:T(8,128)(2,1)S(1)}, u32[]{:S(2)}, u32[]{:S(2)}) collective-permute-start(bf16[32,2560]{1,0:T(8,128)(2,1)S(1)} %pad_maximum_fusion.refs_0_), channel_id=1, source_target_pairs={{0,6},{1,7},{2,4},{3,5},{4,2},{5,3},{6,0},{7,1},{8,14},{9,15},{10,... | collective-permute-start | bytes 491528 | tf_op jit(solution)/shard_map/ppermute | solution.py:45
  137.5 5.3 %stage_weights.9 = (bf16[2560,1280]{1,0:T(8,128)(2,1)S(1)}, bf16[2560,1280]{1,0:T(8,128)(2,1)S(1)}, f32[8,128]{1,0:T(8,128)}) custom-call(bf16[2,2560,1280]{2,1,0:T(8,128)(2,1)} %refs_0_.9, bf16[2,2560,1280]{2,1,0:T(8,128)(2,1)} %refs_1_.1, bf16[64,2560]{1,0:T(8,128)(2,1)S(1)} %get-tuple-element.50.refs_2_), custom_call_target="tpu_custom_call" | custom-call | bytes 26214400 | tf_op jit(solution)/shard_map/stage_weights/pallas_call | solution.py:225
  142.9 2.6 %expand.3.near_ref = bf16[128,2688]{1,0:T(8,128)(2,1)S(1)} custom-call(bf16[32,2560]{1,0:T(8,128)(2,1)S(1)} %pad_maximum_fusion.refs_0_, bf16[32,2560]{1,0:T(8,128)(2,1)S(1)} %collective-permute-done.13.refs_1_, bf16[32,2560]{1,0:T(8,128)(2,1)S(1)} %collective-permute-done.14.refs_2_, bf16[32,2560]{1,0:T(8,128)(2,1)S(1)} %collective-permute-done.15.refs_3_, ...), custom_call_target="tpu_custom_call" | custom-call | tf_op jit(solution)/shard_map/expand/pallas_call | solution.py:280
  145.5 2.1 %collective-permute-done.16.far_ref = bf16[128,2688]{1,0:T(8,128)(2,1)S(1)} collective-permute-done((bf16[128,2688]{1,0:T(8,128)(2,1)S(1)}, bf16[128,2688]{1,0:T(8,128)(2,1)S(1)}, u32[]{:S(2)}, u32[]{:S(2)}) %collective-permute-start.16) | collective-permute-done | bytes 688160 | tf_op jit(solution)/shard_map/ppermute | solution.py:419
  148.9 2.1 %collective-permute-start.17 = (bf16[64,2560]{1,0:T(8,128)(2,1)S(1)}, bf16[64,2560]{1,0:T(8,128)(2,1)S(1)}, u32[]{:S(2)}, u32[]{:S(2)}) collective-permute-start(bf16[64,2560]{1,0:T(8,128)(2,1)S(1)} %get-tuple-element.58), channel_id=1, source_target_pairs={{0,2},{1,5},{2,0},{3,7},{4,6},{5,1},{6,4},{7,3},{8,10},{9,13},{10,... | collective-permute-start | bytes 983048 | tf_op jit(solution)/shard_map/ppermute | solution.py:45
  151.0 5.1 %collective-permute-done.17 = bf16[64,2560]{1,0:T(8,128)(2,1)S(1)} collective-permute-done((bf16[64,2560]{1,0:T(8,128)(2,1)S(1)}, bf16[64,2560]{1,0:T(8,128)(2,1)S(1)}, u32[]{:S(2)}, u32[]{:S(2)}) %collective-permute-start.17) | collective-permute-done | bytes 327712 | tf_op jit(solution)/shard_map/ppermute | solution.py:45
  157.3 4.2 %collective-permute-done.18 = bf16[32,2560]{1,0:T(8,128)(2,1)S(1)} collective-permute-done((bf16[32,2560]{1,0:T(8,128)(2,1)S(1)}, bf16[32,2560]{1,0:T(8,128)(2,1)S(1)}, u32[]{:S(2)}, u32[]{:S(2)}) %collective-permute-start.18) | collective-permute-done | bytes 163872 | tf_op jit(solution)/shard_map/ppermute | solution.py:45
  161.5 2.1 %collective-permute-start.19 = (bf16[16,2560]{1,0:T(8,128)(2,1)S(1)}, bf16[16,2560]{1,0:T(8,128)(2,1)S(1)}, u32[]{:S(2)}, u32[]{:S(2)}) collective-permute-start(bf16[16,2560]{1,0:T(8,128)(2,1)S(1)} %slice.109), channel_id=1, source_target_pairs={{0,8},{1,9},{2,10},{3,11},{4,12},{5,13},{6,14},{7,15},{8,0},{9,1},... | collective-permute-start | bytes 245768 | tf_op jit(solution)/shard_map/ppermute | solution.py:45
  163.6 2.4 %collective-permute-done.19 = bf16[16,2560]{1,0:T(8,128)(2,1)S(1)} collective-permute-done((bf16[16,2560]{1,0:T(8,128)(2,1)S(1)}, bf16[16,2560]{1,0:T(8,128)(2,1)S(1)}, u32[]{:S(2)}, u32[]{:S(2)}) %collective-permute-start.19) | collective-permute-done | bytes 81952 | tf_op jit(solution)/shard_map/ppermute | solution.py:45
  167.0 4.1 %collective-permute-done.20 = bf16[8,2560]{1,0:T(8,128)(2,1)S(1)} collective-permute-done((bf16[8,2560]{1,0:T(8,128)(2,1)S(1)}, bf16[8,2560]{1,0:T(8,128)(2,1)S(1)}, u32[]{:S(2)}, u32[]{:S(2)}) %collective-permute-start.20) | collective-permute-done | bytes 40992 | tf_op jit(solution)/shard_map/ppermute | solution.py:45
  (89 shorter events, 30.1 us)
Async XLA Ops:
  0.9 1.3 copy-start.3
  3.5 20.3 %copy-start.8 = (s32[64,2]{0,1:T(2,128)S(1)}, s32[64,2]{0,1:T(2,128)}, u32[]{:S(2)}) copy-start(s32[64,2]{0,1:T(2,128)} %param.15) | copy-start | bytes 1540
  3.5 23.1 %copy-start.9 = (s32[64]{0:T(128)S(1)}, s32[64]{0:T(128)}, u32[]{:S(2)}) copy-start(s32[64]{0:T(128)} %param.16) | copy-start | bytes 772
  3.5 16.7 %all-to-all-start = ((bf16[8,16,2560]{2,1,0:T(8,128)(2,1)}), bf16[8,16,2560]{2,1,0:T(8,128)(2,1)S(1)}, u32[]{:S(2)}, u32[]{:S(2)}) async-start(bf16[8,16,2560]{2,1,0:T(8,128)(2,1)} %arrange.3), calls=%async_computation | async-start | bytes 1310720 | tf_op jit(solution)/shard_map/all_to_all | solution.py:373
  10.2 1.3 copy-start.4
  11.5 1.3 copy-start.5
  14.2 1.5 copy-start.2
  20.2 47.6 %all-to-all-start.1 = ((bf16[8,64,2560]{2,1,0:T(8,128)(2,1)}), bf16[8,64,2560]{2,1,0:T(8,128)(2,1)S(1)}, u32[]{:S(2)}, u32[]{:S(2)}) async-start(bf16[8,64,2560]{2,1,0:T(8,128)(2,1)} %copy-done.2), calls=%async_computation.1 | async-start | bytes 5242880 | tf_op jit(solution)/shard_map/all_to_all | solution.py:386
  24.0 43.9 %collective-permute-start = (bf16[128,2560]{1,0:T(8,128)(2,1)S(1)}, bf16[128,2560]{1,0:T(8,128)(2,1)}, u32[]{:S(2)}, u32[]{:S(2)}) collective-permute-start(bf16[128,2560]{1,0:T(8,128)(2,1)S(1)} %bitcast.16), channel_id=1, source_target_pairs={{0,16},{1,17},{2,18},{3,19},{4,20},{5,21},{6,22},{7,23},{8,24},{9,... | collective-permute-start | bytes 1966088 | tf_op jit(solution)/shard_map/ppermute | solution.py:45
  71.7 5.5 %collective-permute-start.1 = (f32[128,128]{1,0:T(8,128)S(1)}, f32[128,128]{1,0:T(8,128)S(1)}, u32[]{:S(2)}, u32[]{:S(2)}) collective-permute-start(f32[128,128]{1,0:T(8,128)S(1)} %get-tuple-element.36.refs_1_.lse_ref), channel_id=1, source_target_pairs={{0,16},{1,17},{2,18},{3,19},{4,20},{5,21},{6,22},{7,23},{8,24},{9,... | collective-permute-start | bytes 196616 | tf_op jit(solution)/shard_map/ppermute | solution.py:45
  79.2 15.7 %copy-start.7 = (f32[2,3,2560]{2,0,1:T(2,128)S(1)}, f32[2,3,2560]{2,0,1:T(2,128)}, u32[]{:S(2)}) copy-start(f32[2,3,2560]{2,0,1:T(2,128)} %param.17) | copy-start | bytes 184324
  79.2 5.5 %collective-permute-start.2 = (bf16[16,2560]{1,0:T(8,128)(2,1)S(1)}, bf16[16,2560]{1,0:T(8,128)(2,1)S(1)}, u32[]{:S(2)}, u32[]{:S(2)}) collective-permute-start(bf16[16,2560]{1,0:T(8,128)(2,1)S(1)} %half_pool.1.refs_1_), channel_id=1, source_target_pairs={{0,16},{1,17},{2,18},{3,19},{4,20},{5,21},{6,22},{7,23},{8,24},{9,... | collective-permute-start | bytes 245768 | tf_op jit(solution)/shard_map/ppermute | solution.py:45
  84.7 5.8 %collective-permute-start.3 = (bf16[16,2560]{1,0:T(8,128)(2,1)S(1)}, bf16[16,2560]{1,0:T(8,128)(2,1)S(1)}, u32[]{:S(2)}, u32[]{:S(2)}) collective-permute-start(bf16[16,2560]{1,0:T(8,128)(2,1)S(1)} %add_convert_fusion.1), channel_id=1, source_target_pairs={{0,8},{1,9},{2,10},{3,11},{4,12},{5,13},{6,14},{7,15},{8,0},{9,1},... | collective-permute-start | bytes 245768 | tf_op jit(solution)/shard_map/ppermute | solution.py:45
  90.5 7.3 %collective-permute-start.6 = (bf16[32,2560]{1,0:T(8,128)(2,1)S(1)}, bf16[32,2560]{1,0:T(8,128)(2,1)S(1)}, u32[]{:S(2)}, u32[]{:S(2)}) collective-permute-start(bf16[32,2560]{1,0:T(8,128)(2,1)S(1)} %constant_dynamic-update-slice_fusion.refs_0_), channel_id=1, source_target_pairs={{0,6},{1,7},{2,4},{3,5},{4,2},{5,3},{6,0},{7,1},{8,14},{9,15},{10,... | collective-permute-start | bytes 491528 | tf_op jit(solution)/shard_map/ppermute | solution.py:45
  94.3 5.3 %collective-permute-start.5 = (bf16[32,2560]{1,0:T(8,128)(2,1)S(1)}, bf16[32,2560]{1,0:T(8,128)(2,1)S(1)}, u32[]{:S(2)}, u32[]{:S(2)}) collective-permute-start(bf16[32,2560]{1,0:T(8,128)(2,1)S(1)} %constant_dynamic-update-slice_fusion.refs_0_), channel_id=1, source_target_pairs={{0,2},{1,5},{2,0},{3,7},{4,6},{5,1},{6,4},{7,3},{8,10},{9,13},{10,... | collective-permute-start | bytes 491528 | tf_op jit(solution)/shard_map/ppermute | solution.py:45
  94.3 5.3 %collective-permute-start.4 = (bf16[32,2560]{1,0:T(8,128)(2,1)S(1)}, bf16[32,2560]{1,0:T(8,128)(2,1)S(1)}, u32[]{:S(2)}, u32[]{:S(2)}) collective-permute-start(bf16[32,2560]{1,0:T(8,128)(2,1)S(1)} %constant_dynamic-update-slice_fusion.refs_0_), channel_id=1, source_target_pairs={{0,4},{1,3},{2,6},{3,1},{4,0},{5,7},{6,2},{7,5},{8,12},{9,11},{10,... | collective-permute-start | bytes 491528 | tf_op jit(solution)/shard_map/ppermute | solution.py:45
  94.9 4.7 %copy-start.6 = (f32[2,2560]{1,0:T(2,128)S(1)}, f32[2,2560]{1,0:T(2,128)}, u32[]{:S(2)}) copy-start(f32[2,2560]{1,0:T(2,128)} %refs_6_.3) | copy-start | bytes 61444
  102.2 2.2 %collective-permute-start.7 = (bf16[128,2688]{1,0:T(8,128)(2,1)S(1)}, bf16[128,2688]{1,0:T(8,128)(2,1)S(1)}, u32[]{:S(2)}, u32[]{:S(2)}) collective-permute-start(bf16[128,2688]{1,0:T(8,128)(2,1)S(1)} %expand.2.near_ref), channel_id=1, source_target_pairs={{0,1},{1,0},{2,3},{3,2},{4,5},{5,4},{6,7},{7,6},{8,9},{9,8},{10,11... | collective-permute-start | bytes 2064392 | tf_op jit(solution)/shard_map/ppermute | solution.py:419
  105.7 7.1 %collective-permute-start.8 = (bf16[64,2560]{1,0:T(8,128)(2,1)S(1)}, bf16[64,2560]{1,0:T(8,128)(2,1)S(1)}, u32[]{:S(2)}, u32[]{:S(2)}) collective-permute-start(bf16[64,2560]{1,0:T(8,128)(2,1)S(1)} %get-tuple-element.50.refs_2_), channel_id=1, source_target_pairs={{0,2},{1,5},{2,0},{3,7},{4,6},{5,1},{6,4},{7,3},{8,10},{9,13},{10,... | collective-permute-start | bytes 983048 | tf_op jit(solution)/shard_map/ppermute | solution.py:45
  112.9 5.4 %collective-permute-start.9 = (bf16[32,2560]{1,0:T(8,128)(2,1)S(1)}, bf16[32,2560]{1,0:T(8,128)(2,1)S(1)}, u32[]{:S(2)}, u32[]{:S(2)}) collective-permute-start(bf16[32,2560]{1,0:T(8,128)(2,1)S(1)} %slice.108.refs_1_), channel_id=1, source_target_pairs={{0,4},{1,3},{2,6},{3,1},{4,0},{5,7},{6,2},{7,5},{8,12},{9,11},{10,... | collective-permute-start | bytes 491528 | tf_op jit(solution)/shard_map/ppermute | solution.py:45
  118.4 4.5 %collective-permute-start.10 = (bf16[16,2560]{1,0:T(8,128)(2,1)S(1)}, bf16[16,2560]{1,0:T(8,128)(2,1)S(1)}, u32[]{:S(2)}, u32[]{:S(2)}) collective-permute-start(bf16[16,2560]{1,0:T(8,128)(2,1)S(1)} %slice.110), channel_id=1, source_target_pairs={{0,8},{1,9},{2,10},{3,11},{4,12},{5,13},{6,14},{7,15},{8,0},{9,1},... | collective-permute-start | bytes 245768 | tf_op jit(solution)/shard_map/ppermute | solution.py:45
  122.9 5.5 %collective-permute-start.11 = (bf16[16,2560]{1,0:T(8,128)(2,1)S(1)}, bf16[16,2560]{1,0:T(8,128)(2,1)S(1)}, u32[]{:S(2)}, u32[]{:S(2)}) collective-permute-start(bf16[16,2560]{1,0:T(8,128)(2,1)S(1)} %fusion.2), channel_id=1, source_target_pairs={{0,16},{1,17},{2,18},{3,19},{4,20},{5,21},{6,22},{7,23},{8,24},{9,... | collective-permute-start | bytes 245768 | tf_op jit(solution)/shard_map/ppermute | solution.py:45
  128.4 5.1 %collective-permute-start.12 = (bf16[16,2560]{1,0:T(8,128)(2,1)S(1)}, bf16[16,2560]{1,0:T(8,128)(2,1)S(1)}, u32[]{:S(2)}, u32[]{:S(2)}) collective-permute-start(bf16[16,2560]{1,0:T(8,128)(2,1)S(1)} %add_convert_fusion), channel_id=1, source_target_pairs={{0,8},{1,9},{2,10},{3,11},{4,12},{5,13},{6,14},{7,15},{8,0},{9,1},... | collective-permute-start | bytes 245768 | tf_op jit(solution)/shard_map/ppermute | solution.py:45
  133.5 9.3 %collective-permute-start.15 = (bf16[32,2560]{1,0:T(8,128)(2,1)S(1)}, bf16[32,2560]{1,0:T(8,128)(2,1)S(1)}, u32[]{:S(2)}, u32[]{:S(2)}) collective-permute-start(bf16[32,2560]{1,0:T(8,128)(2,1)S(1)} %pad_maximum_fusion.refs_0_), channel_id=1, source_target_pairs={{0,6},{1,7},{2,4},{3,5},{4,2},{5,3},{6,0},{7,1},{8,14},{9,15},{10,... | collective-permute-start | bytes 491528 | tf_op jit(solution)/shard_map/ppermute | solution.py:45
  136.6 6.2 %collective-permute-start.14 = (bf16[32,2560]{1,0:T(8,128)(2,1)S(1)}, bf16[32,2560]{1,0:T(8,128)(2,1)S(1)}, u32[]{:S(2)}, u32[]{:S(2)}) collective-permute-start(bf16[32,2560]{1,0:T(8,128)(2,1)S(1)} %pad_maximum_fusion.refs_0_), channel_id=1, source_target_pairs={{0,2},{1,5},{2,0},{3,7},{4,6},{5,1},{6,4},{7,3},{8,10},{9,13},{10,... | collective-permute-start | bytes 491528 | tf_op jit(solution)/shard_map/ppermute | solution.py:45
  136.6 6.2 %collective-permute-start.13 = (bf16[32,2560]{1,0:T(8,128)(2,1)S(1)}, bf16[32,2560]{1,0:T(8,128)(2,1)S(1)}, u32[]{:S(2)}, u32[]{:S(2)}) collective-permute-start(bf16[32,2560]{1,0:T(8,128)(2,1)S(1)} %pad_maximum_fusion.refs_0_), channel_id=1, source_target_pairs={{0,4},{1,3},{2,6},{3,1},{4,0},{5,7},{6,2},{7,5},{8,12},{9,11},{10,... | collective-permute-start | bytes 491528 | tf_op jit(solution)/shard_map/ppermute | solution.py:45
  142.9 28.8 %copy-start.1 = (s32[16,16]{1,0:T(8,128)S(1)}, s32[16,16]{1,0:T(8,128)}, u32[]{:S(2)}) copy-start(s32[16,16]{1,0:T(8,128)} %param.14) | copy-start | bytes 3076
  145.4 2.2 %collective-permute-start.16 = (bf16[128,2688]{1,0:T(8,128)(2,1)S(1)}, bf16[128,2688]{1,0:T(8,128)(2,1)S(1)}, u32[]{:S(2)}, u32[]{:S(2)}) collective-permute-start(bf16[128,2688]{1,0:T(8,128)(2,1)S(1)} %expand.3.near_ref), channel_id=1, source_target_pairs={{0,1},{1,0},{2,3},{3,2},{4,5},{5,4},{6,7},{7,6},{8,9},{9,8},{10,11... | collective-permute-start | bytes 2064392 | tf_op jit(solution)/shard_map/ppermute | solution.py:419
  148.9 7.2 %collective-permute-start.17 = (bf16[64,2560]{1,0:T(8,128)(2,1)S(1)}, bf16[64,2560]{1,0:T(8,128)(2,1)S(1)}, u32[]{:S(2)}, u32[]{:S(2)}) collective-permute-start(bf16[64,2560]{1,0:T(8,128)(2,1)S(1)} %get-tuple-element.58), channel_id=1, source_target_pairs={{0,2},{1,5},{2,0},{3,7},{4,6},{5,1},{6,4},{7,3},{8,10},{9,13},{10,... | collective-permute-start | bytes 983048 | tf_op jit(solution)/shard_map/ppermute | solution.py:45
  156.1 5.4 %collective-permute-start.18 = (bf16[32,2560]{1,0:T(8,128)(2,1)S(1)}, bf16[32,2560]{1,0:T(8,128)(2,1)S(1)}, u32[]{:S(2)}, u32[]{:S(2)}) collective-permute-start(bf16[32,2560]{1,0:T(8,128)(2,1)S(1)} %slice.107), channel_id=1, source_target_pairs={{0,4},{1,3},{2,6},{3,1},{4,0},{5,7},{6,2},{7,5},{8,12},{9,11},{10,... | collective-permute-start | bytes 491528 | tf_op jit(solution)/shard_map/ppermute | solution.py:45
  161.5 4.5 %collective-permute-start.19 = (bf16[16,2560]{1,0:T(8,128)(2,1)S(1)}, bf16[16,2560]{1,0:T(8,128)(2,1)S(1)}, u32[]{:S(2)}, u32[]{:S(2)}) collective-permute-start(bf16[16,2560]{1,0:T(8,128)(2,1)S(1)} %slice.109), channel_id=1, source_target_pairs={{0,8},{1,9},{2,10},{3,11},{4,12},{5,13},{6,14},{7,15},{8,0},{9,1},... | collective-permute-start | bytes 245768 | tf_op jit(solution)/shard_map/ppermute | solution.py:45
  166.1 5.0 %collective-permute-start.20 = (bf16[8,2560]{1,0:T(8,128)(2,1)S(1)}, bf16[8,2560]{1,0:T(8,128)(2,1)S(1)}, u32[]{:S(2)}, u32[]{:S(2)}) collective-permute-start(bf16[8,2560]{1,0:T(8,128)(2,1)S(1)} %slice.111), channel_id=1, source_target_pairs={{0,16},{1,17},{2,18},{3,19},{4,20},{5,21},{6,22},{7,23},{8,24},{9,... | collective-permute-start | bytes 122888 | tf_op jit(solution)/shard_map/ppermute | solution.py:45
  (1 other events, 0.7 us)

commit v7 on v6

--- a/solution.py
+++ b/solution.py
@@ -20,6 +20,7 @@
 ROWS_HALF = HALF_VENUES * NODE_STEPS
 KEYS_HALF = HALF_VENUES * STEPS
 LSE_ITEM = 64
+SUM_PARTS = 2
 VMEM_LIMIT = 8 << 20
 
 
@@ -135,7 +136,7 @@
     lse_ref[...] = lse
 
 
-def half_scores(own, far, kv):
+def half_scores(own, far, keys):
     width = own.shape[1]
     rows = own.shape[0]
     heads = width // HEAD_DIM
@@ -157,48 +158,71 @@
         ],
         compiler_params=pltpu.CompilerParams(vmem_limit_bytes=VMEM_LIMIT),
         name="half_scores",
-    )(own, far, kv)
-
-
-def pool_body(probs_ref, lse_ref, far_ref, value_ref, out_ref):
+    )(*[pltpu.with_memory_space_constraint(a, pltpu.HBM) for a in (own, far)], keys)
+
+
+def weigh_body(probs_ref, lse_ref, far_ref, weights_ref):
     step = pl.program_id(0)
     far = jnp.concatenate([far_ref[ROWS_HALF:, :], far_ref[:ROWS_HALF, :]], axis=0)
     far = jnp.concatenate([far[:, LSE_ITEM:], far[:, :LSE_ITEM]], axis=1)
     share = 1.0 / (1.0 + jnp.exp(far - lse_ref[...])) * (1.0 / VENUES)
     lane = lax.broadcasted_iota(jnp.int32, lse_ref.shape, 1)
     for head in range(HEADS_STEP):
-        span = slice(head * HEAD_DIM, (head + 1) * HEAD_DIM)
-        pooled = []
+        means = []
         for item in range(2):
             column = step * HEADS_STEP + head + item * LSE_ITEM
             factor = jnp.sum(jnp.where(lane == column, share, 0.0), axis=1, keepdims=True)
             weights = probs_ref[head, item].astype(jnp.float32) * factor
-            weights = jnp.sum(weights.reshape(VENUES, NODE_STEPS, KEYS_HALF), axis=0)
-            values = value_ref[:, item, :, span].reshape(KEYS_HALF, HEAD_DIM)
-            pooled.append(
-                jnp.dot(
-                    weights.astype(jnp.bfloat16), values, preferred_element_type=jnp.float32
-                )
+            means.append(jnp.sum(weights.reshape(VENUES, NODE_STEPS, KEYS_HALF), axis=0))
+        weights_ref[head] = jnp.concatenate(means, axis=0).astype(jnp.bfloat16)
+
+
+def mean_weights(probs, lse, far_lse):
+    heads = probs.shape[0]
+    return pl.pallas_call(
+        weigh_body,
+        grid=(heads // HEADS_STEP,),
+        in_specs=[
+            pl.BlockSpec((HEADS_STEP, 2, 2 * ROWS_HALF, KEYS_HALF), lambda j: (j, 0, 0, 0)),
+            pl.BlockSpec((2 * ROWS_HALF, 128), lambda j: (0, 0)),
+            pl.BlockSpec((2 * ROWS_HALF, 128), lambda j: (0, 0)),
+        ],
+        out_specs=pl.BlockSpec((HEADS_STEP, 2 * NODE_STEPS, KEYS_HALF), lambda j: (j, 0, 0)),
+        out_shape=jax.ShapeDtypeStruct((heads, 2 * NODE_STEPS, KEYS_HALF), jnp.bfloat16),
+        compiler_params=pltpu.CompilerParams(vmem_limit_bytes=VMEM_LIMIT),
+        name="mean_weights",
+    )(probs, lse, far_lse)
+
+
+def pool_body(weights_ref, value_ref, out_ref):
+    row = lax.broadcasted_iota(jnp.int32, (2 * NODE_STEPS, HEAD_DIM), 0)
+    for head in range(HEADS_STEP):
+        span = slice(head * HEAD_DIM, (head + 1) * HEAD_DIM)
+        pooled = [
+            jnp.dot(
+                weights_ref[head],
+                value_ref[:, item, :, span].reshape(KEYS_HALF, HEAD_DIM),
+                preferred_element_type=jnp.float32,
             )
-        out_ref[:, span] = jnp.concatenate(pooled, axis=0).astype(jnp.bfloat16)
-
-
-def half_pool(probs, lse, far_lse, kv):
-    width = kv.shape[3]
+            for item in range(2)
+        ]
+        out_ref[:, span] = jnp.where(row < NODE_STEPS, *pooled).astype(jnp.bfloat16)
+
+
+def half_pool(weights, values):
+    width = values.shape[3]
     return pl.pallas_call(
         pool_body,
         grid=(width // COLS_STEP,),
         in_specs=[
-            pl.BlockSpec((HEADS_STEP, 2, 2 * ROWS_HALF, KEYS_HALF), lambda j: (j, 0, 0, 0)),
-            pl.BlockSpec((2 * ROWS_HALF, 128), lambda j: (0, 0)),
-            pl.BlockSpec((2 * ROWS_HALF, 128), lambda j: (0, 0)),
-            pl.BlockSpec((HALF_VENUES, 2, STEPS, COLS_STEP), lambda j: (0, 1, 0, j)),
+            pl.BlockSpec((HEADS_STEP, 2 * NODE_STEPS, KEYS_HALF), lambda j: (j, 0, 0)),
+            pl.BlockSpec((HALF_VENUES, 2, STEPS, COLS_STEP), lambda j: (0, 0, 0, j)),
         ],
         out_specs=pl.BlockSpec((2 * NODE_STEPS, COLS_STEP), lambda j: (0, j)),
         out_shape=jax.ShapeDtypeStruct((2 * NODE_STEPS, width), jnp.bfloat16),
         compiler_params=pltpu.CompilerParams(vmem_limit_bytes=VMEM_LIMIT),
         name="half_pool",
-    )(probs, lse, far_lse, kv)
+    )(weights, values)
 
 
 def pad_lanes(width):
@@ -288,7 +312,7 @@
     )(*operands)
 
 
-def contract_body(near_ref, far_ref, down_ref, keep_ref, give_ref, *, swap):
+def contract_body(near_ref, far_ref, down_ref, *out_refs, swap):
     rows = near_ref.shape[0]
     width, feat = down_ref.shape
     padded = pad_lanes(width)
@@ -310,26 +334,32 @@
         up = both(slice(padded + span.start, padded + span.stop)) * scale
         hidden.append((gate * (1.0 / (1.0 + jnp.exp(-gate))) * up).astype(jnp.bfloat16))
     hidden = hidden[0] if len(hidden) == 1 else jnp.concatenate(hidden, axis=1)
-    for span in column_tiles(feat, 512):
+    held = feat // (len(out_refs) // 2)
+    for span in column_tiles(feat, 640):
         total = jnp.dot(hidden, down_ref[:, span], preferred_element_type=jnp.float32)
-        keep_ref[:, span] = total[: rows // 2]
-        give_ref[:, span] = total[rows // 2 :].astype(jnp.bfloat16)
-
-
-def contract(near, far, down, swap):
+        part = span.start // held
+        local = slice(span.start % held, span.start % held + span.stop - span.start)
+        out_refs[2 * part][:, local] = total[: rows // 2]
+        out_refs[2 * part + 1][:, local] = total[rows // 2 :].astype(jnp.bfloat16)
+
+
+def contract(near, far, down, parts, swap):
     half, feat = near.shape[0] // 2, down.shape[1]
     held = pltpu.with_memory_space_constraint(down, pltpu.VMEM)
-    return pl.pallas_call(
+    shape = (half, feat // parts)
+    out = pl.pallas_call(
         functools.partial(contract_body, swap=swap),
         in_specs=[pl.BlockSpec(memory_space=pltpu.VMEM)] * 3,
-        out_specs=[pl.BlockSpec(memory_space=pltpu.VMEM)] * 2,
+        out_specs=[pl.BlockSpec(memory_space=pltpu.VMEM)] * (2 * parts),
         out_shape=[
-            jax.ShapeDtypeStruct((half, feat), jnp.float32),
-            jax.ShapeDtypeStruct((half, feat), jnp.bfloat16),
-        ],
+            jax.ShapeDtypeStruct(shape, jnp.float32),
+            jax.ShapeDtypeStruct(shape, jnp.bfloat16),
+        ]
+        * parts,
         compiler_params=pltpu.CompilerParams(vmem_limit_bytes=VMEM_LIMIT),
         name="contract",
     )(near, far, held)
+    return [out[2 * part : 2 * part + 2] for part in range(parts)]
 
 
 def per_device(
@@ -372,20 +402,25 @@
     queries = arrange(picker(query_pairs), [query_vecs.reshape(rows, feat_width)], chunks)
     queries = lax.all_to_all(queries, "gx", 0, 0, axis_index_groups=groups, tiled=True)
     queries = queries.reshape(query_pairs * inst_total, feat_width)
-    kv = arrange(
-        picker(pairs_dev),
-        [key_vecs.reshape(rows, feat_width), value_vecs.reshape(rows, feat_width)],
-        chunks,
-    )
-    kv, queries = lax.optimization_barrier((kv, queries))
+    pick = picker(pairs_dev)
+    keys, values = (a.reshape(rows, feat_width) for a in (key_vecs, value_vecs))
+    values = arrange(pick, [values], chunks)
+    keys = arrange(pick, [keys], chunks)
+    keys, queries = lax.optimization_barrier((keys, queries))
+
+    def exchange(block):
+        block = lax.all_to_all(block, "gx", 0, 0, axis_index_groups=groups, tiled=True)
+        block = block.reshape(HALF_VENUES, STEPS // pairs_dev, 2, pairs_dev, feat_width)
+        return block.transpose(0, 2, 1, 3, 4).reshape(HALF_VENUES, 2, STEPS, feat_width)
+
     if not whole_venue:
         queries = queries.reshape(HALF_VENUES, STEPS // pairs_dev, 2, pairs_dev, feat_width)
         queries = queries[:, (STEPS - NODE_STEPS) // pairs_dev :].transpose(0, 2, 1, 3, 4)
         queries = queries.reshape(2 * ROWS_HALF, feat_width)
     far = swap_stage(queries, orders, last)
-    kv = lax.all_to_all(kv, "gx", 0, 0, axis_index_groups=groups, tiled=True)
-    kv = kv.reshape(HALF_VENUES, STEPS // pairs_dev, 4, pairs_dev, feat_width)
-    kv = kv.transpose(0, 2, 1, 3, 4).reshape(HALF_VENUES, 4, STEPS, feat_width)
+    keys = exchange(keys)
+    values, keys, far = lax.optimization_barrier((values, keys, far))
+    values = exchange(values)
     row_total = inst_total * NODE_STEPS
     row = jnp.arange(row_total)
     place = row // NODE_STEPS
@@ -402,16 +437,16 @@
         "ter,ec->trc", typed.astype(jnp.bfloat16), at_source, preferred_element_type=jnp.float32
     )
     mix = jnp.where(same_step[None], mix, 0.0).astype(jnp.bfloat16)
-    kv, mix, type_gain = lax.optimization_barrier((kv, mix, type_gain))
-    probs, lse = half_scores(queries, far, kv)
+    keys, mix, type_gain = lax.optimization_barrier((keys, mix, type_gain))
+    probs, lse = half_scores(queries, far, keys)
     far_lse = swap_stage(lse, orders, last)
-    (gate,), token = stage_weights([gate_proj], 0, [lse])
-    far_lse, token = lax.optimization_barrier((far_lse, token))
-    pooled = half_pool(probs, lse, far_lse, kv)
-    (up,), token = stage_weights([up_proj], 0, [pooled, token])
+    pooled = half_pool(mean_weights(probs, lse, far_lse), values)
+    (gate,), token = stage_weights([gate_proj], 0, [pooled])
     pooled = join_pair(pooled, orders, last).astype(jnp.bfloat16)
     pooled, token = lax.optimization_barrier((pooled, token))
-    (down,), token = stage_weights([down_proj], 0, [token])
+    (up, down), token = stage_weights([up_proj, down_proj], 0, [token])
+    parts = SUM_PARTS if feat_width % (SUM_PARTS * 128) == 0 else 1
+    part_width = feat_width // parts
     for layer_idx in range(ROUNDS):
         nodes = gather_rows(pooled, orders, last)
         near_sums = expand(nodes, mix, type_gain, norm_gain, gate, up, token, layer_idx)
@@ -419,24 +454,27 @@
             far_sums = lax.ppermute(near_sums, "ta", [(0, 1), (1, 0)])
         else:
             far_sums = lax.psum(near_sums.astype(jnp.float32), "ta") - near_sums.astype(jnp.float32)
-        held, give = contract(near_sums, far_sums, down, ta_count == 2)
+        sums = contract(near_sums, far_sums, down, parts, ta_count == 2)
         final = layer_idx + 1 == ROUNDS
-        for stage in range(last + 1 if final else last):
-            if stage:
-                half = held.shape[0] // 2
-                held, give = held[:half], held[half:].astype(jnp.bfloat16)
-            taken = swap_stage(give, orders, stage)
-            if not final and stage == 0:
-                (gate, up), token = stage_weights([gate_proj, up_proj], layer_idx + 1, [give])
-                taken, token = lax.optimization_barrier((taken, token))
-            elif not final and stage == 1:
-                (down,), token = stage_weights([down_proj], layer_idx + 1, [give])
-                taken, token = lax.optimization_barrier((taken, token))
-            held = held + taken.astype(jnp.float32)
-        if final:
-            return (pooled[:NODE_STEPS].astype(jnp.float32) + held).astype(jnp.bfloat16)
-        held = join_pair(held.astype(jnp.bfloat16), orders, last)
-        pooled = (pooled.astype(jnp.float32) + held).astype(jnp.bfloat16)
+        settled = []
+        for part, (held, give) in enumerate(sums):
+            for stage in range(last + 1 if final else last):
+                if stage:
+                    half = held.shape[0] // 2
+                    held, give = held[:half], held[half:].astype(jnp.bfloat16)
+                taken = swap_stage(give, orders, stage)
+                if not final and part == 0 and stage == 0:
+                    (down,), token = stage_weights([down_proj], layer_idx + 1, [give])
+                    taken, token = lax.optimization_barrier((taken, token))
+                held = held + taken.astype(jnp.float32)
+            if not final:
+                held = join_pair(held.astype(jnp.bfloat16), orders, last)
+            rows_kept = pooled[: held.shape[0], part * part_width : (part + 1) * part_width]
+            settled.append((rows_kept.astype(jnp.float32) + held).astype(jnp.bfloat16))
+        pooled = jnp.concatenate(settled, axis=1)
+        if not final:
+            (gate, up), token = stage_weights([gate_proj, up_proj], layer_idx + 1, [pooled, token])
+    return pooled
 
 
 def solution(mesh):

time: 172 us -> 165 us (0.959)
  waiting for transfers between devices: 87.5 us -> 63.8 us
  starting transfers between devices: 42.6 us -> 60.4 us
  local copies, waits for them, and re-layouts: 6.22 us -> 3.56 us
    all_to_all x1 -> x2, waiting for transfers between devices: 40.8 us -> 3.44 us  [exchange(): lax.all_to_all(block, 'gx', 0, 0, axis_index_groups=groups, tiled=True)]
    ppermute x19 -> x27, starting transfers between devices: 32.5 us -> 44.8 us  [swap_stage(): return lax.ppermute(block, ('gx', 'ta'), pairs)]
    ppermute x19 -> x27, waiting for transfers between devices: 38 us -> 49.1 us  [swap_stage(): return lax.ppermute(block, ('gx', 'ta'), pairs)]
    all_to_all x1 -> x2, starting transfers between devices: 3.63 us -> 9.15 us  [exchange(): lax.all_to_all(block, 'gx', 0, 0, axis_index_groups=groups, tiled=True)]
    unnamed x21, local copies, waits for them, and re-layouts: 6.1 us -> 3.43 us
    all_to_all x1, waiting for transfers between devices: 4.46 us -> 6.99 us  [per_device(): lax.all_to_all(queries, 'gx', 0, 0, axis_index_groups=groups, tiled=True)]
    pallas_call x2 -> x3, Pallas kernels: 2.66 us -> 4.68 us  [arrange(): pl.pallas_call(arrange_body, grid=(width // cols,), in_specs=[pl.BlockSpe...]
    pallas_call x5 -> x4, Pallas kernels: 16.9 us -> 15.3 us  [stage_weights(): pl.pallas_call(functools.partial(stage_body, layer=layer, count=len(held)...]
  transfers between devices with their start and end apart: 23 -> 32, of which waited for: 17 -> 23; matrix products, arithmetic and copies ran while one was open for 0% -> 1% of each run, Pallas kernels for 11% -> 15%
where the time goes in v7:
time: 165 us
  waiting for transfers between devices  63.8 us (39%)
  starting transfers between devices  60.4 us (37%)
  Pallas kernels  34.6 us (21%)
  local copies, waits for them, and re-layouts  3.56 us (2%)
  other arithmetic  1.74 us (1%)
    ppermute x27, waiting for transfers between devices, swap_stage(): return lax.ppermute(block, ('gx', 'ta'), pairs)  49.1 us
    ppermute x27, starting transfers between devices, swap_stage(): return lax.ppermute(block, ('gx', 'ta'), pairs)  44.8 us
    pallas_call x4, Pallas kernels, stage_weights(): pl.pallas_call(functools.partial(stage_body, layer=layer, count=len(held)...  15.3 us
    all_to_all x2, starting transfers between devices, exchange(): lax.all_to_all(block, 'gx', 0, 0, axis_index_groups=groups, tiled=True)  9.15 us
    all_to_all x1, waiting for transfers between devices, per_device(): lax.all_to_all(queries, 'gx', 0, 0, axis_index_groups=groups, tiled=True)  6.99 us
    all_to_all x1, starting transfers between devices, per_device(): lax.all_to_all(queries, 'gx', 0, 0, axis_index_groups=groups, tiled=True)  6.31 us
    pallas_call x2, Pallas kernels, expand(): pl.pallas_call(functools.partial(expand_body, layer=layer), in_specs=[pl....  5.37 us
    pallas_call x3, Pallas kernels, arrange(): pl.pallas_call(arrange_body, grid=(width // cols,), in_specs=[pl.BlockSpe...  4.68 us
  transfers between devices with their start and end apart: 32, of which 23 were waited for; matrix products, arithmetic and copies ran while one was open for 1% of the time, Pallas kernels for 15%

profile of v7, /device:TPU:0, one launch (start us, length us, event | category | flops | bytes accessed | tf_op | source)
XLA Modules:
  0.0 164.9 jit_solution(2589550568536577312)
XLA Ops:
  3.7 6.3 %all-to-all-start = ((bf16[8,16,2560]{2,1,0:T(8,128)(2,1)}), bf16[8,16,2560]{2,1,0:T(8,128)(2,1)S(1)}, u32[]{:S(2)}, u32[]{:S(2)}) async-start(bf16[8,16,2560]{2,1,0:T(8,128)(2,1)} %arrange.4), calls=%async_computation | async-start | bytes 1310720 | tf_op jit(solution)/shard_map/all_to_all | solution.py:403
  13.4 7.0 %all-to-all-done = bf16[8,16,2560]{2,1,0:T(8,128)(2,1)S(1)} async-done(((bf16[8,16,2560]{2,1,0:T(8,128)(2,1)}), bf16[8,16,2560]{2,1,0:T(8,128)(2,1)S(1)}, u32[]{:S(2)}, u32[]{:S(2)}) %all-to-all-start) | async-done | bytes 655392 | tf_op jit(solution)/shard_map/all_to_all | solution.py:403
  20.3 3.6 %all-to-all-start.1 = ((bf16[8,32,2560]{2,1,0:T(8,128)(2,1)}), bf16[8,32,2560]{2,1,0:T(8,128)(2,1)S(1)}, u32[]{:S(2)}, u32[]{:S(2)}) async-start(bf16[8,32,2560]{2,1,0:T(8,128)(2,1)} %arrange.3), calls=%async_computation.1 | async-start | bytes 2621440 | tf_op jit(solution)/shard_map/all_to_all | solution.py:412
  23.9 2.7 %collective-permute-start = (bf16[128,2560]{1,0:T(8,128)(2,1)S(1)}, bf16[128,2560]{1,0:T(8,128)(2,1)}, u32[]{:S(2)}, u32[]{:S(2)}) collective-permute-start(bf16[128,2560]{1,0:T(8,128)(2,1)S(1)} %bitcast.20), channel_id=1, source_target_pairs={{0,16},{1,17},{2,18},{3,19},{4,20},{5,21},{6,22},{7,23},{8,24},{9,... | collective-permute-start | bytes 1966088 | tf_op jit(solution)/shard_map/ppermute | solution.py:46
  28.3 23.2 %collective-permute-done.far_ref = bf16[128,2560]{1,0:T(8,128)(2,1)} collective-permute-done((bf16[128,2560]{1,0:T(8,128)(2,1)S(1)}, bf16[128,2560]{1,0:T(8,128)(2,1)}, u32[]{:S(2)}, u32[]{:S(2)}) %collective-permute-start) | collective-permute-done | bytes 655392 | tf_op jit(solution)/shard_map/ppermute | solution.py:46
  51.5 2.4 %all-to-all-done.1 = bf16[8,32,2560]{2,1,0:T(8,128)(2,1)S(1)} async-done(((bf16[8,32,2560]{2,1,0:T(8,128)(2,1)}), bf16[8,32,2560]{2,1,0:T(8,128)(2,1)S(1)}, u32[]{:S(2)}, u32[]{:S(2)}) %all-to-all-start.1) | async-done | bytes 1310752 | tf_op jit(solution)/shard_map/all_to_all | solution.py:412
  53.9 5.6 %all-to-all-start.2 = ((bf16[8,32,2560]{2,1,0:T(8,128)(2,1)}), bf16[8,32,2560]{2,1,0:T(8,128)(2,1)S(1)}, u32[]{:S(2)}, u32[]{:S(2)}) async-start(bf16[8,32,2560]{2,1,0:T(8,128)(2,1)} %arrange.5), calls=%async_computation.2 | async-start | bytes 2621440 | tf_op jit(solution)/shard_map/all_to_all | solution.py:412
  60.0 4.0 %half_scores.1 = (bf16[20,2,128,128]{3,2,1,0:T(8,128)(2,1)S(1)}, f32[128,128]{1,0:T(8,128)S(1)}) custom-call(bf16[128,2560]{1,0:T(8,128)(2,1)} %bitcast.21, bf16[128,2560]{1,0:T(8,128)(2,1)} %collective-permute-done.far_ref, bf16[8,2,16,2560]{3,2,1,0:T(8,128)(2,1)S(1)} %bitcast.16), custom_call_target="tpu_custom_call" | custom-call | tf_op jit(solution)/shard_map/half_scores/pallas_call | solution.py:143
  64.1 2.5 %collective-permute-start.1 = (f32[128,128]{1,0:T(8,128)S(1)}, f32[128,128]{1,0:T(8,128)S(1)}, u32[]{:S(2)}, u32[]{:S(2)}) collective-permute-start(f32[128,128]{1,0:T(8,128)S(1)} %get-tuple-element.43.lse_ref), channel_id=1, source_target_pairs={{0,16},{1,17},{2,18},{3,19},{4,20},{5,21},{6,22},{7,23},{8,24},{9,... | collective-permute-start | bytes 196616 | tf_op jit(solution)/shard_map/ppermute | solution.py:46
  66.6 6.9 %collective-permute-done.1.far_ref = f32[128,128]{1,0:T(8,128)S(1)} collective-permute-done((f32[128,128]{1,0:T(8,128)S(1)}, f32[128,128]{1,0:T(8,128)S(1)}, u32[]{:S(2)}, u32[]{:S(2)}) %collective-permute-start.1) | collective-permute-done | bytes 65568 | tf_op jit(solution)/shard_map/ppermute | solution.py:46
  76.9 2.4 %collective-permute-start.2 = (bf16[16,2560]{1,0:T(8,128)(2,1)S(1)}, bf16[16,2560]{1,0:T(8,128)(2,1)S(1)}, u32[]{:S(2)}, u32[]{:S(2)}) collective-permute-start(bf16[16,2560]{1,0:T(8,128)(2,1)S(1)} %half_pool.1.refs_1_), channel_id=1, source_target_pairs={{0,16},{1,17},{2,18},{3,19},{4,20},{5,21},{6,22},{7,23},{8,24},{9,... | collective-permute-start | bytes 245768 | tf_op jit(solution)/shard_map/ppermute | solution.py:46
  79.3 2.9 %stage_weights.4 = (bf16[2560,1280]{1,0:T(8,128)(2,1)S(1)}, f32[8,128]{1,0:T(8,128)S(1)}) custom-call(bf16[2,2560,1280]{2,1,0:T(8,128)(2,1)} %refs_0_.7, bf16[16,2560]{1,0:T(8,128)(2,1)S(1)} %half_pool.1.refs_1_), custom_call_target="tpu_custom_call" | custom-call | bytes 13107200 | tf_op jit(solution)/shard_map/stage_weights/pallas_call | solution.py:249
  82.4 2.9 %collective-permute-start.3 = (bf16[16,2560]{1,0:T(8,128)(2,1)S(1)}, bf16[16,2560]{1,0:T(8,128)(2,1)S(1)}, u32[]{:S(2)}, u32[]{:S(2)}) collective-permute-start(bf16[16,2560]{1,0:T(8,128)(2,1)S(1)} %add_convert_fusion), channel_id=1, source_target_pairs={{0,8},{1,9},{2,10},{3,11},{4,12},{5,13},{6,14},{7,15},{8,0},{9,1},... | collective-permute-start | bytes 245768 | tf_op jit(solution)/shard_map/ppermute | solution.py:46
  85.3 2.4 %collective-permute-done.3 = bf16[16,2560]{1,0:T(8,128)(2,1)S(1)} collective-permute-done((bf16[16,2560]{1,0:T(8,128)(2,1)S(1)}, bf16[16,2560]{1,0:T(8,128)(2,1)S(1)}, u32[]{:S(2)}, u32[]{:S(2)}) %collective-permute-start.3) | collective-permute-done | bytes 81952 | tf_op jit(solution)/shard_map/ppermute | solution.py:46
  87.7 2.7 %collective-permute-start.6 = (bf16[32,2560]{1,0:T(8,128)(2,1)S(1)}, bf16[32,2560]{1,0:T(8,128)(2,1)S(1)}, u32[]{:S(2)}, u32[]{:S(2)}) collective-permute-start(bf16[32,2560]{1,0:T(8,128)(2,1)S(1)} %constant_dynamic-update-slice_fusion.refs_0_), channel_id=1, source_target_pairs={{0,6},{1,7},{2,4},{3,5},{4,2},{5,3},{6,0},{7,1},{8,14},{9,15},{10,... | collective-permute-start | bytes 491528 | tf_op jit(solution)/shard_map/ppermute | solution.py:46
  91.3 4.8 %stage_weights.5 = (bf16[2560,1280]{1,0:T(8,128)(2,1)S(1)}, bf16[1280,2560]{1,0:T(8,128)(2,1)S(1)}, f32[8,128]{1,0:T(8,128)S(1)}) custom-call(bf16[2,2560,1280]{2,1,0:T(8,128)(2,1)} %refs_1_.3, bf16[2,1280,2560]{2,1,0:T(8,128)(2,1)} %refs_0_.6, f32[8,128]{1,0:T(8,128)S(1)} %get-tuple-element.50.refs_2_), custom_call_target="tpu_custom_call" | custom-call | bytes 26214400 | tf_op jit(solution)/shard_map/stage_weights/pallas_call | solution.py:249
  96.1 2.7 %expand.2.near_ref = bf16[128,2688]{1,0:T(8,128)(2,1)S(1)} custom-call(bf16[32,2560]{1,0:T(8,128)(2,1)S(1)} %constant_dynamic-update-slice_fusion.refs_0_, bf16[32,2560]{1,0:T(8,128)(2,1)S(1)} %collective-permute-done.4.refs_1_, bf16[32,2560]{1,0:T(8,128)(2,1)S(1)} %collective-permute-done.5.refs_2_, bf16[32,2560]{1,0:T(8,128)(2,1)S(1)} %collective-permute-done.6.refs_3_, ...), custom_call_target="tpu_custom_call" | custom-call | tf_op jit(solution)/shard_map/expand/pallas_call | solution.py:304
  98.9 2.1 %collective-permute-done.7.far_ref = bf16[128,2688]{1,0:T(8,128)(2,1)S(1)} collective-permute-done((bf16[128,2688]{1,0:T(8,128)(2,1)S(1)}, bf16[128,2688]{1,0:T(8,128)(2,1)S(1)}, u32[]{:S(2)}, u32[]{:S(2)}) %collective-permute-start.7) | collective-permute-done | bytes 688160 | tf_op jit(solution)/shard_map/ppermute | solution.py:454
  102.4 1.9 %collective-permute-start.12 = (bf16[64,1280]{1,0:T(8,128)(2,1)S(1)}, bf16[64,1280]{1,0:T(8,128)(2,1)S(1)}, u32[]{:S(2)}, u32[]{:S(2)}) collective-permute-start(bf16[64,1280]{1,0:T(8,128)(2,1)S(1)} %get-tuple-element.59), channel_id=1, source_target_pairs={{0,2},{1,5},{2,0},{3,7},{4,6},{5,1},{6,4},{7,3},{8,10},{9,13},{10,... | collective-permute-start | bytes 491528 | tf_op jit(solution)/shard_map/ppermute | solution.py:46
  104.5 2.9 %stage_weights.6 = (bf16[1280,2560]{1,0:T(8,128)(2,1)S(1)}, f32[8,128]{1,0:T(8,128)S(1)}) custom-call(bf16[2,1280,2560]{2,1,0:T(8,128)(2,1)} %refs_0_.6, bf16[64,1280]{1,0:T(8,128)(2,1)S(1)} %get-tuple-element.55.refs_1_), custom_call_target="tpu_custom_call" | custom-call | bytes 13107200 | tf_op jit(solution)/shard_map/stage_weights/pallas_call | solution.py:249
  112.4 2.1 %collective-permute-start.14 = (bf16[16,1280]{1,0:T(8,128)(2,1)S(1)}, bf16[16,1280]{1,0:T(8,128)(2,1)S(1)}, u32[]{:S(2)}, u32[]{:S(2)}) collective-permute-start(bf16[16,1280]{1,0:T(8,128)(2,1)S(1)} %slice.210), channel_id=1, source_target_pairs={{0,8},{1,9},{2,10},{3,11},{4,12},{5,13},{6,14},{7,15},{8,0},{9,1},... | collective-permute-start | bytes 122888 | tf_op jit(solution)/shard_map/ppermute | solution.py:46
  116.5 2.3 %collective-permute-start.15 = (bf16[16,1280]{1,0:T(8,128)(2,1)S(1)}, bf16[16,1280]{1,0:T(8,128)(2,1)S(1)}, u32[]{:S(2)}, u32[]{:S(2)}) collective-permute-start(bf16[16,1280]{1,0:T(8,128)(2,1)S(1)} %fusion.3), channel_id=1, source_target_pairs={{0,16},{1,17},{2,18},{3,19},{4,20},{5,21},{6,22},{7,23},{8,24},{9,... | collective-permute-start | bytes 122888 | tf_op jit(solution)/shard_map/ppermute | solution.py:46
  121.5 2.4 %collective-permute-done.11 = bf16[16,1280]{1,0:T(8,128)(2,1)S(1)} collective-permute-done((bf16[16,1280]{1,0:T(8,128)(2,1)S(1)}, bf16[16,1280]{1,0:T(8,128)(2,1)S(1)}, u32[]{:S(2)}, u32[]{:S(2)}) %collective-permute-start.11) | collective-permute-done | bytes 40992 | tf_op jit(solution)/shard_map/ppermute | solution.py:46
  125.7 2.7 %collective-permute-done.16 = bf16[16,2560]{1,0:T(8,128)(2,1)S(1)} collective-permute-done((bf16[16,2560]{1,0:T(8,128)(2,1)S(1)}, bf16[16,2560]{1,0:T(8,128)(2,1)S(1)}, u32[]{:S(2)}, u32[]{:S(2)}) %collective-permute-start.16) | collective-permute-done | bytes 81952 | tf_op jit(solution)/shard_map/ppermute | solution.py:46
  128.5 2.7 %collective-permute-start.19 = (bf16[32,2560]{1,0:T(8,128)(2,1)S(1)}, bf16[32,2560]{1,0:T(8,128)(2,1)S(1)}, u32[]{:S(2)}, u32[]{:S(2)}) collective-permute-start(bf16[32,2560]{1,0:T(8,128)(2,1)S(1)} %pad_maximum_fusion.refs_0_), channel_id=1, source_target_pairs={{0,6},{1,7},{2,4},{3,5},{4,2},{5,3},{6,0},{7,1},{8,14},{9,15},{10,... | collective-permute-start | bytes 491528 | tf_op jit(solution)/shard_map/ppermute | solution.py:46
  132.0 4.8 %stage_weights.7 = (bf16[2560,1280]{1,0:T(8,128)(2,1)S(1)}, bf16[2560,1280]{1,0:T(8,128)(2,1)S(1)}, f32[8,128]{1,0:T(8,128)S(1)}) custom-call(bf16[2,2560,1280]{2,1,0:T(8,128)(2,1)} %refs_0_.7, bf16[2,2560,1280]{2,1,0:T(8,128)(2,1)} %refs_1_.3, bf16[16,2560]{1,0:T(8,128)(2,1)S(1)} %pad_maximum_fusion.1.refs_2_, f32[8,128]{1,0:T(8,128)S(1)} %get-tuple-element.60.refs_3_), custom_call_target="tpu_custom_call" | custom-call | bytes 26214400 | tf_op jit(solution)/shard_map/stage_weights/pallas_call | solution.py:249
  136.8 2.6 %expand.3.near_ref = bf16[128,2688]{1,0:T(8,128)(2,1)S(1)} custom-call(bf16[32,2560]{1,0:T(8,128)(2,1)S(1)} %pad_maximum_fusion.refs_0_, bf16[32,2560]{1,0:T(8,128)(2,1)S(1)} %collective-permute-done.17.refs_1_, bf16[32,2560]{1,0:T(8,128)(2,1)S(1)} %collective-permute-done.18.refs_2_, bf16[32,2560]{1,0:T(8,128)(2,1)S(1)} %collective-permute-done.19.refs_3_, ...), custom_call_target="tpu_custom_call" | custom-call | tf_op jit(solution)/shard_map/expand/pallas_call | solution.py:304
  139.6 2.1 %collective-permute-done.20.far_ref = bf16[128,2688]{1,0:T(8,128)(2,1)S(1)} collective-permute-done((bf16[128,2688]{1,0:T(8,128)(2,1)S(1)}, bf16[128,2688]{1,0:T(8,128)(2,1)S(1)}, u32[]{:S(2)}, u32[]{:S(2)}) %collective-permute-start.20) | collective-permute-done | bytes 688160 | tf_op jit(solution)/shard_map/ppermute | solution.py:454
  143.1 1.9 %collective-permute-start.21 = (bf16[64,1280]{1,0:T(8,128)(2,1)S(1)}, bf16[64,1280]{1,0:T(8,128)(2,1)S(1)}, u32[]{:S(2)}, u32[]{:S(2)}) collective-permute-start(bf16[64,1280]{1,0:T(8,128)(2,1)S(1)} %get-tuple-element.66), channel_id=1, source_target_pairs={{0,2},{1,5},{2,0},{3,7},{4,6},{5,1},{6,4},{7,3},{8,10},{9,13},{10,... | collective-permute-start | bytes 491528 | tf_op jit(solution)/shard_map/ppermute | solution.py:46
  145.2 3.3 %collective-permute-done.21 = bf16[64,1280]{1,0:T(8,128)(2,1)S(1)} collective-permute-done((bf16[64,1280]{1,0:T(8,128)(2,1)S(1)}, bf16[64,1280]{1,0:T(8,128)(2,1)S(1)}, u32[]{:S(2)}, u32[]{:S(2)}) %collective-permute-start.21) | collective-permute-done | bytes 163872 | tf_op jit(solution)/shard_map/ppermute | solution.py:46
  157.2 2.3 %collective-permute-start.24 = (bf16[8,1280]{1,0:T(8,128)(2,1)S(1)}, bf16[8,1280]{1,0:T(8,128)(2,1)S(1)}, u32[]{:S(2)}, u32[]{:S(2)}) collective-permute-start(bf16[8,1280]{1,0:T(8,128)(2,1)S(1)} %slice.213), channel_id=1, source_target_pairs={{0,16},{1,17},{2,18},{3,19},{4,20},{5,21},{6,22},{7,23},{8,24},{9,... | collective-permute-start | bytes 61448 | tf_op jit(solution)/shard_map/ppermute | solution.py:46
  162.0 2.3 %collective-permute-done.28 = bf16[8,1280]{1,0:T(8,128)(2,1)S(1)} collective-permute-done((bf16[8,1280]{1,0:T(8,128)(2,1)S(1)}, bf16[8,1280]{1,0:T(8,128)(2,1)S(1)}, u32[]{:S(2)}, u32[]{:S(2)}) %collective-permute-start.28) | collective-permute-done | bytes 20512 | tf_op jit(solution)/shard_map/ppermute | solution.py:46
  (123 shorter events, 41.0 us)
Async XLA Ops:
  3.7 16.7 %all-to-all-start = ((bf16[8,16,2560]{2,1,0:T(8,128)(2,1)}), bf16[8,16,2560]{2,1,0:T(8,128)(2,1)S(1)}, u32[]{:S(2)}, u32[]{:S(2)}) async-start(bf16[8,16,2560]{2,1,0:T(8,128)(2,1)} %arrange.4), calls=%async_computation | async-start | bytes 1310720 | tf_op jit(solution)/shard_map/all_to_all | solution.py:403
  20.3 33.5 %all-to-all-start.1 = ((bf16[8,32,2560]{2,1,0:T(8,128)(2,1)}), bf16[8,32,2560]{2,1,0:T(8,128)(2,1)S(1)}, u32[]{:S(2)}, u32[]{:S(2)}) async-start(bf16[8,32,2560]{2,1,0:T(8,128)(2,1)} %arrange.3), calls=%async_computation.1 | async-start | bytes 2621440 | tf_op jit(solution)/shard_map/all_to_all | solution.py:412
  23.9 27.6 %collective-permute-start = (bf16[128,2560]{1,0:T(8,128)(2,1)S(1)}, bf16[128,2560]{1,0:T(8,128)(2,1)}, u32[]{:S(2)}, u32[]{:S(2)}) collective-permute-start(bf16[128,2560]{1,0:T(8,128)(2,1)S(1)} %bitcast.20), channel_id=1, source_target_pairs={{0,16},{1,17},{2,18},{3,19},{4,20},{5,21},{6,22},{7,23},{8,24},{9,... | collective-permute-start | bytes 1966088 | tf_op jit(solution)/shard_map/ppermute | solution.py:46
  53.9 22.1 %all-to-all-start.2 = ((bf16[8,32,2560]{2,1,0:T(8,128)(2,1)}), bf16[8,32,2560]{2,1,0:T(8,128)(2,1)S(1)}, u32[]{:S(2)}, u32[]{:S(2)}) async-start(bf16[8,32,2560]{2,1,0:T(8,128)(2,1)} %arrange.5), calls=%async_computation.2 | async-start | bytes 2621440 | tf_op jit(solution)/shard_map/all_to_all | solution.py:412
  64.1 9.4 %collective-permute-start.1 = (f32[128,128]{1,0:T(8,128)S(1)}, f32[128,128]{1,0:T(8,128)S(1)}, u32[]{:S(2)}, u32[]{:S(2)}) collective-permute-start(f32[128,128]{1,0:T(8,128)S(1)} %get-tuple-element.43.lse_ref), channel_id=1, source_target_pairs={{0,16},{1,17},{2,18},{3,19},{4,20},{5,21},{6,22},{7,23},{8,24},{9,... | collective-permute-start | bytes 196616 | tf_op jit(solution)/shard_map/ppermute | solution.py:46
  76.9 5.5 %collective-permute-start.2 = (bf16[16,2560]{1,0:T(8,128)(2,1)S(1)}, bf16[16,2560]{1,0:T(8,128)(2,1)S(1)}, u32[]{:S(2)}, u32[]{:S(2)}) collective-permute-start(bf16[16,2560]{1,0:T(8,128)(2,1)S(1)} %half_pool.1.refs_1_), channel_id=1, source_target_pairs={{0,16},{1,17},{2,18},{3,19},{4,20},{5,21},{6,22},{7,23},{8,24},{9,... | collective-permute-start | bytes 245768 | tf_op jit(solution)/shard_map/ppermute | solution.py:46
  82.4 5.3 %collective-permute-start.3 = (bf16[16,2560]{1,0:T(8,128)(2,1)S(1)}, bf16[16,2560]{1,0:T(8,128)(2,1)S(1)}, u32[]{:S(2)}, u32[]{:S(2)}) collective-permute-start(bf16[16,2560]{1,0:T(8,128)(2,1)S(1)} %add_convert_fusion), channel_id=1, source_target_pairs={{0,8},{1,9},{2,10},{3,11},{4,12},{5,13},{6,14},{7,15},{8,0},{9,1},... | collective-permute-start | bytes 245768 | tf_op jit(solution)/shard_map/ppermute | solution.py:46
  87.7 8.3 %collective-permute-start.6 = (bf16[32,2560]{1,0:T(8,128)(2,1)S(1)}, bf16[32,2560]{1,0:T(8,128)(2,1)S(1)}, u32[]{:S(2)}, u32[]{:S(2)}) collective-permute-start(bf16[32,2560]{1,0:T(8,128)(2,1)S(1)} %constant_dynamic-update-slice_fusion.refs_0_), channel_id=1, source_target_pairs={{0,6},{1,7},{2,4},{3,5},{4,2},{5,3},{6,0},{7,1},{8,14},{9,15},{10,... | collective-permute-start | bytes 491528 | tf_op jit(solution)/shard_map/ppermute | solution.py:46
  90.4 5.7 %collective-permute-start.5 = (bf16[32,2560]{1,0:T(8,128)(2,1)S(1)}, bf16[32,2560]{1,0:T(8,128)(2,1)S(1)}, u32[]{:S(2)}, u32[]{:S(2)}) collective-permute-start(bf16[32,2560]{1,0:T(8,128)(2,1)S(1)} %constant_dynamic-update-slice_fusion.refs_0_), channel_id=1, source_target_pairs={{0,2},{1,5},{2,0},{3,7},{4,6},{5,1},{6,4},{7,3},{8,10},{9,13},{10,... | collective-permute-start | bytes 491528 | tf_op jit(solution)/shard_map/ppermute | solution.py:46
  90.5 5.5 %collective-permute-start.4 = (bf16[32,2560]{1,0:T(8,128)(2,1)S(1)}, bf16[32,2560]{1,0:T(8,128)(2,1)S(1)}, u32[]{:S(2)}, u32[]{:S(2)}) collective-permute-start(bf16[32,2560]{1,0:T(8,128)(2,1)S(1)} %constant_dynamic-update-slice_fusion.refs_0_), channel_id=1, source_target_pairs={{0,4},{1,3},{2,6},{3,1},{4,0},{5,7},{6,2},{7,5},{8,12},{9,11},{10,... | collective-permute-start | bytes 491528 | tf_op jit(solution)/shard_map/ppermute | solution.py:46
  98.8 2.2 %collective-permute-start.7 = (bf16[128,2688]{1,0:T(8,128)(2,1)S(1)}, bf16[128,2688]{1,0:T(8,128)(2,1)S(1)}, u32[]{:S(2)}, u32[]{:S(2)}) collective-permute-start(bf16[128,2688]{1,0:T(8,128)(2,1)S(1)} %expand.2.near_ref), channel_id=1, source_target_pairs={{0,1},{1,0},{2,3},{3,2},{4,5},{5,4},{6,7},{7,6},{8,9},{9,8},{10,11... | collective-permute-start | bytes 2064392 | tf_op jit(solution)/shard_map/ppermute | solution.py:454
  102.4 5.4 %collective-permute-start.12 = (bf16[64,1280]{1,0:T(8,128)(2,1)S(1)}, bf16[64,1280]{1,0:T(8,128)(2,1)S(1)}, u32[]{:S(2)}, u32[]{:S(2)}) collective-permute-start(bf16[64,1280]{1,0:T(8,128)(2,1)S(1)} %get-tuple-element.59), channel_id=1, source_target_pairs={{0,2},{1,5},{2,0},{3,7},{4,6},{5,1},{6,4},{7,3},{8,10},{9,13},{10,... | collective-permute-start | bytes 491528 | tf_op jit(solution)/shard_map/ppermute | solution.py:46
  104.4 5.3 %collective-permute-start.8 = (bf16[64,1280]{1,0:T(8,128)(2,1)S(1)}, bf16[64,1280]{1,0:T(8,128)(2,1)S(1)}, u32[]{:S(2)}, u32[]{:S(2)}) collective-permute-start(bf16[64,1280]{1,0:T(8,128)(2,1)S(1)} %get-tuple-element.55.refs_1_), channel_id=1, source_target_pairs={{0,2},{1,5},{2,0},{3,7},{4,6},{5,1},{6,4},{7,3},{8,10},{9,13},{10,... | collective-permute-start | bytes 491528 | tf_op jit(solution)/shard_map/ppermute | solution.py:46
  107.9 4.5 %collective-permute-start.13 = (bf16[32,1280]{1,0:T(8,128)(2,1)S(1)}, bf16[32,1280]{1,0:T(8,128)(2,1)S(1)}, u32[]{:S(2)}, u32[]{:S(2)}) collective-permute-start(bf16[32,1280]{1,0:T(8,128)(2,1)S(1)} %slice.206), channel_id=1, source_target_pairs={{0,4},{1,3},{2,6},{3,1},{4,0},{5,7},{6,2},{7,5},{8,12},{9,11},{10,... | collective-permute-start | bytes 245768 | tf_op jit(solution)/shard_map/ppermute | solution.py:46
  109.8 4.7 %collective-permute-start.9 = (bf16[32,1280]{1,0:T(8,128)(2,1)S(1)}, bf16[32,1280]{1,0:T(8,128)(2,1)S(1)}, u32[]{:S(2)}, u32[]{:S(2)}) collective-permute-start(bf16[32,1280]{1,0:T(8,128)(2,1)S(1)} %slice.207), channel_id=1, source_target_pairs={{0,4},{1,3},{2,6},{3,1},{4,0},{5,7},{6,2},{7,5},{8,12},{9,11},{10,... | collective-permute-start | bytes 245768 | tf_op jit(solution)/shard_map/ppermute | solution.py:46
  112.4 4.1 %collective-permute-start.14 = (bf16[16,1280]{1,0:T(8,128)(2,1)S(1)}, bf16[16,1280]{1,0:T(8,128)(2,1)S(1)}, u32[]{:S(2)}, u32[]{:S(2)}) collective-permute-start(bf16[16,1280]{1,0:T(8,128)(2,1)S(1)} %slice.210), channel_id=1, source_target_pairs={{0,8},{1,9},{2,10},{3,11},{4,12},{5,13},{6,14},{7,15},{8,0},{9,1},... | collective-permute-start | bytes 122888 | tf_op jit(solution)/shard_map/ppermute | solution.py:46
  114.5 4.3 %collective-permute-start.10 = (bf16[16,1280]{1,0:T(8,128)(2,1)S(1)}, bf16[16,1280]{1,0:T(8,128)(2,1)S(1)}, u32[]{:S(2)}, u32[]{:S(2)}) collective-permute-start(bf16[16,1280]{1,0:T(8,128)(2,1)S(1)} %slice.211), channel_id=1, source_target_pairs={{0,8},{1,9},{2,10},{3,11},{4,12},{5,13},{6,14},{7,15},{8,0},{9,1},... | collective-permute-start | bytes 122888 | tf_op jit(solution)/shard_map/ppermute | solution.py:46
  116.5 5.0 %collective-permute-start.15 = (bf16[16,1280]{1,0:T(8,128)(2,1)S(1)}, bf16[16,1280]{1,0:T(8,128)(2,1)S(1)}, u32[]{:S(2)}, u32[]{:S(2)}) collective-permute-start(bf16[16,1280]{1,0:T(8,128)(2,1)S(1)} %fusion.3), channel_id=1, source_target_pairs={{0,16},{1,17},{2,18},{3,19},{4,20},{5,21},{6,22},{7,23},{8,24},{9,... | collective-permute-start | bytes 122888 | tf_op jit(solution)/shard_map/ppermute | solution.py:46
  118.9 5.0 %collective-permute-start.11 = (bf16[16,1280]{1,0:T(8,128)(2,1)S(1)}, bf16[16,1280]{1,0:T(8,128)(2,1)S(1)}, u32[]{:S(2)}, u32[]{:S(2)}) collective-permute-start(bf16[16,1280]{1,0:T(8,128)(2,1)S(1)} %fusion.4), channel_id=1, source_target_pairs={{0,16},{1,17},{2,18},{3,19},{4,20},{5,21},{6,22},{7,23},{8,24},{9,... | collective-permute-start | bytes 122888 | tf_op jit(solution)/shard_map/ppermute | solution.py:46
  124.0 4.5 %collective-permute-start.16 = (bf16[16,2560]{1,0:T(8,128)(2,1)S(1)}, bf16[16,2560]{1,0:T(8,128)(2,1)S(1)}, u32[]{:S(2)}, u32[]{:S(2)}) collective-permute-start(bf16[16,2560]{1,0:T(8,128)(2,1)S(1)} %pad_maximum_fusion.1.refs_2_), channel_id=1, source_target_pairs={{0,8},{1,9},{2,10},{3,11},{4,12},{5,13},{6,14},{7,15},{8,0},{9,1},... | collective-permute-start | bytes 245768 | tf_op jit(solution)/shard_map/ppermute | solution.py:46
  128.5 8.3 %collective-permute-start.19 = (bf16[32,2560]{1,0:T(8,128)(2,1)S(1)}, bf16[32,2560]{1,0:T(8,128)(2,1)S(1)}, u32[]{:S(2)}, u32[]{:S(2)}) collective-permute-start(bf16[32,2560]{1,0:T(8,128)(2,1)S(1)} %pad_maximum_fusion.refs_0_), channel_id=1, source_target_pairs={{0,6},{1,7},{2,4},{3,5},{4,2},{5,3},{6,0},{7,1},{8,14},{9,15},{10,... | collective-permute-start | bytes 491528 | tf_op jit(solution)/shard_map/ppermute | solution.py:46
  131.2 5.7 %collective-permute-start.18 = (bf16[32,2560]{1,0:T(8,128)(2,1)S(1)}, bf16[32,2560]{1,0:T(8,128)(2,1)S(1)}, u32[]{:S(2)}, u32[]{:S(2)}) collective-permute-start(bf16[32,2560]{1,0:T(8,128)(2,1)S(1)} %pad_maximum_fusion.refs_0_), channel_id=1, source_target_pairs={{0,2},{1,5},{2,0},{3,7},{4,6},{5,1},{6,4},{7,3},{8,10},{9,13},{10,... | collective-permute-start | bytes 491528 | tf_op jit(solution)/shard_map/ppermute | solution.py:46
  131.3 5.5 %collective-permute-start.17 = (bf16[32,2560]{1,0:T(8,128)(2,1)S(1)}, bf16[32,2560]{1,0:T(8,128)(2,1)S(1)}, u32[]{:S(2)}, u32[]{:S(2)}) collective-permute-start(bf16[32,2560]{1,0:T(8,128)(2,1)S(1)} %pad_maximum_fusion.refs_0_), channel_id=1, source_target_pairs={{0,4},{1,3},{2,6},{3,1},{4,0},{5,7},{6,2},{7,5},{8,12},{9,11},{10,... | collective-permute-start | bytes 491528 | tf_op jit(solution)/shard_map/ppermute | solution.py:46
  139.5 2.2 %collective-permute-start.20 = (bf16[128,2688]{1,0:T(8,128)(2,1)S(1)}, bf16[128,2688]{1,0:T(8,128)(2,1)S(1)}, u32[]{:S(2)}, u32[]{:S(2)}) collective-permute-start(bf16[128,2688]{1,0:T(8,128)(2,1)S(1)} %expand.3.near_ref), channel_id=1, source_target_pairs={{0,1},{1,0},{2,3},{3,2},{4,5},{5,4},{6,7},{7,6},{8,9},{9,8},{10,11... | collective-permute-start | bytes 2064392 | tf_op jit(solution)/shard_map/ppermute | solution.py:454
  143.1 5.4 %collective-permute-start.21 = (bf16[64,1280]{1,0:T(8,128)(2,1)S(1)}, bf16[64,1280]{1,0:T(8,128)(2,1)S(1)}, u32[]{:S(2)}, u32[]{:S(2)}) collective-permute-start(bf16[64,1280]{1,0:T(8,128)(2,1)S(1)} %get-tuple-element.66), channel_id=1, source_target_pairs={{0,2},{1,5},{2,0},{3,7},{4,6},{5,1},{6,4},{7,3},{8,10},{9,13},{10,... | collective-permute-start | bytes 491528 | tf_op jit(solution)/shard_map/ppermute | solution.py:46
  145.0 5.3 %collective-permute-start.25 = (bf16[64,1280]{1,0:T(8,128)(2,1)S(1)}, bf16[64,1280]{1,0:T(8,128)(2,1)S(1)}, u32[]{:S(2)}, u32[]{:S(2)}) collective-permute-start(bf16[64,1280]{1,0:T(8,128)(2,1)S(1)} %get-tuple-element.68), channel_id=1, source_target_pairs={{0,2},{1,5},{2,0},{3,7},{4,6},{5,1},{6,4},{7,3},{8,10},{9,13},{10,... | collective-permute-start | bytes 491528 | tf_op jit(solution)/shard_map/ppermute | solution.py:46
  148.6 4.5 %collective-permute-start.22 = (bf16[32,1280]{1,0:T(8,128)(2,1)S(1)}, bf16[32,1280]{1,0:T(8,128)(2,1)S(1)}, u32[]{:S(2)}, u32[]{:S(2)}) collective-permute-start(bf16[32,1280]{1,0:T(8,128)(2,1)S(1)} %slice.205), channel_id=1, source_target_pairs={{0,4},{1,3},{2,6},{3,1},{4,0},{5,7},{6,2},{7,5},{8,12},{9,11},{10,... | collective-permute-start | bytes 245768 | tf_op jit(solution)/shard_map/ppermute | solution.py:46
  150.4 4.5 %collective-permute-start.26 = (bf16[32,1280]{1,0:T(8,128)(2,1)S(1)}, bf16[32,1280]{1,0:T(8,128)(2,1)S(1)}, u32[]{:S(2)}, u32[]{:S(2)}) collective-permute-start(bf16[32,1280]{1,0:T(8,128)(2,1)S(1)} %slice.204), channel_id=1, source_target_pairs={{0,4},{1,3},{2,6},{3,1},{4,0},{5,7},{6,2},{7,5},{8,12},{9,11},{10,... | collective-permute-start | bytes 245768 | tf_op jit(solution)/shard_map/ppermute | solution.py:46
  153.1 4.1 %collective-permute-start.23 = (bf16[16,1280]{1,0:T(8,128)(2,1)S(1)}, bf16[16,1280]{1,0:T(8,128)(2,1)S(1)}, u32[]{:S(2)}, u32[]{:S(2)}) collective-permute-start(bf16[16,1280]{1,0:T(8,128)(2,1)S(1)} %slice.209), channel_id=1, source_target_pairs={{0,8},{1,9},{2,10},{3,11},{4,12},{5,13},{6,14},{7,15},{8,0},{9,1},... | collective-permute-start | bytes 122888 | tf_op jit(solution)/shard_map/ppermute | solution.py:46
  155.0 4.5 %collective-permute-start.27 = (bf16[16,1280]{1,0:T(8,128)(2,1)S(1)}, bf16[16,1280]{1,0:T(8,128)(2,1)S(1)}, u32[]{:S(2)}, u32[]{:S(2)}) collective-permute-start(bf16[16,1280]{1,0:T(8,128)(2,1)S(1)} %slice.208), channel_id=1, source_target_pairs={{0,8},{1,9},{2,10},{3,11},{4,12},{5,13},{6,14},{7,15},{8,0},{9,1},... | collective-permute-start | bytes 122888 | tf_op jit(solution)/shard_map/ppermute | solution.py:46
  157.2 4.7 %collective-permute-start.24 = (bf16[8,1280]{1,0:T(8,128)(2,1)S(1)}, bf16[8,1280]{1,0:T(8,128)(2,1)S(1)}, u32[]{:S(2)}, u32[]{:S(2)}) collective-permute-start(bf16[8,1280]{1,0:T(8,128)(2,1)S(1)} %slice.213), channel_id=1, source_target_pairs={{0,16},{1,17},{2,18},{3,19},{4,20},{5,21},{6,22},{7,23},{8,24},{9,... | collective-permute-start | bytes 61448 | tf_op jit(solution)/shard_map/ppermute | solution.py:46
  159.5 4.7 %collective-permute-start.28 = (bf16[8,1280]{1,0:T(8,128)(2,1)S(1)}, bf16[8,1280]{1,0:T(8,128)(2,1)S(1)}, u32[]{:S(2)}, u32[]{:S(2)}) collective-permute-start(bf16[8,1280]{1,0:T(8,128)(2,1)S(1)} %slice.212), channel_id=1, source_target_pairs={{0,16},{1,17},{2,18},{3,19},{4,20},{5,21},{6,22},{7,23},{8,24},{9,... | collective-permute-start | bytes 61448 | tf_op jit(solution)/shard_map/ppermute | solution.py:46
  (10 other events, 227.8 us)

commit v8 on v7

--- a/solution.py
+++ b/solution.py
@@ -64,45 +64,43 @@
     return mine.astype(jnp.float32) + taken.astype(jnp.float32)
 
 
-def arrange_body(pick_ref, *refs):
-    sources, out_ref = refs[:-1], refs[-1]
-    chunks, rows, cols = out_ref.shape
-    part = rows // len(sources)
-    pick = pick_ref[...]
-    for side, ref in enumerate(sources):
-        moved = jnp.dot(pick, ref[...], preferred_element_type=jnp.float32)
-        moved = moved.reshape(chunks, part, cols).astype(jnp.bfloat16)
-        out_ref[:, side * part : (side + 1) * part, :] = moved
-
-
-def arrange(pick, sources, chunks):
-    rows = pick.shape[0]
-    total, width = sources[0].shape
-    per_chunk = len(sources) * rows // chunks
-    last = total // rows - 1
+def arrange_body(pick_ref, source_ref, *out_refs):
+    moved = jnp.dot(pick_ref[...], source_ref[...], preferred_element_type=jnp.float32)
+    moved = moved.astype(jnp.bfloat16)
+    rows = moved.shape[0] // len(out_refs)
+    for place, ref in enumerate(out_refs):
+        ref[...] = moved[place * rows : (place + 1) * rows]
+
+
+def arrange(pick, source, pieces=1):
+    rows, taken = pick.shape
+    total, width = source.shape
+    last = total // taken - 1
     cols = 1280 if width % 1280 == 0 else COLS_STEP
     return pl.pallas_call(
         arrange_body,
         grid=(width // cols,),
-        in_specs=[pl.BlockSpec((rows, rows), lambda j: (0, 0))]
-        + [pl.BlockSpec((rows, cols), lambda j: (last, j)) for _ in sources],
-        out_specs=pl.BlockSpec((chunks, per_chunk, cols), lambda j: (0, 0, j)),
-        out_shape=jax.ShapeDtypeStruct((chunks, per_chunk, width), jnp.bfloat16),
+        in_specs=[
+            pl.BlockSpec((rows, taken), lambda j: (0, 0)),
+            pl.BlockSpec((taken, cols), lambda j: (last, j)),
+        ],
+        out_specs=[pl.BlockSpec((rows // pieces, cols), lambda j: (0, j))] * pieces,
+        out_shape=[jax.ShapeDtypeStruct((rows // pieces, width), jnp.bfloat16)] * pieces,
         compiler_params=pltpu.CompilerParams(vmem_limit_bytes=VMEM_LIMIT),
         name="arrange",
-    )(pick, *sources)
-
-
-def score_body(own_ref, far_ref, key_ref, probs_ref, lse_ref):
+    )(pick, source)
+
+
+def score_body(query_ref, *refs):
+    key_refs, probs_ref, lse_ref = refs[:HALF_VENUES], refs[-2], refs[-1]
     step = pl.program_id(0)
 
     @pl.when(step == 0)
     def _():
         lse_ref[...] = jnp.zeros_like(lse_ref)
 
-    shape = (HALF_VENUES, 2, NODE_STEPS, COLS_STEP)
-    own = own_ref[...].astype(jnp.float32).reshape(shape)
-    far = far_ref[...].astype(jnp.float32).reshape(shape)
+    shape = (VENUES, 2, NODE_STEPS, COLS_STEP)
+    both = query_ref[...].astype(jnp.float32).reshape(shape)
     full = (2 * ROWS_HALF, KEYS_HALF)
     query_step = lax.broadcasted_iota(jnp.int32, full, 0) % NODE_STEPS + (STEPS - NODE_STEPS)
     key_step = lax.broadcasted_iota(jnp.int32, full, 1) % STEPS
@@ -110,14 +108,10 @@
     lane = lax.broadcasted_iota(jnp.int32, lse_ref.shape, 1)
     lse = lse_ref[...]
     for item in range(2):
-        queries = jnp.concatenate(
-            [
-                own[:, item].reshape(ROWS_HALF, COLS_STEP),
-                far[:, 1 - item].reshape(ROWS_HALF, COLS_STEP),
-            ],
-            axis=0,
-        ).astype(jnp.bfloat16)
-        keys = key_ref[:, item].reshape(KEYS_HALF, COLS_STEP)
+        queries = both[:, item].reshape(2 * ROWS_HALF, COLS_STEP).astype(jnp.bfloat16)
+        keys = jnp.concatenate(
+            [ref[item * STEPS : (item + 1) * STEPS, :] for ref in key_refs], axis=0
+        )
         for head in range(HEADS_STEP):
             span = slice(head * HEAD_DIM, (head + 1) * HEAD_DIM)
             scores = lax.dot_general(
@@ -136,18 +130,15 @@
     lse_ref[...] = lse
 
 
-def half_scores(own, far, keys):
-    width = own.shape[1]
-    rows = own.shape[0]
+def half_scores(queries, keys):
+    rows, width = queries.shape
     heads = width // HEAD_DIM
+    held = pltpu.with_memory_space_constraint(queries, pltpu.HBM)
     return pl.pallas_call(
         score_body,
         grid=(width // COLS_STEP,),
-        in_specs=[
-            pl.BlockSpec((rows, COLS_STEP), lambda j: (0, j)),
-            pl.BlockSpec((rows, COLS_STEP), lambda j: (0, j)),
-            pl.BlockSpec((HALF_VENUES, 2, STEPS, COLS_STEP), lambda j: (0, 0, 0, j)),
-        ],
+        in_specs=[pl.BlockSpec((rows, COLS_STEP), lambda j: (0, j))]
+        + [pl.BlockSpec((2 * STEPS, COLS_STEP), lambda j: (0, j))] * HALF_VENUES,
         out_specs=[
             pl.BlockSpec((HEADS_STEP, 2, 2 * ROWS_HALF, KEYS_HALF), lambda j: (j, 0, 0, 0)),
             pl.BlockSpec((2 * ROWS_HALF, 128), lambda j: (0, 0)),
@@ -158,13 +149,12 @@
         ],
         compiler_params=pltpu.CompilerParams(vmem_limit_bytes=VMEM_LIMIT),
         name="half_scores",
-    )(*[pltpu.with_memory_space_constraint(a, pltpu.HBM) for a in (own, far)], keys)
+    )(held, *keys)
 
 
 def weigh_body(probs_ref, lse_ref, far_ref, weights_ref):
     step = pl.program_id(0)
-    far = jnp.concatenate([far_ref[ROWS_HALF:, :], far_ref[:ROWS_HALF, :]], axis=0)
-    far = jnp.concatenate([far[:, LSE_ITEM:], far[:, :LSE_ITEM]], axis=1)
+    far = jnp.concatenate([far_ref[:, LSE_ITEM:], far_ref[:, :LSE_ITEM]], axis=1)
     share = 1.0 / (1.0 + jnp.exp(far - lse_ref[...])) * (1.0 / VENUES)
     lane = lax.broadcasted_iota(jnp.int32, lse_ref.shape, 1)
     for head in range(HEADS_STEP):
@@ -194,14 +184,17 @@
     )(probs, lse, far_lse)
 
 
-def pool_body(weights_ref, value_ref, out_ref):
+def pool_body(first_ref, weights_ref, value_ref, out_ref):
+    first = first_ref[0]
     row = lax.broadcasted_iota(jnp.int32, (2 * NODE_STEPS, HEAD_DIM), 0)
     for head in range(HEADS_STEP):
         span = slice(head * HEAD_DIM, (head + 1) * HEAD_DIM)
         pooled = [
             jnp.dot(
                 weights_ref[head],
-                value_ref[:, item, :, span].reshape(KEYS_HALF, HEAD_DIM),
+                jnp.concatenate(
+                    [value_ref[first ^ venue, item, :, span] for venue in range(HALF_VENUES)], axis=0
+                ),
                 preferred_element_type=jnp.float32,
             )
             for item in range(2)
@@ -209,12 +202,13 @@
         out_ref[:, span] = jnp.where(row < NODE_STEPS, *pooled).astype(jnp.bfloat16)
 
 
-def half_pool(weights, values):
+def half_pool(first, weights, values):
     width = values.shape[3]
     return pl.pallas_call(
         pool_body,
         grid=(width // COLS_STEP,),
         in_specs=[
+            pl.BlockSpec(memory_space=pltpu.SMEM),
             pl.BlockSpec((HEADS_STEP, 2 * NODE_STEPS, KEYS_HALF), lambda j: (j, 0, 0)),
             pl.BlockSpec((HALF_VENUES, 2, STEPS, COLS_STEP), lambda j: (0, 0, 0, j)),
         ],
@@ -222,7 +216,7 @@
         out_shape=jax.ShapeDtypeStruct((2 * NODE_STEPS, width), jnp.bfloat16),
         compiler_params=pltpu.CompilerParams(vmem_limit_bytes=VMEM_LIMIT),
         name="half_pool",
-    )(weights, values)
+    )(first, weights, values)
 
 
 def pad_lanes(width):
@@ -386,41 +380,60 @@
     venue_idx = me * pairs_dev // STEPS
     slot_order = lax.dynamic_index_in_dim(slot_map, venue_idx, 0, keepdims=False)
 
-    def picker(pairs):
-        rows = pairs * inst_total
-        row = lax.broadcasted_iota(jnp.int32, (rows, inst_total), 0)
-        inst = (row // pairs % 2 ^ me // chunks) * chunks + row // (2 * pairs)
-        hit = inst == lax.broadcasted_iota(jnp.int32, (rows, inst_total), 1)
+    def picker(pairs, inst_of, places):
+        shape = (places * 2 * pairs, pairs * inst_total)
+        row = lax.broadcasted_iota(jnp.int32, (shape[0], inst_total), 0)
+        inst = inst_of(row // (2 * pairs), row // pairs % 2)
+        hit = inst == lax.broadcasted_iota(jnp.int32, (shape[0], inst_total), 1)
         slot = jnp.sum(jnp.where(hit, slot_order[None, :], 0), axis=1, keepdims=True)
-        line = lax.broadcasted_iota(jnp.int32, (rows, rows), 0)
-        source = line % pairs * inst_total + slot
-        return (source == lax.broadcasted_iota(jnp.int32, (rows, rows), 1)).astype(jnp.bfloat16)
+        source = lax.broadcasted_iota(jnp.int32, shape, 0) % pairs * inst_total + slot
+        return (source == lax.broadcasted_iota(jnp.int32, shape, 1)).astype(jnp.bfloat16)
 
     whole_venue = pairs_dev == STEPS
+    direct = whole_venue and chunks == HALF_VENUES
     query_pairs = NODE_STEPS if whole_venue else pairs_dev
     rows = pairs_dev * inst_total
-    queries = arrange(picker(query_pairs), [query_vecs.reshape(rows, feat_width)], chunks)
-    queries = lax.all_to_all(queries, "gx", 0, 0, axis_index_groups=groups, tiled=True)
-    queries = queries.reshape(query_pairs * inst_total, feat_width)
-    pick = picker(pairs_dev)
-    keys, values = (a.reshape(rows, feat_width) for a in (key_vecs, value_vecs))
-    values = arrange(pick, [values], chunks)
-    keys = arrange(pick, [keys], chunks)
-    keys, queries = lax.optimization_barrier((keys, queries))
-
-    def exchange(block):
-        block = lax.all_to_all(block, "gx", 0, 0, axis_index_groups=groups, tiled=True)
-        block = block.reshape(HALF_VENUES, STEPS // pairs_dev, 2, pairs_dev, feat_width)
-        return block.transpose(0, 2, 1, 3, 4).reshape(HALF_VENUES, 2, STEPS, feat_width)
-
+    query_vecs, key_vecs, value_vecs = (
+        a.reshape(rows, feat_width) for a in (query_vecs, key_vecs, value_vecs)
+    )
+
+    def by_venue(block, venues):
+        block = block.reshape(venues, -1, 2, rows // inst_total, feat_width)
+        return block.transpose(0, 2, 1, 3, 4).reshape(venues, 2, -1, feat_width)
+
+    def in_half(block):
+        block = lax.all_to_all(
+            block.reshape(chunks, -1, feat_width), "gx", 0, 0, axis_index_groups=groups, tiled=True
+        )
+        return by_venue(block, HALF_VENUES)
+
+    def own_first(flip):
+        return lambda place, item: (item ^ me // chunks) * chunks + (place ^ flip)
+
+    pick = picker(query_pairs, lambda place, item: place ^ item * chunks, gx_count)
+    (queries,) = arrange(pick, query_vecs)
+    queries = lax.all_to_all(queries.reshape(gx_count, -1, feat_width), "gx", 0, 0, tiled=True)
     if not whole_venue:
-        queries = queries.reshape(HALF_VENUES, STEPS // pairs_dev, 2, pairs_dev, feat_width)
-        queries = queries[:, (STEPS - NODE_STEPS) // pairs_dev :].transpose(0, 2, 1, 3, 4)
-        queries = queries.reshape(2 * ROWS_HALF, feat_width)
-    far = swap_stage(queries, orders, last)
-    keys = exchange(keys)
-    values, keys, far = lax.optimization_barrier((values, keys, far))
-    values = exchange(values)
+        queries = by_venue(queries, VENUES)[:, :, STEPS - NODE_STEPS :]
+    queries = queries.reshape(4 * ROWS_HALF, feat_width)
+    (values,) = arrange(picker(pairs_dev, own_first(0), chunks), value_vecs)
+    if direct:
+        first = me % chunks
+        pieces = arrange(picker(pairs_dev, own_first(first), chunks), key_vecs, chunks)
+        keys = [pieces[0]]
+        for flip in range(1, chunks):
+            pairs = [(g, g ^ flip) for g in range(gx_count)]
+            keys.append(lax.ppermute(pieces[flip], "gx", pairs))
+        waited = keys[-7:]
+        values, queries, waited = lax.optimization_barrier((values, queries, waited))
+        keys[-7:] = waited
+    else:
+        first = me * 0
+        (keys,) = arrange(picker(pairs_dev, own_first(0), chunks), key_vecs)
+        keys = in_half(keys)
+        keys = [keys[venue].reshape(2 * STEPS, feat_width) for venue in range(HALF_VENUES)]
+    first = first[None].astype(jnp.int32)
+    values = in_half(values)
     row_total = inst_total * NODE_STEPS
     row = jnp.arange(row_total)
     place = row // NODE_STEPS
@@ -438,9 +451,9 @@
     )
     mix = jnp.where(same_step[None], mix, 0.0).astype(jnp.bfloat16)
     keys, mix, type_gain = lax.optimization_barrier((keys, mix, type_gain))
-    probs, lse = half_scores(queries, far, keys)
+    probs, lse = half_scores(queries, keys)
     far_lse = swap_stage(lse, orders, last)
-    pooled = half_pool(mean_weights(probs, lse, far_lse), values)
+    pooled = half_pool(first, mean_weights(probs, lse, far_lse), values)
     (gate,), token = stage_weights([gate_proj], 0, [pooled])
     pooled = join_pair(pooled, orders, last).astype(jnp.bfloat16)
     pooled, token = lax.optimization_barrier((pooled, token))

time: 165 us -> 163 us (0.988)
  waiting for transfers between devices: 63.8 us -> 61.2 us
    ppermute x0 -> x7, waiting for transfers between devices: none -> 24.9 us  [per_device(): keys.append(lax.ppermute(pieces[flip], 'gx', pairs))]
    ppermute x27 -> x26, waiting for transfers between devices: 49.1 us -> 31.3 us  [swap_stage(): return lax.ppermute(block, ('gx', 'ta'), pairs)]
    ppermute x0 -> x7, starting transfers between devices: none -> 10.5 us  [per_device(): keys.append(lax.ppermute(pieces[flip], 'gx', pairs))]
    all_to_all x3 -> x2, waiting for transfers between devices: 10.4 us -> 0.75 us  [the longest x1 0.74 us: in_half(): lax.all_to_all(block.reshape(chunks, -1, feat_width), 'gx', 0, 0, axis_in...]
    ppermute x27 -> x26, starting transfers between devices: 44.8 us -> 38.9 us  [swap_stage(): return lax.ppermute(block, ('gx', 'ta'), pairs)]
    all_to_all x3 -> x2, starting transfers between devices: 15.5 us -> 12.1 us  [the longest x1 8.36 us: per_device(): lax.all_to_all(queries.reshape(gx_count, -1, feat_width), 'gx', 0, 0, til...]
    unnamed x21 -> x19, local copies, waits for them, and re-layouts: 3.43 us -> 3.24 us
  transfers between devices with their start and end apart: 32 -> 37, of which waited for: 23 -> 27; matrix products, arithmetic and copies ran while one was open for 1% -> 1% of each run, Pallas kernels for 15% -> 14%
where the time goes in v8:
time: 163 us
  starting transfers between devices  61.6 us (38%)
  waiting for transfers between devices  61.2 us (38%)
  Pallas kernels  34.1 us (21%)
  local copies, waits for them, and re-layouts  3.38 us (2%)
  other arithmetic  1.75 us (1%)
    ppermute x26, starting transfers between devices, swap_stage(): return lax.ppermute(block, ('gx', 'ta'), pairs)  38.9 us
    ppermute x26, waiting for transfers between devices, swap_stage(): return lax.ppermute(block, ('gx', 'ta'), pairs)  31.3 us
    ppermute x7, waiting for transfers between devices, per_device(): keys.append(lax.ppermute(pieces[flip], 'gx', pairs))  24.9 us
    pallas_call x4, Pallas kernels, stage_weights(): pl.pallas_call(functools.partial(stage_body, layer=layer, count=len(held)...  15.3 us
    ppermute x7, starting transfers between devices, per_device(): keys.append(lax.ppermute(pieces[flip], 'gx', pairs))  10.5 us
    all_to_all x1, starting transfers between devices, per_device(): lax.all_to_all(queries.reshape(gx_count, -1, feat_width), 'gx', 0, 0, til...  8.36 us
    pallas_call x2, Pallas kernels, expand(): pl.pallas_call(functools.partial(expand_body, layer=layer), in_specs=[pl....  5.37 us
    ppermute x2, waiting for transfers between devices, per_device(): far_sums = lax.ppermute(near_sums, 'ta', [(0, 1), (1, 0)])  4.26 us
  transfers between devices with their start and end apart: 37, of which 27 were waited for; matrix products, arithmetic and copies ran while one was open for 1% of the time, Pallas kernels for 14%

profile of v8, /device:TPU:0, one launch (start us, length us, event | category | flops | bytes accessed | tf_op | source)
XLA Modules:
  0.0 162.9 jit_solution(14937711501171139674)
XLA Ops:
  3.9 8.4 %all-to-all-start = ((bf16[16,16,2560]{2,1,0:T(8,128)(2,1)}), bf16[16,16,2560]{2,1,0:T(8,128)(2,1)}, u32[]{:S(2)}, u32[]{:S(2)}) async-start(bf16[16,16,2560]{2,1,0:T(8,128)(2,1)} %bitcast.4), calls=%async_computation | async-start | bytes 2621440 | tf_op jit(solution)/shard_map/all_to_all | solution.py:415
  14.8 1.9 %collective-permute-start = (bf16[32,2560]{1,0:T(8,128)(2,1)S(1)}, bf16[32,2560]{1,0:T(8,128)(2,1)S(1)}, u32[]{:S(2)}, u32[]{:S(2)}) collective-permute-start(bf16[32,2560]{1,0:T(8,128)(2,1)S(1)} %get-tuple-element.56), channel_id=1, source_target_pairs={{0,2},{2,0},{4,6},{6,4},{8,10},{10,8},{12,14},{14,12},{16,18},{18,... | collective-permute-start | bytes 491528 | tf_op jit(solution)/shard_map/ppermute | solution.py:426
  22.6 2.8 %collective-permute-start.5 = (bf16[32,2560]{1,0:T(8,128)(2,1)S(1)}, bf16[32,2560]{1,0:T(8,128)(2,1)S(1)}, u32[]{:S(2)}, u32[]{:S(2)}) collective-permute-start(bf16[32,2560]{1,0:T(8,128)(2,1)S(1)} %get-tuple-element.61), channel_id=1, source_target_pairs={{0,12},{2,14},{4,8},{6,10},{8,4},{10,6},{12,0},{14,2},{16,28},{18,... | collective-permute-start | bytes 491528 | tf_op jit(solution)/shard_map/ppermute | solution.py:426
  25.4 6.7 %collective-permute-done.1.refs_2_ = bf16[32,2560]{1,0:T(8,128)(2,1)S(1)} collective-permute-done((bf16[32,2560]{1,0:T(8,128)(2,1)S(1)}, bf16[32,2560]{1,0:T(8,128)(2,1)S(1)}, u32[]{:S(2)}, u32[]{:S(2)}) %collective-permute-start.1) | collective-permute-done | bytes 163872 | tf_op jit(solution)/shard_map/ppermute | solution.py:426
  34.5 4.6 %collective-permute-done.3.refs_4_ = bf16[32,2560]{1,0:T(8,128)(2,1)S(1)} collective-permute-done((bf16[32,2560]{1,0:T(8,128)(2,1)S(1)}, bf16[32,2560]{1,0:T(8,128)(2,1)S(1)}, u32[]{:S(2)}, u32[]{:S(2)}) %collective-permute-start.3) | collective-permute-done | bytes 163872 | tf_op jit(solution)/shard_map/ppermute | solution.py:426
  39.1 5.4 %collective-permute-done.4.refs_5_ = bf16[32,2560]{1,0:T(8,128)(2,1)S(1)} collective-permute-done((bf16[32,2560]{1,0:T(8,128)(2,1)S(1)}, bf16[32,2560]{1,0:T(8,128)(2,1)S(1)}, u32[]{:S(2)}, u32[]{:S(2)}) %collective-permute-start.4) | collective-permute-done | bytes 163872 | tf_op jit(solution)/shard_map/ppermute | solution.py:426
  44.5 4.2 %collective-permute-done.5.refs_6_ = bf16[32,2560]{1,0:T(8,128)(2,1)S(1)} collective-permute-done((bf16[32,2560]{1,0:T(8,128)(2,1)S(1)}, bf16[32,2560]{1,0:T(8,128)(2,1)S(1)}, u32[]{:S(2)}, u32[]{:S(2)}) %collective-permute-start.5) | collective-permute-done | bytes 163872 | tf_op jit(solution)/shard_map/ppermute | solution.py:426
  48.7 3.2 %collective-permute-done.6.refs_7_ = bf16[32,2560]{1,0:T(8,128)(2,1)S(1)} collective-permute-done((bf16[32,2560]{1,0:T(8,128)(2,1)S(1)}, bf16[32,2560]{1,0:T(8,128)(2,1)S(1)}, u32[]{:S(2)}, u32[]{:S(2)}) %collective-permute-start.6) | collective-permute-done | bytes 163872 | tf_op jit(solution)/shard_map/ppermute | solution.py:426
  51.9 3.8 %all-to-all-start.1 = ((bf16[8,32,2560]{2,1,0:T(8,128)(2,1)}), bf16[8,32,2560]{2,1,0:T(8,128)(2,1)S(1)}, u32[]{:S(2)}, u32[]{:S(2)}) async-start(bf16[8,32,2560]{2,1,0:T(8,128)(2,1)} %bitcast.10), calls=%async_computation.1 | async-start | bytes 2621440 | tf_op jit(solution)/shard_map/all_to_all | solution.py:405
  56.2 4.0 %half_scores.1 = (bf16[20,2,128,128]{3,2,1,0:T(8,128)(2,1)S(1)}, f32[128,128]{1,0:T(8,128)S(1)}) custom-call(bf16[256,2560]{1,0:T(8,128)(2,1)} %bitcast.5.query_ref, bf16[32,2560]{1,0:T(8,128)(2,1)S(1)} %get-tuple-element.72.refs_0_, bf16[32,2560]{1,0:T(8,128)(2,1)S(1)} %collective-permute-done.refs_1_, bf16[32,2560]{1,0:T(8,128)(2,1)S(1)} %collective-permute-done.1.refs_2_, ...), custom_call_target="tpu_custom_call" | custom-call | tf_op jit(solution)/shard_map/half_scores/pallas_call | solution.py:137
  60.2 2.7 %collective-permute-start.7 = (f32[128,128]{1,0:T(8,128)S(1)}, f32[128,128]{1,0:T(8,128)S(1)}, u32[]{:S(2)}, u32[]{:S(2)}) collective-permute-start(f32[128,128]{1,0:T(8,128)S(1)} %get-tuple-element.81.lse_ref), channel_id=1, source_target_pairs={{0,16},{1,17},{2,18},{3,19},{4,20},{5,21},{6,22},{7,23},{8,24},{9,... | collective-permute-start | bytes 196616 | tf_op jit(solution)/shard_map/ppermute | solution.py:46
  62.9 7.7 %collective-permute-done.7.far_ref = f32[128,128]{1,0:T(8,128)S(1)} collective-permute-done((f32[128,128]{1,0:T(8,128)S(1)}, f32[128,128]{1,0:T(8,128)S(1)}, u32[]{:S(2)}, u32[]{:S(2)}) %collective-permute-start.7) | collective-permute-done | bytes 65568 | tf_op jit(solution)/shard_map/ppermute | solution.py:46
  73.8 2.7 %collective-permute-start.8 = (bf16[16,2560]{1,0:T(8,128)(2,1)S(1)}, bf16[16,2560]{1,0:T(8,128)(2,1)S(1)}, u32[]{:S(2)}, u32[]{:S(2)}) collective-permute-start(bf16[16,2560]{1,0:T(8,128)(2,1)S(1)} %half_pool.1.refs_1_), channel_id=1, source_target_pairs={{0,16},{1,17},{2,18},{3,19},{4,20},{5,21},{6,22},{7,23},{8,24},{9,... | collective-permute-start | bytes 245768 | tf_op jit(solution)/shard_map/ppermute | solution.py:46
  76.5 2.9 %stage_weights.4 = (bf16[2560,1280]{1,0:T(8,128)(2,1)S(1)}, f32[8,128]{1,0:T(8,128)S(1)}) custom-call(bf16[2,2560,1280]{2,1,0:T(8,128)(2,1)} %refs_0_.7, bf16[16,2560]{1,0:T(8,128)(2,1)S(1)} %half_pool.1.refs_1_), custom_call_target="tpu_custom_call" | custom-call | bytes 13107200 | tf_op jit(solution)/shard_map/stage_weights/pallas_call | solution.py:243
  80.1 3.7 %collective-permute-start.9 = (bf16[16,2560]{1,0:T(8,128)(2,1)S(1)}, bf16[16,2560]{1,0:T(8,128)(2,1)S(1)}, u32[]{:S(2)}, u32[]{:S(2)}) collective-permute-start(bf16[16,2560]{1,0:T(8,128)(2,1)S(1)} %add_convert_fusion), channel_id=1, source_target_pairs={{0,8},{1,9},{2,10},{3,11},{4,12},{5,13},{6,14},{7,15},{8,0},{9,1},... | collective-permute-start | bytes 245768 | tf_op jit(solution)/shard_map/ppermute | solution.py:46
  83.8 2.4 %collective-permute-done.9 = bf16[16,2560]{1,0:T(8,128)(2,1)S(1)} collective-permute-done((bf16[16,2560]{1,0:T(8,128)(2,1)S(1)}, bf16[16,2560]{1,0:T(8,128)(2,1)S(1)}, u32[]{:S(2)}, u32[]{:S(2)}) %collective-permute-start.9) | collective-permute-done | bytes 81952 | tf_op jit(solution)/shard_map/ppermute | solution.py:46
  86.2 2.5 %collective-permute-start.12 = (bf16[32,2560]{1,0:T(8,128)(2,1)S(1)}, bf16[32,2560]{1,0:T(8,128)(2,1)S(1)}, u32[]{:S(2)}, u32[]{:S(2)}) collective-permute-start(bf16[32,2560]{1,0:T(8,128)(2,1)S(1)} %constant_dynamic-update-slice_fusion.refs_0_), channel_id=1, source_target_pairs={{0,6},{1,7},{2,4},{3,5},{4,2},{5,3},{6,0},{7,1},{8,14},{9,15},{10,... | collective-permute-start | bytes 491528 | tf_op jit(solution)/shard_map/ppermute | solution.py:46
  89.8 4.8 %stage_weights.5 = (bf16[2560,1280]{1,0:T(8,128)(2,1)S(1)}, bf16[1280,2560]{1,0:T(8,128)(2,1)S(1)}, f32[8,128]{1,0:T(8,128)S(1)}) custom-call(bf16[2,2560,1280]{2,1,0:T(8,128)(2,1)} %refs_1_.3, bf16[2,1280,2560]{2,1,0:T(8,128)(2,1)} %refs_0_.6, f32[8,128]{1,0:T(8,128)S(1)} %get-tuple-element.88.refs_2_), custom_call_target="tpu_custom_call" | custom-call | bytes 26214400 | tf_op jit(solution)/shard_map/stage_weights/pallas_call | solution.py:243
  94.6 2.7 %expand.2.near_ref = bf16[128,2688]{1,0:T(8,128)(2,1)S(1)} custom-call(bf16[32,2560]{1,0:T(8,128)(2,1)S(1)} %constant_dynamic-update-slice_fusion.refs_0_, bf16[32,2560]{1,0:T(8,128)(2,1)S(1)} %collective-permute-done.10.refs_1_, bf16[32,2560]{1,0:T(8,128)(2,1)S(1)} %collective-permute-done.11.refs_2_, bf16[32,2560]{1,0:T(8,128)(2,1)S(1)} %collective-permute-done.12.refs_3_, ...), custom_call_target="tpu_custom_call" | custom-call | tf_op jit(solution)/shard_map/expand/pallas_call | solution.py:298
  97.4 2.1 %collective-permute-done.13.far_ref = bf16[128,2688]{1,0:T(8,128)(2,1)S(1)} collective-permute-done((bf16[128,2688]{1,0:T(8,128)(2,1)S(1)}, bf16[128,2688]{1,0:T(8,128)(2,1)S(1)}, u32[]{:S(2)}, u32[]{:S(2)}) %collective-permute-start.13) | collective-permute-done | bytes 688160 | tf_op jit(solution)/shard_map/ppermute | solution.py:467
  103.0 2.9 %stage_weights.6 = (bf16[1280,2560]{1,0:T(8,128)(2,1)S(1)}, f32[8,128]{1,0:T(8,128)S(1)}) custom-call(bf16[2,1280,2560]{2,1,0:T(8,128)(2,1)} %refs_0_.6, bf16[64,1280]{1,0:T(8,128)(2,1)S(1)} %get-tuple-element.93.refs_1_), custom_call_target="tpu_custom_call" | custom-call | bytes 13107200 | tf_op jit(solution)/shard_map/stage_weights/pallas_call | solution.py:243
  110.9 2.1 %collective-permute-start.20 = (bf16[16,1280]{1,0:T(8,128)(2,1)S(1)}, bf16[16,1280]{1,0:T(8,128)(2,1)S(1)}, u32[]{:S(2)}, u32[]{:S(2)}) collective-permute-start(bf16[16,1280]{1,0:T(8,128)(2,1)S(1)} %slice.210), channel_id=1, source_target_pairs={{0,8},{1,9},{2,10},{3,11},{4,12},{5,13},{6,14},{7,15},{8,0},{9,1},... | collective-permute-start | bytes 122888 | tf_op jit(solution)/shard_map/ppermute | solution.py:46
  115.4 1.9 %collective-permute-done.16 = bf16[16,1280]{1,0:T(8,128)(2,1)S(1)} collective-permute-done((bf16[16,1280]{1,0:T(8,128)(2,1)S(1)}, bf16[16,1280]{1,0:T(8,128)(2,1)S(1)}, u32[]{:S(2)}, u32[]{:S(2)}) %collective-permute-start.16) | collective-permute-done | bytes 40992 | tf_op jit(solution)/shard_map/ppermute | solution.py:46
  120.0 2.3 %collective-permute-done.17 = bf16[16,1280]{1,0:T(8,128)(2,1)S(1)} collective-permute-done((bf16[16,1280]{1,0:T(8,128)(2,1)S(1)}, bf16[16,1280]{1,0:T(8,128)(2,1)S(1)}, u32[]{:S(2)}, u32[]{:S(2)}) %collective-permute-start.17) | collective-permute-done | bytes 40992 | tf_op jit(solution)/shard_map/ppermute | solution.py:46
  124.2 2.6 %collective-permute-done.22 = bf16[16,2560]{1,0:T(8,128)(2,1)S(1)} collective-permute-done((bf16[16,2560]{1,0:T(8,128)(2,1)S(1)}, bf16[16,2560]{1,0:T(8,128)(2,1)S(1)}, u32[]{:S(2)}, u32[]{:S(2)}) %collective-permute-start.22) | collective-permute-done | bytes 81952 | tf_op jit(solution)/shard_map/ppermute | solution.py:46
  126.9 2.5 %collective-permute-start.25 = (bf16[32,2560]{1,0:T(8,128)(2,1)S(1)}, bf16[32,2560]{1,0:T(8,128)(2,1)S(1)}, u32[]{:S(2)}, u32[]{:S(2)}) collective-permute-start(bf16[32,2560]{1,0:T(8,128)(2,1)S(1)} %pad_maximum_fusion.refs_0_), channel_id=1, source_target_pairs={{0,6},{1,7},{2,4},{3,5},{4,2},{5,3},{6,0},{7,1},{8,14},{9,15},{10,... | collective-permute-start | bytes 491528 | tf_op jit(solution)/shard_map/ppermute | solution.py:46
  130.4 4.8 %stage_weights.7 = (bf16[2560,1280]{1,0:T(8,128)(2,1)S(1)}, bf16[2560,1280]{1,0:T(8,128)(2,1)S(1)}, f32[8,128]{1,0:T(8,128)S(1)}) custom-call(bf16[2,2560,1280]{2,1,0:T(8,128)(2,1)} %refs_0_.7, bf16[2,2560,1280]{2,1,0:T(8,128)(2,1)} %refs_1_.3, bf16[16,2560]{1,0:T(8,128)(2,1)S(1)} %pad_maximum_fusion.1.refs_2_, f32[8,128]{1,0:T(8,128)S(1)} %get-tuple-element.98.refs_3_), custom_call_target="tpu_custom_call" | custom-call | bytes 26214400 | tf_op jit(solution)/shard_map/stage_weights/pallas_call | solution.py:243
  135.2 2.6 %expand.3.near_ref = bf16[128,2688]{1,0:T(8,128)(2,1)S(1)} custom-call(bf16[32,2560]{1,0:T(8,128)(2,1)S(1)} %pad_maximum_fusion.refs_0_, bf16[32,2560]{1,0:T(8,128)(2,1)S(1)} %collective-permute-done.23.refs_1_, bf16[32,2560]{1,0:T(8,128)(2,1)S(1)} %collective-permute-done.24.refs_2_, bf16[32,2560]{1,0:T(8,128)(2,1)S(1)} %collective-permute-done.25.refs_3_, ...), custom_call_target="tpu_custom_call" | custom-call | tf_op jit(solution)/shard_map/expand/pallas_call | solution.py:298
  138.0 2.1 %collective-permute-done.26.far_ref = bf16[128,2688]{1,0:T(8,128)(2,1)S(1)} collective-permute-done((bf16[128,2688]{1,0:T(8,128)(2,1)S(1)}, bf16[128,2688]{1,0:T(8,128)(2,1)S(1)}, u32[]{:S(2)}, u32[]{:S(2)}) %collective-permute-start.26) | collective-permute-done | bytes 688160 | tf_op jit(solution)/shard_map/ppermute | solution.py:467
  143.6 3.3 %collective-permute-done.27 = bf16[64,1280]{1,0:T(8,128)(2,1)S(1)} collective-permute-done((bf16[64,1280]{1,0:T(8,128)(2,1)S(1)}, bf16[64,1280]{1,0:T(8,128)(2,1)S(1)}, u32[]{:S(2)}, u32[]{:S(2)}) %collective-permute-start.27) | collective-permute-done | bytes 163872 | tf_op jit(solution)/shard_map/ppermute | solution.py:46
  151.5 1.9 %collective-permute-start.29 = (bf16[16,1280]{1,0:T(8,128)(2,1)S(1)}, bf16[16,1280]{1,0:T(8,128)(2,1)S(1)}, u32[]{:S(2)}, u32[]{:S(2)}) collective-permute-start(bf16[16,1280]{1,0:T(8,128)(2,1)S(1)} %slice.209), channel_id=1, source_target_pairs={{0,8},{1,9},{2,10},{3,11},{4,12},{5,13},{6,14},{7,15},{8,0},{9,1},... | collective-permute-start | bytes 122888 | tf_op jit(solution)/shard_map/ppermute | solution.py:46
  160.3 1.9 %collective-permute-done.34 = bf16[8,1280]{1,0:T(8,128)(2,1)S(1)} collective-permute-done((bf16[8,1280]{1,0:T(8,128)(2,1)S(1)}, bf16[8,1280]{1,0:T(8,128)(2,1)S(1)}, u32[]{:S(2)}, u32[]{:S(2)}) %collective-permute-start.34) | collective-permute-done | bytes 20512 | tf_op jit(solution)/shard_map/ppermute | solution.py:46
  (129 shorter events, 52.3 us)
Async XLA Ops:
  3.9 48.0 %all-to-all-start = ((bf16[16,16,2560]{2,1,0:T(8,128)(2,1)}), bf16[16,16,2560]{2,1,0:T(8,128)(2,1)}, u32[]{:S(2)}, u32[]{:S(2)}) async-start(bf16[16,16,2560]{2,1,0:T(8,128)(2,1)} %bitcast.4), calls=%async_computation | async-start | bytes 2621440 | tf_op jit(solution)/shard_map/all_to_all | solution.py:415
  14.8 7.8 %collective-permute-start = (bf16[32,2560]{1,0:T(8,128)(2,1)S(1)}, bf16[32,2560]{1,0:T(8,128)(2,1)S(1)}, u32[]{:S(2)}, u32[]{:S(2)}) collective-permute-start(bf16[32,2560]{1,0:T(8,128)(2,1)S(1)} %get-tuple-element.56), channel_id=1, source_target_pairs={{0,2},{2,0},{4,6},{6,4},{8,10},{10,8},{12,14},{14,12},{16,18},{18,... | collective-permute-start | bytes 491528 | tf_op jit(solution)/shard_map/ppermute | solution.py:426
  16.7 15.3 %collective-permute-start.1 = (bf16[32,2560]{1,0:T(8,128)(2,1)S(1)}, bf16[32,2560]{1,0:T(8,128)(2,1)S(1)}, u32[]{:S(2)}, u32[]{:S(2)}) collective-permute-start(bf16[32,2560]{1,0:T(8,128)(2,1)S(1)} %get-tuple-element.57), channel_id=1, source_target_pairs={{0,4},{2,6},{4,0},{6,2},{8,12},{10,14},{12,8},{14,10},{16,20},{18,... | collective-permute-start | bytes 491528 | tf_op jit(solution)/shard_map/ppermute | solution.py:426
  18.2 16.3 %collective-permute-start.2 = (bf16[32,2560]{1,0:T(8,128)(2,1)S(1)}, bf16[32,2560]{1,0:T(8,128)(2,1)S(1)}, u32[]{:S(2)}, u32[]{:S(2)}) collective-permute-start(bf16[32,2560]{1,0:T(8,128)(2,1)S(1)} %get-tuple-element.58), channel_id=1, source_target_pairs={{0,6},{2,4},{4,2},{6,0},{8,14},{10,12},{12,10},{14,8},{16,22},{18,... | collective-permute-start | bytes 491528 | tf_op jit(solution)/shard_map/ppermute | solution.py:426
  18.4 20.8 %collective-permute-start.3 = (bf16[32,2560]{1,0:T(8,128)(2,1)S(1)}, bf16[32,2560]{1,0:T(8,128)(2,1)S(1)}, u32[]{:S(2)}, u32[]{:S(2)}) collective-permute-start(bf16[32,2560]{1,0:T(8,128)(2,1)S(1)} %get-tuple-element.59), channel_id=1, source_target_pairs={{0,8},{2,10},{4,12},{6,14},{8,0},{10,2},{12,4},{14,6},{16,24},{18,... | collective-permute-start | bytes 491528 | tf_op jit(solution)/shard_map/ppermute | solution.py:426
  20.2 24.3 %collective-permute-start.4 = (bf16[32,2560]{1,0:T(8,128)(2,1)S(1)}, bf16[32,2560]{1,0:T(8,128)(2,1)S(1)}, u32[]{:S(2)}, u32[]{:S(2)}) collective-permute-start(bf16[32,2560]{1,0:T(8,128)(2,1)S(1)} %get-tuple-element.60), channel_id=1, source_target_pairs={{0,10},{2,8},{4,14},{6,12},{8,2},{10,0},{12,6},{14,4},{16,26},{18,... | collective-permute-start | bytes 491528 | tf_op jit(solution)/shard_map/ppermute | solution.py:426
  22.6 26.1 %collective-permute-start.5 = (bf16[32,2560]{1,0:T(8,128)(2,1)S(1)}, bf16[32,2560]{1,0:T(8,128)(2,1)S(1)}, u32[]{:S(2)}, u32[]{:S(2)}) collective-permute-start(bf16[32,2560]{1,0:T(8,128)(2,1)S(1)} %get-tuple-element.61), channel_id=1, source_target_pairs={{0,12},{2,14},{4,8},{6,10},{8,4},{10,6},{12,0},{14,2},{16,28},{18,... | collective-permute-start | bytes 491528 | tf_op jit(solution)/shard_map/ppermute | solution.py:426
  32.1 19.8 %collective-permute-start.6 = (bf16[32,2560]{1,0:T(8,128)(2,1)S(1)}, bf16[32,2560]{1,0:T(8,128)(2,1)S(1)}, u32[]{:S(2)}, u32[]{:S(2)}) collective-permute-start(bf16[32,2560]{1,0:T(8,128)(2,1)S(1)} %get-tuple-element.62), channel_id=1, source_target_pairs={{0,14},{2,12},{4,10},{6,8},{8,6},{10,4},{12,2},{14,0},{16,30},{18,... | collective-permute-start | bytes 491528 | tf_op jit(solution)/shard_map/ppermute | solution.py:426
  51.9 20.9 %all-to-all-start.1 = ((bf16[8,32,2560]{2,1,0:T(8,128)(2,1)}), bf16[8,32,2560]{2,1,0:T(8,128)(2,1)S(1)}, u32[]{:S(2)}, u32[]{:S(2)}) async-start(bf16[8,32,2560]{2,1,0:T(8,128)(2,1)} %bitcast.10), calls=%async_computation.1 | async-start | bytes 2621440 | tf_op jit(solution)/shard_map/all_to_all | solution.py:405
  60.2 10.4 %collective-permute-start.7 = (f32[128,128]{1,0:T(8,128)S(1)}, f32[128,128]{1,0:T(8,128)S(1)}, u32[]{:S(2)}, u32[]{:S(2)}) collective-permute-start(f32[128,128]{1,0:T(8,128)S(1)} %get-tuple-element.81.lse_ref), channel_id=1, source_target_pairs={{0,16},{1,17},{2,18},{3,19},{4,20},{5,21},{6,22},{7,23},{8,24},{9,... | collective-permute-start | bytes 196616 | tf_op jit(solution)/shard_map/ppermute | solution.py:46
  73.8 6.3 %collective-permute-start.8 = (bf16[16,2560]{1,0:T(8,128)(2,1)S(1)}, bf16[16,2560]{1,0:T(8,128)(2,1)S(1)}, u32[]{:S(2)}, u32[]{:S(2)}) collective-permute-start(bf16[16,2560]{1,0:T(8,128)(2,1)S(1)} %half_pool.1.refs_1_), channel_id=1, source_target_pairs={{0,16},{1,17},{2,18},{3,19},{4,20},{5,21},{6,22},{7,23},{8,24},{9,... | collective-permute-start | bytes 245768 | tf_op jit(solution)/shard_map/ppermute | solution.py:46
  80.1 6.1 %collective-permute-start.9 = (bf16[16,2560]{1,0:T(8,128)(2,1)S(1)}, bf16[16,2560]{1,0:T(8,128)(2,1)S(1)}, u32[]{:S(2)}, u32[]{:S(2)}) collective-permute-start(bf16[16,2560]{1,0:T(8,128)(2,1)S(1)} %add_convert_fusion), channel_id=1, source_target_pairs={{0,8},{1,9},{2,10},{3,11},{4,12},{5,13},{6,14},{7,15},{8,0},{9,1},... | collective-permute-start | bytes 245768 | tf_op jit(solution)/shard_map/ppermute | solution.py:46
  86.2 8.3 %collective-permute-start.12 = (bf16[32,2560]{1,0:T(8,128)(2,1)S(1)}, bf16[32,2560]{1,0:T(8,128)(2,1)S(1)}, u32[]{:S(2)}, u32[]{:S(2)}) collective-permute-start(bf16[32,2560]{1,0:T(8,128)(2,1)S(1)} %constant_dynamic-update-slice_fusion.refs_0_), channel_id=1, source_target_pairs={{0,6},{1,7},{2,4},{3,5},{4,2},{5,3},{6,0},{7,1},{8,14},{9,15},{10,... | collective-permute-start | bytes 491528 | tf_op jit(solution)/shard_map/ppermute | solution.py:46
  88.7 5.9 %collective-permute-start.11 = (bf16[32,2560]{1,0:T(8,128)(2,1)S(1)}, bf16[32,2560]{1,0:T(8,128)(2,1)S(1)}, u32[]{:S(2)}, u32[]{:S(2)}) collective-permute-start(bf16[32,2560]{1,0:T(8,128)(2,1)S(1)} %constant_dynamic-update-slice_fusion.refs_0_), channel_id=1, source_target_pairs={{0,2},{1,5},{2,0},{3,7},{4,6},{5,1},{6,4},{7,3},{8,10},{9,13},{10,... | collective-permute-start | bytes 491528 | tf_op jit(solution)/shard_map/ppermute | solution.py:46
  89.1 5.5 %collective-permute-start.10 = (bf16[32,2560]{1,0:T(8,128)(2,1)S(1)}, bf16[32,2560]{1,0:T(8,128)(2,1)S(1)}, u32[]{:S(2)}, u32[]{:S(2)}) collective-permute-start(bf16[32,2560]{1,0:T(8,128)(2,1)S(1)} %constant_dynamic-update-slice_fusion.refs_0_), channel_id=1, source_target_pairs={{0,4},{1,3},{2,6},{3,1},{4,0},{5,7},{6,2},{7,5},{8,12},{9,11},{10,... | collective-permute-start | bytes 491528 | tf_op jit(solution)/shard_map/ppermute | solution.py:46
  100.9 5.4 %collective-permute-start.18 = (bf16[64,1280]{1,0:T(8,128)(2,1)S(1)}, bf16[64,1280]{1,0:T(8,128)(2,1)S(1)}, u32[]{:S(2)}, u32[]{:S(2)}) collective-permute-start(bf16[64,1280]{1,0:T(8,128)(2,1)S(1)} %get-tuple-element.97), channel_id=1, source_target_pairs={{0,2},{1,5},{2,0},{3,7},{4,6},{5,1},{6,4},{7,3},{8,10},{9,13},{10,... | collective-permute-start | bytes 491528 | tf_op jit(solution)/shard_map/ppermute | solution.py:46
  102.5 5.5 %collective-permute-start.14 = (bf16[64,1280]{1,0:T(8,128)(2,1)S(1)}, bf16[64,1280]{1,0:T(8,128)(2,1)S(1)}, u32[]{:S(2)}, u32[]{:S(2)}) collective-permute-start(bf16[64,1280]{1,0:T(8,128)(2,1)S(1)} %get-tuple-element.93.refs_1_), channel_id=1, source_target_pairs={{0,2},{1,5},{2,0},{3,7},{4,6},{5,1},{6,4},{7,3},{8,10},{9,13},{10,... | collective-permute-start | bytes 491528 | tf_op jit(solution)/shard_map/ppermute | solution.py:46
  106.4 4.5 %collective-permute-start.19 = (bf16[32,1280]{1,0:T(8,128)(2,1)S(1)}, bf16[32,1280]{1,0:T(8,128)(2,1)S(1)}, u32[]{:S(2)}, u32[]{:S(2)}) collective-permute-start(bf16[32,1280]{1,0:T(8,128)(2,1)S(1)} %slice.206), channel_id=1, source_target_pairs={{0,4},{1,3},{2,6},{3,1},{4,0},{5,7},{6,2},{7,5},{8,12},{9,11},{10,... | collective-permute-start | bytes 245768 | tf_op jit(solution)/shard_map/ppermute | solution.py:46
  108.1 4.9 %collective-permute-start.15 = (bf16[32,1280]{1,0:T(8,128)(2,1)S(1)}, bf16[32,1280]{1,0:T(8,128)(2,1)S(1)}, u32[]{:S(2)}, u32[]{:S(2)}) collective-permute-start(bf16[32,1280]{1,0:T(8,128)(2,1)S(1)} %slice.207), channel_id=1, source_target_pairs={{0,4},{1,3},{2,6},{3,1},{4,0},{5,7},{6,2},{7,5},{8,12},{9,11},{10,... | collective-permute-start | bytes 245768 | tf_op jit(solution)/shard_map/ppermute | solution.py:46
  113.0 4.2 %collective-permute-start.16 = (bf16[16,1280]{1,0:T(8,128)(2,1)S(1)}, bf16[16,1280]{1,0:T(8,128)(2,1)S(1)}, u32[]{:S(2)}, u32[]{:S(2)}) collective-permute-start(bf16[16,1280]{1,0:T(8,128)(2,1)S(1)} %slice.211), channel_id=1, source_target_pairs={{0,8},{1,9},{2,10},{3,11},{4,12},{5,13},{6,14},{7,15},{8,0},{9,1},... | collective-permute-start | bytes 122888 | tf_op jit(solution)/shard_map/ppermute | solution.py:46
  115.0 5.0 %collective-permute-start.21 = (bf16[16,1280]{1,0:T(8,128)(2,1)S(1)}, bf16[16,1280]{1,0:T(8,128)(2,1)S(1)}, u32[]{:S(2)}, u32[]{:S(2)}) collective-permute-start(bf16[16,1280]{1,0:T(8,128)(2,1)S(1)} %fusion.5), channel_id=1, source_target_pairs={{0,16},{1,17},{2,18},{3,19},{4,20},{5,21},{6,22},{7,23},{8,24},{9,... | collective-permute-start | bytes 122888 | tf_op jit(solution)/shard_map/ppermute | solution.py:46
  117.3 5.0 %collective-permute-start.17 = (bf16[16,1280]{1,0:T(8,128)(2,1)S(1)}, bf16[16,1280]{1,0:T(8,128)(2,1)S(1)}, u32[]{:S(2)}, u32[]{:S(2)}) collective-permute-start(bf16[16,1280]{1,0:T(8,128)(2,1)S(1)} %fusion.6), channel_id=1, source_target_pairs={{0,16},{1,17},{2,18},{3,19},{4,20},{5,21},{6,22},{7,23},{8,24},{9,... | collective-permute-start | bytes 122888 | tf_op jit(solution)/shard_map/ppermute | solution.py:46
  122.3 4.5 %collective-permute-start.22 = (bf16[16,2560]{1,0:T(8,128)(2,1)S(1)}, bf16[16,2560]{1,0:T(8,128)(2,1)S(1)}, u32[]{:S(2)}, u32[]{:S(2)}) collective-permute-start(bf16[16,2560]{1,0:T(8,128)(2,1)S(1)} %pad_maximum_fusion.1.refs_2_), channel_id=1, source_target_pairs={{0,8},{1,9},{2,10},{3,11},{4,12},{5,13},{6,14},{7,15},{8,0},{9,1},... | collective-permute-start | bytes 245768 | tf_op jit(solution)/shard_map/ppermute | solution.py:46
  126.9 8.3 %collective-permute-start.25 = (bf16[32,2560]{1,0:T(8,128)(2,1)S(1)}, bf16[32,2560]{1,0:T(8,128)(2,1)S(1)}, u32[]{:S(2)}, u32[]{:S(2)}) collective-permute-start(bf16[32,2560]{1,0:T(8,128)(2,1)S(1)} %pad_maximum_fusion.refs_0_), channel_id=1, source_target_pairs={{0,6},{1,7},{2,4},{3,5},{4,2},{5,3},{6,0},{7,1},{8,14},{9,15},{10,... | collective-permute-start | bytes 491528 | tf_op jit(solution)/shard_map/ppermute | solution.py:46
  129.4 5.8 %collective-permute-start.24 = (bf16[32,2560]{1,0:T(8,128)(2,1)S(1)}, bf16[32,2560]{1,0:T(8,128)(2,1)S(1)}, u32[]{:S(2)}, u32[]{:S(2)}) collective-permute-start(bf16[32,2560]{1,0:T(8,128)(2,1)S(1)} %pad_maximum_fusion.refs_0_), channel_id=1, source_target_pairs={{0,2},{1,5},{2,0},{3,7},{4,6},{5,1},{6,4},{7,3},{8,10},{9,13},{10,... | collective-permute-start | bytes 491528 | tf_op jit(solution)/shard_map/ppermute | solution.py:46
  129.8 5.4 %collective-permute-start.23 = (bf16[32,2560]{1,0:T(8,128)(2,1)S(1)}, bf16[32,2560]{1,0:T(8,128)(2,1)S(1)}, u32[]{:S(2)}, u32[]{:S(2)}) collective-permute-start(bf16[32,2560]{1,0:T(8,128)(2,1)S(1)} %pad_maximum_fusion.refs_0_), channel_id=1, source_target_pairs={{0,4},{1,3},{2,6},{3,1},{4,0},{5,7},{6,2},{7,5},{8,12},{9,11},{10,... | collective-permute-start | bytes 491528 | tf_op jit(solution)/shard_map/ppermute | solution.py:46
  141.5 5.4 %collective-permute-start.27 = (bf16[64,1280]{1,0:T(8,128)(2,1)S(1)}, bf16[64,1280]{1,0:T(8,128)(2,1)S(1)}, u32[]{:S(2)}, u32[]{:S(2)}) collective-permute-start(bf16[64,1280]{1,0:T(8,128)(2,1)S(1)} %get-tuple-element.104), channel_id=1, source_target_pairs={{0,2},{1,5},{2,0},{3,7},{4,6},{5,1},{6,4},{7,3},{8,10},{9,13},{10,... | collective-permute-start | bytes 491528 | tf_op jit(solution)/shard_map/ppermute | solution.py:46
  143.1 5.5 %collective-permute-start.31 = (bf16[64,1280]{1,0:T(8,128)(2,1)S(1)}, bf16[64,1280]{1,0:T(8,128)(2,1)S(1)}, u32[]{:S(2)}, u32[]{:S(2)}) collective-permute-start(bf16[64,1280]{1,0:T(8,128)(2,1)S(1)} %get-tuple-element.106), channel_id=1, source_target_pairs={{0,2},{1,5},{2,0},{3,7},{4,6},{5,1},{6,4},{7,3},{8,10},{9,13},{10,... | collective-permute-start | bytes 491528 | tf_op jit(solution)/shard_map/ppermute | solution.py:46
  146.9 4.5 %collective-permute-start.28 = (bf16[32,1280]{1,0:T(8,128)(2,1)S(1)}, bf16[32,1280]{1,0:T(8,128)(2,1)S(1)}, u32[]{:S(2)}, u32[]{:S(2)}) collective-permute-start(bf16[32,1280]{1,0:T(8,128)(2,1)S(1)} %slice.205), channel_id=1, source_target_pairs={{0,4},{1,3},{2,6},{3,1},{4,0},{5,7},{6,2},{7,5},{8,12},{9,11},{10,... | collective-permute-start | bytes 245768 | tf_op jit(solution)/shard_map/ppermute | solution.py:46
  148.7 4.7 %collective-permute-start.32 = (bf16[32,1280]{1,0:T(8,128)(2,1)S(1)}, bf16[32,1280]{1,0:T(8,128)(2,1)S(1)}, u32[]{:S(2)}, u32[]{:S(2)}) collective-permute-start(bf16[32,1280]{1,0:T(8,128)(2,1)S(1)} %slice.204), channel_id=1, source_target_pairs={{0,4},{1,3},{2,6},{3,1},{4,0},{5,7},{6,2},{7,5},{8,12},{9,11},{10,... | collective-permute-start | bytes 245768 | tf_op jit(solution)/shard_map/ppermute | solution.py:46
  155.6 4.7 %collective-permute-start.30 = (bf16[8,1280]{1,0:T(8,128)(2,1)S(1)}, bf16[8,1280]{1,0:T(8,128)(2,1)S(1)}, u32[]{:S(2)}, u32[]{:S(2)}) collective-permute-start(bf16[8,1280]{1,0:T(8,128)(2,1)S(1)} %slice.213), channel_id=1, source_target_pairs={{0,16},{1,17},{2,18},{3,19},{4,20},{5,21},{6,22},{7,23},{8,24},{9,... | collective-permute-start | bytes 61448 | tf_op jit(solution)/shard_map/ppermute | solution.py:46
  157.5 4.7 %collective-permute-start.34 = (bf16[8,1280]{1,0:T(8,128)(2,1)S(1)}, bf16[8,1280]{1,0:T(8,128)(2,1)S(1)}, u32[]{:S(2)}, u32[]{:S(2)}) collective-permute-start(bf16[8,1280]{1,0:T(8,128)(2,1)S(1)} %slice.212), channel_id=1, source_target_pairs={{0,16},{1,17},{2,18},{3,19},{4,20},{5,21},{6,22},{7,23},{8,24},{9,... | collective-permute-start | bytes 61448 | tf_op jit(solution)/shard_map/ppermute | solution.py:46
  (14 other events, 210.3 us)

commit v9 on v8

--- a/solution.py
+++ b/solution.py
@@ -20,7 +20,6 @@
 ROWS_HALF = HALF_VENUES * NODE_STEPS
 KEYS_HALF = HALF_VENUES * STEPS
 LSE_ITEM = 64
-SUM_PARTS = 2
 VMEM_LIMIT = 8 << 20
 
 
@@ -328,32 +327,25 @@
         up = both(slice(padded + span.start, padded + span.stop)) * scale
         hidden.append((gate * (1.0 / (1.0 + jnp.exp(-gate))) * up).astype(jnp.bfloat16))
     hidden = hidden[0] if len(hidden) == 1 else jnp.concatenate(hidden, axis=1)
-    held = feat // (len(out_refs) // 2)
+    part = rows // 4
     for span in column_tiles(feat, 640):
         total = jnp.dot(hidden, down_ref[:, span], preferred_element_type=jnp.float32)
-        part = span.start // held
-        local = slice(span.start % held, span.start % held + span.stop - span.start)
-        out_refs[2 * part][:, local] = total[: rows // 2]
-        out_refs[2 * part + 1][:, local] = total[rows // 2 :].astype(jnp.bfloat16)
-
-
-def contract(near, far, down, parts, swap):
-    half, feat = near.shape[0] // 2, down.shape[1]
+        for place, ref in enumerate(out_refs):
+            ref[:, span] = total[place * part : (place + 1) * part].astype(ref.dtype)
+
+
+def contract(near, far, down, swap):
+    shape = (near.shape[0] // 4, down.shape[1])
     held = pltpu.with_memory_space_constraint(down, pltpu.VMEM)
-    shape = (half, feat // parts)
-    out = pl.pallas_call(
+    return pl.pallas_call(
         functools.partial(contract_body, swap=swap),
         in_specs=[pl.BlockSpec(memory_space=pltpu.VMEM)] * 3,
-        out_specs=[pl.BlockSpec(memory_space=pltpu.VMEM)] * (2 * parts),
-        out_shape=[
-            jax.ShapeDtypeStruct(shape, jnp.float32),
-            jax.ShapeDtypeStruct(shape, jnp.bfloat16),
-        ]
-        * parts,
+        out_specs=[pl.BlockSpec(memory_space=pltpu.VMEM)] * 4,
+        out_shape=[jax.ShapeDtypeStruct(shape, jnp.float32)]
+        + [jax.ShapeDtypeStruct(shape, jnp.bfloat16)] * 3,
         compiler_params=pltpu.CompilerParams(vmem_limit_bytes=VMEM_LIMIT),
         name="contract",
     )(near, far, held)
-    return [out[2 * part : 2 * part + 2] for part in range(parts)]
 
 
 def per_device(
@@ -454,12 +446,10 @@
     probs, lse = half_scores(queries, keys)
     far_lse = swap_stage(lse, orders, last)
     pooled = half_pool(first, mean_weights(probs, lse, far_lse), values)
-    (gate,), token = stage_weights([gate_proj], 0, [pooled])
+    (gate, up), token = stage_weights([gate_proj, up_proj], 0, [pooled])
     pooled = join_pair(pooled, orders, last).astype(jnp.bfloat16)
     pooled, token = lax.optimization_barrier((pooled, token))
-    (up, down), token = stage_weights([up_proj, down_proj], 0, [token])
-    parts = SUM_PARTS if feat_width % (SUM_PARTS * 128) == 0 else 1
-    part_width = feat_width // parts
+    (down,), token = stage_weights([down_proj], 0, [token])
     for layer_idx in range(ROUNDS):
         nodes = gather_rows(pooled, orders, last)
         near_sums = expand(nodes, mix, type_gain, norm_gain, gate, up, token, layer_idx)
@@ -467,26 +457,26 @@
             far_sums = lax.ppermute(near_sums, "ta", [(0, 1), (1, 0)])
         else:
             far_sums = lax.psum(near_sums.astype(jnp.float32), "ta") - near_sums.astype(jnp.float32)
-        sums = contract(near_sums, far_sums, down, parts, ta_count == 2)
+        held, *gives = contract(near_sums, far_sums, down, ta_count == 2)
         final = layer_idx + 1 == ROUNDS
-        settled = []
-        for part, (held, give) in enumerate(sums):
-            for stage in range(last + 1 if final else last):
-                if stage:
-                    half = held.shape[0] // 2
-                    held, give = held[:half], held[half:].astype(jnp.bfloat16)
-                taken = swap_stage(give, orders, stage)
-                if not final and part == 0 and stage == 0:
-                    (down,), token = stage_weights([down_proj], layer_idx + 1, [give])
-                    taken, token = lax.optimization_barrier((taken, token))
-                held = held + taken.astype(jnp.float32)
-            if not final:
-                held = join_pair(held.astype(jnp.bfloat16), orders, last)
-            rows_kept = pooled[: held.shape[0], part * part_width : (part + 1) * part_width]
-            settled.append((rows_kept.astype(jnp.float32) + held).astype(jnp.bfloat16))
-        pooled = jnp.concatenate(settled, axis=1)
+        taken = [
+            swap_stage(give, orders, *stages)
+            for give, stages in zip(gives, ((1,), (0,), (0, 1)))
+        ]
         if not final:
-            (gate, up), token = stage_weights([gate_proj, up_proj], layer_idx + 1, [pooled, token])
+            (gate, up), token = stage_weights([gate_proj, up_proj], layer_idx + 1, gives)
+            taken, token = lax.optimization_barrier((taken, token))
+        for block in taken:
+            held = held + block.astype(jnp.float32)
+        for stage in range(2, last + 1 if final else last):
+            half = held.shape[0] // 2
+            held, give = held[:half], held[half:].astype(jnp.bfloat16)
+            held = held + swap_stage(give, orders, stage).astype(jnp.float32)
+        if not final:
+            held = join_pair(held.astype(jnp.bfloat16), orders, last)
+        pooled = (pooled[: held.shape[0]].astype(jnp.float32) + held).astype(jnp.bfloat16)
+        if not final:
+            (down,), token = stage_weights([down_proj], layer_idx + 1, [pooled, token])
     return pooled
 
 

time: 163 us -> 161 us (0.988)
  starting transfers between devices: 61.6 us -> 54.5 us
  waiting for transfers between devices: 61.2 us -> 66.3 us
    ppermute x26 -> x20, starting transfers between devices: 38.9 us -> 31.8 us  [swap_stage(): return lax.ppermute(block, ('gx', 'ta'), pairs)]
    ppermute x26 -> x20, waiting for transfers between devices: 31.3 us -> 36.3 us  [swap_stage(): return lax.ppermute(block, ('gx', 'ta'), pairs)]
  transfers between devices with their start and end apart: 37 -> 31, of which waited for: 27 -> 23; matrix products, arithmetic and copies ran while one was open for 1% -> 0% of each run, Pallas kernels for 14% -> 15%
where the time goes in v9:
time: 161 us
  waiting for transfers between devices  66.3 us (41%)
  starting transfers between devices  54.5 us (34%)
  Pallas kernels  34.1 us (21%)
  local copies, waits for them, and re-layouts  3.32 us (2%)
  other arithmetic  1.65 us (1%)
    ppermute x20, waiting for transfers between devices, swap_stage(): return lax.ppermute(block, ('gx', 'ta'), pairs)  36.3 us
    ppermute x20, starting transfers between devices, swap_stage(): return lax.ppermute(block, ('gx', 'ta'), pairs)  31.8 us
    ppermute x7, waiting for transfers between devices, per_device(): keys.append(lax.ppermute(pieces[flip], 'gx', pairs))  24.9 us
    pallas_call x4, Pallas kernels, stage_weights(): pl.pallas_call(functools.partial(stage_body, layer=layer, count=len(held)...  15.3 us
    ppermute x7, starting transfers between devices, per_device(): keys.append(lax.ppermute(pieces[flip], 'gx', pairs))  10.5 us
    all_to_all x1, starting transfers between devices, per_device(): lax.all_to_all(queries.reshape(gx_count, -1, feat_width), 'gx', 0, 0, til...  8.36 us
    pallas_call x2, Pallas kernels, expand(): pl.pallas_call(functools.partial(expand_body, layer=layer), in_specs=[pl....  5.42 us
    ppermute x2, waiting for transfers between devices, per_device(): far_sums = lax.ppermute(near_sums, 'ta', [(0, 1), (1, 0)])  4.26 us
  transfers between devices with their start and end apart: 31, of which 23 were waited for; matrix products, arithmetic and copies ran while one was open for 0% of the time, Pallas kernels for 15%

profile of v9, /device:TPU:0, one launch (start us, length us, event | category | flops | bytes accessed | tf_op | source)
XLA Modules:
  0.0 160.7 jit_solution(12373819664371250036)
XLA Ops:
  3.9 8.4 %all-to-all-start = ((bf16[16,16,2560]{2,1,0:T(8,128)(2,1)}), bf16[16,16,2560]{2,1,0:T(8,128)(2,1)}, u32[]{:S(2)}, u32[]{:S(2)}) async-start(bf16[16,16,2560]{2,1,0:T(8,128)(2,1)} %bitcast.4), calls=%async_computation | async-start | bytes 2621440 | tf_op jit(solution)/shard_map/all_to_all | solution.py:407
  22.6 2.8 %collective-permute-start.5 = (bf16[32,2560]{1,0:T(8,128)(2,1)S(1)}, bf16[32,2560]{1,0:T(8,128)(2,1)S(1)}, u32[]{:S(2)}, u32[]{:S(2)}) collective-permute-start(bf16[32,2560]{1,0:T(8,128)(2,1)S(1)} %get-tuple-element.63), channel_id=1, source_target_pairs={{0,12},{2,14},{4,8},{6,10},{8,4},{10,6},{12,0},{14,2},{16,28},{18,... | collective-permute-start | bytes 491528 | tf_op jit(solution)/shard_map/ppermute | solution.py:418
  25.4 6.7 %collective-permute-done.1.refs_2_ = bf16[32,2560]{1,0:T(8,128)(2,1)S(1)} collective-permute-done((bf16[32,2560]{1,0:T(8,128)(2,1)S(1)}, bf16[32,2560]{1,0:T(8,128)(2,1)S(1)}, u32[]{:S(2)}, u32[]{:S(2)}) %collective-permute-start.1) | collective-permute-done | bytes 163872 | tf_op jit(solution)/shard_map/ppermute | solution.py:418
  34.5 4.6 %collective-permute-done.3.refs_4_ = bf16[32,2560]{1,0:T(8,128)(2,1)S(1)} collective-permute-done((bf16[32,2560]{1,0:T(8,128)(2,1)S(1)}, bf16[32,2560]{1,0:T(8,128)(2,1)S(1)}, u32[]{:S(2)}, u32[]{:S(2)}) %collective-permute-start.3) | collective-permute-done | bytes 163872 | tf_op jit(solution)/shard_map/ppermute | solution.py:418
  39.1 5.4 %collective-permute-done.4.refs_5_ = bf16[32,2560]{1,0:T(8,128)(2,1)S(1)} collective-permute-done((bf16[32,2560]{1,0:T(8,128)(2,1)S(1)}, bf16[32,2560]{1,0:T(8,128)(2,1)S(1)}, u32[]{:S(2)}, u32[]{:S(2)}) %collective-permute-start.4) | collective-permute-done | bytes 163872 | tf_op jit(solution)/shard_map/ppermute | solution.py:418
  44.5 4.2 %collective-permute-done.5.refs_6_ = bf16[32,2560]{1,0:T(8,128)(2,1)S(1)} collective-permute-done((bf16[32,2560]{1,0:T(8,128)(2,1)S(1)}, bf16[32,2560]{1,0:T(8,128)(2,1)S(1)}, u32[]{:S(2)}, u32[]{:S(2)}) %collective-permute-start.5) | collective-permute-done | bytes 163872 | tf_op jit(solution)/shard_map/ppermute | solution.py:418
  48.7 3.2 %collective-permute-done.6.refs_7_ = bf16[32,2560]{1,0:T(8,128)(2,1)S(1)} collective-permute-done((bf16[32,2560]{1,0:T(8,128)(2,1)S(1)}, bf16[32,2560]{1,0:T(8,128)(2,1)S(1)}, u32[]{:S(2)}, u32[]{:S(2)}) %collective-permute-start.6) | collective-permute-done | bytes 163872 | tf_op jit(solution)/shard_map/ppermute | solution.py:418
  51.9 3.8 %all-to-all-start.1 = ((bf16[8,32,2560]{2,1,0:T(8,128)(2,1)}), bf16[8,32,2560]{2,1,0:T(8,128)(2,1)S(1)}, u32[]{:S(2)}, u32[]{:S(2)}) async-start(bf16[8,32,2560]{2,1,0:T(8,128)(2,1)} %bitcast.10), calls=%async_computation.1 | async-start | bytes 2621440 | tf_op jit(solution)/shard_map/all_to_all | solution.py:397
  56.2 4.0 %half_scores.1 = (bf16[20,2,128,128]{3,2,1,0:T(8,128)(2,1)S(1)}, f32[128,128]{1,0:T(8,128)S(1)}) custom-call(bf16[256,2560]{1,0:T(8,128)(2,1)} %bitcast.5.query_ref, bf16[32,2560]{1,0:T(8,128)(2,1)S(1)} %get-tuple-element.74.refs_0_, bf16[32,2560]{1,0:T(8,128)(2,1)S(1)} %collective-permute-done.refs_1_, bf16[32,2560]{1,0:T(8,128)(2,1)S(1)} %collective-permute-done.1.refs_2_, ...), custom_call_target="tpu_custom_call" | custom-call | tf_op jit(solution)/shard_map/half_scores/pallas_call | solution.py:136
  60.2 2.7 %collective-permute-start.7 = (f32[128,128]{1,0:T(8,128)S(1)}, f32[128,128]{1,0:T(8,128)S(1)}, u32[]{:S(2)}, u32[]{:S(2)}) collective-permute-start(f32[128,128]{1,0:T(8,128)S(1)} %get-tuple-element.83.lse_ref), channel_id=1, source_target_pairs={{0,16},{1,17},{2,18},{3,19},{4,20},{5,21},{6,22},{7,23},{8,24},{9,... | collective-permute-start | bytes 196616 | tf_op jit(solution)/shard_map/ppermute | solution.py:45
  62.9 7.7 %collective-permute-done.7.far_ref = f32[128,128]{1,0:T(8,128)S(1)} collective-permute-done((f32[128,128]{1,0:T(8,128)S(1)}, f32[128,128]{1,0:T(8,128)S(1)}, u32[]{:S(2)}, u32[]{:S(2)}) %collective-permute-start.7) | collective-permute-done | bytes 65568 | tf_op jit(solution)/shard_map/ppermute | solution.py:45
  73.8 2.7 %collective-permute-start.8 = (bf16[16,2560]{1,0:T(8,128)(2,1)S(1)}, bf16[16,2560]{1,0:T(8,128)(2,1)S(1)}, u32[]{:S(2)}, u32[]{:S(2)}) collective-permute-start(bf16[16,2560]{1,0:T(8,128)(2,1)S(1)} %half_pool.1.refs_2_), channel_id=1, source_target_pairs={{0,16},{1,17},{2,18},{3,19},{4,20},{5,21},{6,22},{7,23},{8,24},{9,... | collective-permute-start | bytes 245768 | tf_op jit(solution)/shard_map/ppermute | solution.py:45
  76.6 4.8 %stage_weights.4 = (bf16[2560,1280]{1,0:T(8,128)(2,1)S(1)}, bf16[2560,1280]{1,0:T(8,128)(2,1)S(1)}, f32[8,128]{1,0:T(8,128)S(1)}) custom-call(bf16[2,2560,1280]{2,1,0:T(8,128)(2,1)} %refs_0_.6, bf16[2,2560,1280]{2,1,0:T(8,128)(2,1)} %refs_1_.3, bf16[16,2560]{1,0:T(8,128)(2,1)S(1)} %half_pool.1.refs_2_), custom_call_target="tpu_custom_call" | custom-call | bytes 26214400 | tf_op jit(solution)/shard_map/stage_weights/pallas_call | solution.py:242
  83.2 2.7 %collective-permute-done.9 = bf16[16,2560]{1,0:T(8,128)(2,1)S(1)} collective-permute-done((bf16[16,2560]{1,0:T(8,128)(2,1)S(1)}, bf16[16,2560]{1,0:T(8,128)(2,1)S(1)}, u32[]{:S(2)}, u32[]{:S(2)}) %collective-permute-start.9) | collective-permute-done | bytes 81952 | tf_op jit(solution)/shard_map/ppermute | solution.py:45
  85.9 2.4 %collective-permute-start.12 = (bf16[32,2560]{1,0:T(8,128)(2,1)S(1)}, bf16[32,2560]{1,0:T(8,128)(2,1)S(1)}, u32[]{:S(2)}, u32[]{:S(2)}) collective-permute-start(bf16[32,2560]{1,0:T(8,128)(2,1)S(1)} %constant_dynamic-update-slice_fusion.refs_0_), channel_id=1, source_target_pairs={{0,6},{1,7},{2,4},{3,5},{4,2},{5,3},{6,0},{7,1},{8,14},{9,15},{10,... | collective-permute-start | bytes 491528 | tf_op jit(solution)/shard_map/ppermute | solution.py:45
  89.4 2.9 %stage_weights.5 = (bf16[1280,2560]{1,0:T(8,128)(2,1)S(1)}, f32[8,128]{1,0:T(8,128)S(1)}) custom-call(bf16[2,1280,2560]{2,1,0:T(8,128)(2,1)} %refs_0_.7, f32[8,128]{1,0:T(8,128)S(1)} %get-tuple-element.91.refs_1_), custom_call_target="tpu_custom_call" | custom-call | bytes 13107200 | tf_op jit(solution)/shard_map/stage_weights/pallas_call | solution.py:242
  94.2 2.7 %expand.2.near_ref = bf16[128,2688]{1,0:T(8,128)(2,1)S(1)} custom-call(bf16[32,2560]{1,0:T(8,128)(2,1)S(1)} %constant_dynamic-update-slice_fusion.refs_0_, bf16[32,2560]{1,0:T(8,128)(2,1)S(1)} %collective-permute-done.10.refs_1_, bf16[32,2560]{1,0:T(8,128)(2,1)S(1)} %collective-permute-done.11.refs_2_, bf16[32,2560]{1,0:T(8,128)(2,1)S(1)} %collective-permute-done.12.refs_3_, ...), custom_call_target="tpu_custom_call" | custom-call | tf_op jit(solution)/shard_map/expand/pallas_call | solution.py:297
  97.0 2.1 %collective-permute-done.13.far_ref = bf16[128,2688]{1,0:T(8,128)(2,1)S(1)} collective-permute-done((bf16[128,2688]{1,0:T(8,128)(2,1)S(1)}, bf16[128,2688]{1,0:T(8,128)(2,1)S(1)}, u32[]{:S(2)}, u32[]{:S(2)}) %collective-permute-start.13) | collective-permute-done | bytes 688160 | tf_op jit(solution)/shard_map/ppermute | solution.py:457
  104.1 4.8 %stage_weights.6 = (bf16[2560,1280]{1,0:T(8,128)(2,1)S(1)}, bf16[2560,1280]{1,0:T(8,128)(2,1)S(1)}, f32[8,128]{1,0:T(8,128)S(1)}) custom-call(bf16[2,2560,1280]{2,1,0:T(8,128)(2,1)} %refs_0_.6, bf16[2,2560,1280]{2,1,0:T(8,128)(2,1)} %refs_1_.3, bf16[32,2560]{1,0:T(8,128)(2,1)S(1)} %get-tuple-element.95.refs_2_, ...), custom_call_target="tpu_custom_call" | custom-call | bytes 26214400 | tf_op jit(solution)/shard_map/stage_weights/pallas_call | solution.py:242
  108.9 2.2 %collective-permute-done.16 = bf16[32,2560]{1,0:T(8,128)(2,1)S(1)} collective-permute-done((bf16[32,2560]{1,0:T(8,128)(2,1)S(1)}, bf16[32,2560]{1,0:T(8,128)(2,1)S(1)}, u32[]{:S(2)}, u32[]{:S(2)}) %collective-permute-start.16) | collective-permute-done | bytes 163872 | tf_op jit(solution)/shard_map/ppermute | solution.py:45
  112.9 2.8 %collective-permute-done.17 = bf16[16,2560]{1,0:T(8,128)(2,1)S(1)} collective-permute-done((bf16[16,2560]{1,0:T(8,128)(2,1)S(1)}, bf16[16,2560]{1,0:T(8,128)(2,1)S(1)}, u32[]{:S(2)}, u32[]{:S(2)}) %collective-permute-start.17) | collective-permute-done | bytes 81952 | tf_op jit(solution)/shard_map/ppermute | solution.py:45
  115.7 2.3 %collective-permute-start.18 = (bf16[16,2560]{1,0:T(8,128)(2,1)S(1)}, bf16[16,2560]{1,0:T(8,128)(2,1)S(1)}, u32[]{:S(2)}, u32[]{:S(2)}) collective-permute-start(bf16[16,2560]{1,0:T(8,128)(2,1)S(1)} %fusion.3), channel_id=1, source_target_pairs={{0,16},{1,17},{2,18},{3,19},{4,20},{5,21},{6,22},{7,23},{8,24},{9,... | collective-permute-start | bytes 245768 | tf_op jit(solution)/shard_map/ppermute | solution.py:45
  118.0 3.1 %collective-permute-done.18 = bf16[16,2560]{1,0:T(8,128)(2,1)S(1)} collective-permute-done((bf16[16,2560]{1,0:T(8,128)(2,1)S(1)}, bf16[16,2560]{1,0:T(8,128)(2,1)S(1)}, u32[]{:S(2)}, u32[]{:S(2)}) %collective-permute-start.18) | collective-permute-done | bytes 81952 | tf_op jit(solution)/shard_map/ppermute | solution.py:45
  122.8 2.8 %collective-permute-done.19 = bf16[16,2560]{1,0:T(8,128)(2,1)S(1)} collective-permute-done((bf16[16,2560]{1,0:T(8,128)(2,1)S(1)}, bf16[16,2560]{1,0:T(8,128)(2,1)S(1)}, u32[]{:S(2)}, u32[]{:S(2)}) %collective-permute-start.19) | collective-permute-done | bytes 81952 | tf_op jit(solution)/shard_map/ppermute | solution.py:45
  129.2 2.9 %stage_weights.7 = (bf16[1280,2560]{1,0:T(8,128)(2,1)S(1)}, f32[8,128]{1,0:T(8,128)S(1)}) custom-call(bf16[2,1280,2560]{2,1,0:T(8,128)(2,1)} %refs_0_.7, bf16[16,2560]{1,0:T(8,128)(2,1)S(1)} %add_convert_fusion.refs_1_, f32[8,128]{1,0:T(8,128)S(1)} %get-tuple-element.104.refs_2_), custom_call_target="tpu_custom_call" | custom-call | bytes 13107200 | tf_op jit(solution)/shard_map/stage_weights/pallas_call | solution.py:242
  133.7 2.7 %expand.3.near_ref = bf16[128,2688]{1,0:T(8,128)(2,1)S(1)} custom-call(bf16[32,2560]{1,0:T(8,128)(2,1)S(1)} %pad_maximum_fusion.refs_0_, bf16[32,2560]{1,0:T(8,128)(2,1)S(1)} %collective-permute-done.20.refs_1_, bf16[32,2560]{1,0:T(8,128)(2,1)S(1)} %collective-permute-done.21.refs_2_, bf16[32,2560]{1,0:T(8,128)(2,1)S(1)} %collective-permute-done.22.refs_3_, ...), custom_call_target="tpu_custom_call" | custom-call | tf_op jit(solution)/shard_map/expand/pallas_call | solution.py:297
  136.5 2.1 %collective-permute-done.23.far_ref = bf16[128,2688]{1,0:T(8,128)(2,1)S(1)} collective-permute-done((bf16[128,2688]{1,0:T(8,128)(2,1)S(1)}, bf16[128,2688]{1,0:T(8,128)(2,1)S(1)}, u32[]{:S(2)}, u32[]{:S(2)}) %collective-permute-start.23) | collective-permute-done | bytes 688160 | tf_op jit(solution)/shard_map/ppermute | solution.py:457
  143.6 4.6 %collective-permute-done.24 = bf16[32,2560]{1,0:T(8,128)(2,1)S(1)} collective-permute-done((bf16[32,2560]{1,0:T(8,128)(2,1)S(1)}, bf16[32,2560]{1,0:T(8,128)(2,1)S(1)}, u32[]{:S(2)}, u32[]{:S(2)}) %collective-permute-start.24) | collective-permute-done | bytes 163872 | tf_op jit(solution)/shard_map/ppermute | solution.py:45
  148.2 2.3 %collective-permute-done.26 = bf16[32,2560]{1,0:T(8,128)(2,1)S(1)} collective-permute-done((bf16[32,2560]{1,0:T(8,128)(2,1)S(1)}, bf16[32,2560]{1,0:T(8,128)(2,1)S(1)}, u32[]{:S(2)}, u32[]{:S(2)}) %collective-permute-start.26) | collective-permute-done | bytes 163872 | tf_op jit(solution)/shard_map/ppermute | solution.py:45
  152.3 2.8 %collective-permute-done.27 = bf16[16,2560]{1,0:T(8,128)(2,1)S(1)} collective-permute-done((bf16[16,2560]{1,0:T(8,128)(2,1)S(1)}, bf16[16,2560]{1,0:T(8,128)(2,1)S(1)}, u32[]{:S(2)}, u32[]{:S(2)}) %collective-permute-start.27) | collective-permute-done | bytes 81952 | tf_op jit(solution)/shard_map/ppermute | solution.py:45
  155.1 3.0 %collective-permute-start.28 = (bf16[8,2560]{1,0:T(8,128)(2,1)S(1)}, bf16[8,2560]{1,0:T(8,128)(2,1)S(1)}, u32[]{:S(2)}, u32[]{:S(2)}) collective-permute-start(bf16[8,2560]{1,0:T(8,128)(2,1)S(1)} %slice.83), channel_id=1, source_target_pairs={{0,16},{1,17},{2,18},{3,19},{4,20},{5,21},{6,22},{7,23},{8,24},{9,... | collective-permute-start | bytes 122888 | tf_op jit(solution)/shard_map/ppermute | solution.py:45
  158.1 2.0 %collective-permute-done.28 = bf16[8,2560]{1,0:T(8,128)(2,1)S(1)} collective-permute-done((bf16[8,2560]{1,0:T(8,128)(2,1)S(1)}, bf16[8,2560]{1,0:T(8,128)(2,1)S(1)}, u32[]{:S(2)}, u32[]{:S(2)}) %collective-permute-start.28) | collective-permute-done | bytes 40992 | tf_op jit(solution)/shard_map/ppermute | solution.py:45
  (98 shorter events, 46.3 us)
Async XLA Ops:
  0.0 55.7 %copy-start.7 = (s32[64,2]{0,1:T(2,128)S(1)}, s32[64,2]{0,1:T(2,128)}, u32[]{:S(2)}) copy-start(s32[64,2]{0,1:T(2,128)} %param.15) | copy-start | bytes 1540
  3.9 48.0 %all-to-all-start = ((bf16[16,16,2560]{2,1,0:T(8,128)(2,1)}), bf16[16,16,2560]{2,1,0:T(8,128)(2,1)}, u32[]{:S(2)}, u32[]{:S(2)}) async-start(bf16[16,16,2560]{2,1,0:T(8,128)(2,1)} %bitcast.4), calls=%async_computation | async-start | bytes 2621440 | tf_op jit(solution)/shard_map/all_to_all | solution.py:407
  14.8 7.8 %collective-permute-start = (bf16[32,2560]{1,0:T(8,128)(2,1)S(1)}, bf16[32,2560]{1,0:T(8,128)(2,1)S(1)}, u32[]{:S(2)}, u32[]{:S(2)}) collective-permute-start(bf16[32,2560]{1,0:T(8,128)(2,1)S(1)} %get-tuple-element.58), channel_id=1, source_target_pairs={{0,2},{2,0},{4,6},{6,4},{8,10},{10,8},{12,14},{14,12},{16,18},{18,... | collective-permute-start | bytes 491528 | tf_op jit(solution)/shard_map/ppermute | solution.py:418
  16.8 15.3 %collective-permute-start.1 = (bf16[32,2560]{1,0:T(8,128)(2,1)S(1)}, bf16[32,2560]{1,0:T(8,128)(2,1)S(1)}, u32[]{:S(2)}, u32[]{:S(2)}) collective-permute-start(bf16[32,2560]{1,0:T(8,128)(2,1)S(1)} %get-tuple-element.59), channel_id=1, source_target_pairs={{0,4},{2,6},{4,0},{6,2},{8,12},{10,14},{12,8},{14,10},{16,20},{18,... | collective-permute-start | bytes 491528 | tf_op jit(solution)/shard_map/ppermute | solution.py:418
  18.2 16.3 %collective-permute-start.2 = (bf16[32,2560]{1,0:T(8,128)(2,1)S(1)}, bf16[32,2560]{1,0:T(8,128)(2,1)S(1)}, u32[]{:S(2)}, u32[]{:S(2)}) collective-permute-start(bf16[32,2560]{1,0:T(8,128)(2,1)S(1)} %get-tuple-element.60), channel_id=1, source_target_pairs={{0,6},{2,4},{4,2},{6,0},{8,14},{10,12},{12,10},{14,8},{16,22},{18,... | collective-permute-start | bytes 491528 | tf_op jit(solution)/shard_map/ppermute | solution.py:418
  18.4 20.8 %collective-permute-start.3 = (bf16[32,2560]{1,0:T(8,128)(2,1)S(1)}, bf16[32,2560]{1,0:T(8,128)(2,1)S(1)}, u32[]{:S(2)}, u32[]{:S(2)}) collective-permute-start(bf16[32,2560]{1,0:T(8,128)(2,1)S(1)} %get-tuple-element.61), channel_id=1, source_target_pairs={{0,8},{2,10},{4,12},{6,14},{8,0},{10,2},{12,4},{14,6},{16,24},{18,... | collective-permute-start | bytes 491528 | tf_op jit(solution)/shard_map/ppermute | solution.py:418
  20.3 24.3 %collective-permute-start.4 = (bf16[32,2560]{1,0:T(8,128)(2,1)S(1)}, bf16[32,2560]{1,0:T(8,128)(2,1)S(1)}, u32[]{:S(2)}, u32[]{:S(2)}) collective-permute-start(bf16[32,2560]{1,0:T(8,128)(2,1)S(1)} %get-tuple-element.62), channel_id=1, source_target_pairs={{0,10},{2,8},{4,14},{6,12},{8,2},{10,0},{12,6},{14,4},{16,26},{18,... | collective-permute-start | bytes 491528 | tf_op jit(solution)/shard_map/ppermute | solution.py:418
  22.6 26.1 %collective-permute-start.5 = (bf16[32,2560]{1,0:T(8,128)(2,1)S(1)}, bf16[32,2560]{1,0:T(8,128)(2,1)S(1)}, u32[]{:S(2)}, u32[]{:S(2)}) collective-permute-start(bf16[32,2560]{1,0:T(8,128)(2,1)S(1)} %get-tuple-element.63), channel_id=1, source_target_pairs={{0,12},{2,14},{4,8},{6,10},{8,4},{10,6},{12,0},{14,2},{16,28},{18,... | collective-permute-start | bytes 491528 | tf_op jit(solution)/shard_map/ppermute | solution.py:418
  32.1 19.8 %collective-permute-start.6 = (bf16[32,2560]{1,0:T(8,128)(2,1)S(1)}, bf16[32,2560]{1,0:T(8,128)(2,1)S(1)}, u32[]{:S(2)}, u32[]{:S(2)}) collective-permute-start(bf16[32,2560]{1,0:T(8,128)(2,1)S(1)} %get-tuple-element.64), channel_id=1, source_target_pairs={{0,14},{2,12},{4,10},{6,8},{8,6},{10,4},{12,2},{14,0},{16,30},{18,... | collective-permute-start | bytes 491528 | tf_op jit(solution)/shard_map/ppermute | solution.py:418
  51.9 20.9 %all-to-all-start.1 = ((bf16[8,32,2560]{2,1,0:T(8,128)(2,1)}), bf16[8,32,2560]{2,1,0:T(8,128)(2,1)S(1)}, u32[]{:S(2)}, u32[]{:S(2)}) async-start(bf16[8,32,2560]{2,1,0:T(8,128)(2,1)} %bitcast.10), calls=%async_computation.1 | async-start | bytes 2621440 | tf_op jit(solution)/shard_map/all_to_all | solution.py:397
  60.2 10.4 %collective-permute-start.7 = (f32[128,128]{1,0:T(8,128)S(1)}, f32[128,128]{1,0:T(8,128)S(1)}, u32[]{:S(2)}, u32[]{:S(2)}) collective-permute-start(f32[128,128]{1,0:T(8,128)S(1)} %get-tuple-element.83.lse_ref), channel_id=1, source_target_pairs={{0,16},{1,17},{2,18},{3,19},{4,20},{5,21},{6,22},{7,23},{8,24},{9,... | collective-permute-start | bytes 196616 | tf_op jit(solution)/shard_map/ppermute | solution.py:45
  73.8 7.5 %collective-permute-start.8 = (bf16[16,2560]{1,0:T(8,128)(2,1)S(1)}, bf16[16,2560]{1,0:T(8,128)(2,1)S(1)}, u32[]{:S(2)}, u32[]{:S(2)}) collective-permute-start(bf16[16,2560]{1,0:T(8,128)(2,1)S(1)} %half_pool.1.refs_2_), channel_id=1, source_target_pairs={{0,16},{1,17},{2,18},{3,19},{4,20},{5,21},{6,22},{7,23},{8,24},{9,... | collective-permute-start | bytes 245768 | tf_op jit(solution)/shard_map/ppermute | solution.py:45
  81.4 4.5 %collective-permute-start.9 = (bf16[16,2560]{1,0:T(8,128)(2,1)S(1)}, bf16[16,2560]{1,0:T(8,128)(2,1)S(1)}, u32[]{:S(2)}, u32[]{:S(2)}) collective-permute-start(bf16[16,2560]{1,0:T(8,128)(2,1)S(1)} %add_convert_fusion.1), channel_id=1, source_target_pairs={{0,8},{1,9},{2,10},{3,11},{4,12},{5,13},{6,14},{7,15},{8,0},{9,1},... | collective-permute-start | bytes 245768 | tf_op jit(solution)/shard_map/ppermute | solution.py:45
  85.9 6.4 %collective-permute-start.12 = (bf16[32,2560]{1,0:T(8,128)(2,1)S(1)}, bf16[32,2560]{1,0:T(8,128)(2,1)S(1)}, u32[]{:S(2)}, u32[]{:S(2)}) collective-permute-start(bf16[32,2560]{1,0:T(8,128)(2,1)S(1)} %constant_dynamic-update-slice_fusion.refs_0_), channel_id=1, source_target_pairs={{0,6},{1,7},{2,4},{3,5},{4,2},{5,3},{6,0},{7,1},{8,14},{9,15},{10,... | collective-permute-start | bytes 491528 | tf_op jit(solution)/shard_map/ppermute | solution.py:45
  88.3 5.6 %collective-permute-start.11 = (bf16[32,2560]{1,0:T(8,128)(2,1)S(1)}, bf16[32,2560]{1,0:T(8,128)(2,1)S(1)}, u32[]{:S(2)}, u32[]{:S(2)}) collective-permute-start(bf16[32,2560]{1,0:T(8,128)(2,1)S(1)} %constant_dynamic-update-slice_fusion.refs_0_), channel_id=1, source_target_pairs={{0,2},{1,5},{2,0},{3,7},{4,6},{5,1},{6,4},{7,3},{8,10},{9,13},{10,... | collective-permute-start | bytes 491528 | tf_op jit(solution)/shard_map/ppermute | solution.py:45
  88.9 5.3 %collective-permute-start.10 = (bf16[32,2560]{1,0:T(8,128)(2,1)S(1)}, bf16[32,2560]{1,0:T(8,128)(2,1)S(1)}, u32[]{:S(2)}, u32[]{:S(2)}) collective-permute-start(bf16[32,2560]{1,0:T(8,128)(2,1)S(1)} %constant_dynamic-update-slice_fusion.refs_0_), channel_id=1, source_target_pairs={{0,4},{1,3},{2,6},{3,1},{4,0},{5,7},{6,2},{7,5},{8,12},{9,11},{10,... | collective-permute-start | bytes 491528 | tf_op jit(solution)/shard_map/ppermute | solution.py:45
  96.9 2.2 %collective-permute-start.13 = (bf16[128,2688]{1,0:T(8,128)(2,1)S(1)}, bf16[128,2688]{1,0:T(8,128)(2,1)S(1)}, u32[]{:S(2)}, u32[]{:S(2)}) collective-permute-start(bf16[128,2688]{1,0:T(8,128)(2,1)S(1)} %expand.2.near_ref), channel_id=1, source_target_pairs={{0,1},{1,0},{2,3},{3,2},{4,5},{5,4},{6,7},{7,6},{8,9},{9,8},{10,11... | collective-permute-start | bytes 2064392 | tf_op jit(solution)/shard_map/ppermute | solution.py:457
  100.5 8.3 %collective-permute-start.14 = (bf16[32,2560]{1,0:T(8,128)(2,1)S(1)}, bf16[32,2560]{1,0:T(8,128)(2,1)S(1)}, u32[]{:S(2)}, u32[]{:S(2)}) collective-permute-start(bf16[32,2560]{1,0:T(8,128)(2,1)S(1)} %get-tuple-element.95.refs_2_), channel_id=1, source_target_pairs={{0,4},{1,3},{2,6},{3,1},{4,0},{5,7},{6,2},{7,5},{8,12},{9,11},{10,... | collective-permute-start | bytes 491528 | tf_op jit(solution)/shard_map/ppermute | solution.py:45
  101.8 7.1 %collective-permute-start.15 = (bf16[32,2560]{1,0:T(8,128)(2,1)S(1)}, bf16[32,2560]{1,0:T(8,128)(2,1)S(1)}, u32[]{:S(2)}, u32[]{:S(2)}) collective-permute-start(bf16[32,2560]{1,0:T(8,128)(2,1)S(1)} %get-tuple-element.96.refs_3_), channel_id=1, source_target_pairs={{0,2},{1,5},{2,0},{3,7},{4,6},{5,1},{6,4},{7,3},{8,10},{9,13},{10,... | collective-permute-start | bytes 491528 | tf_op jit(solution)/shard_map/ppermute | solution.py:45
  103.3 7.8 %collective-permute-start.16 = (bf16[32,2560]{1,0:T(8,128)(2,1)S(1)}, bf16[32,2560]{1,0:T(8,128)(2,1)S(1)}, u32[]{:S(2)}, u32[]{:S(2)}) collective-permute-start(bf16[32,2560]{1,0:T(8,128)(2,1)S(1)} %get-tuple-element.97.refs_4_), channel_id=1, source_target_pairs={{0,6},{1,7},{2,4},{3,5},{4,2},{5,3},{6,0},{7,1},{8,14},{9,15},{10,... | collective-permute-start | bytes 491528 | tf_op jit(solution)/shard_map/ppermute | solution.py:45
  111.1 4.5 %collective-permute-start.17 = (bf16[16,2560]{1,0:T(8,128)(2,1)S(1)}, bf16[16,2560]{1,0:T(8,128)(2,1)S(1)}, u32[]{:S(2)}, u32[]{:S(2)}) collective-permute-start(bf16[16,2560]{1,0:T(8,128)(2,1)S(1)} %slice.82), channel_id=1, source_target_pairs={{0,8},{1,9},{2,10},{3,11},{4,12},{5,13},{6,14},{7,15},{8,0},{9,1},... | collective-permute-start | bytes 245768 | tf_op jit(solution)/shard_map/ppermute | solution.py:45
  115.7 5.4 %collective-permute-start.18 = (bf16[16,2560]{1,0:T(8,128)(2,1)S(1)}, bf16[16,2560]{1,0:T(8,128)(2,1)S(1)}, u32[]{:S(2)}, u32[]{:S(2)}) collective-permute-start(bf16[16,2560]{1,0:T(8,128)(2,1)S(1)} %fusion.3), channel_id=1, source_target_pairs={{0,16},{1,17},{2,18},{3,19},{4,20},{5,21},{6,22},{7,23},{8,24},{9,... | collective-permute-start | bytes 245768 | tf_op jit(solution)/shard_map/ppermute | solution.py:45
  121.1 4.5 %collective-permute-start.19 = (bf16[16,2560]{1,0:T(8,128)(2,1)S(1)}, bf16[16,2560]{1,0:T(8,128)(2,1)S(1)}, u32[]{:S(2)}, u32[]{:S(2)}) collective-permute-start(bf16[16,2560]{1,0:T(8,128)(2,1)S(1)} %add_convert_fusion.refs_1_), channel_id=1, source_target_pairs={{0,8},{1,9},{2,10},{3,11},{4,12},{5,13},{6,14},{7,15},{8,0},{9,1},... | collective-permute-start | bytes 245768 | tf_op jit(solution)/shard_map/ppermute | solution.py:45
  125.7 6.5 %collective-permute-start.22 = (bf16[32,2560]{1,0:T(8,128)(2,1)S(1)}, bf16[32,2560]{1,0:T(8,128)(2,1)S(1)}, u32[]{:S(2)}, u32[]{:S(2)}) collective-permute-start(bf16[32,2560]{1,0:T(8,128)(2,1)S(1)} %pad_maximum_fusion.refs_0_), channel_id=1, source_target_pairs={{0,6},{1,7},{2,4},{3,5},{4,2},{5,3},{6,0},{7,1},{8,14},{9,15},{10,... | collective-permute-start | bytes 491528 | tf_op jit(solution)/shard_map/ppermute | solution.py:45
  127.6 5.7 %collective-permute-start.21 = (bf16[32,2560]{1,0:T(8,128)(2,1)S(1)}, bf16[32,2560]{1,0:T(8,128)(2,1)S(1)}, u32[]{:S(2)}, u32[]{:S(2)}) collective-permute-start(bf16[32,2560]{1,0:T(8,128)(2,1)S(1)} %pad_maximum_fusion.refs_0_), channel_id=1, source_target_pairs={{0,2},{1,5},{2,0},{3,7},{4,6},{5,1},{6,4},{7,3},{8,10},{9,13},{10,... | collective-permute-start | bytes 491528 | tf_op jit(solution)/shard_map/ppermute | solution.py:45
  128.3 5.4 %collective-permute-start.20 = (bf16[32,2560]{1,0:T(8,128)(2,1)S(1)}, bf16[32,2560]{1,0:T(8,128)(2,1)S(1)}, u32[]{:S(2)}, u32[]{:S(2)}) collective-permute-start(bf16[32,2560]{1,0:T(8,128)(2,1)S(1)} %pad_maximum_fusion.refs_0_), channel_id=1, source_target_pairs={{0,4},{1,3},{2,6},{3,1},{4,0},{5,7},{6,2},{7,5},{8,12},{9,11},{10,... | collective-permute-start | bytes 491528 | tf_op jit(solution)/shard_map/ppermute | solution.py:45
  136.4 2.2 %collective-permute-start.23 = (bf16[128,2688]{1,0:T(8,128)(2,1)S(1)}, bf16[128,2688]{1,0:T(8,128)(2,1)S(1)}, u32[]{:S(2)}, u32[]{:S(2)}) collective-permute-start(bf16[128,2688]{1,0:T(8,128)(2,1)S(1)} %expand.3.near_ref), channel_id=1, source_target_pairs={{0,1},{1,0},{2,3},{3,2},{4,5},{5,4},{6,7},{7,6},{8,9},{9,8},{10,11... | collective-permute-start | bytes 2064392 | tf_op jit(solution)/shard_map/ppermute | solution.py:457
  140.0 8.2 %collective-permute-start.24 = (bf16[32,2560]{1,0:T(8,128)(2,1)S(1)}, bf16[32,2560]{1,0:T(8,128)(2,1)S(1)}, u32[]{:S(2)}, u32[]{:S(2)}) collective-permute-start(bf16[32,2560]{1,0:T(8,128)(2,1)S(1)} %get-tuple-element.108), channel_id=1, source_target_pairs={{0,4},{1,3},{2,6},{3,1},{4,0},{5,7},{6,2},{7,5},{8,12},{9,11},{10,... | collective-permute-start | bytes 491528 | tf_op jit(solution)/shard_map/ppermute | solution.py:45
  141.2 7.0 %collective-permute-start.25 = (bf16[32,2560]{1,0:T(8,128)(2,1)S(1)}, bf16[32,2560]{1,0:T(8,128)(2,1)S(1)}, u32[]{:S(2)}, u32[]{:S(2)}) collective-permute-start(bf16[32,2560]{1,0:T(8,128)(2,1)S(1)} %get-tuple-element.109), channel_id=1, source_target_pairs={{0,2},{1,5},{2,0},{3,7},{4,6},{5,1},{6,4},{7,3},{8,10},{9,13},{10,... | collective-permute-start | bytes 491528 | tf_op jit(solution)/shard_map/ppermute | solution.py:45
  142.5 7.9 %collective-permute-start.26 = (bf16[32,2560]{1,0:T(8,128)(2,1)S(1)}, bf16[32,2560]{1,0:T(8,128)(2,1)S(1)}, u32[]{:S(2)}, u32[]{:S(2)}) collective-permute-start(bf16[32,2560]{1,0:T(8,128)(2,1)S(1)} %get-tuple-element.110), channel_id=1, source_target_pairs={{0,6},{1,7},{2,4},{3,5},{4,2},{5,3},{6,0},{7,1},{8,14},{9,15},{10,... | collective-permute-start | bytes 491528 | tf_op jit(solution)/shard_map/ppermute | solution.py:45
  150.5 4.5 %collective-permute-start.27 = (bf16[16,2560]{1,0:T(8,128)(2,1)S(1)}, bf16[16,2560]{1,0:T(8,128)(2,1)S(1)}, u32[]{:S(2)}, u32[]{:S(2)}) collective-permute-start(bf16[16,2560]{1,0:T(8,128)(2,1)S(1)} %slice.81), channel_id=1, source_target_pairs={{0,8},{1,9},{2,10},{3,11},{4,12},{5,13},{6,14},{7,15},{8,0},{9,1},... | collective-permute-start | bytes 245768 | tf_op jit(solution)/shard_map/ppermute | solution.py:45
  155.1 5.0 %collective-permute-start.28 = (bf16[8,2560]{1,0:T(8,128)(2,1)S(1)}, bf16[8,2560]{1,0:T(8,128)(2,1)S(1)}, u32[]{:S(2)}, u32[]{:S(2)}) collective-permute-start(bf16[8,2560]{1,0:T(8,128)(2,1)S(1)} %slice.83), channel_id=1, source_target_pairs={{0,16},{1,17},{2,18},{3,19},{4,20},{5,21},{6,22},{7,23},{8,24},{9,... | collective-permute-start | bytes 122888 | tf_op jit(solution)/shard_map/ppermute | solution.py:45
  (8 other events, 136.9 us)

commit v10 on v9

--- a/solution.py
+++ b/solution.py
@@ -19,7 +19,7 @@
 COLS_STEP = HEADS_STEP * HEAD_DIM
 ROWS_HALF = HALF_VENUES * NODE_STEPS
 KEYS_HALF = HALF_VENUES * STEPS
-LSE_ITEM = 64
+LSE_ITEM = 32
 VMEM_LIMIT = 8 << 20
 
 
@@ -91,7 +91,8 @@
 
 
 def score_body(query_ref, *refs):
-    key_refs, probs_ref, lse_ref = refs[:HALF_VENUES], refs[-2], refs[-1]
+    key_refs = refs[:HALF_VENUES]
+    probs_ref, lse_ref, packed_ref = refs[HALF_VENUES:]
     step = pl.program_id(0)
 
     @pl.when(step == 0)
@@ -127,6 +128,8 @@
             column = step * HEADS_STEP + head + item * LSE_ITEM
             lse = jnp.where(lane == column, top + jnp.log(total), lse)
     lse_ref[...] = lse
+    low, high = lse[:ROWS_HALF], pltpu.roll(lse[ROWS_HALF:], 2 * LSE_ITEM, 1)
+    packed_ref[...] = jnp.where(lane[:ROWS_HALF] < 2 * LSE_ITEM, low, high)
 
 
 def half_scores(queries, keys):
@@ -141,10 +144,12 @@
         out_specs=[
             pl.BlockSpec((HEADS_STEP, 2, 2 * ROWS_HALF, KEYS_HALF), lambda j: (j, 0, 0, 0)),
             pl.BlockSpec((2 * ROWS_HALF, 128), lambda j: (0, 0)),
+            pl.BlockSpec((ROWS_HALF, 128), lambda j: (0, 0)),
         ],
         out_shape=[
             jax.ShapeDtypeStruct((heads, 2, 2 * ROWS_HALF, KEYS_HALF), jnp.bfloat16),
             jax.ShapeDtypeStruct((2 * ROWS_HALF, 128), jnp.float32),
+            jax.ShapeDtypeStruct((ROWS_HALF, 128), jnp.float32),
         ],
         compiler_params=pltpu.CompilerParams(vmem_limit_bytes=VMEM_LIMIT),
         name="half_scores",
@@ -153,9 +158,12 @@
 
 def weigh_body(probs_ref, lse_ref, far_ref, weights_ref):
     step = pl.program_id(0)
-    far = jnp.concatenate([far_ref[:, LSE_ITEM:], far_ref[:, :LSE_ITEM]], axis=1)
+    lane = lax.broadcasted_iota(jnp.int32, lse_ref.shape, 1)
+    far = jnp.concatenate([far_ref[...], pltpu.roll(far_ref[...], 2 * LSE_ITEM, 1)], axis=0)
+    far = jnp.where(
+        lane < LSE_ITEM, pltpu.roll(far, 128 - LSE_ITEM, 1), pltpu.roll(far, LSE_ITEM, 1)
+    )
     share = 1.0 / (1.0 + jnp.exp(far - lse_ref[...])) * (1.0 / VENUES)
-    lane = lax.broadcasted_iota(jnp.int32, lse_ref.shape, 1)
     for head in range(HEADS_STEP):
         means = []
         for item in range(2):
@@ -174,7 +182,7 @@
         in_specs=[
             pl.BlockSpec((HEADS_STEP, 2, 2 * ROWS_HALF, KEYS_HALF), lambda j: (j, 0, 0, 0)),
             pl.BlockSpec((2 * ROWS_HALF, 128), lambda j: (0, 0)),
-            pl.BlockSpec((2 * ROWS_HALF, 128), lambda j: (0, 0)),
+            pl.BlockSpec((ROWS_HALF, 128), lambda j: (0, 0)),
         ],
         out_specs=pl.BlockSpec((HEADS_STEP, 2 * NODE_STEPS, KEYS_HALF), lambda j: (j, 0, 0)),
         out_shape=jax.ShapeDtypeStruct((heads, 2 * NODE_STEPS, KEYS_HALF), jnp.bfloat16),
@@ -262,16 +270,17 @@
     mix_ref, gain_ref, norm_ref, gate_ref, up_ref, _, out_ref, scaled_ref = refs
     feat, width = gate_ref.shape
     padded = pad_lanes(width)
-    edges = sum(mix_ref[kind].astype(jnp.float32) for kind in range(ETYPES))
+    rows = mix_ref.shape[1]
+    kinds = [slice(kind * rows, (kind + 1) * rows) for kind in range(ETYPES)]
+    edges = sum(mix_ref[kind, :].astype(jnp.float32) for kind in kinds)
     inverse = 1.0 / jnp.maximum(jnp.sum(edges, axis=1, keepdims=True), 1.0)
     squares = 0.0
     for span in column_tiles(feat, 512):
         nodes = jnp.concatenate([ref[:, span] for ref in node_refs], axis=0)
-        message = 0.0
-        for kind in range(ETYPES):
-            message += gain_ref[layer, kind : kind + 1, span] * jnp.dot(
-                mix_ref[kind], nodes, preferred_element_type=jnp.float32
-            )
+        mixed = jnp.dot(mix_ref[...], nodes, preferred_element_type=jnp.float32)
+        message = sum(
+            gain_ref[layer, kind : kind + 1, span] * mixed[kinds[kind]] for kind in range(ETYPES)
+        )
         pre = nodes.astype(jnp.float32) + message * inverse
         squares += jnp.sum(pre * pre, axis=1, keepdims=True)
         scaled_ref[:, span] = (pre * norm_ref[layer : layer + 1, span]).astype(jnp.bfloat16)
@@ -442,9 +451,10 @@
         "ter,ec->trc", typed.astype(jnp.bfloat16), at_source, preferred_element_type=jnp.float32
     )
     mix = jnp.where(same_step[None], mix, 0.0).astype(jnp.bfloat16)
+    mix = mix.reshape(ETYPES * row_total, row_total)
     keys, mix, type_gain = lax.optimization_barrier((keys, mix, type_gain))
-    probs, lse = half_scores(queries, keys)
-    far_lse = swap_stage(lse, orders, last)
+    probs, lse, packed = half_scores(queries, keys)
+    far_lse = swap_stage(packed, orders, last)
     pooled = half_pool(first, mean_weights(probs, lse, far_lse), values)
     (gate, up), token = stage_weights([gate_proj, up_proj], 0, [pooled])
     pooled = join_pair(pooled, orders, last).astype(jnp.bfloat16)

time: 161 us -> 160 us (level)
  no operation moved by 1% of the time
where the time goes in v10:
time: 160 us
  waiting for transfers between devices  66 us (41%)
  starting transfers between devices  54 us (34%)
  Pallas kernels  34 us (21%)
  local copies, waits for them, and re-layouts  3.32 us (2%)
  other arithmetic  1.65 us (1%)
    ppermute x20, waiting for transfers between devices, swap_stage(): return lax.ppermute(block, ('gx', 'ta'), pairs)  35.6 us
    ppermute x20, starting transfers between devices, swap_stage(): return lax.ppermute(block, ('gx', 'ta'), pairs)  31.3 us
    ppermute x7, waiting for transfers between devices, per_device(): keys.append(lax.ppermute(pieces[flip], 'gx', pairs))  24.9 us
    pallas_call x4, Pallas kernels, stage_weights(): pl.pallas_call(functools.partial(stage_body, layer=layer, count=len(held)...  15.3 us
    ppermute x7, starting transfers between devices, per_device(): keys.append(lax.ppermute(pieces[flip], 'gx', pairs))  10.5 us
    all_to_all x1, starting transfers between devices, per_device(): lax.all_to_all(queries.reshape(gx_count, -1, feat_width), 'gx', 0, 0, til...  8.36 us
    pallas_call x2, Pallas kernels, expand(): pl.pallas_call(functools.partial(expand_body, layer=layer), in_specs=[pl....  5.2 us
    ppermute x2, waiting for transfers between devices, per_device(): far_sums = lax.ppermute(near_sums, 'ta', [(0, 1), (1, 0)])  4.26 us
  transfers between devices with their start and end apart: 31, of which 23 were waited for; matrix products, arithmetic and copies ran while one was open for 0% of the time, Pallas kernels for 15%

profile of v10, /device:TPU:0, one launch (start us, length us, event | category | flops | bytes accessed | tf_op | source)
XLA Modules:
  0.0 159.8 jit_solution(1651753805578510039)
XLA Ops:
  3.9 8.4 %all-to-all-start = ((bf16[16,16,2560]{2,1,0:T(8,128)(2,1)}), bf16[16,16,2560]{2,1,0:T(8,128)(2,1)}, u32[]{:S(2)}, u32[]{:S(2)}) async-start(bf16[16,16,2560]{2,1,0:T(8,128)(2,1)} %bitcast.4), calls=%async_computation | async-start | bytes 2621440 | tf_op jit(solution)/shard_map/all_to_all | solution.py:416
  22.6 2.8 %collective-permute-start.5 = (bf16[32,2560]{1,0:T(8,128)(2,1)S(1)}, bf16[32,2560]{1,0:T(8,128)(2,1)S(1)}, u32[]{:S(2)}, u32[]{:S(2)}) collective-permute-start(bf16[32,2560]{1,0:T(8,128)(2,1)S(1)} %get-tuple-element.64), channel_id=1, source_target_pairs={{0,12},{2,14},{4,8},{6,10},{8,4},{10,6},{12,0},{14,2},{16,28},{18,... | collective-permute-start | bytes 491528 | tf_op jit(solution)/shard_map/ppermute | solution.py:427
  25.4 6.7 %collective-permute-done.1.refs_2_ = bf16[32,2560]{1,0:T(8,128)(2,1)S(1)} collective-permute-done((bf16[32,2560]{1,0:T(8,128)(2,1)S(1)}, bf16[32,2560]{1,0:T(8,128)(2,1)S(1)}, u32[]{:S(2)}, u32[]{:S(2)}) %collective-permute-start.1) | collective-permute-done | bytes 163872 | tf_op jit(solution)/shard_map/ppermute | solution.py:427
  34.5 4.6 %collective-permute-done.3.refs_4_ = bf16[32,2560]{1,0:T(8,128)(2,1)S(1)} collective-permute-done((bf16[32,2560]{1,0:T(8,128)(2,1)S(1)}, bf16[32,2560]{1,0:T(8,128)(2,1)S(1)}, u32[]{:S(2)}, u32[]{:S(2)}) %collective-permute-start.3) | collective-permute-done | bytes 163872 | tf_op jit(solution)/shard_map/ppermute | solution.py:427
  39.1 5.4 %collective-permute-done.4.refs_5_ = bf16[32,2560]{1,0:T(8,128)(2,1)S(1)} collective-permute-done((bf16[32,2560]{1,0:T(8,128)(2,1)S(1)}, bf16[32,2560]{1,0:T(8,128)(2,1)S(1)}, u32[]{:S(2)}, u32[]{:S(2)}) %collective-permute-start.4) | collective-permute-done | bytes 163872 | tf_op jit(solution)/shard_map/ppermute | solution.py:427
  44.5 4.2 %collective-permute-done.5.refs_6_ = bf16[32,2560]{1,0:T(8,128)(2,1)S(1)} collective-permute-done((bf16[32,2560]{1,0:T(8,128)(2,1)S(1)}, bf16[32,2560]{1,0:T(8,128)(2,1)S(1)}, u32[]{:S(2)}, u32[]{:S(2)}) %collective-permute-start.5) | collective-permute-done | bytes 163872 | tf_op jit(solution)/shard_map/ppermute | solution.py:427
  48.7 3.2 %collective-permute-done.6.refs_7_ = bf16[32,2560]{1,0:T(8,128)(2,1)S(1)} collective-permute-done((bf16[32,2560]{1,0:T(8,128)(2,1)S(1)}, bf16[32,2560]{1,0:T(8,128)(2,1)S(1)}, u32[]{:S(2)}, u32[]{:S(2)}) %collective-permute-start.6) | collective-permute-done | bytes 163872 | tf_op jit(solution)/shard_map/ppermute | solution.py:427
  51.9 3.8 %all-to-all-start.1 = ((bf16[8,32,2560]{2,1,0:T(8,128)(2,1)}), bf16[8,32,2560]{2,1,0:T(8,128)(2,1)S(1)}, u32[]{:S(2)}, u32[]{:S(2)}) async-start(bf16[8,32,2560]{2,1,0:T(8,128)(2,1)} %bitcast.11), calls=%async_computation.1 | async-start | bytes 2621440 | tf_op jit(solution)/shard_map/all_to_all | solution.py:406
  56.2 4.1 %half_scores.1 = (bf16[20,2,128,128]{3,2,1,0:T(8,128)(2,1)S(1)}, f32[128,128]{1,0:T(8,128)S(1)}, f32[64,128]{1,0:T(8,128)S(1)}) custom-call(bf16[256,2560]{1,0:T(8,128)(2,1)} %bitcast.5.query_ref, bf16[32,2560]{1,0:T(8,128)(2,1)S(1)} %get-tuple-element.75.refs_0_, bf16[32,2560]{1,0:T(8,128)(2,1)S(1)} %collective-permute-done.refs_1_, ...), custom_call_target="tpu_custom_call" | custom-call | tf_op jit(solution)/shard_map/half_scores/pallas_call | solution.py:139
  60.4 2.7 %collective-permute-start.7 = (f32[64,128]{1,0:T(8,128)S(1)}, f32[64,128]{1,0:T(8,128)S(1)}, u32[]{:S(2)}, u32[]{:S(2)}) collective-permute-start(f32[64,128]{1,0:T(8,128)S(1)} %get-tuple-element.85), channel_id=1, source_target_pairs={{0,16},{1,17},{2,18},{3,19},{4,20},{5,21},{6,22},{7,23},{8,24},{9,... | collective-permute-start | bytes 98312 | tf_op jit(solution)/shard_map/ppermute | solution.py:45
  63.1 6.9 %collective-permute-done.7.far_ref = f32[64,128]{1,0:T(8,128)S(1)} collective-permute-done((f32[64,128]{1,0:T(8,128)S(1)}, f32[64,128]{1,0:T(8,128)S(1)}, u32[]{:S(2)}, u32[]{:S(2)}) %collective-permute-start.7) | collective-permute-done | bytes 32800 | tf_op jit(solution)/shard_map/ppermute | solution.py:45
  73.6 2.4 %collective-permute-start.8 = (bf16[16,2560]{1,0:T(8,128)(2,1)S(1)}, bf16[16,2560]{1,0:T(8,128)(2,1)S(1)}, u32[]{:S(2)}, u32[]{:S(2)}) collective-permute-start(bf16[16,2560]{1,0:T(8,128)(2,1)S(1)} %half_pool.1.refs_2_), channel_id=1, source_target_pairs={{0,16},{1,17},{2,18},{3,19},{4,20},{5,21},{6,22},{7,23},{8,24},{9,... | collective-permute-start | bytes 245768 | tf_op jit(solution)/shard_map/ppermute | solution.py:45
  76.0 4.8 %stage_weights.4 = (bf16[2560,1280]{1,0:T(8,128)(2,1)S(1)}, bf16[2560,1280]{1,0:T(8,128)(2,1)S(1)}, f32[8,128]{1,0:T(8,128)S(1)}) custom-call(bf16[2,2560,1280]{2,1,0:T(8,128)(2,1)} %refs_0_.6, bf16[2,2560,1280]{2,1,0:T(8,128)(2,1)} %refs_1_.3, bf16[16,2560]{1,0:T(8,128)(2,1)S(1)} %half_pool.1.refs_2_), custom_call_target="tpu_custom_call" | custom-call | bytes 26214400 | tf_op jit(solution)/shard_map/stage_weights/pallas_call | solution.py:250
  82.5 2.9 %collective-permute-done.9 = bf16[16,2560]{1,0:T(8,128)(2,1)S(1)} collective-permute-done((bf16[16,2560]{1,0:T(8,128)(2,1)S(1)}, bf16[16,2560]{1,0:T(8,128)(2,1)S(1)}, u32[]{:S(2)}, u32[]{:S(2)}) %collective-permute-start.9) | collective-permute-done | bytes 81952 | tf_op jit(solution)/shard_map/ppermute | solution.py:45
  85.4 2.3 %collective-permute-start.12 = (bf16[32,2560]{1,0:T(8,128)(2,1)S(1)}, bf16[32,2560]{1,0:T(8,128)(2,1)S(1)}, u32[]{:S(2)}, u32[]{:S(2)}) collective-permute-start(bf16[32,2560]{1,0:T(8,128)(2,1)S(1)} %constant_dynamic-update-slice_fusion.refs_0_), channel_id=1, source_target_pairs={{0,6},{1,7},{2,4},{3,5},{4,2},{5,3},{6,0},{7,1},{8,14},{9,15},{10,... | collective-permute-start | bytes 491528 | tf_op jit(solution)/shard_map/ppermute | solution.py:45
  88.9 2.9 %stage_weights.5 = (bf16[1280,2560]{1,0:T(8,128)(2,1)S(1)}, f32[8,128]{1,0:T(8,128)S(1)}) custom-call(bf16[2,1280,2560]{2,1,0:T(8,128)(2,1)} %refs_0_.7, f32[8,128]{1,0:T(8,128)S(1)} %get-tuple-element.93.refs_1_), custom_call_target="tpu_custom_call" | custom-call | bytes 13107200 | tf_op jit(solution)/shard_map/stage_weights/pallas_call | solution.py:250
  93.5 2.6 %expand.2.near_ref = bf16[128,2688]{1,0:T(8,128)(2,1)S(1)} custom-call(bf16[32,2560]{1,0:T(8,128)(2,1)S(1)} %constant_dynamic-update-slice_fusion.refs_0_, bf16[32,2560]{1,0:T(8,128)(2,1)S(1)} %collective-permute-done.10.refs_1_, bf16[32,2560]{1,0:T(8,128)(2,1)S(1)} %collective-permute-done.11.refs_2_, bf16[32,2560]{1,0:T(8,128)(2,1)S(1)} %collective-permute-done.12.refs_3_, ...), custom_call_target="tpu_custom_call" | custom-call | tf_op jit(solution)/shard_map/expand/pallas_call | solution.py:306
  96.2 2.1 %collective-permute-done.13.far_ref = bf16[128,2688]{1,0:T(8,128)(2,1)S(1)} collective-permute-done((bf16[128,2688]{1,0:T(8,128)(2,1)S(1)}, bf16[128,2688]{1,0:T(8,128)(2,1)S(1)}, u32[]{:S(2)}, u32[]{:S(2)}) %collective-permute-start.13) | collective-permute-done | bytes 688160 | tf_op jit(solution)/shard_map/ppermute | solution.py:467
  103.3 4.8 %stage_weights.6 = (bf16[2560,1280]{1,0:T(8,128)(2,1)S(1)}, bf16[2560,1280]{1,0:T(8,128)(2,1)S(1)}, f32[8,128]{1,0:T(8,128)S(1)}) custom-call(bf16[2,2560,1280]{2,1,0:T(8,128)(2,1)} %refs_0_.6, bf16[2,2560,1280]{2,1,0:T(8,128)(2,1)} %refs_1_.3, bf16[32,2560]{1,0:T(8,128)(2,1)S(1)} %get-tuple-element.97.refs_2_, ...), custom_call_target="tpu_custom_call" | custom-call | bytes 26214400 | tf_op jit(solution)/shard_map/stage_weights/pallas_call | solution.py:250
  108.1 2.2 %collective-permute-done.16 = bf16[32,2560]{1,0:T(8,128)(2,1)S(1)} collective-permute-done((bf16[32,2560]{1,0:T(8,128)(2,1)S(1)}, bf16[32,2560]{1,0:T(8,128)(2,1)S(1)}, u32[]{:S(2)}, u32[]{:S(2)}) %collective-permute-start.16) | collective-permute-done | bytes 163872 | tf_op jit(solution)/shard_map/ppermute | solution.py:45
  112.1 2.8 %collective-permute-done.17 = bf16[16,2560]{1,0:T(8,128)(2,1)S(1)} collective-permute-done((bf16[16,2560]{1,0:T(8,128)(2,1)S(1)}, bf16[16,2560]{1,0:T(8,128)(2,1)S(1)}, u32[]{:S(2)}, u32[]{:S(2)}) %collective-permute-start.17) | collective-permute-done | bytes 81952 | tf_op jit(solution)/shard_map/ppermute | solution.py:45
  114.9 2.3 %collective-permute-start.18 = (bf16[16,2560]{1,0:T(8,128)(2,1)S(1)}, bf16[16,2560]{1,0:T(8,128)(2,1)S(1)}, u32[]{:S(2)}, u32[]{:S(2)}) collective-permute-start(bf16[16,2560]{1,0:T(8,128)(2,1)S(1)} %fusion.3), channel_id=1, source_target_pairs={{0,16},{1,17},{2,18},{3,19},{4,20},{5,21},{6,22},{7,23},{8,24},{9,... | collective-permute-start | bytes 245768 | tf_op jit(solution)/shard_map/ppermute | solution.py:45
  117.2 3.1 %collective-permute-done.18 = bf16[16,2560]{1,0:T(8,128)(2,1)S(1)} collective-permute-done((bf16[16,2560]{1,0:T(8,128)(2,1)S(1)}, bf16[16,2560]{1,0:T(8,128)(2,1)S(1)}, u32[]{:S(2)}, u32[]{:S(2)}) %collective-permute-start.18) | collective-permute-done | bytes 81952 | tf_op jit(solution)/shard_map/ppermute | solution.py:45
  122.1 2.8 %collective-permute-done.19 = bf16[16,2560]{1,0:T(8,128)(2,1)S(1)} collective-permute-done((bf16[16,2560]{1,0:T(8,128)(2,1)S(1)}, bf16[16,2560]{1,0:T(8,128)(2,1)S(1)}, u32[]{:S(2)}, u32[]{:S(2)}) %collective-permute-start.19) | collective-permute-done | bytes 81952 | tf_op jit(solution)/shard_map/ppermute | solution.py:45
  128.4 2.9 %stage_weights.7 = (bf16[1280,2560]{1,0:T(8,128)(2,1)S(1)}, f32[8,128]{1,0:T(8,128)S(1)}) custom-call(bf16[2,1280,2560]{2,1,0:T(8,128)(2,1)} %refs_0_.7, bf16[16,2560]{1,0:T(8,128)(2,1)S(1)} %add_convert_fusion.refs_1_, f32[8,128]{1,0:T(8,128)S(1)} %get-tuple-element.106.refs_2_), custom_call_target="tpu_custom_call" | custom-call | bytes 13107200 | tf_op jit(solution)/shard_map/stage_weights/pallas_call | solution.py:250
  132.9 2.6 %expand.3.near_ref = bf16[128,2688]{1,0:T(8,128)(2,1)S(1)} custom-call(bf16[32,2560]{1,0:T(8,128)(2,1)S(1)} %pad_maximum_fusion.refs_0_, bf16[32,2560]{1,0:T(8,128)(2,1)S(1)} %collective-permute-done.20.refs_1_, bf16[32,2560]{1,0:T(8,128)(2,1)S(1)} %collective-permute-done.21.refs_2_, bf16[32,2560]{1,0:T(8,128)(2,1)S(1)} %collective-permute-done.22.refs_3_, ...), custom_call_target="tpu_custom_call" | custom-call | tf_op jit(solution)/shard_map/expand/pallas_call | solution.py:306
  135.6 2.1 %collective-permute-done.23.far_ref = bf16[128,2688]{1,0:T(8,128)(2,1)S(1)} collective-permute-done((bf16[128,2688]{1,0:T(8,128)(2,1)S(1)}, bf16[128,2688]{1,0:T(8,128)(2,1)S(1)}, u32[]{:S(2)}, u32[]{:S(2)}) %collective-permute-start.23) | collective-permute-done | bytes 688160 | tf_op jit(solution)/shard_map/ppermute | solution.py:467
  142.7 4.5 %collective-permute-done.24 = bf16[32,2560]{1,0:T(8,128)(2,1)S(1)} collective-permute-done((bf16[32,2560]{1,0:T(8,128)(2,1)S(1)}, bf16[32,2560]{1,0:T(8,128)(2,1)S(1)}, u32[]{:S(2)}, u32[]{:S(2)}) %collective-permute-start.24) | collective-permute-done | bytes 163872 | tf_op jit(solution)/shard_map/ppermute | solution.py:45
  147.1 2.4 %collective-permute-done.26 = bf16[32,2560]{1,0:T(8,128)(2,1)S(1)} collective-permute-done((bf16[32,2560]{1,0:T(8,128)(2,1)S(1)}, bf16[32,2560]{1,0:T(8,128)(2,1)S(1)}, u32[]{:S(2)}, u32[]{:S(2)}) %collective-permute-start.26) | collective-permute-done | bytes 163872 | tf_op jit(solution)/shard_map/ppermute | solution.py:45
  151.4 2.8 %collective-permute-done.27 = bf16[16,2560]{1,0:T(8,128)(2,1)S(1)} collective-permute-done((bf16[16,2560]{1,0:T(8,128)(2,1)S(1)}, bf16[16,2560]{1,0:T(8,128)(2,1)S(1)}, u32[]{:S(2)}, u32[]{:S(2)}) %collective-permute-start.27) | collective-permute-done | bytes 81952 | tf_op jit(solution)/shard_map/ppermute | solution.py:45
  154.2 2.9 %collective-permute-start.28 = (bf16[8,2560]{1,0:T(8,128)(2,1)S(1)}, bf16[8,2560]{1,0:T(8,128)(2,1)S(1)}, u32[]{:S(2)}, u32[]{:S(2)}) collective-permute-start(bf16[8,2560]{1,0:T(8,128)(2,1)S(1)} %slice.83), channel_id=1, source_target_pairs={{0,16},{1,17},{2,18},{3,19},{4,20},{5,21},{6,22},{7,23},{8,24},{9,... | collective-permute-start | bytes 122888 | tf_op jit(solution)/shard_map/ppermute | solution.py:45
  157.2 2.0 %collective-permute-done.28 = bf16[8,2560]{1,0:T(8,128)(2,1)S(1)} collective-permute-done((bf16[8,2560]{1,0:T(8,128)(2,1)S(1)}, bf16[8,2560]{1,0:T(8,128)(2,1)S(1)}, u32[]{:S(2)}, u32[]{:S(2)}) %collective-permute-start.28) | collective-permute-done | bytes 40992 | tf_op jit(solution)/shard_map/ppermute | solution.py:45
  (98 shorter events, 46.7 us)
Async XLA Ops:
  0.0 55.7 %copy-start.7 = (s32[64,2]{0,1:T(2,128)S(1)}, s32[64,2]{0,1:T(2,128)}, u32[]{:S(2)}) copy-start(s32[64,2]{0,1:T(2,128)} %param.15) | copy-start | bytes 1540
  3.9 48.0 %all-to-all-start = ((bf16[16,16,2560]{2,1,0:T(8,128)(2,1)}), bf16[16,16,2560]{2,1,0:T(8,128)(2,1)}, u32[]{:S(2)}, u32[]{:S(2)}) async-start(bf16[16,16,2560]{2,1,0:T(8,128)(2,1)} %bitcast.4), calls=%async_computation | async-start | bytes 2621440 | tf_op jit(solution)/shard_map/all_to_all | solution.py:416
  14.8 7.8 %collective-permute-start = (bf16[32,2560]{1,0:T(8,128)(2,1)S(1)}, bf16[32,2560]{1,0:T(8,128)(2,1)S(1)}, u32[]{:S(2)}, u32[]{:S(2)}) collective-permute-start(bf16[32,2560]{1,0:T(8,128)(2,1)S(1)} %get-tuple-element.59), channel_id=1, source_target_pairs={{0,2},{2,0},{4,6},{6,4},{8,10},{10,8},{12,14},{14,12},{16,18},{18,... | collective-permute-start | bytes 491528 | tf_op jit(solution)/shard_map/ppermute | solution.py:427
  16.8 15.3 %collective-permute-start.1 = (bf16[32,2560]{1,0:T(8,128)(2,1)S(1)}, bf16[32,2560]{1,0:T(8,128)(2,1)S(1)}, u32[]{:S(2)}, u32[]{:S(2)}) collective-permute-start(bf16[32,2560]{1,0:T(8,128)(2,1)S(1)} %get-tuple-element.60), channel_id=1, source_target_pairs={{0,4},{2,6},{4,0},{6,2},{8,12},{10,14},{12,8},{14,10},{16,20},{18,... | collective-permute-start | bytes 491528 | tf_op jit(solution)/shard_map/ppermute | solution.py:427
  18.2 16.3 %collective-permute-start.2 = (bf16[32,2560]{1,0:T(8,128)(2,1)S(1)}, bf16[32,2560]{1,0:T(8,128)(2,1)S(1)}, u32[]{:S(2)}, u32[]{:S(2)}) collective-permute-start(bf16[32,2560]{1,0:T(8,128)(2,1)S(1)} %get-tuple-element.61), channel_id=1, source_target_pairs={{0,6},{2,4},{4,2},{6,0},{8,14},{10,12},{12,10},{14,8},{16,22},{18,... | collective-permute-start | bytes 491528 | tf_op jit(solution)/shard_map/ppermute | solution.py:427
  18.4 20.8 %collective-permute-start.3 = (bf16[32,2560]{1,0:T(8,128)(2,1)S(1)}, bf16[32,2560]{1,0:T(8,128)(2,1)S(1)}, u32[]{:S(2)}, u32[]{:S(2)}) collective-permute-start(bf16[32,2560]{1,0:T(8,128)(2,1)S(1)} %get-tuple-element.62), channel_id=1, source_target_pairs={{0,8},{2,10},{4,12},{6,14},{8,0},{10,2},{12,4},{14,6},{16,24},{18,... | collective-permute-start | bytes 491528 | tf_op jit(solution)/shard_map/ppermute | solution.py:427
  20.3 24.3 %collective-permute-start.4 = (bf16[32,2560]{1,0:T(8,128)(2,1)S(1)}, bf16[32,2560]{1,0:T(8,128)(2,1)S(1)}, u32[]{:S(2)}, u32[]{:S(2)}) collective-permute-start(bf16[32,2560]{1,0:T(8,128)(2,1)S(1)} %get-tuple-element.63), channel_id=1, source_target_pairs={{0,10},{2,8},{4,14},{6,12},{8,2},{10,0},{12,6},{14,4},{16,26},{18,... | collective-permute-start | bytes 491528 | tf_op jit(solution)/shard_map/ppermute | solution.py:427
  22.6 26.1 %collective-permute-start.5 = (bf16[32,2560]{1,0:T(8,128)(2,1)S(1)}, bf16[32,2560]{1,0:T(8,128)(2,1)S(1)}, u32[]{:S(2)}, u32[]{:S(2)}) collective-permute-start(bf16[32,2560]{1,0:T(8,128)(2,1)S(1)} %get-tuple-element.64), channel_id=1, source_target_pairs={{0,12},{2,14},{4,8},{6,10},{8,4},{10,6},{12,0},{14,2},{16,28},{18,... | collective-permute-start | bytes 491528 | tf_op jit(solution)/shard_map/ppermute | solution.py:427
  32.1 19.8 %collective-permute-start.6 = (bf16[32,2560]{1,0:T(8,128)(2,1)S(1)}, bf16[32,2560]{1,0:T(8,128)(2,1)S(1)}, u32[]{:S(2)}, u32[]{:S(2)}) collective-permute-start(bf16[32,2560]{1,0:T(8,128)(2,1)S(1)} %get-tuple-element.65), channel_id=1, source_target_pairs={{0,14},{2,12},{4,10},{6,8},{8,6},{10,4},{12,2},{14,0},{16,30},{18,... | collective-permute-start | bytes 491528 | tf_op jit(solution)/shard_map/ppermute | solution.py:427
  51.9 20.7 %all-to-all-start.1 = ((bf16[8,32,2560]{2,1,0:T(8,128)(2,1)}), bf16[8,32,2560]{2,1,0:T(8,128)(2,1)S(1)}, u32[]{:S(2)}, u32[]{:S(2)}) async-start(bf16[8,32,2560]{2,1,0:T(8,128)(2,1)} %bitcast.11), calls=%async_computation.1 | async-start | bytes 2621440 | tf_op jit(solution)/shard_map/all_to_all | solution.py:406
  60.4 9.6 %collective-permute-start.7 = (f32[64,128]{1,0:T(8,128)S(1)}, f32[64,128]{1,0:T(8,128)S(1)}, u32[]{:S(2)}, u32[]{:S(2)}) collective-permute-start(f32[64,128]{1,0:T(8,128)S(1)} %get-tuple-element.85), channel_id=1, source_target_pairs={{0,16},{1,17},{2,18},{3,19},{4,20},{5,21},{6,22},{7,23},{8,24},{9,... | collective-permute-start | bytes 98312 | tf_op jit(solution)/shard_map/ppermute | solution.py:45
  73.6 7.1 %collective-permute-start.8 = (bf16[16,2560]{1,0:T(8,128)(2,1)S(1)}, bf16[16,2560]{1,0:T(8,128)(2,1)S(1)}, u32[]{:S(2)}, u32[]{:S(2)}) collective-permute-start(bf16[16,2560]{1,0:T(8,128)(2,1)S(1)} %half_pool.1.refs_2_), channel_id=1, source_target_pairs={{0,16},{1,17},{2,18},{3,19},{4,20},{5,21},{6,22},{7,23},{8,24},{9,... | collective-permute-start | bytes 245768 | tf_op jit(solution)/shard_map/ppermute | solution.py:45
  80.8 4.5 %collective-permute-start.9 = (bf16[16,2560]{1,0:T(8,128)(2,1)S(1)}, bf16[16,2560]{1,0:T(8,128)(2,1)S(1)}, u32[]{:S(2)}, u32[]{:S(2)}) collective-permute-start(bf16[16,2560]{1,0:T(8,128)(2,1)S(1)} %add_convert_fusion.1), channel_id=1, source_target_pairs={{0,8},{1,9},{2,10},{3,11},{4,12},{5,13},{6,14},{7,15},{8,0},{9,1},... | collective-permute-start | bytes 245768 | tf_op jit(solution)/shard_map/ppermute | solution.py:45
  85.4 6.4 %collective-permute-start.12 = (bf16[32,2560]{1,0:T(8,128)(2,1)S(1)}, bf16[32,2560]{1,0:T(8,128)(2,1)S(1)}, u32[]{:S(2)}, u32[]{:S(2)}) collective-permute-start(bf16[32,2560]{1,0:T(8,128)(2,1)S(1)} %constant_dynamic-update-slice_fusion.refs_0_), channel_id=1, source_target_pairs={{0,6},{1,7},{2,4},{3,5},{4,2},{5,3},{6,0},{7,1},{8,14},{9,15},{10,... | collective-permute-start | bytes 491528 | tf_op jit(solution)/shard_map/ppermute | solution.py:45
  87.6 5.6 %collective-permute-start.11 = (bf16[32,2560]{1,0:T(8,128)(2,1)S(1)}, bf16[32,2560]{1,0:T(8,128)(2,1)S(1)}, u32[]{:S(2)}, u32[]{:S(2)}) collective-permute-start(bf16[32,2560]{1,0:T(8,128)(2,1)S(1)} %constant_dynamic-update-slice_fusion.refs_0_), channel_id=1, source_target_pairs={{0,2},{1,5},{2,0},{3,7},{4,6},{5,1},{6,4},{7,3},{8,10},{9,13},{10,... | collective-permute-start | bytes 491528 | tf_op jit(solution)/shard_map/ppermute | solution.py:45
  88.2 5.3 %collective-permute-start.10 = (bf16[32,2560]{1,0:T(8,128)(2,1)S(1)}, bf16[32,2560]{1,0:T(8,128)(2,1)S(1)}, u32[]{:S(2)}, u32[]{:S(2)}) collective-permute-start(bf16[32,2560]{1,0:T(8,128)(2,1)S(1)} %constant_dynamic-update-slice_fusion.refs_0_), channel_id=1, source_target_pairs={{0,4},{1,3},{2,6},{3,1},{4,0},{5,7},{6,2},{7,5},{8,12},{9,11},{10,... | collective-permute-start | bytes 491528 | tf_op jit(solution)/shard_map/ppermute | solution.py:45
  96.1 2.2 %collective-permute-start.13 = (bf16[128,2688]{1,0:T(8,128)(2,1)S(1)}, bf16[128,2688]{1,0:T(8,128)(2,1)S(1)}, u32[]{:S(2)}, u32[]{:S(2)}) collective-permute-start(bf16[128,2688]{1,0:T(8,128)(2,1)S(1)} %expand.2.near_ref), channel_id=1, source_target_pairs={{0,1},{1,0},{2,3},{3,2},{4,5},{5,4},{6,7},{7,6},{8,9},{9,8},{10,11... | collective-permute-start | bytes 2064392 | tf_op jit(solution)/shard_map/ppermute | solution.py:467
  99.8 8.3 %collective-permute-start.14 = (bf16[32,2560]{1,0:T(8,128)(2,1)S(1)}, bf16[32,2560]{1,0:T(8,128)(2,1)S(1)}, u32[]{:S(2)}, u32[]{:S(2)}) collective-permute-start(bf16[32,2560]{1,0:T(8,128)(2,1)S(1)} %get-tuple-element.97.refs_2_), channel_id=1, source_target_pairs={{0,4},{1,3},{2,6},{3,1},{4,0},{5,7},{6,2},{7,5},{8,12},{9,11},{10,... | collective-permute-start | bytes 491528 | tf_op jit(solution)/shard_map/ppermute | solution.py:45
  101.0 7.1 %collective-permute-start.15 = (bf16[32,2560]{1,0:T(8,128)(2,1)S(1)}, bf16[32,2560]{1,0:T(8,128)(2,1)S(1)}, u32[]{:S(2)}, u32[]{:S(2)}) collective-permute-start(bf16[32,2560]{1,0:T(8,128)(2,1)S(1)} %get-tuple-element.98.refs_3_), channel_id=1, source_target_pairs={{0,2},{1,5},{2,0},{3,7},{4,6},{5,1},{6,4},{7,3},{8,10},{9,13},{10,... | collective-permute-start | bytes 491528 | tf_op jit(solution)/shard_map/ppermute | solution.py:45
  102.5 7.8 %collective-permute-start.16 = (bf16[32,2560]{1,0:T(8,128)(2,1)S(1)}, bf16[32,2560]{1,0:T(8,128)(2,1)S(1)}, u32[]{:S(2)}, u32[]{:S(2)}) collective-permute-start(bf16[32,2560]{1,0:T(8,128)(2,1)S(1)} %get-tuple-element.99.refs_4_), channel_id=1, source_target_pairs={{0,6},{1,7},{2,4},{3,5},{4,2},{5,3},{6,0},{7,1},{8,14},{9,15},{10,... | collective-permute-start | bytes 491528 | tf_op jit(solution)/shard_map/ppermute | solution.py:45
  110.4 4.5 %collective-permute-start.17 = (bf16[16,2560]{1,0:T(8,128)(2,1)S(1)}, bf16[16,2560]{1,0:T(8,128)(2,1)S(1)}, u32[]{:S(2)}, u32[]{:S(2)}) collective-permute-start(bf16[16,2560]{1,0:T(8,128)(2,1)S(1)} %slice.82), channel_id=1, source_target_pairs={{0,8},{1,9},{2,10},{3,11},{4,12},{5,13},{6,14},{7,15},{8,0},{9,1},... | collective-permute-start | bytes 245768 | tf_op jit(solution)/shard_map/ppermute | solution.py:45
  114.9 5.4 %collective-permute-start.18 = (bf16[16,2560]{1,0:T(8,128)(2,1)S(1)}, bf16[16,2560]{1,0:T(8,128)(2,1)S(1)}, u32[]{:S(2)}, u32[]{:S(2)}) collective-permute-start(bf16[16,2560]{1,0:T(8,128)(2,1)S(1)} %fusion.3), channel_id=1, source_target_pairs={{0,16},{1,17},{2,18},{3,19},{4,20},{5,21},{6,22},{7,23},{8,24},{9,... | collective-permute-start | bytes 245768 | tf_op jit(solution)/shard_map/ppermute | solution.py:45
  120.3 4.5 %collective-permute-start.19 = (bf16[16,2560]{1,0:T(8,128)(2,1)S(1)}, bf16[16,2560]{1,0:T(8,128)(2,1)S(1)}, u32[]{:S(2)}, u32[]{:S(2)}) collective-permute-start(bf16[16,2560]{1,0:T(8,128)(2,1)S(1)} %add_convert_fusion.refs_1_), channel_id=1, source_target_pairs={{0,8},{1,9},{2,10},{3,11},{4,12},{5,13},{6,14},{7,15},{8,0},{9,1},... | collective-permute-start | bytes 245768 | tf_op jit(solution)/shard_map/ppermute | solution.py:45
  124.9 6.5 %collective-permute-start.22 = (bf16[32,2560]{1,0:T(8,128)(2,1)S(1)}, bf16[32,2560]{1,0:T(8,128)(2,1)S(1)}, u32[]{:S(2)}, u32[]{:S(2)}) collective-permute-start(bf16[32,2560]{1,0:T(8,128)(2,1)S(1)} %pad_maximum_fusion.refs_0_), channel_id=1, source_target_pairs={{0,6},{1,7},{2,4},{3,5},{4,2},{5,3},{6,0},{7,1},{8,14},{9,15},{10,... | collective-permute-start | bytes 491528 | tf_op jit(solution)/shard_map/ppermute | solution.py:45
  126.9 5.7 %collective-permute-start.21 = (bf16[32,2560]{1,0:T(8,128)(2,1)S(1)}, bf16[32,2560]{1,0:T(8,128)(2,1)S(1)}, u32[]{:S(2)}, u32[]{:S(2)}) collective-permute-start(bf16[32,2560]{1,0:T(8,128)(2,1)S(1)} %pad_maximum_fusion.refs_0_), channel_id=1, source_target_pairs={{0,2},{1,5},{2,0},{3,7},{4,6},{5,1},{6,4},{7,3},{8,10},{9,13},{10,... | collective-permute-start | bytes 491528 | tf_op jit(solution)/shard_map/ppermute | solution.py:45
  127.6 5.3 %collective-permute-start.20 = (bf16[32,2560]{1,0:T(8,128)(2,1)S(1)}, bf16[32,2560]{1,0:T(8,128)(2,1)S(1)}, u32[]{:S(2)}, u32[]{:S(2)}) collective-permute-start(bf16[32,2560]{1,0:T(8,128)(2,1)S(1)} %pad_maximum_fusion.refs_0_), channel_id=1, source_target_pairs={{0,4},{1,3},{2,6},{3,1},{4,0},{5,7},{6,2},{7,5},{8,12},{9,11},{10,... | collective-permute-start | bytes 491528 | tf_op jit(solution)/shard_map/ppermute | solution.py:45
  135.5 2.2 %collective-permute-start.23 = (bf16[128,2688]{1,0:T(8,128)(2,1)S(1)}, bf16[128,2688]{1,0:T(8,128)(2,1)S(1)}, u32[]{:S(2)}, u32[]{:S(2)}) collective-permute-start(bf16[128,2688]{1,0:T(8,128)(2,1)S(1)} %expand.3.near_ref), channel_id=1, source_target_pairs={{0,1},{1,0},{2,3},{3,2},{4,5},{5,4},{6,7},{7,6},{8,9},{9,8},{10,11... | collective-permute-start | bytes 2064392 | tf_op jit(solution)/shard_map/ppermute | solution.py:467
  139.1 8.0 %collective-permute-start.24 = (bf16[32,2560]{1,0:T(8,128)(2,1)S(1)}, bf16[32,2560]{1,0:T(8,128)(2,1)S(1)}, u32[]{:S(2)}, u32[]{:S(2)}) collective-permute-start(bf16[32,2560]{1,0:T(8,128)(2,1)S(1)} %get-tuple-element.110), channel_id=1, source_target_pairs={{0,4},{1,3},{2,6},{3,1},{4,0},{5,7},{6,2},{7,5},{8,12},{9,11},{10,... | collective-permute-start | bytes 491528 | tf_op jit(solution)/shard_map/ppermute | solution.py:45
  140.4 6.8 %collective-permute-start.25 = (bf16[32,2560]{1,0:T(8,128)(2,1)S(1)}, bf16[32,2560]{1,0:T(8,128)(2,1)S(1)}, u32[]{:S(2)}, u32[]{:S(2)}) collective-permute-start(bf16[32,2560]{1,0:T(8,128)(2,1)S(1)} %get-tuple-element.111), channel_id=1, source_target_pairs={{0,2},{1,5},{2,0},{3,7},{4,6},{5,1},{6,4},{7,3},{8,10},{9,13},{10,... | collective-permute-start | bytes 491528 | tf_op jit(solution)/shard_map/ppermute | solution.py:45
  141.7 7.9 %collective-permute-start.26 = (bf16[32,2560]{1,0:T(8,128)(2,1)S(1)}, bf16[32,2560]{1,0:T(8,128)(2,1)S(1)}, u32[]{:S(2)}, u32[]{:S(2)}) collective-permute-start(bf16[32,2560]{1,0:T(8,128)(2,1)S(1)} %get-tuple-element.112), channel_id=1, source_target_pairs={{0,6},{1,7},{2,4},{3,5},{4,2},{5,3},{6,0},{7,1},{8,14},{9,15},{10,... | collective-permute-start | bytes 491528 | tf_op jit(solution)/shard_map/ppermute | solution.py:45
  149.7 4.5 %collective-permute-start.27 = (bf16[16,2560]{1,0:T(8,128)(2,1)S(1)}, bf16[16,2560]{1,0:T(8,128)(2,1)S(1)}, u32[]{:S(2)}, u32[]{:S(2)}) collective-permute-start(bf16[16,2560]{1,0:T(8,128)(2,1)S(1)} %slice.81), channel_id=1, source_target_pairs={{0,8},{1,9},{2,10},{3,11},{4,12},{5,13},{6,14},{7,15},{8,0},{9,1},... | collective-permute-start | bytes 245768 | tf_op jit(solution)/shard_map/ppermute | solution.py:45
  154.2 5.0 %collective-permute-start.28 = (bf16[8,2560]{1,0:T(8,128)(2,1)S(1)}, bf16[8,2560]{1,0:T(8,128)(2,1)S(1)}, u32[]{:S(2)}, u32[]{:S(2)}) collective-permute-start(bf16[8,2560]{1,0:T(8,128)(2,1)S(1)} %slice.83), channel_id=1, source_target_pairs={{0,16},{1,17},{2,18},{3,19},{4,20},{5,21},{6,22},{7,23},{8,24},{9,... | collective-permute-start | bytes 122888 | tf_op jit(solution)/shard_map/ppermute | solution.py:45
  (8 other events, 136.3 us)

commit v11 on v10

--- a/solution.py
+++ b/solution.py
@@ -336,7 +336,7 @@
         up = both(slice(padded + span.start, padded + span.stop)) * scale
         hidden.append((gate * (1.0 / (1.0 + jnp.exp(-gate))) * up).astype(jnp.bfloat16))
     hidden = hidden[0] if len(hidden) == 1 else jnp.concatenate(hidden, axis=1)
-    part = rows // 4
+    part = rows // len(out_refs)
     for span in column_tiles(feat, 640):
         total = jnp.dot(hidden, down_ref[:, span], preferred_element_type=jnp.float32)
         for place, ref in enumerate(out_refs):
@@ -344,14 +344,14 @@
 
 
 def contract(near, far, down, swap):
-    shape = (near.shape[0] // 4, down.shape[1])
+    shape = (near.shape[0] // 8, down.shape[1])
     held = pltpu.with_memory_space_constraint(down, pltpu.VMEM)
     return pl.pallas_call(
         functools.partial(contract_body, swap=swap),
         in_specs=[pl.BlockSpec(memory_space=pltpu.VMEM)] * 3,
-        out_specs=[pl.BlockSpec(memory_space=pltpu.VMEM)] * 4,
+        out_specs=[pl.BlockSpec(memory_space=pltpu.VMEM)] * 8,
         out_shape=[jax.ShapeDtypeStruct(shape, jnp.float32)]
-        + [jax.ShapeDtypeStruct(shape, jnp.bfloat16)] * 3,
+        + [jax.ShapeDtypeStruct(shape, jnp.bfloat16)] * 7,
         compiler_params=pltpu.CompilerParams(vmem_limit_bytes=VMEM_LIMIT),
         name="contract",
     )(near, far, held)
@@ -470,15 +470,15 @@
         held, *gives = contract(near_sums, far_sums, down, ta_count == 2)
         final = layer_idx + 1 == ROUNDS
         taken = [
-            swap_stage(give, orders, *stages)
-            for give, stages in zip(gives, ((1,), (0,), (0, 1)))
+            swap_stage(give, orders, *[stage for stage in range(3) if place >> (2 - stage) & 1])
+            for place, give in enumerate(gives, 1)
         ]
         if not final:
-            (gate, up), token = stage_weights([gate_proj, up_proj], layer_idx + 1, gives)
+            (gate,), token = stage_weights([gate_proj], layer_idx + 1, gives)
             taken, token = lax.optimization_barrier((taken, token))
         for block in taken:
             held = held + block.astype(jnp.float32)
-        for stage in range(2, last + 1 if final else last):
+        for stage in range(3, last + 1 if final else last):
             half = held.shape[0] // 2
             held, give = held[:half], held[half:].astype(jnp.bfloat16)
             held = held + swap_stage(give, orders, stage).astype(jnp.float32)
@@ -486,7 +486,7 @@
             held = join_pair(held.astype(jnp.bfloat16), orders, last)
         pooled = (pooled[: held.shape[0]].astype(jnp.float32) + held).astype(jnp.bfloat16)
         if not final:
-            (down,), token = stage_weights([down_proj], layer_idx + 1, [pooled, token])
+            (up, down), token = stage_weights([up_proj, down_proj], layer_idx + 1, [pooled, token])
     return pooled
 
 

time: 160 us -> 159 us (level)
  waiting for transfers between devices: 66 us -> 58.8 us
  starting transfers between devices: 54 us -> 59.9 us
    ppermute x20 -> x26, waiting for transfers between devices: 35.6 us -> 28.4 us  [swap_stage(): return lax.ppermute(block, ('gx', 'ta'), pairs)]
    ppermute x20 -> x26, starting transfers between devices: 31.3 us -> 37.2 us  [swap_stage(): return lax.ppermute(block, ('gx', 'ta'), pairs)]
  transfers between devices with their start and end apart: 31 -> 37, of which waited for: 23 -> 20; matrix products, arithmetic and copies ran while one was open for 0% -> 0% of each run, Pallas kernels for 15% -> 15%
where the time goes in v11:
time: 159 us
  starting transfers between devices  59.9 us (38%)
  waiting for transfers between devices  58.8 us (37%)
  Pallas kernels  34.2 us (22%)
  local copies, waits for them, and re-layouts  3.3 us (2%)
  other arithmetic  1.64 us (1%)
    ppermute x26, starting transfers between devices, swap_stage(): return lax.ppermute(block, ('gx', 'ta'), pairs)  37.2 us
    ppermute x26, waiting for transfers between devices, swap_stage(): return lax.ppermute(block, ('gx', 'ta'), pairs)  28.4 us
    ppermute x7, waiting for transfers between devices, per_device(): keys.append(lax.ppermute(pieces[flip], 'gx', pairs))  24.9 us
    pallas_call x4, Pallas kernels, stage_weights(): pl.pallas_call(functools.partial(stage_body, layer=layer, count=len(held)...  15.3 us
    ppermute x7, starting transfers between devices, per_device(): keys.append(lax.ppermute(pieces[flip], 'gx', pairs))  10.5 us
    all_to_all x1, starting transfers between devices, per_device(): lax.all_to_all(queries.reshape(gx_count, -1, feat_width), 'gx', 0, 0, til...  8.36 us
    pallas_call x2, Pallas kernels, expand(): pl.pallas_call(functools.partial(expand_body, layer=layer), in_specs=[pl....  5.21 us
    ppermute x2, waiting for transfers between devices, per_device(): far_sums = lax.ppermute(near_sums, 'ta', [(0, 1), (1, 0)])  4.26 us
  transfers between devices with their start and end apart: 37, of which 20 were waited for; matrix products, arithmetic and copies ran while one was open for 0% of the time, Pallas kernels for 15%

profile of v11, /device:TPU:0, one launch (start us, length us, event | category | flops | bytes accessed | tf_op | source)
XLA Modules:
  0.0 158.7 jit_solution(15054270064152218386)
XLA Ops:
  3.9 8.4 %all-to-all-start = ((bf16[16,16,2560]{2,1,0:T(8,128)(2,1)}), bf16[16,16,2560]{2,1,0:T(8,128)(2,1)}, u32[]{:S(2)}, u32[]{:S(2)}) async-start(bf16[16,16,2560]{2,1,0:T(8,128)(2,1)} %bitcast.4), calls=%async_computation | async-start | bytes 2621440 | tf_op jit(solution)/shard_map/all_to_all | solution.py:416
  22.6 2.8 %collective-permute-start.5 = (bf16[32,2560]{1,0:T(8,128)(2,1)S(1)}, bf16[32,2560]{1,0:T(8,128)(2,1)S(1)}, u32[]{:S(2)}, u32[]{:S(2)}) collective-permute-start(bf16[32,2560]{1,0:T(8,128)(2,1)S(1)} %get-tuple-element.76), channel_id=1, source_target_pairs={{0,12},{2,14},{4,8},{6,10},{8,4},{10,6},{12,0},{14,2},{16,28},{18,... | collective-permute-start | bytes 491528 | tf_op jit(solution)/shard_map/ppermute | solution.py:427
  25.4 6.7 %collective-permute-done.1.refs_2_ = bf16[32,2560]{1,0:T(8,128)(2,1)S(1)} collective-permute-done((bf16[32,2560]{1,0:T(8,128)(2,1)S(1)}, bf16[32,2560]{1,0:T(8,128)(2,1)S(1)}, u32[]{:S(2)}, u32[]{:S(2)}) %collective-permute-start.1) | collective-permute-done | bytes 163872 | tf_op jit(solution)/shard_map/ppermute | solution.py:427
  34.6 4.6 %collective-permute-done.3.refs_4_ = bf16[32,2560]{1,0:T(8,128)(2,1)S(1)} collective-permute-done((bf16[32,2560]{1,0:T(8,128)(2,1)S(1)}, bf16[32,2560]{1,0:T(8,128)(2,1)S(1)}, u32[]{:S(2)}, u32[]{:S(2)}) %collective-permute-start.3) | collective-permute-done | bytes 163872 | tf_op jit(solution)/shard_map/ppermute | solution.py:427
  39.1 5.4 %collective-permute-done.4.refs_5_ = bf16[32,2560]{1,0:T(8,128)(2,1)S(1)} collective-permute-done((bf16[32,2560]{1,0:T(8,128)(2,1)S(1)}, bf16[32,2560]{1,0:T(8,128)(2,1)S(1)}, u32[]{:S(2)}, u32[]{:S(2)}) %collective-permute-start.4) | collective-permute-done | bytes 163872 | tf_op jit(solution)/shard_map/ppermute | solution.py:427
  44.5 4.2 %collective-permute-done.5.refs_6_ = bf16[32,2560]{1,0:T(8,128)(2,1)S(1)} collective-permute-done((bf16[32,2560]{1,0:T(8,128)(2,1)S(1)}, bf16[32,2560]{1,0:T(8,128)(2,1)S(1)}, u32[]{:S(2)}, u32[]{:S(2)}) %collective-permute-start.5) | collective-permute-done | bytes 163872 | tf_op jit(solution)/shard_map/ppermute | solution.py:427
  48.7 3.2 %collective-permute-done.6.refs_7_ = bf16[32,2560]{1,0:T(8,128)(2,1)S(1)} collective-permute-done((bf16[32,2560]{1,0:T(8,128)(2,1)S(1)}, bf16[32,2560]{1,0:T(8,128)(2,1)S(1)}, u32[]{:S(2)}, u32[]{:S(2)}) %collective-permute-start.6) | collective-permute-done | bytes 163872 | tf_op jit(solution)/shard_map/ppermute | solution.py:427
  51.9 3.8 %all-to-all-start.1 = ((bf16[8,32,2560]{2,1,0:T(8,128)(2,1)}), bf16[8,32,2560]{2,1,0:T(8,128)(2,1)S(1)}, u32[]{:S(2)}, u32[]{:S(2)}) async-start(bf16[8,32,2560]{2,1,0:T(8,128)(2,1)} %bitcast.11), calls=%async_computation.1 | async-start | bytes 2621440 | tf_op jit(solution)/shard_map/all_to_all | solution.py:406
  56.2 4.1 %half_scores.1 = (bf16[20,2,128,128]{3,2,1,0:T(8,128)(2,1)S(1)}, f32[128,128]{1,0:T(8,128)S(1)}, f32[64,128]{1,0:T(8,128)S(1)}) custom-call(bf16[256,2560]{1,0:T(8,128)(2,1)} %bitcast.5.query_ref, bf16[32,2560]{1,0:T(8,128)(2,1)S(1)} %get-tuple-element.87.refs_0_, bf16[32,2560]{1,0:T(8,128)(2,1)S(1)} %collective-permute-done.refs_1_, ...), custom_call_target="tpu_custom_call" | custom-call | tf_op jit(solution)/shard_map/half_scores/pallas_call | solution.py:139
  60.3 2.7 %collective-permute-start.7 = (f32[64,128]{1,0:T(8,128)S(1)}, f32[64,128]{1,0:T(8,128)S(1)}, u32[]{:S(2)}, u32[]{:S(2)}) collective-permute-start(f32[64,128]{1,0:T(8,128)S(1)} %get-tuple-element.97), channel_id=1, source_target_pairs={{0,16},{1,17},{2,18},{3,19},{4,20},{5,21},{6,22},{7,23},{8,24},{9,... | collective-permute-start | bytes 98312 | tf_op jit(solution)/shard_map/ppermute | solution.py:45
  63.1 6.9 %collective-permute-done.7.far_ref = f32[64,128]{1,0:T(8,128)S(1)} collective-permute-done((f32[64,128]{1,0:T(8,128)S(1)}, f32[64,128]{1,0:T(8,128)S(1)}, u32[]{:S(2)}, u32[]{:S(2)}) %collective-permute-start.7) | collective-permute-done | bytes 32800 | tf_op jit(solution)/shard_map/ppermute | solution.py:45
  73.6 2.4 %collective-permute-start.8 = (bf16[16,2560]{1,0:T(8,128)(2,1)S(1)}, bf16[16,2560]{1,0:T(8,128)(2,1)S(1)}, u32[]{:S(2)}, u32[]{:S(2)}) collective-permute-start(bf16[16,2560]{1,0:T(8,128)(2,1)S(1)} %half_pool.1.refs_2_), channel_id=1, source_target_pairs={{0,16},{1,17},{2,18},{3,19},{4,20},{5,21},{6,22},{7,23},{8,24},{9,... | collective-permute-start | bytes 245768 | tf_op jit(solution)/shard_map/ppermute | solution.py:45
  76.0 4.8 %stage_weights.4 = (bf16[2560,1280]{1,0:T(8,128)(2,1)S(1)}, bf16[2560,1280]{1,0:T(8,128)(2,1)S(1)}, f32[8,128]{1,0:T(8,128)S(1)}) custom-call(bf16[2,2560,1280]{2,1,0:T(8,128)(2,1)} %refs_0_.6, bf16[2,2560,1280]{2,1,0:T(8,128)(2,1)} %refs_0_.7, bf16[16,2560]{1,0:T(8,128)(2,1)S(1)} %half_pool.1.refs_2_), custom_call_target="tpu_custom_call" | custom-call | bytes 26214400 | tf_op jit(solution)/shard_map/stage_weights/pallas_call | solution.py:250
  82.5 2.9 %collective-permute-done.9 = bf16[16,2560]{1,0:T(8,128)(2,1)S(1)} collective-permute-done((bf16[16,2560]{1,0:T(8,128)(2,1)S(1)}, bf16[16,2560]{1,0:T(8,128)(2,1)S(1)}, u32[]{:S(2)}, u32[]{:S(2)}) %collective-permute-start.9) | collective-permute-done | bytes 81952 | tf_op jit(solution)/shard_map/ppermute | solution.py:45
  85.3 2.3 %collective-permute-start.12 = (bf16[32,2560]{1,0:T(8,128)(2,1)S(1)}, bf16[32,2560]{1,0:T(8,128)(2,1)S(1)}, u32[]{:S(2)}, u32[]{:S(2)}) collective-permute-start(bf16[32,2560]{1,0:T(8,128)(2,1)S(1)} %constant_dynamic-update-slice_fusion.refs_0_), channel_id=1, source_target_pairs={{0,6},{1,7},{2,4},{3,5},{4,2},{5,3},{6,0},{7,1},{8,14},{9,15},{10,... | collective-permute-start | bytes 491528 | tf_op jit(solution)/shard_map/ppermute | solution.py:45
  88.9 2.9 %stage_weights.5 = (bf16[1280,2560]{1,0:T(8,128)(2,1)S(1)}, f32[8,128]{1,0:T(8,128)S(1)}) custom-call(bf16[2,1280,2560]{2,1,0:T(8,128)(2,1)} %refs_1_.3, f32[8,128]{1,0:T(8,128)S(1)} %get-tuple-element.105.refs_1_), custom_call_target="tpu_custom_call" | custom-call | bytes 13107200 | tf_op jit(solution)/shard_map/stage_weights/pallas_call | solution.py:250
  93.5 2.6 %expand.2.near_ref = bf16[128,2688]{1,0:T(8,128)(2,1)S(1)} custom-call(bf16[32,2560]{1,0:T(8,128)(2,1)S(1)} %constant_dynamic-update-slice_fusion.refs_0_, bf16[32,2560]{1,0:T(8,128)(2,1)S(1)} %collective-permute-done.10.refs_1_, bf16[32,2560]{1,0:T(8,128)(2,1)S(1)} %collective-permute-done.11.refs_2_, bf16[32,2560]{1,0:T(8,128)(2,1)S(1)} %collective-permute-done.12.refs_3_, ...), custom_call_target="tpu_custom_call" | custom-call | tf_op jit(solution)/shard_map/expand/pallas_call | solution.py:306
  96.2 2.1 %collective-permute-done.13.far_ref = bf16[128,2688]{1,0:T(8,128)(2,1)S(1)} collective-permute-done((bf16[128,2688]{1,0:T(8,128)(2,1)S(1)}, bf16[128,2688]{1,0:T(8,128)(2,1)S(1)}, u32[]{:S(2)}, u32[]{:S(2)}) %collective-permute-start.13) | collective-permute-done | bytes 688160 | tf_op jit(solution)/shard_map/ppermute | solution.py:467
  106.4 2.1 %collective-permute-start.19 = (bf16[16,2560]{1,0:T(8,128)(2,1)S(1)}, bf16[16,2560]{1,0:T(8,128)(2,1)S(1)}, u32[]{:S(2)}, u32[]{:S(2)}) collective-permute-start(bf16[16,2560]{1,0:T(8,128)(2,1)S(1)} %get-tuple-element.114.refs_6_), channel_id=1, source_target_pairs={{0,6},{1,7},{2,4},{3,5},{4,2},{5,3},{6,0},{7,1},{8,14},{9,15},{10,... | collective-permute-start | bytes 245768 | tf_op jit(solution)/shard_map/ppermute | solution.py:45
  109.2 2.9 %stage_weights.6 = (bf16[2560,1280]{1,0:T(8,128)(2,1)S(1)}, f32[8,128]{1,0:T(8,128)S(1)}) custom-call(bf16[2,2560,1280]{2,1,0:T(8,128)(2,1)} %refs_0_.6, bf16[16,2560]{1,0:T(8,128)(2,1)S(1)} %get-tuple-element.109.refs_1_, bf16[16,2560]{1,0:T(8,128)(2,1)S(1)} %get-tuple-element.110.refs_2_, bf16[16,2560]{1,0:T(8,128)(2,1)S(1)} %get-tuple-element.111.refs_3_, ...), custom_call_target="tpu_custom_call" | custom-call | bytes 13107200 | tf_op jit(solution)/shard_map/stage_weights/pallas_call | solution.py:250
  112.7 2.1 %collective-permute-done.20 = bf16[16,2560]{1,0:T(8,128)(2,1)S(1)} collective-permute-done((bf16[16,2560]{1,0:T(8,128)(2,1)S(1)}, bf16[16,2560]{1,0:T(8,128)(2,1)S(1)}, u32[]{:S(2)}, u32[]{:S(2)}) %collective-permute-start.20) | collective-permute-done | bytes 81952 | tf_op jit(solution)/shard_map/ppermute | solution.py:45
  114.8 2.4 %collective-permute-start.21 = (bf16[16,2560]{1,0:T(8,128)(2,1)S(1)}, bf16[16,2560]{1,0:T(8,128)(2,1)S(1)}, u32[]{:S(2)}, u32[]{:S(2)}) collective-permute-start(bf16[16,2560]{1,0:T(8,128)(2,1)S(1)} %add_convert_fusion.1), channel_id=1, source_target_pairs={{0,16},{1,17},{2,18},{3,19},{4,20},{5,21},{6,22},{7,23},{8,24},{9,... | collective-permute-start | bytes 245768 | tf_op jit(solution)/shard_map/ppermute | solution.py:45
  117.3 3.8 %collective-permute-done.21 = bf16[16,2560]{1,0:T(8,128)(2,1)S(1)} collective-permute-done((bf16[16,2560]{1,0:T(8,128)(2,1)S(1)}, bf16[16,2560]{1,0:T(8,128)(2,1)S(1)}, u32[]{:S(2)}, u32[]{:S(2)}) %collective-permute-start.21) | collective-permute-done | bytes 81952 | tf_op jit(solution)/shard_map/ppermute | solution.py:45
  121.2 4.4 %collective-permute-done.22 = bf16[16,2560]{1,0:T(8,128)(2,1)S(1)} collective-permute-done((bf16[16,2560]{1,0:T(8,128)(2,1)S(1)}, bf16[16,2560]{1,0:T(8,128)(2,1)S(1)}, u32[]{:S(2)}, u32[]{:S(2)}) %collective-permute-start.22) | collective-permute-done | bytes 81952 | tf_op jit(solution)/shard_map/ppermute | solution.py:45
  129.2 4.8 %stage_weights.7 = (bf16[2560,1280]{1,0:T(8,128)(2,1)S(1)}, bf16[1280,2560]{1,0:T(8,128)(2,1)S(1)}, f32[8,128]{1,0:T(8,128)S(1)}) custom-call(bf16[2,2560,1280]{2,1,0:T(8,128)(2,1)} %refs_0_.7, bf16[2,1280,2560]{2,1,0:T(8,128)(2,1)} %refs_1_.3, bf16[16,2560]{1,0:T(8,128)(2,1)S(1)} %add_convert_fusion.refs_2_, f32[8,128]{1,0:T(8,128)S(1)} %get-tuple-element.125.refs_3_), custom_call_target="tpu_custom_call" | custom-call | bytes 26214400 | tf_op jit(solution)/shard_map/stage_weights/pallas_call | solution.py:250
  134.1 2.6 %expand.3.near_ref = bf16[128,2688]{1,0:T(8,128)(2,1)S(1)} custom-call(bf16[32,2560]{1,0:T(8,128)(2,1)S(1)} %pad_maximum_fusion.refs_0_, bf16[32,2560]{1,0:T(8,128)(2,1)S(1)} %collective-permute-done.23.refs_1_, bf16[32,2560]{1,0:T(8,128)(2,1)S(1)} %collective-permute-done.24.refs_2_, bf16[32,2560]{1,0:T(8,128)(2,1)S(1)} %collective-permute-done.25.refs_3_, ...), custom_call_target="tpu_custom_call" | custom-call | tf_op jit(solution)/shard_map/expand/pallas_call | solution.py:306
  136.8 2.1 %collective-permute-done.26.far_ref = bf16[128,2688]{1,0:T(8,128)(2,1)S(1)} collective-permute-done((bf16[128,2688]{1,0:T(8,128)(2,1)S(1)}, bf16[128,2688]{1,0:T(8,128)(2,1)S(1)}, u32[]{:S(2)}, u32[]{:S(2)}) %collective-permute-start.26) | collective-permute-done | bytes 688160 | tf_op jit(solution)/shard_map/ppermute | solution.py:467
  141.3 2.6 %collective-permute-start.29 = (bf16[16,2560]{1,0:T(8,128)(2,1)S(1)}, bf16[16,2560]{1,0:T(8,128)(2,1)S(1)}, u32[]{:S(2)}, u32[]{:S(2)}) collective-permute-start(bf16[16,2560]{1,0:T(8,128)(2,1)S(1)} %get-tuple-element.132), channel_id=1, source_target_pairs={{0,12},{1,11},{2,14},{3,9},{4,8},{5,15},{6,10},{7,13},{8,4},{9,3},... | collective-permute-start | bytes 245768 | tf_op jit(solution)/shard_map/ppermute | solution.py:45
  146.4 3.4 %collective-permute-start.33 = (bf16[16,2560]{1,0:T(8,128)(2,1)S(1)}, bf16[16,2560]{1,0:T(8,128)(2,1)S(1)}, u32[]{:S(2)}, u32[]{:S(2)}) collective-permute-start(bf16[16,2560]{1,0:T(8,128)(2,1)S(1)} %get-tuple-element.136), channel_id=1, source_target_pairs={{0,14},{1,15},{2,12},{3,13},{4,10},{5,11},{6,8},{7,9},{8,6},{9,7},... | collective-permute-start | bytes 245768 | tf_op jit(solution)/shard_map/ppermute | solution.py:45
  150.6 2.4 %collective-permute-done.32 = bf16[16,2560]{1,0:T(8,128)(2,1)S(1)} collective-permute-done((bf16[16,2560]{1,0:T(8,128)(2,1)S(1)}, bf16[16,2560]{1,0:T(8,128)(2,1)S(1)}, u32[]{:S(2)}, u32[]{:S(2)}) %collective-permute-start.32) | collective-permute-done | bytes 81952 | tf_op jit(solution)/shard_map/ppermute | solution.py:45
  153.1 2.2 %collective-permute-start.34 = (bf16[8,2560]{1,0:T(8,128)(2,1)S(1)}, bf16[8,2560]{1,0:T(8,128)(2,1)S(1)}, u32[]{:S(2)}, u32[]{:S(2)}) collective-permute-start(bf16[8,2560]{1,0:T(8,128)(2,1)S(1)} %slice.53), channel_id=1, source_target_pairs={{0,16},{1,17},{2,18},{3,19},{4,20},{5,21},{6,22},{7,23},{8,24},{9,... | collective-permute-start | bytes 122888 | tf_op jit(solution)/shard_map/ppermute | solution.py:45
  155.2 2.8 %collective-permute-done.34 = bf16[8,2560]{1,0:T(8,128)(2,1)S(1)} collective-permute-done((bf16[8,2560]{1,0:T(8,128)(2,1)S(1)}, bf16[8,2560]{1,0:T(8,128)(2,1)S(1)}, u32[]{:S(2)}, u32[]{:S(2)}) %collective-permute-start.34) | collective-permute-done | bytes 40992 | tf_op jit(solution)/shard_map/ppermute | solution.py:45
  (106 shorter events, 45.2 us)
Async XLA Ops:
  3.9 48.0 %all-to-all-start = ((bf16[16,16,2560]{2,1,0:T(8,128)(2,1)}), bf16[16,16,2560]{2,1,0:T(8,128)(2,1)}, u32[]{:S(2)}, u32[]{:S(2)}) async-start(bf16[16,16,2560]{2,1,0:T(8,128)(2,1)} %bitcast.4), calls=%async_computation | async-start | bytes 2621440 | tf_op jit(solution)/shard_map/all_to_all | solution.py:416
  14.8 7.8 %collective-permute-start = (bf16[32,2560]{1,0:T(8,128)(2,1)S(1)}, bf16[32,2560]{1,0:T(8,128)(2,1)S(1)}, u32[]{:S(2)}, u32[]{:S(2)}) collective-permute-start(bf16[32,2560]{1,0:T(8,128)(2,1)S(1)} %get-tuple-element.71), channel_id=1, source_target_pairs={{0,2},{2,0},{4,6},{6,4},{8,10},{10,8},{12,14},{14,12},{16,18},{18,... | collective-permute-start | bytes 491528 | tf_op jit(solution)/shard_map/ppermute | solution.py:427
  16.8 15.3 %collective-permute-start.1 = (bf16[32,2560]{1,0:T(8,128)(2,1)S(1)}, bf16[32,2560]{1,0:T(8,128)(2,1)S(1)}, u32[]{:S(2)}, u32[]{:S(2)}) collective-permute-start(bf16[32,2560]{1,0:T(8,128)(2,1)S(1)} %get-tuple-element.72), channel_id=1, source_target_pairs={{0,4},{2,6},{4,0},{6,2},{8,12},{10,14},{12,8},{14,10},{16,20},{18,... | collective-permute-start | bytes 491528 | tf_op jit(solution)/shard_map/ppermute | solution.py:427
  18.2 16.3 %collective-permute-start.2 = (bf16[32,2560]{1,0:T(8,128)(2,1)S(1)}, bf16[32,2560]{1,0:T(8,128)(2,1)S(1)}, u32[]{:S(2)}, u32[]{:S(2)}) collective-permute-start(bf16[32,2560]{1,0:T(8,128)(2,1)S(1)} %get-tuple-element.73), channel_id=1, source_target_pairs={{0,6},{2,4},{4,2},{6,0},{8,14},{10,12},{12,10},{14,8},{16,22},{18,... | collective-permute-start | bytes 491528 | tf_op jit(solution)/shard_map/ppermute | solution.py:427
  18.4 20.8 %collective-permute-start.3 = (bf16[32,2560]{1,0:T(8,128)(2,1)S(1)}, bf16[32,2560]{1,0:T(8,128)(2,1)S(1)}, u32[]{:S(2)}, u32[]{:S(2)}) collective-permute-start(bf16[32,2560]{1,0:T(8,128)(2,1)S(1)} %get-tuple-element.74), channel_id=1, source_target_pairs={{0,8},{2,10},{4,12},{6,14},{8,0},{10,2},{12,4},{14,6},{16,24},{18,... | collective-permute-start | bytes 491528 | tf_op jit(solution)/shard_map/ppermute | solution.py:427
  20.2 24.3 %collective-permute-start.4 = (bf16[32,2560]{1,0:T(8,128)(2,1)S(1)}, bf16[32,2560]{1,0:T(8,128)(2,1)S(1)}, u32[]{:S(2)}, u32[]{:S(2)}) collective-permute-start(bf16[32,2560]{1,0:T(8,128)(2,1)S(1)} %get-tuple-element.75), channel_id=1, source_target_pairs={{0,10},{2,8},{4,14},{6,12},{8,2},{10,0},{12,6},{14,4},{16,26},{18,... | collective-permute-start | bytes 491528 | tf_op jit(solution)/shard_map/ppermute | solution.py:427
  22.6 26.1 %collective-permute-start.5 = (bf16[32,2560]{1,0:T(8,128)(2,1)S(1)}, bf16[32,2560]{1,0:T(8,128)(2,1)S(1)}, u32[]{:S(2)}, u32[]{:S(2)}) collective-permute-start(bf16[32,2560]{1,0:T(8,128)(2,1)S(1)} %get-tuple-element.76), channel_id=1, source_target_pairs={{0,12},{2,14},{4,8},{6,10},{8,4},{10,6},{12,0},{14,2},{16,28},{18,... | collective-permute-start | bytes 491528 | tf_op jit(solution)/shard_map/ppermute | solution.py:427
  32.1 19.8 %collective-permute-start.6 = (bf16[32,2560]{1,0:T(8,128)(2,1)S(1)}, bf16[32,2560]{1,0:T(8,128)(2,1)S(1)}, u32[]{:S(2)}, u32[]{:S(2)}) collective-permute-start(bf16[32,2560]{1,0:T(8,128)(2,1)S(1)} %get-tuple-element.77), channel_id=1, source_target_pairs={{0,14},{2,12},{4,10},{6,8},{8,6},{10,4},{12,2},{14,0},{16,30},{18,... | collective-permute-start | bytes 491528 | tf_op jit(solution)/shard_map/ppermute | solution.py:427
  51.9 20.7 %all-to-all-start.1 = ((bf16[8,32,2560]{2,1,0:T(8,128)(2,1)}), bf16[8,32,2560]{2,1,0:T(8,128)(2,1)S(1)}, u32[]{:S(2)}, u32[]{:S(2)}) async-start(bf16[8,32,2560]{2,1,0:T(8,128)(2,1)} %bitcast.11), calls=%async_computation.1 | async-start | bytes 2621440 | tf_op jit(solution)/shard_map/all_to_all | solution.py:406
  60.3 9.6 %collective-permute-start.7 = (f32[64,128]{1,0:T(8,128)S(1)}, f32[64,128]{1,0:T(8,128)S(1)}, u32[]{:S(2)}, u32[]{:S(2)}) collective-permute-start(f32[64,128]{1,0:T(8,128)S(1)} %get-tuple-element.97), channel_id=1, source_target_pairs={{0,16},{1,17},{2,18},{3,19},{4,20},{5,21},{6,22},{7,23},{8,24},{9,... | collective-permute-start | bytes 98312 | tf_op jit(solution)/shard_map/ppermute | solution.py:45
  73.6 7.1 %collective-permute-start.8 = (bf16[16,2560]{1,0:T(8,128)(2,1)S(1)}, bf16[16,2560]{1,0:T(8,128)(2,1)S(1)}, u32[]{:S(2)}, u32[]{:S(2)}) collective-permute-start(bf16[16,2560]{1,0:T(8,128)(2,1)S(1)} %half_pool.1.refs_2_), channel_id=1, source_target_pairs={{0,16},{1,17},{2,18},{3,19},{4,20},{5,21},{6,22},{7,23},{8,24},{9,... | collective-permute-start | bytes 245768 | tf_op jit(solution)/shard_map/ppermute | solution.py:45
  85.3 6.4 %collective-permute-start.12 = (bf16[32,2560]{1,0:T(8,128)(2,1)S(1)}, bf16[32,2560]{1,0:T(8,128)(2,1)S(1)}, u32[]{:S(2)}, u32[]{:S(2)}) collective-permute-start(bf16[32,2560]{1,0:T(8,128)(2,1)S(1)} %constant_dynamic-update-slice_fusion.refs_0_), channel_id=1, source_target_pairs={{0,6},{1,7},{2,4},{3,5},{4,2},{5,3},{6,0},{7,1},{8,14},{9,15},{10,... | collective-permute-start | bytes 491528 | tf_op jit(solution)/shard_map/ppermute | solution.py:45
  87.6 5.6 %collective-permute-start.11 = (bf16[32,2560]{1,0:T(8,128)(2,1)S(1)}, bf16[32,2560]{1,0:T(8,128)(2,1)S(1)}, u32[]{:S(2)}, u32[]{:S(2)}) collective-permute-start(bf16[32,2560]{1,0:T(8,128)(2,1)S(1)} %constant_dynamic-update-slice_fusion.refs_0_), channel_id=1, source_target_pairs={{0,2},{1,5},{2,0},{3,7},{4,6},{5,1},{6,4},{7,3},{8,10},{9,13},{10,... | collective-permute-start | bytes 491528 | tf_op jit(solution)/shard_map/ppermute | solution.py:45
  88.2 5.3 %collective-permute-start.10 = (bf16[32,2560]{1,0:T(8,128)(2,1)S(1)}, bf16[32,2560]{1,0:T(8,128)(2,1)S(1)}, u32[]{:S(2)}, u32[]{:S(2)}) collective-permute-start(bf16[32,2560]{1,0:T(8,128)(2,1)S(1)} %constant_dynamic-update-slice_fusion.refs_0_), channel_id=1, source_target_pairs={{0,4},{1,3},{2,6},{3,1},{4,0},{5,7},{6,2},{7,5},{8,12},{9,11},{10,... | collective-permute-start | bytes 491528 | tf_op jit(solution)/shard_map/ppermute | solution.py:45
  99.8 6.7 %collective-permute-start.14 = (bf16[16,2560]{1,0:T(8,128)(2,1)S(1)}, bf16[16,2560]{1,0:T(8,128)(2,1)S(1)}, u32[]{:S(2)}, u32[]{:S(2)}) collective-permute-start(bf16[16,2560]{1,0:T(8,128)(2,1)S(1)} %get-tuple-element.109.refs_1_), channel_id=1, source_target_pairs={{0,8},{1,9},{2,10},{3,11},{4,12},{5,13},{6,14},{7,15},{8,0},{9,1},... | collective-permute-start | bytes 245768 | tf_op jit(solution)/shard_map/ppermute | solution.py:45
  101.5 7.0 %collective-permute-start.15 = (bf16[16,2560]{1,0:T(8,128)(2,1)S(1)}, bf16[16,2560]{1,0:T(8,128)(2,1)S(1)}, u32[]{:S(2)}, u32[]{:S(2)}) collective-permute-start(bf16[16,2560]{1,0:T(8,128)(2,1)S(1)} %get-tuple-element.110.refs_2_), channel_id=1, source_target_pairs={{0,4},{1,3},{2,6},{3,1},{4,0},{5,7},{6,2},{7,5},{8,12},{9,11},{10,... | collective-permute-start | bytes 245768 | tf_op jit(solution)/shard_map/ppermute | solution.py:45
  102.7 9.4 %collective-permute-start.16 = (bf16[16,2560]{1,0:T(8,128)(2,1)S(1)}, bf16[16,2560]{1,0:T(8,128)(2,1)S(1)}, u32[]{:S(2)}, u32[]{:S(2)}) collective-permute-start(bf16[16,2560]{1,0:T(8,128)(2,1)S(1)} %get-tuple-element.111.refs_3_), channel_id=1, source_target_pairs={{0,12},{1,11},{2,14},{3,9},{4,8},{5,15},{6,10},{7,13},{8,4},{9,3},... | collective-permute-start | bytes 245768 | tf_op jit(solution)/shard_map/ppermute | solution.py:45
  103.3 8.7 %collective-permute-start.17 = (bf16[16,2560]{1,0:T(8,128)(2,1)S(1)}, bf16[16,2560]{1,0:T(8,128)(2,1)S(1)}, u32[]{:S(2)}, u32[]{:S(2)}) collective-permute-start(bf16[16,2560]{1,0:T(8,128)(2,1)S(1)} %get-tuple-element.112.refs_4_), channel_id=1, source_target_pairs={{0,2},{1,5},{2,0},{3,7},{4,6},{5,1},{6,4},{7,3},{8,10},{9,13},{10,... | collective-permute-start | bytes 245768 | tf_op jit(solution)/shard_map/ppermute | solution.py:45
  104.8 7.3 %collective-permute-start.18 = (bf16[16,2560]{1,0:T(8,128)(2,1)S(1)}, bf16[16,2560]{1,0:T(8,128)(2,1)S(1)}, u32[]{:S(2)}, u32[]{:S(2)}) collective-permute-start(bf16[16,2560]{1,0:T(8,128)(2,1)S(1)} %get-tuple-element.113.refs_5_), channel_id=1, source_target_pairs={{0,10},{1,13},{2,8},{3,15},{4,14},{5,9},{6,12},{7,11},{8,2},{9,5},... | collective-permute-start | bytes 245768 | tf_op jit(solution)/shard_map/ppermute | solution.py:45
  106.4 6.2 %collective-permute-start.19 = (bf16[16,2560]{1,0:T(8,128)(2,1)S(1)}, bf16[16,2560]{1,0:T(8,128)(2,1)S(1)}, u32[]{:S(2)}, u32[]{:S(2)}) collective-permute-start(bf16[16,2560]{1,0:T(8,128)(2,1)S(1)} %get-tuple-element.114.refs_6_), channel_id=1, source_target_pairs={{0,6},{1,7},{2,4},{3,5},{4,2},{5,3},{6,0},{7,1},{8,14},{9,15},{10,... | collective-permute-start | bytes 245768 | tf_op jit(solution)/shard_map/ppermute | solution.py:45
  108.5 6.2 %collective-permute-start.20 = (bf16[16,2560]{1,0:T(8,128)(2,1)S(1)}, bf16[16,2560]{1,0:T(8,128)(2,1)S(1)}, u32[]{:S(2)}, u32[]{:S(2)}) collective-permute-start(bf16[16,2560]{1,0:T(8,128)(2,1)S(1)} %get-tuple-element.115.refs_7_), channel_id=1, source_target_pairs={{0,14},{1,15},{2,12},{3,13},{4,10},{5,11},{6,8},{7,9},{8,6},{9,7},... | collective-permute-start | bytes 245768 | tf_op jit(solution)/shard_map/ppermute | solution.py:45
  114.8 6.2 %collective-permute-start.21 = (bf16[16,2560]{1,0:T(8,128)(2,1)S(1)}, bf16[16,2560]{1,0:T(8,128)(2,1)S(1)}, u32[]{:S(2)}, u32[]{:S(2)}) collective-permute-start(bf16[16,2560]{1,0:T(8,128)(2,1)S(1)} %add_convert_fusion.1), channel_id=1, source_target_pairs={{0,16},{1,17},{2,18},{3,19},{4,20},{5,21},{6,22},{7,23},{8,24},{9,... | collective-permute-start | bytes 245768 | tf_op jit(solution)/shard_map/ppermute | solution.py:45
  125.6 8.4 %collective-permute-start.25 = (bf16[32,2560]{1,0:T(8,128)(2,1)S(1)}, bf16[32,2560]{1,0:T(8,128)(2,1)S(1)}, u32[]{:S(2)}, u32[]{:S(2)}) collective-permute-start(bf16[32,2560]{1,0:T(8,128)(2,1)S(1)} %pad_maximum_fusion.refs_0_), channel_id=1, source_target_pairs={{0,6},{1,7},{2,4},{3,5},{4,2},{5,3},{6,0},{7,1},{8,14},{9,15},{10,... | collective-permute-start | bytes 491528 | tf_op jit(solution)/shard_map/ppermute | solution.py:45
  126.6 7.4 %collective-permute-start.24 = (bf16[32,2560]{1,0:T(8,128)(2,1)S(1)}, bf16[32,2560]{1,0:T(8,128)(2,1)S(1)}, u32[]{:S(2)}, u32[]{:S(2)}) collective-permute-start(bf16[32,2560]{1,0:T(8,128)(2,1)S(1)} %pad_maximum_fusion.refs_0_), channel_id=1, source_target_pairs={{0,2},{1,5},{2,0},{3,7},{4,6},{5,1},{6,4},{7,3},{8,10},{9,13},{10,... | collective-permute-start | bytes 491528 | tf_op jit(solution)/shard_map/ppermute | solution.py:45
  128.0 6.1 %collective-permute-start.23 = (bf16[32,2560]{1,0:T(8,128)(2,1)S(1)}, bf16[32,2560]{1,0:T(8,128)(2,1)S(1)}, u32[]{:S(2)}, u32[]{:S(2)}) collective-permute-start(bf16[32,2560]{1,0:T(8,128)(2,1)S(1)} %pad_maximum_fusion.refs_0_), channel_id=1, source_target_pairs={{0,4},{1,3},{2,6},{3,1},{4,0},{5,7},{6,2},{7,5},{8,12},{9,11},{10,... | collective-permute-start | bytes 491528 | tf_op jit(solution)/shard_map/ppermute | solution.py:45
  140.3 5.1 %collective-permute-start.27 = (bf16[16,2560]{1,0:T(8,128)(2,1)S(1)}, bf16[16,2560]{1,0:T(8,128)(2,1)S(1)}, u32[]{:S(2)}, u32[]{:S(2)}) collective-permute-start(bf16[16,2560]{1,0:T(8,128)(2,1)S(1)} %get-tuple-element.130), channel_id=1, source_target_pairs={{0,8},{1,9},{2,10},{3,11},{4,12},{5,13},{6,14},{7,15},{8,0},{9,1},... | collective-permute-start | bytes 245768 | tf_op jit(solution)/shard_map/ppermute | solution.py:45
  140.4 6.0 %collective-permute-start.28 = (bf16[16,2560]{1,0:T(8,128)(2,1)S(1)}, bf16[16,2560]{1,0:T(8,128)(2,1)S(1)}, u32[]{:S(2)}, u32[]{:S(2)}) collective-permute-start(bf16[16,2560]{1,0:T(8,128)(2,1)S(1)} %get-tuple-element.131), channel_id=1, source_target_pairs={{0,4},{1,3},{2,6},{3,1},{4,0},{5,7},{6,2},{7,5},{8,12},{9,11},{10,... | collective-permute-start | bytes 245768 | tf_op jit(solution)/shard_map/ppermute | solution.py:45
  141.3 8.4 %collective-permute-start.29 = (bf16[16,2560]{1,0:T(8,128)(2,1)S(1)}, bf16[16,2560]{1,0:T(8,128)(2,1)S(1)}, u32[]{:S(2)}, u32[]{:S(2)}) collective-permute-start(bf16[16,2560]{1,0:T(8,128)(2,1)S(1)} %get-tuple-element.132), channel_id=1, source_target_pairs={{0,12},{1,11},{2,14},{3,9},{4,8},{5,15},{6,10},{7,13},{8,4},{9,3},... | collective-permute-start | bytes 245768 | tf_op jit(solution)/shard_map/ppermute | solution.py:45
  143.9 5.9 %collective-permute-start.30 = (bf16[16,2560]{1,0:T(8,128)(2,1)S(1)}, bf16[16,2560]{1,0:T(8,128)(2,1)S(1)}, u32[]{:S(2)}, u32[]{:S(2)}) collective-permute-start(bf16[16,2560]{1,0:T(8,128)(2,1)S(1)} %get-tuple-element.133), channel_id=1, source_target_pairs={{0,2},{1,5},{2,0},{3,7},{4,6},{5,1},{6,4},{7,3},{8,10},{9,13},{10,... | collective-permute-start | bytes 245768 | tf_op jit(solution)/shard_map/ppermute | solution.py:45
  144.5 6.1 %collective-permute-start.31 = (bf16[16,2560]{1,0:T(8,128)(2,1)S(1)}, bf16[16,2560]{1,0:T(8,128)(2,1)S(1)}, u32[]{:S(2)}, u32[]{:S(2)}) collective-permute-start(bf16[16,2560]{1,0:T(8,128)(2,1)S(1)} %get-tuple-element.134), channel_id=1, source_target_pairs={{0,10},{1,13},{2,8},{3,15},{4,14},{5,9},{6,12},{7,11},{8,2},{9,5},... | collective-permute-start | bytes 245768 | tf_op jit(solution)/shard_map/ppermute | solution.py:45
  145.4 7.5 %collective-permute-start.32 = (bf16[16,2560]{1,0:T(8,128)(2,1)S(1)}, bf16[16,2560]{1,0:T(8,128)(2,1)S(1)}, u32[]{:S(2)}, u32[]{:S(2)}) collective-permute-start(bf16[16,2560]{1,0:T(8,128)(2,1)S(1)} %get-tuple-element.135), channel_id=1, source_target_pairs={{0,6},{1,7},{2,4},{3,5},{4,2},{5,3},{6,0},{7,1},{8,14},{9,15},{10,... | collective-permute-start | bytes 245768 | tf_op jit(solution)/shard_map/ppermute | solution.py:45
  146.4 6.6 %collective-permute-start.33 = (bf16[16,2560]{1,0:T(8,128)(2,1)S(1)}, bf16[16,2560]{1,0:T(8,128)(2,1)S(1)}, u32[]{:S(2)}, u32[]{:S(2)}) collective-permute-start(bf16[16,2560]{1,0:T(8,128)(2,1)S(1)} %get-tuple-element.136), channel_id=1, source_target_pairs={{0,14},{1,15},{2,12},{3,13},{4,10},{5,11},{6,8},{7,9},{8,6},{9,7},... | collective-permute-start | bytes 245768 | tf_op jit(solution)/shard_map/ppermute | solution.py:45
  (14 other events, 208.1 us)

commit v12 on v11

--- a/solution.py
+++ b/solution.py
@@ -156,6 +156,10 @@
     )(held, *keys)
 
 
+def heads_held(heads):
+    return 2 * HEADS_STEP if heads % (2 * HEADS_STEP) == 0 else HEADS_STEP
+
+
 def weigh_body(probs_ref, lse_ref, far_ref, weights_ref):
     step = pl.program_id(0)
     lane = lax.broadcasted_iota(jnp.int32, lse_ref.shape, 1)
@@ -164,10 +168,11 @@
         lane < LSE_ITEM, pltpu.roll(far, 128 - LSE_ITEM, 1), pltpu.roll(far, LSE_ITEM, 1)
     )
     share = 1.0 / (1.0 + jnp.exp(far - lse_ref[...])) * (1.0 / VENUES)
-    for head in range(HEADS_STEP):
+    held = probs_ref.shape[0]
+    for head in range(held):
         means = []
         for item in range(2):
-            column = step * HEADS_STEP + head + item * LSE_ITEM
+            column = step * held + head + item * LSE_ITEM
             factor = jnp.sum(jnp.where(lane == column, share, 0.0), axis=1, keepdims=True)
             weights = probs_ref[head, item].astype(jnp.float32) * factor
             means.append(jnp.sum(weights.reshape(VENUES, NODE_STEPS, KEYS_HALF), axis=0))
@@ -176,15 +181,16 @@
 
 def mean_weights(probs, lse, far_lse):
     heads = probs.shape[0]
+    held = heads_held(heads)
     return pl.pallas_call(
         weigh_body,
-        grid=(heads // HEADS_STEP,),
+        grid=(heads // held,),
         in_specs=[
-            pl.BlockSpec((HEADS_STEP, 2, 2 * ROWS_HALF, KEYS_HALF), lambda j: (j, 0, 0, 0)),
+            pl.BlockSpec((held, 2, 2 * ROWS_HALF, KEYS_HALF), lambda j: (j, 0, 0, 0)),
             pl.BlockSpec((2 * ROWS_HALF, 128), lambda j: (0, 0)),
             pl.BlockSpec((ROWS_HALF, 128), lambda j: (0, 0)),
         ],
-        out_specs=pl.BlockSpec((HEADS_STEP, 2 * NODE_STEPS, KEYS_HALF), lambda j: (j, 0, 0)),
+        out_specs=pl.BlockSpec((held, 2 * NODE_STEPS, KEYS_HALF), lambda j: (j, 0, 0)),
         out_shape=jax.ShapeDtypeStruct((heads, 2 * NODE_STEPS, KEYS_HALF), jnp.bfloat16),
         compiler_params=pltpu.CompilerParams(vmem_limit_bytes=VMEM_LIMIT),
         name="mean_weights",
@@ -194,7 +200,7 @@
 def pool_body(first_ref, weights_ref, value_ref, out_ref):
     first = first_ref[0]
     row = lax.broadcasted_iota(jnp.int32, (2 * NODE_STEPS, HEAD_DIM), 0)
-    for head in range(HEADS_STEP):
+    for head in range(weights_ref.shape[0]):
         span = slice(head * HEAD_DIM, (head + 1) * HEAD_DIM)
         pooled = [
             jnp.dot(
@@ -211,15 +217,17 @@
 
 def half_pool(first, weights, values):
     width = values.shape[3]
+    held = heads_held(width // HEAD_DIM)
+    cols = held * HEAD_DIM
     return pl.pallas_call(
         pool_body,
-        grid=(width // COLS_STEP,),
+        grid=(width // cols,),
         in_specs=[
             pl.BlockSpec(memory_space=pltpu.SMEM),
-            pl.BlockSpec((HEADS_STEP, 2 * NODE_STEPS, KEYS_HALF), lambda j: (j, 0, 0)),
-            pl.BlockSpec((HALF_VENUES, 2, STEPS, COLS_STEP), lambda j: (0, 0, 0, j)),
+            pl.BlockSpec((held, 2 * NODE_STEPS, KEYS_HALF), lambda j: (j, 0, 0)),
+            pl.BlockSpec((HALF_VENUES, 2, STEPS, cols), lambda j: (0, 0, 0, j)),
         ],
-        out_specs=pl.BlockSpec((2 * NODE_STEPS, COLS_STEP), lambda j: (0, j)),
+        out_specs=pl.BlockSpec((2 * NODE_STEPS, cols), lambda j: (0, j)),
         out_shape=jax.ShapeDtypeStruct((2 * NODE_STEPS, width), jnp.bfloat16),
         compiler_params=pltpu.CompilerParams(vmem_limit_bytes=VMEM_LIMIT),
         name="half_pool",

time: 159 us -> 159 us (level)
  no operation moved by 1% of the time
where the time goes in v12:
time: 159 us; the launch traced here: 158 us
  starting transfers between devices  59.5 us (37%)
  waiting for transfers between devices  59.3 us (37%)
  Pallas kernels  33.5 us (21%)
  local copies, waits for them, and re-layouts  3.3 us (2%)
  other arithmetic  1.64 us (1%)
    ppermute x26, starting transfers between devices, swap_stage(): return lax.ppermute(block, ('gx', 'ta'), pairs)  36.8 us
    ppermute x26, waiting for transfers between devices, swap_stage(): return lax.ppermute(block, ('gx', 'ta'), pairs)  28.6 us
    ppermute x7, waiting for transfers between devices, per_device(): keys.append(lax.ppermute(pieces[flip], 'gx', pairs))  24.9 us
    pallas_call x4, Pallas kernels, stage_weights(): pl.pallas_call(functools.partial(stage_body, layer=layer, count=len(held)...  15.3 us
    ppermute x7, starting transfers between devices, per_device(): keys.append(lax.ppermute(pieces[flip], 'gx', pairs))  10.5 us
    all_to_all x1, starting transfers between devices, per_device(): lax.all_to_all(queries.reshape(gx_count, -1, feat_width), 'gx', 0, 0, til...  8.36 us
    pallas_call x2, Pallas kernels, expand(): pl.pallas_call(functools.partial(expand_body, layer=layer), in_specs=[pl....  5.21 us
    ppermute x2, waiting for transfers between devices, per_device(): far_sums = lax.ppermute(near_sums, 'ta', [(0, 1), (1, 0)])  4.26 us
  transfers between devices with their start and end apart: 37, of which 20 were waited for; matrix products, arithmetic and copies ran while one was open for 0% of the time, Pallas kernels for 15%

profile of v12, /device:TPU:0, one launch (start us, length us, event | category | flops | bytes accessed | tf_op | source)
XLA Modules:
  0.0 158.1 jit_solution(14235050026051077341)
XLA Ops:
  3.9 8.4 %all-to-all-start = ((bf16[16,16,2560]{2,1,0:T(8,128)(2,1)}), bf16[16,16,2560]{2,1,0:T(8,128)(2,1)}, u32[]{:S(2)}, u32[]{:S(2)}) async-start(bf16[16,16,2560]{2,1,0:T(8,128)(2,1)} %bitcast.4), calls=%async_computation | async-start | bytes 2621440 | tf_op jit(solution)/shard_map/all_to_all | solution.py:424
  14.8 1.9 %collective-permute-start = (bf16[32,2560]{1,0:T(8,128)(2,1)S(1)}, bf16[32,2560]{1,0:T(8,128)(2,1)S(1)}, u32[]{:S(2)}, u32[]{:S(2)}) collective-permute-start(bf16[32,2560]{1,0:T(8,128)(2,1)S(1)} %get-tuple-element.71), channel_id=1, source_target_pairs={{0,2},{2,0},{4,6},{6,4},{8,10},{10,8},{12,14},{14,12},{16,18},{18,... | collective-permute-start | bytes 491528 | tf_op jit(solution)/shard_map/ppermute | solution.py:435
  22.6 2.8 %collective-permute-start.5 = (bf16[32,2560]{1,0:T(8,128)(2,1)S(1)}, bf16[32,2560]{1,0:T(8,128)(2,1)S(1)}, u32[]{:S(2)}, u32[]{:S(2)}) collective-permute-start(bf16[32,2560]{1,0:T(8,128)(2,1)S(1)} %get-tuple-element.76), channel_id=1, source_target_pairs={{0,12},{2,14},{4,8},{6,10},{8,4},{10,6},{12,0},{14,2},{16,28},{18,... | collective-permute-start | bytes 491528 | tf_op jit(solution)/shard_map/ppermute | solution.py:435
  25.4 6.7 %collective-permute-done.1.refs_2_ = bf16[32,2560]{1,0:T(8,128)(2,1)S(1)} collective-permute-done((bf16[32,2560]{1,0:T(8,128)(2,1)S(1)}, bf16[32,2560]{1,0:T(8,128)(2,1)S(1)}, u32[]{:S(2)}, u32[]{:S(2)}) %collective-permute-start.1) | collective-permute-done | bytes 163872 | tf_op jit(solution)/shard_map/ppermute | solution.py:435
  34.6 4.6 %collective-permute-done.3.refs_4_ = bf16[32,2560]{1,0:T(8,128)(2,1)S(1)} collective-permute-done((bf16[32,2560]{1,0:T(8,128)(2,1)S(1)}, bf16[32,2560]{1,0:T(8,128)(2,1)S(1)}, u32[]{:S(2)}, u32[]{:S(2)}) %collective-permute-start.3) | collective-permute-done | bytes 163872 | tf_op jit(solution)/shard_map/ppermute | solution.py:435
  39.1 5.4 %collective-permute-done.4.refs_5_ = bf16[32,2560]{1,0:T(8,128)(2,1)S(1)} collective-permute-done((bf16[32,2560]{1,0:T(8,128)(2,1)S(1)}, bf16[32,2560]{1,0:T(8,128)(2,1)S(1)}, u32[]{:S(2)}, u32[]{:S(2)}) %collective-permute-start.4) | collective-permute-done | bytes 163872 | tf_op jit(solution)/shard_map/ppermute | solution.py:435
  44.5 4.2 %collective-permute-done.5.refs_6_ = bf16[32,2560]{1,0:T(8,128)(2,1)S(1)} collective-permute-done((bf16[32,2560]{1,0:T(8,128)(2,1)S(1)}, bf16[32,2560]{1,0:T(8,128)(2,1)S(1)}, u32[]{:S(2)}, u32[]{:S(2)}) %collective-permute-start.5) | collective-permute-done | bytes 163872 | tf_op jit(solution)/shard_map/ppermute | solution.py:435
  48.7 3.2 %collective-permute-done.6.refs_7_ = bf16[32,2560]{1,0:T(8,128)(2,1)S(1)} collective-permute-done((bf16[32,2560]{1,0:T(8,128)(2,1)S(1)}, bf16[32,2560]{1,0:T(8,128)(2,1)S(1)}, u32[]{:S(2)}, u32[]{:S(2)}) %collective-permute-start.6) | collective-permute-done | bytes 163872 | tf_op jit(solution)/shard_map/ppermute | solution.py:435
  51.9 3.8 %all-to-all-start.1 = ((bf16[8,32,2560]{2,1,0:T(8,128)(2,1)}), bf16[8,32,2560]{2,1,0:T(8,128)(2,1)S(1)}, u32[]{:S(2)}, u32[]{:S(2)}) async-start(bf16[8,32,2560]{2,1,0:T(8,128)(2,1)} %bitcast.11), calls=%async_computation.1 | async-start | bytes 2621440 | tf_op jit(solution)/shard_map/all_to_all | solution.py:414
  56.2 4.1 %half_scores.1 = (bf16[20,2,128,128]{3,2,1,0:T(8,128)(2,1)S(1)}, f32[128,128]{1,0:T(8,128)S(1)}, f32[64,128]{1,0:T(8,128)S(1)}) custom-call(bf16[256,2560]{1,0:T(8,128)(2,1)} %bitcast.5.query_ref, bf16[32,2560]{1,0:T(8,128)(2,1)S(1)} %get-tuple-element.87.refs_0_, bf16[32,2560]{1,0:T(8,128)(2,1)S(1)} %collective-permute-done.refs_1_, ...), custom_call_target="tpu_custom_call" | custom-call | tf_op jit(solution)/shard_map/half_scores/pallas_call | solution.py:139
  60.3 2.7 %collective-permute-start.7 = (f32[64,128]{1,0:T(8,128)S(1)}, f32[64,128]{1,0:T(8,128)S(1)}, u32[]{:S(2)}, u32[]{:S(2)}) collective-permute-start(f32[64,128]{1,0:T(8,128)S(1)} %get-tuple-element.97), channel_id=1, source_target_pairs={{0,16},{1,17},{2,18},{3,19},{4,20},{5,21},{6,22},{7,23},{8,24},{9,... | collective-permute-start | bytes 98312 | tf_op jit(solution)/shard_map/ppermute | solution.py:45
  63.1 6.9 %collective-permute-done.7.far_ref = f32[64,128]{1,0:T(8,128)S(1)} collective-permute-done((f32[64,128]{1,0:T(8,128)S(1)}, f32[64,128]{1,0:T(8,128)S(1)}, u32[]{:S(2)}, u32[]{:S(2)}) %collective-permute-start.7) | collective-permute-done | bytes 32800 | tf_op jit(solution)/shard_map/ppermute | solution.py:45
  73.3 2.4 %collective-permute-start.8 = (bf16[16,2560]{1,0:T(8,128)(2,1)S(1)}, bf16[16,2560]{1,0:T(8,128)(2,1)S(1)}, u32[]{:S(2)}, u32[]{:S(2)}) collective-permute-start(bf16[16,2560]{1,0:T(8,128)(2,1)S(1)} %half_pool.1.refs_2_), channel_id=1, source_target_pairs={{0,16},{1,17},{2,18},{3,19},{4,20},{5,21},{6,22},{7,23},{8,24},{9,... | collective-permute-start | bytes 245768 | tf_op jit(solution)/shard_map/ppermute | solution.py:45
  75.7 4.8 %stage_weights.4 = (bf16[2560,1280]{1,0:T(8,128)(2,1)S(1)}, bf16[2560,1280]{1,0:T(8,128)(2,1)S(1)}, f32[8,128]{1,0:T(8,128)S(1)}) custom-call(bf16[2,2560,1280]{2,1,0:T(8,128)(2,1)} %refs_0_.6, bf16[2,2560,1280]{2,1,0:T(8,128)(2,1)} %refs_0_.7, bf16[16,2560]{1,0:T(8,128)(2,1)S(1)} %half_pool.1.refs_2_), custom_call_target="tpu_custom_call" | custom-call | bytes 26214400 | tf_op jit(solution)/shard_map/stage_weights/pallas_call | solution.py:258
  81.8 3.2 %collective-permute-done.9 = bf16[16,2560]{1,0:T(8,128)(2,1)S(1)} collective-permute-done((bf16[16,2560]{1,0:T(8,128)(2,1)S(1)}, bf16[16,2560]{1,0:T(8,128)(2,1)S(1)}, u32[]{:S(2)}, u32[]{:S(2)}) %collective-permute-start.9) | collective-permute-done | bytes 81952 | tf_op jit(solution)/shard_map/ppermute | solution.py:45
  85.0 1.9 %collective-permute-start.12 = (bf16[32,2560]{1,0:T(8,128)(2,1)S(1)}, bf16[32,2560]{1,0:T(8,128)(2,1)S(1)}, u32[]{:S(2)}, u32[]{:S(2)}) collective-permute-start(bf16[32,2560]{1,0:T(8,128)(2,1)S(1)} %constant_dynamic-update-slice_fusion.refs_0_), channel_id=1, source_target_pairs={{0,6},{1,7},{2,4},{3,5},{4,2},{5,3},{6,0},{7,1},{8,14},{9,15},{10,... | collective-permute-start | bytes 491528 | tf_op jit(solution)/shard_map/ppermute | solution.py:45
  88.6 2.9 %stage_weights.5 = (bf16[1280,2560]{1,0:T(8,128)(2,1)S(1)}, f32[8,128]{1,0:T(8,128)S(1)}) custom-call(bf16[2,1280,2560]{2,1,0:T(8,128)(2,1)} %refs_1_.3, f32[8,128]{1,0:T(8,128)S(1)} %get-tuple-element.105.refs_1_), custom_call_target="tpu_custom_call" | custom-call | bytes 13107200 | tf_op jit(solution)/shard_map/stage_weights/pallas_call | solution.py:258
  93.1 2.6 %expand.2.near_ref = bf16[128,2688]{1,0:T(8,128)(2,1)S(1)} custom-call(bf16[32,2560]{1,0:T(8,128)(2,1)S(1)} %constant_dynamic-update-slice_fusion.refs_0_, bf16[32,2560]{1,0:T(8,128)(2,1)S(1)} %collective-permute-done.10.refs_1_, bf16[32,2560]{1,0:T(8,128)(2,1)S(1)} %collective-permute-done.11.refs_2_, bf16[32,2560]{1,0:T(8,128)(2,1)S(1)} %collective-permute-done.12.refs_3_, ...), custom_call_target="tpu_custom_call" | custom-call | tf_op jit(solution)/shard_map/expand/pallas_call | solution.py:314
  95.8 2.1 %collective-permute-done.13.far_ref = bf16[128,2688]{1,0:T(8,128)(2,1)S(1)} collective-permute-done((bf16[128,2688]{1,0:T(8,128)(2,1)S(1)}, bf16[128,2688]{1,0:T(8,128)(2,1)S(1)}, u32[]{:S(2)}, u32[]{:S(2)}) %collective-permute-start.13) | collective-permute-done | bytes 688160 | tf_op jit(solution)/shard_map/ppermute | solution.py:475
  104.2 1.9 %collective-permute-start.18 = (bf16[16,2560]{1,0:T(8,128)(2,1)S(1)}, bf16[16,2560]{1,0:T(8,128)(2,1)S(1)}, u32[]{:S(2)}, u32[]{:S(2)}) collective-permute-start(bf16[16,2560]{1,0:T(8,128)(2,1)S(1)} %get-tuple-element.113.refs_5_), channel_id=1, source_target_pairs={{0,10},{1,13},{2,8},{3,15},{4,14},{5,9},{6,12},{7,11},{8,2},{9,5},... | collective-permute-start | bytes 245768 | tf_op jit(solution)/shard_map/ppermute | solution.py:45
  108.8 2.9 %stage_weights.6 = (bf16[2560,1280]{1,0:T(8,128)(2,1)S(1)}, f32[8,128]{1,0:T(8,128)S(1)}) custom-call(bf16[2,2560,1280]{2,1,0:T(8,128)(2,1)} %refs_0_.6, bf16[16,2560]{1,0:T(8,128)(2,1)S(1)} %get-tuple-element.109.refs_1_, bf16[16,2560]{1,0:T(8,128)(2,1)S(1)} %get-tuple-element.110.refs_2_, bf16[16,2560]{1,0:T(8,128)(2,1)S(1)} %get-tuple-element.111.refs_3_, ...), custom_call_target="tpu_custom_call" | custom-call | bytes 13107200 | tf_op jit(solution)/shard_map/stage_weights/pallas_call | solution.py:258
  114.1 2.4 %collective-permute-start.21 = (bf16[16,2560]{1,0:T(8,128)(2,1)S(1)}, bf16[16,2560]{1,0:T(8,128)(2,1)S(1)}, u32[]{:S(2)}, u32[]{:S(2)}) collective-permute-start(bf16[16,2560]{1,0:T(8,128)(2,1)S(1)} %add_convert_fusion.1), channel_id=1, source_target_pairs={{0,16},{1,17},{2,18},{3,19},{4,20},{5,21},{6,22},{7,23},{8,24},{9,... | collective-permute-start | bytes 245768 | tf_op jit(solution)/shard_map/ppermute | solution.py:45
  116.6 3.8 %collective-permute-done.21 = bf16[16,2560]{1,0:T(8,128)(2,1)S(1)} collective-permute-done((bf16[16,2560]{1,0:T(8,128)(2,1)S(1)}, bf16[16,2560]{1,0:T(8,128)(2,1)S(1)}, u32[]{:S(2)}, u32[]{:S(2)}) %collective-permute-start.21) | collective-permute-done | bytes 81952 | tf_op jit(solution)/shard_map/ppermute | solution.py:45
  120.5 4.4 %collective-permute-done.22 = bf16[16,2560]{1,0:T(8,128)(2,1)S(1)} collective-permute-done((bf16[16,2560]{1,0:T(8,128)(2,1)S(1)}, bf16[16,2560]{1,0:T(8,128)(2,1)S(1)}, u32[]{:S(2)}, u32[]{:S(2)}) %collective-permute-start.22) | collective-permute-done | bytes 81952 | tf_op jit(solution)/shard_map/ppermute | solution.py:45
  128.5 4.8 %stage_weights.7 = (bf16[2560,1280]{1,0:T(8,128)(2,1)S(1)}, bf16[1280,2560]{1,0:T(8,128)(2,1)S(1)}, f32[8,128]{1,0:T(8,128)S(1)}) custom-call(bf16[2,2560,1280]{2,1,0:T(8,128)(2,1)} %refs_0_.7, bf16[2,1280,2560]{2,1,0:T(8,128)(2,1)} %refs_1_.3, bf16[16,2560]{1,0:T(8,128)(2,1)S(1)} %add_convert_fusion.refs_2_, f32[8,128]{1,0:T(8,128)S(1)} %get-tuple-element.125.refs_3_), custom_call_target="tpu_custom_call" | custom-call | bytes 26214400 | tf_op jit(solution)/shard_map/stage_weights/pallas_call | solution.py:258
  133.4 2.6 %expand.3.near_ref = bf16[128,2688]{1,0:T(8,128)(2,1)S(1)} custom-call(bf16[32,2560]{1,0:T(8,128)(2,1)S(1)} %pad_maximum_fusion.refs_0_, bf16[32,2560]{1,0:T(8,128)(2,1)S(1)} %collective-permute-done.23.refs_1_, bf16[32,2560]{1,0:T(8,128)(2,1)S(1)} %collective-permute-done.24.refs_2_, bf16[32,2560]{1,0:T(8,128)(2,1)S(1)} %collective-permute-done.25.refs_3_, ...), custom_call_target="tpu_custom_call" | custom-call | tf_op jit(solution)/shard_map/expand/pallas_call | solution.py:314
  136.1 2.1 %collective-permute-done.26.far_ref = bf16[128,2688]{1,0:T(8,128)(2,1)S(1)} collective-permute-done((bf16[128,2688]{1,0:T(8,128)(2,1)S(1)}, bf16[128,2688]{1,0:T(8,128)(2,1)S(1)}, u32[]{:S(2)}, u32[]{:S(2)}) %collective-permute-start.26) | collective-permute-done | bytes 688160 | tf_op jit(solution)/shard_map/ppermute | solution.py:475
  140.7 2.5 %collective-permute-start.29 = (bf16[16,2560]{1,0:T(8,128)(2,1)S(1)}, bf16[16,2560]{1,0:T(8,128)(2,1)S(1)}, u32[]{:S(2)}, u32[]{:S(2)}) collective-permute-start(bf16[16,2560]{1,0:T(8,128)(2,1)S(1)} %get-tuple-element.132), channel_id=1, source_target_pairs={{0,12},{1,11},{2,14},{3,9},{4,8},{5,15},{6,10},{7,13},{8,4},{9,3},... | collective-permute-start | bytes 245768 | tf_op jit(solution)/shard_map/ppermute | solution.py:45
  145.8 3.2 %collective-permute-start.33 = (bf16[16,2560]{1,0:T(8,128)(2,1)S(1)}, bf16[16,2560]{1,0:T(8,128)(2,1)S(1)}, u32[]{:S(2)}, u32[]{:S(2)}) collective-permute-start(bf16[16,2560]{1,0:T(8,128)(2,1)S(1)} %get-tuple-element.136), channel_id=1, source_target_pairs={{0,14},{1,15},{2,12},{3,13},{4,10},{5,11},{6,8},{7,9},{8,6},{9,7},... | collective-permute-start | bytes 245768 | tf_op jit(solution)/shard_map/ppermute | solution.py:45
  150.0 2.4 %collective-permute-done.32 = bf16[16,2560]{1,0:T(8,128)(2,1)S(1)} collective-permute-done((bf16[16,2560]{1,0:T(8,128)(2,1)S(1)}, bf16[16,2560]{1,0:T(8,128)(2,1)S(1)}, u32[]{:S(2)}, u32[]{:S(2)}) %collective-permute-start.32) | collective-permute-done | bytes 81952 | tf_op jit(solution)/shard_map/ppermute | solution.py:45
  152.4 2.1 %collective-permute-start.34 = (bf16[8,2560]{1,0:T(8,128)(2,1)S(1)}, bf16[8,2560]{1,0:T(8,128)(2,1)S(1)}, u32[]{:S(2)}, u32[]{:S(2)}) collective-permute-start(bf16[8,2560]{1,0:T(8,128)(2,1)S(1)} %slice.53), channel_id=1, source_target_pairs={{0,16},{1,17},{2,18},{3,19},{4,20},{5,21},{6,22},{7,23},{8,24},{9,... | collective-permute-start | bytes 122888 | tf_op jit(solution)/shard_map/ppermute | solution.py:45
  154.6 2.8 %collective-permute-done.34 = bf16[8,2560]{1,0:T(8,128)(2,1)S(1)} collective-permute-done((bf16[8,2560]{1,0:T(8,128)(2,1)S(1)}, bf16[8,2560]{1,0:T(8,128)(2,1)S(1)}, u32[]{:S(2)}, u32[]{:S(2)}) %collective-permute-start.34) | collective-permute-done | bytes 40992 | tf_op jit(solution)/shard_map/ppermute | solution.py:45
  (106 shorter events, 45.1 us)
Async XLA Ops:
  3.9 48.0 %all-to-all-start = ((bf16[16,16,2560]{2,1,0:T(8,128)(2,1)}), bf16[16,16,2560]{2,1,0:T(8,128)(2,1)}, u32[]{:S(2)}, u32[]{:S(2)}) async-start(bf16[16,16,2560]{2,1,0:T(8,128)(2,1)} %bitcast.4), calls=%async_computation | async-start | bytes 2621440 | tf_op jit(solution)/shard_map/all_to_all | solution.py:424
  14.8 7.8 %collective-permute-start = (bf16[32,2560]{1,0:T(8,128)(2,1)S(1)}, bf16[32,2560]{1,0:T(8,128)(2,1)S(1)}, u32[]{:S(2)}, u32[]{:S(2)}) collective-permute-start(bf16[32,2560]{1,0:T(8,128)(2,1)S(1)} %get-tuple-element.71), channel_id=1, source_target_pairs={{0,2},{2,0},{4,6},{6,4},{8,10},{10,8},{12,14},{14,12},{16,18},{18,... | collective-permute-start | bytes 491528 | tf_op jit(solution)/shard_map/ppermute | solution.py:435
  16.8 15.3 %collective-permute-start.1 = (bf16[32,2560]{1,0:T(8,128)(2,1)S(1)}, bf16[32,2560]{1,0:T(8,128)(2,1)S(1)}, u32[]{:S(2)}, u32[]{:S(2)}) collective-permute-start(bf16[32,2560]{1,0:T(8,128)(2,1)S(1)} %get-tuple-element.72), channel_id=1, source_target_pairs={{0,4},{2,6},{4,0},{6,2},{8,12},{10,14},{12,8},{14,10},{16,20},{18,... | collective-permute-start | bytes 491528 | tf_op jit(solution)/shard_map/ppermute | solution.py:435
  18.2 16.3 %collective-permute-start.2 = (bf16[32,2560]{1,0:T(8,128)(2,1)S(1)}, bf16[32,2560]{1,0:T(8,128)(2,1)S(1)}, u32[]{:S(2)}, u32[]{:S(2)}) collective-permute-start(bf16[32,2560]{1,0:T(8,128)(2,1)S(1)} %get-tuple-element.73), channel_id=1, source_target_pairs={{0,6},{2,4},{4,2},{6,0},{8,14},{10,12},{12,10},{14,8},{16,22},{18,... | collective-permute-start | bytes 491528 | tf_op jit(solution)/shard_map/ppermute | solution.py:435
  18.4 20.8 %collective-permute-start.3 = (bf16[32,2560]{1,0:T(8,128)(2,1)S(1)}, bf16[32,2560]{1,0:T(8,128)(2,1)S(1)}, u32[]{:S(2)}, u32[]{:S(2)}) collective-permute-start(bf16[32,2560]{1,0:T(8,128)(2,1)S(1)} %get-tuple-element.74), channel_id=1, source_target_pairs={{0,8},{2,10},{4,12},{6,14},{8,0},{10,2},{12,4},{14,6},{16,24},{18,... | collective-permute-start | bytes 491528 | tf_op jit(solution)/shard_map/ppermute | solution.py:435
  20.2 24.3 %collective-permute-start.4 = (bf16[32,2560]{1,0:T(8,128)(2,1)S(1)}, bf16[32,2560]{1,0:T(8,128)(2,1)S(1)}, u32[]{:S(2)}, u32[]{:S(2)}) collective-permute-start(bf16[32,2560]{1,0:T(8,128)(2,1)S(1)} %get-tuple-element.75), channel_id=1, source_target_pairs={{0,10},{2,8},{4,14},{6,12},{8,2},{10,0},{12,6},{14,4},{16,26},{18,... | collective-permute-start | bytes 491528 | tf_op jit(solution)/shard_map/ppermute | solution.py:435
  22.6 26.1 %collective-permute-start.5 = (bf16[32,2560]{1,0:T(8,128)(2,1)S(1)}, bf16[32,2560]{1,0:T(8,128)(2,1)S(1)}, u32[]{:S(2)}, u32[]{:S(2)}) collective-permute-start(bf16[32,2560]{1,0:T(8,128)(2,1)S(1)} %get-tuple-element.76), channel_id=1, source_target_pairs={{0,12},{2,14},{4,8},{6,10},{8,4},{10,6},{12,0},{14,2},{16,28},{18,... | collective-permute-start | bytes 491528 | tf_op jit(solution)/shard_map/ppermute | solution.py:435
  32.1 19.8 %collective-permute-start.6 = (bf16[32,2560]{1,0:T(8,128)(2,1)S(1)}, bf16[32,2560]{1,0:T(8,128)(2,1)S(1)}, u32[]{:S(2)}, u32[]{:S(2)}) collective-permute-start(bf16[32,2560]{1,0:T(8,128)(2,1)S(1)} %get-tuple-element.77), channel_id=1, source_target_pairs={{0,14},{2,12},{4,10},{6,8},{8,6},{10,4},{12,2},{14,0},{16,30},{18,... | collective-permute-start | bytes 491528 | tf_op jit(solution)/shard_map/ppermute | solution.py:435
  51.9 20.7 %all-to-all-start.1 = ((bf16[8,32,2560]{2,1,0:T(8,128)(2,1)}), bf16[8,32,2560]{2,1,0:T(8,128)(2,1)S(1)}, u32[]{:S(2)}, u32[]{:S(2)}) async-start(bf16[8,32,2560]{2,1,0:T(8,128)(2,1)} %bitcast.11), calls=%async_computation.1 | async-start | bytes 2621440 | tf_op jit(solution)/shard_map/all_to_all | solution.py:414
  60.3 9.6 %collective-permute-start.7 = (f32[64,128]{1,0:T(8,128)S(1)}, f32[64,128]{1,0:T(8,128)S(1)}, u32[]{:S(2)}, u32[]{:S(2)}) collective-permute-start(f32[64,128]{1,0:T(8,128)S(1)} %get-tuple-element.97), channel_id=1, source_target_pairs={{0,16},{1,17},{2,18},{3,19},{4,20},{5,21},{6,22},{7,23},{8,24},{9,... | collective-permute-start | bytes 98312 | tf_op jit(solution)/shard_map/ppermute | solution.py:45
  73.3 7.1 %collective-permute-start.8 = (bf16[16,2560]{1,0:T(8,128)(2,1)S(1)}, bf16[16,2560]{1,0:T(8,128)(2,1)S(1)}, u32[]{:S(2)}, u32[]{:S(2)}) collective-permute-start(bf16[16,2560]{1,0:T(8,128)(2,1)S(1)} %half_pool.1.refs_2_), channel_id=1, source_target_pairs={{0,16},{1,17},{2,18},{3,19},{4,20},{5,21},{6,22},{7,23},{8,24},{9,... | collective-permute-start | bytes 245768 | tf_op jit(solution)/shard_map/ppermute | solution.py:45
  85.0 6.4 %collective-permute-start.12 = (bf16[32,2560]{1,0:T(8,128)(2,1)S(1)}, bf16[32,2560]{1,0:T(8,128)(2,1)S(1)}, u32[]{:S(2)}, u32[]{:S(2)}) collective-permute-start(bf16[32,2560]{1,0:T(8,128)(2,1)S(1)} %constant_dynamic-update-slice_fusion.refs_0_), channel_id=1, source_target_pairs={{0,6},{1,7},{2,4},{3,5},{4,2},{5,3},{6,0},{7,1},{8,14},{9,15},{10,... | collective-permute-start | bytes 491528 | tf_op jit(solution)/shard_map/ppermute | solution.py:45
  86.9 5.6 %collective-permute-start.11 = (bf16[32,2560]{1,0:T(8,128)(2,1)S(1)}, bf16[32,2560]{1,0:T(8,128)(2,1)S(1)}, u32[]{:S(2)}, u32[]{:S(2)}) collective-permute-start(bf16[32,2560]{1,0:T(8,128)(2,1)S(1)} %constant_dynamic-update-slice_fusion.refs_0_), channel_id=1, source_target_pairs={{0,2},{1,5},{2,0},{3,7},{4,6},{5,1},{6,4},{7,3},{8,10},{9,13},{10,... | collective-permute-start | bytes 491528 | tf_op jit(solution)/shard_map/ppermute | solution.py:45
  87.5 5.6 %collective-permute-start.10 = (bf16[32,2560]{1,0:T(8,128)(2,1)S(1)}, bf16[32,2560]{1,0:T(8,128)(2,1)S(1)}, u32[]{:S(2)}, u32[]{:S(2)}) collective-permute-start(bf16[32,2560]{1,0:T(8,128)(2,1)S(1)} %constant_dynamic-update-slice_fusion.refs_0_), channel_id=1, source_target_pairs={{0,4},{1,3},{2,6},{3,1},{4,0},{5,7},{6,2},{7,5},{8,12},{9,11},{10,... | collective-permute-start | bytes 491528 | tf_op jit(solution)/shard_map/ppermute | solution.py:45
  99.4 6.8 %collective-permute-start.14 = (bf16[16,2560]{1,0:T(8,128)(2,1)S(1)}, bf16[16,2560]{1,0:T(8,128)(2,1)S(1)}, u32[]{:S(2)}, u32[]{:S(2)}) collective-permute-start(bf16[16,2560]{1,0:T(8,128)(2,1)S(1)} %get-tuple-element.109.refs_1_), channel_id=1, source_target_pairs={{0,8},{1,9},{2,10},{3,11},{4,12},{5,13},{6,14},{7,15},{8,0},{9,1},... | collective-permute-start | bytes 245768 | tf_op jit(solution)/shard_map/ppermute | solution.py:45
  101.2 6.6 %collective-permute-start.15 = (bf16[16,2560]{1,0:T(8,128)(2,1)S(1)}, bf16[16,2560]{1,0:T(8,128)(2,1)S(1)}, u32[]{:S(2)}, u32[]{:S(2)}) collective-permute-start(bf16[16,2560]{1,0:T(8,128)(2,1)S(1)} %get-tuple-element.110.refs_2_), channel_id=1, source_target_pairs={{0,4},{1,3},{2,6},{3,1},{4,0},{5,7},{6,2},{7,5},{8,12},{9,11},{10,... | collective-permute-start | bytes 245768 | tf_op jit(solution)/shard_map/ppermute | solution.py:45
  102.0 9.7 %collective-permute-start.16 = (bf16[16,2560]{1,0:T(8,128)(2,1)S(1)}, bf16[16,2560]{1,0:T(8,128)(2,1)S(1)}, u32[]{:S(2)}, u32[]{:S(2)}) collective-permute-start(bf16[16,2560]{1,0:T(8,128)(2,1)S(1)} %get-tuple-element.111.refs_3_), channel_id=1, source_target_pairs={{0,12},{1,11},{2,14},{3,9},{4,8},{5,15},{6,10},{7,13},{8,4},{9,3},... | collective-permute-start | bytes 245768 | tf_op jit(solution)/shard_map/ppermute | solution.py:45
  102.9 8.7 %collective-permute-start.17 = (bf16[16,2560]{1,0:T(8,128)(2,1)S(1)}, bf16[16,2560]{1,0:T(8,128)(2,1)S(1)}, u32[]{:S(2)}, u32[]{:S(2)}) collective-permute-start(bf16[16,2560]{1,0:T(8,128)(2,1)S(1)} %get-tuple-element.112.refs_4_), channel_id=1, source_target_pairs={{0,2},{1,5},{2,0},{3,7},{4,6},{5,1},{6,4},{7,3},{8,10},{9,13},{10,... | collective-permute-start | bytes 245768 | tf_op jit(solution)/shard_map/ppermute | solution.py:45
  104.2 7.5 %collective-permute-start.18 = (bf16[16,2560]{1,0:T(8,128)(2,1)S(1)}, bf16[16,2560]{1,0:T(8,128)(2,1)S(1)}, u32[]{:S(2)}, u32[]{:S(2)}) collective-permute-start(bf16[16,2560]{1,0:T(8,128)(2,1)S(1)} %get-tuple-element.113.refs_5_), channel_id=1, source_target_pairs={{0,10},{1,13},{2,8},{3,15},{4,14},{5,9},{6,12},{7,11},{8,2},{9,5},... | collective-permute-start | bytes 245768 | tf_op jit(solution)/shard_map/ppermute | solution.py:45
  106.1 6.2 %collective-permute-start.19 = (bf16[16,2560]{1,0:T(8,128)(2,1)S(1)}, bf16[16,2560]{1,0:T(8,128)(2,1)S(1)}, u32[]{:S(2)}, u32[]{:S(2)}) collective-permute-start(bf16[16,2560]{1,0:T(8,128)(2,1)S(1)} %get-tuple-element.114.refs_6_), channel_id=1, source_target_pairs={{0,6},{1,7},{2,4},{3,5},{4,2},{5,3},{6,0},{7,1},{8,14},{9,15},{10,... | collective-permute-start | bytes 245768 | tf_op jit(solution)/shard_map/ppermute | solution.py:45
  107.8 6.2 %collective-permute-start.20 = (bf16[16,2560]{1,0:T(8,128)(2,1)S(1)}, bf16[16,2560]{1,0:T(8,128)(2,1)S(1)}, u32[]{:S(2)}, u32[]{:S(2)}) collective-permute-start(bf16[16,2560]{1,0:T(8,128)(2,1)S(1)} %get-tuple-element.115.refs_7_), channel_id=1, source_target_pairs={{0,14},{1,15},{2,12},{3,13},{4,10},{5,11},{6,8},{7,9},{8,6},{9,7},... | collective-permute-start | bytes 245768 | tf_op jit(solution)/shard_map/ppermute | solution.py:45
  114.1 6.2 %collective-permute-start.21 = (bf16[16,2560]{1,0:T(8,128)(2,1)S(1)}, bf16[16,2560]{1,0:T(8,128)(2,1)S(1)}, u32[]{:S(2)}, u32[]{:S(2)}) collective-permute-start(bf16[16,2560]{1,0:T(8,128)(2,1)S(1)} %add_convert_fusion.1), channel_id=1, source_target_pairs={{0,16},{1,17},{2,18},{3,19},{4,20},{5,21},{6,22},{7,23},{8,24},{9,... | collective-permute-start | bytes 245768 | tf_op jit(solution)/shard_map/ppermute | solution.py:45
  124.9 8.4 %collective-permute-start.25 = (bf16[32,2560]{1,0:T(8,128)(2,1)S(1)}, bf16[32,2560]{1,0:T(8,128)(2,1)S(1)}, u32[]{:S(2)}, u32[]{:S(2)}) collective-permute-start(bf16[32,2560]{1,0:T(8,128)(2,1)S(1)} %pad_maximum_fusion.refs_0_), channel_id=1, source_target_pairs={{0,6},{1,7},{2,4},{3,5},{4,2},{5,3},{6,0},{7,1},{8,14},{9,15},{10,... | collective-permute-start | bytes 491528 | tf_op jit(solution)/shard_map/ppermute | solution.py:45
  126.1 7.2 %collective-permute-start.24 = (bf16[32,2560]{1,0:T(8,128)(2,1)S(1)}, bf16[32,2560]{1,0:T(8,128)(2,1)S(1)}, u32[]{:S(2)}, u32[]{:S(2)}) collective-permute-start(bf16[32,2560]{1,0:T(8,128)(2,1)S(1)} %pad_maximum_fusion.refs_0_), channel_id=1, source_target_pairs={{0,2},{1,5},{2,0},{3,7},{4,6},{5,1},{6,4},{7,3},{8,10},{9,13},{10,... | collective-permute-start | bytes 491528 | tf_op jit(solution)/shard_map/ppermute | solution.py:45
  127.4 6.0 %collective-permute-start.23 = (bf16[32,2560]{1,0:T(8,128)(2,1)S(1)}, bf16[32,2560]{1,0:T(8,128)(2,1)S(1)}, u32[]{:S(2)}, u32[]{:S(2)}) collective-permute-start(bf16[32,2560]{1,0:T(8,128)(2,1)S(1)} %pad_maximum_fusion.refs_0_), channel_id=1, source_target_pairs={{0,4},{1,3},{2,6},{3,1},{4,0},{5,7},{6,2},{7,5},{8,12},{9,11},{10,... | collective-permute-start | bytes 491528 | tf_op jit(solution)/shard_map/ppermute | solution.py:45
  139.6 5.1 %collective-permute-start.27 = (bf16[16,2560]{1,0:T(8,128)(2,1)S(1)}, bf16[16,2560]{1,0:T(8,128)(2,1)S(1)}, u32[]{:S(2)}, u32[]{:S(2)}) collective-permute-start(bf16[16,2560]{1,0:T(8,128)(2,1)S(1)} %get-tuple-element.130), channel_id=1, source_target_pairs={{0,8},{1,9},{2,10},{3,11},{4,12},{5,13},{6,14},{7,15},{8,0},{9,1},... | collective-permute-start | bytes 245768 | tf_op jit(solution)/shard_map/ppermute | solution.py:45
  139.7 6.1 %collective-permute-start.28 = (bf16[16,2560]{1,0:T(8,128)(2,1)S(1)}, bf16[16,2560]{1,0:T(8,128)(2,1)S(1)}, u32[]{:S(2)}, u32[]{:S(2)}) collective-permute-start(bf16[16,2560]{1,0:T(8,128)(2,1)S(1)} %get-tuple-element.131), channel_id=1, source_target_pairs={{0,4},{1,3},{2,6},{3,1},{4,0},{5,7},{6,2},{7,5},{8,12},{9,11},{10,... | collective-permute-start | bytes 245768 | tf_op jit(solution)/shard_map/ppermute | solution.py:45
  140.7 8.4 %collective-permute-start.29 = (bf16[16,2560]{1,0:T(8,128)(2,1)S(1)}, bf16[16,2560]{1,0:T(8,128)(2,1)S(1)}, u32[]{:S(2)}, u32[]{:S(2)}) collective-permute-start(bf16[16,2560]{1,0:T(8,128)(2,1)S(1)} %get-tuple-element.132), channel_id=1, source_target_pairs={{0,12},{1,11},{2,14},{3,9},{4,8},{5,15},{6,10},{7,13},{8,4},{9,3},... | collective-permute-start | bytes 245768 | tf_op jit(solution)/shard_map/ppermute | solution.py:45
  143.2 5.9 %collective-permute-start.30 = (bf16[16,2560]{1,0:T(8,128)(2,1)S(1)}, bf16[16,2560]{1,0:T(8,128)(2,1)S(1)}, u32[]{:S(2)}, u32[]{:S(2)}) collective-permute-start(bf16[16,2560]{1,0:T(8,128)(2,1)S(1)} %get-tuple-element.133), channel_id=1, source_target_pairs={{0,2},{1,5},{2,0},{3,7},{4,6},{5,1},{6,4},{7,3},{8,10},{9,13},{10,... | collective-permute-start | bytes 245768 | tf_op jit(solution)/shard_map/ppermute | solution.py:45
  143.9 6.1 %collective-permute-start.31 = (bf16[16,2560]{1,0:T(8,128)(2,1)S(1)}, bf16[16,2560]{1,0:T(8,128)(2,1)S(1)}, u32[]{:S(2)}, u32[]{:S(2)}) collective-permute-start(bf16[16,2560]{1,0:T(8,128)(2,1)S(1)} %get-tuple-element.134), channel_id=1, source_target_pairs={{0,10},{1,13},{2,8},{3,15},{4,14},{5,9},{6,12},{7,11},{8,2},{9,5},... | collective-permute-start | bytes 245768 | tf_op jit(solution)/shard_map/ppermute | solution.py:45
  144.7 7.6 %collective-permute-start.32 = (bf16[16,2560]{1,0:T(8,128)(2,1)S(1)}, bf16[16,2560]{1,0:T(8,128)(2,1)S(1)}, u32[]{:S(2)}, u32[]{:S(2)}) collective-permute-start(bf16[16,2560]{1,0:T(8,128)(2,1)S(1)} %get-tuple-element.135), channel_id=1, source_target_pairs={{0,6},{1,7},{2,4},{3,5},{4,2},{5,3},{6,0},{7,1},{8,14},{9,15},{10,... | collective-permute-start | bytes 245768 | tf_op jit(solution)/shard_map/ppermute | solution.py:45
  145.8 6.5 %collective-permute-start.33 = (bf16[16,2560]{1,0:T(8,128)(2,1)S(1)}, bf16[16,2560]{1,0:T(8,128)(2,1)S(1)}, u32[]{:S(2)}, u32[]{:S(2)}) collective-permute-start(bf16[16,2560]{1,0:T(8,128)(2,1)S(1)} %get-tuple-element.136), channel_id=1, source_target_pairs={{0,14},{1,15},{2,12},{3,13},{4,10},{5,11},{6,8},{7,9},{8,6},{9,7},... | collective-permute-start | bytes 245768 | tf_op jit(solution)/shard_map/ppermute | solution.py:45
  (14 other events, 208.1 us)
